TPU v7x, 32 devices: a whole 2x2x4 slice. The times are simulated.
32 devices in a mesh: ctx: 8 (over z, y), head: 4 (over x, core).
Axes of the slice: x: 2, y: 2, z: 4, core: 2. Of those that a mesh axis runs over, the one named last changes fastest.
Arguments:
- queries: bfloat16 [3072, 1024], P('ctx', 'head'), may hold values from -6 to 6
- keys: bfloat16 [3072, 1024], P('ctx', 'head'), may hold values from -6 to 6
- values: bfloat16 [3072, 1024], P('ctx', 'head'), may hold values from -6 to 6
- out_weight: bfloat16 [1024, 5120], P('head'), may hold values from -1.1953125 to 1.1953125
- neighbours: int32 [8, 7], P('ctx'), may hold values from -1 to 7, as said below
- counts: int32 [8], P('ctx'), may hold values from 1 to 7
Outputs:
- projected: bfloat16 [3072, 5120], P(('ctx', 'head'))
Inputs may be any that keep to these rules, and one draw needn't show every extreme that they name: `neighbours`: for query tile g the first counts[g] entries are distinct tiles within 3 of g, g itself among them; the other entries are -1. Some tile lists 7 tiles.
All inputs are finite; a program needn't handle non-finite values.
Results may differ from a plain program's by a relative error of at most 0.019.
Values may be sent and summed in bfloat16 or wider, within the bound.
No kernel may reach another device: no remote copies, remote signals or barrier semaphores. Data moves between devices by JAX's collectives and lax.ppermute only.
A program may use at most 64 MiB of HBM per device.

v0:
```python
import functools
import math

import jax
import jax.numpy as jnp
from jax import lax
from jax.experimental import pallas as pl
from jax.experimental.pallas import tpu as pltpu
from jax.sharding import PartitionSpec as P

HD = 128
REACH = 3
NEG = -1e30
FLAGS = 16
SIDE = 768
COMMON = 1792
PACK = 58
STATE = HD + 8
EXPONENT = math.log2(math.e) / math.sqrt(HD)
BF16, F32 = jnp.bfloat16, jnp.float32

SMEM = pl.BlockSpec(memory_space=pltpu.SMEM)
VMEM = pl.BlockSpec(memory_space=pltpu.VMEM)
HBM = pl.BlockSpec(memory_space=pltpu.HBM)


def call(
    kernel, outs, ins, flops=0, exps=0, moved=1 << 20, scratch=(), alias=None, in_hbm=(), out_hbm=False, vmem=24
):
    scalars = [x.dtype == jnp.int32 for x in ins]
    return pl.pallas_call(
        kernel,
        out_shape=outs,
        in_specs=[SMEM if s else (HBM if i in in_hbm else VMEM) for i, s in enumerate(scalars)],
        out_specs=jax.tree.map(lambda _: HBM if out_hbm else VMEM, outs),
        scratch_shapes=list(scratch),
        input_output_aliases=alias or {},
        compiler_params=pltpu.CompilerParams(vmem_limit_bytes=vmem << 20),
        cost_estimate=pl.CostEstimate(flops=flops, bytes_accessed=moved, transcendentals=exps),
    )(*ins)


def shape(dims, dtype=BF16):
    return jax.ShapeDtypeStruct(dims, dtype)


def pack_kernel(
    tile_ref, list_ref, count_ref, q_ref, k_ref, v_ref, w_ref,
    keep_ref, send_ref, side_ref, common_ref, sems,
):
    parity = tile_ref[0] & 1
    rows = q_ref.shape[0]
    copies = []

    def copy(source, target):
        copies.append(pltpu.make_async_copy(source, target, sems.at[len(copies)]))
        copies[-1].start()

    for out, head in ((send_ref, 1 - parity), (keep_ref, parity)):
        columns = pl.ds(pl.multiple_of(head * HD, HD), HD)
        for i, ref in enumerate((k_ref, v_ref, q_ref)):
            copy(ref.at[:, columns], out.at[pl.ds(i * rows, rows)])
    side = side_ref.shape[1]
    copy(w_ref.at[:, pl.ds(pl.multiple_of(parity * side, HD), side)], side_ref)
    copy(w_ref.at[:, pl.ds(2 * side, common_ref.shape[1])], common_ref)
    lane = lax.broadcasted_iota(jnp.int32, (FLAGS, HD), 1)
    flags = jnp.zeros((FLAGS, HD), F32)
    for offset in range(-REACH, REACH + 1):
        listed = jnp.int32(0)
        for slot in range(list_ref.shape[1]):
            found = (list_ref[0, slot] == tile_ref[0] + offset) & (slot < count_ref[0])
            listed = jnp.where(found, 1, listed)
        flags = jnp.where(lane == offset + REACH, listed.astype(F32), flags)
    keep_ref[3 * rows :, :] = flags.astype(BF16)
    send_ref[3 * rows :, :] = flags.astype(BF16)
    for each in copies:
        each.wait()


def merge_kernel(tile_ref, keep_ref, came_ref, flag_ref, q_ref, both_ref, odd_ref, even_ref):
    parity = tile_ref[0] & 1
    rows = q_ref.shape[1]
    both_ref[0 : 2 * rows, :] = keep_ref[0 : 2 * rows, :]
    both_ref[2 * rows :, :] = came_ref[0 : 2 * rows, :]
    up = (tile_ref[0] & 4) == 0

    def place(out, own):
        @pl.when(own)
        def _():
            out[...] = keep_ref[0 : 2 * rows, :]

        @pl.when(jnp.logical_not(own))
        def _():
            out[...] = came_ref[0 : 2 * rows, :]

    place(odd_ref, up == (parity == 1))
    if even_ref is not None:
        place(even_ref, up == (parity == 0))
    q_ref[parity] = keep_ref[2 * rows : 3 * rows, :]
    q_ref[1 - parity] = came_ref[2 * rows : 3 * rows, :]
    own = keep_ref[3 * rows :, :].astype(F32)
    other = came_ref[3 * rows :, :].astype(F32)
    even = jnp.where(parity == 0, own, other)[0:8]
    odd = jnp.where(parity == 0, other, own)[0:8]
    row = lax.broadcasted_iota(jnp.int32, (8, HD), 0)
    flag_ref[...] = jnp.where(row == 0, even, odd).astype(jnp.int32)


def step(query, key, value, state_ref, a):
    scores = lax.dot_general(
        key, query, (((1,), (1,)), ((), ())), preferred_element_type=F32
    )
    old = state_ref[a, HD : HD + 1, :]
    new = jnp.maximum(old, jnp.max(scores, axis=0, keepdims=True))
    weights = jnp.exp2((scores - new) * EXPONENT)
    shrink = jnp.exp2((old - new) * EXPONENT)
    state_ref[a, HD : HD + 1, :] = new
    state_ref[a, HD + 1 : HD + 2, :] = state_ref[a, HD + 1 : HD + 2, :] * shrink + jnp.sum(
        weights, axis=0, keepdims=True
    )
    state_ref[a, 0:HD, :] = state_ref[a, 0:HD, :] * shrink + lax.dot_general(
        value, weights.astype(BF16), (((0,), (0,)), ((), ())), preferred_element_type=F32
    )


def visit(flag_ref, q_ref, state_ref, pairs):
    rows = q_ref.shape[1]
    for a, tile, ref, at in pairs:

        @pl.when(flag_ref[a, tile - a + REACH] > 0)
        def _():
            key, value = ref[at : at + rows, :], ref[at + rows : at + 2 * rows, :]
            step(q_ref[a], key, value, state_ref, a)


def visit_pair(flag_ref, tile_ref, q_ref, state_ref, base, ref):
    parity = tile_ref[0] & 1
    rows = q_ref.shape[1]
    tiles = ((base + parity, 0), (base + 1 - parity, 2 * rows))
    visit(flag_ref, q_ref, state_ref, [(a, t, ref, at) for t, at in tiles for a in range(2)])


def first_kernel(flag_ref, tile_ref, q_ref, both_ref, state_ref):
    state_ref[...] = jnp.zeros_like(state_ref)
    for a in range(2):
        state_ref[a, HD : HD + 1, :] = jnp.full((1, state_ref.shape[2]), NEG, F32)
    visit_pair(flag_ref, tile_ref, q_ref, state_ref, 0, both_ref)


def second_kernel(flag_ref, tile_ref, q_ref, first_ref, second_ref, _, state_ref):
    base = jnp.where((tile_ref[0] & 2) == 0, 2, -2)
    visit_pair(flag_ref, tile_ref, q_ref, state_ref, base, first_ref)
    visit_pair(flag_ref, tile_ref, q_ref, state_ref, -base, second_ref)


def third_kernel(flag_ref, tile_ref, head_ref, q_ref, state_ref, *refs, far):
    outs, last = refs[far:-1], refs[-1]
    last[...] = state_ref[...]
    for i in range(far):
        above = ((tile_ref[0] & 4) == 0) == (i == 0)
        which = (jnp.where(above, 1, 0), jnp.where(above, 4, -3), refs[i], 0)
        visit(flag_ref, q_ref, last, [which])
    parity = tile_ref[0] & 1
    core = head_ref[0] & 1
    for i, a in enumerate((parity, 1 - parity)):
        done = last[a, 0:HD, :] / last[a, HD + 1 : HD + 2, :]
        rows = done.T.astype(BF16)
        if len(outs) == 2:
            outs[i][...] = rows
        else:
            half = outs[0].shape[1]
            for chip in range(2):
                even = rows[(2 * chip) * half : (2 * chip + 1) * half]
                odd = rows[(2 * chip + 1) * half : (2 * chip + 2) * half]
                outs[2 * i][chip] = jnp.where(core == 0, even, odd)
                outs[2 * i + 1][chip] = jnp.where(core == 0, odd, even)


CHUNK = 512


def multiply(left, weights, start, stop):
    depth = weights[0].shape[0]
    return sum(
        jnp.dot(
            left[:, i * depth : (i + 1) * depth], w[:, start:stop], preferred_element_type=F32
        )
        for i, w in enumerate(weights)
    )


def send_kernel(
    tile_ref, head_ref, own_ref, y_ref, core_ref, cross_ref, w_ref, wp_ref, a_ref, far_ref
):
    parity = tile_ref[0] & 1
    chip = head_ref[0] >> 1
    deep = a_ref.shape[1]
    for out, which in ((a_ref, chip), (far_ref, 1 - chip)):
        for group, (mine, others) in enumerate(((own_ref, y_ref), (core_ref, cross_ref))):
            base = group * 2 * HD
            out[:, pl.ds(pl.multiple_of(base + parity * HD, HD), HD)] = mine[which]
            out[:, pl.ds(pl.multiple_of(base + (1 - parity) * HD, HD), HD)] = others[which]
    far = far_ref[:, 0:deep]
    term = far_ref.shape[1] - deep
    gathered = w_ref.shape[1] - term
    for start in range(0, term, CHUNK):
        stop = min(start + CHUNK, term)
        far_ref[:, deep + start : deep + stop] = multiply(
            far, (w_ref, wp_ref), gathered + start, gathered + stop
        ).astype(BF16)


def near_kernel(a_ref, w_ref, wp_ref, near_ref):
    own = a_ref[...]
    for start in range(0, w_ref.shape[1], CHUNK):
        near_ref[:, start : start + CHUNK] = multiply(own, (w_ref, wp_ref), start, start + CHUNK)


def last_kernel(tile_ref, near_ref, far_ref, *refs):
    weights, out_ref = refs[:-1], refs[-1]
    parity = tile_ref[0] & 1
    deep = 2 * weights[0].shape[0]
    side = weights[0].shape[1]
    far = far_ref[:, 0:deep]
    places = (parity * side, (1 - parity) * side, 2 * side)
    for i, at in enumerate(places):
        pair = weights[2 * i : 2 * i + 2]
        for start in range(0, pair[0].shape[1], CHUNK):
            stop = min(start + CHUNK, pair[0].shape[1])
            columns = pl.ds(at + start, stop - start)
            if i < 2:
                columns = pl.ds(pl.multiple_of(at + start, HD), stop - start)
            out_ref[:, columns] = (
                near_ref[:, columns] + multiply(far, pair, start, stop)
            ).astype(BF16)
    gathered = 2 * side + weights[4].shape[1]
    out_ref[:, gathered:] = (near_ref[:, gathered:] + far_ref[:, deep:].astype(F32)).astype(BF16)


def swap_pairs(value, distance, phase):
    count = lax.axis_size("ctx")
    pairs = []
    for i in range(count - 2 * distance):
        if (i // 2 // distance) % 2 == phase:
            pairs += [(i, i + 2 * distance), (i + 2 * distance, i)]
    return lax.ppermute(value, "ctx", pairs)


def swap_tiles(value):
    return lax.ppermute(value, "ctx", [(i, i ^ 1) for i in range(lax.axis_size("ctx"))])


def swap_cores(value):
    return lax.ppermute(value, "head", [(i, i ^ 1) for i in range(lax.axis_size("head"))])


def swap_both(value):
    heads = lax.axis_size("head")
    count = lax.axis_size("ctx") * heads
    pairs = [(i, ((i // heads) ^ 1) * heads + ((i % heads) ^ 1)) for i in range(count)]
    return lax.ppermute(value, ("ctx", "head"), pairs)


def from_chip(value, steps):
    count = lax.axis_size("head")
    return lax.ppermute(value, "head", [((i + 2 * steps) % count, i) for i in range(count)])


def project_any(attended, out_weight, weight_pair, head_index):
    rows, width = attended.shape
    n_head = lax.axis_size("head")
    chips, own_rows = n_head // 2, rows // n_head
    chip, core = head_index // 2, head_index % 2
    blocks = attended.reshape(chips, 2, own_rows, width)
    mine = lax.dynamic_index_in_dim(blocks, core, 1, keepdims=False)
    theirs = lax.dynamic_index_in_dim(blocks, 1 - core, 1, keepdims=False)
    joined = jnp.concatenate([mine, swap_cores(theirs)], axis=2)

    def project(steps):
        block = lax.dynamic_index_in_dim(joined, (chip - steps) % chips, 0, keepdims=False)
        return multiply(block, (out_weight, weight_pair), 0, out_weight.shape[1])

    total = project(0)
    for steps in range(1, chips):
        total = total + from_chip(project(steps).astype(BF16), steps).astype(F32)
    return total.astype(BF16)


def local(queries, keys, values, out_weight, neighbours, counts):
    rows, width = queries.shape
    n_head = lax.axis_size("head")
    own_rows = rows // n_head
    model = out_weight.shape[1]
    small = n_head == 4 and own_rows % 16 == 0
    head_index = lax.axis_index("head").astype(jnp.int32)
    head = head_index.reshape(1)
    tile = lax.axis_index("ctx").astype(jnp.int32).reshape(1)

    one = (rows, HD)
    payload, kv_shape = shape((3 * rows + FLAGS, HD)), shape((2 * rows, HD))
    keep, send, side_weight, common_weight = call(
        pack_kernel,
        (payload, payload, shape((width, SIDE)), shape((width, COMMON))),
        (tile, neighbours, counts, queries, keys, values, out_weight),
        scratch=(pltpu.SemaphoreType.DMA((8,)),),
        in_hbm=(3, 4, 5, 6),
        vmem=PACK,
    )
    came = swap_tiles(send)
    weight_ready, keep = lax.optimization_barrier((out_weight, keep))
    weight_pair = swap_cores(weight_ready)
    came, weight_pair = lax.optimization_barrier((came, weight_pair))
    if small:
        side_own = from_chip(side_weight, 1)

    far = 1 if lax.axis_size("ctx") <= 8 else 2
    flags, q_pair, both, *to_far = call(
        merge_kernel if far == 2 else functools.partial(merge_kernel, even_ref=None),
        (shape((8, HD), jnp.int32), shape((2,) + one), shape((4 * rows, HD))) + (kv_shape,) * far,
        (tile, keep, came),
    )
    nearest = [swap_pairs(both, 1, phase) for phase in range(2)]
    farther = [swap_pairs(to_far[i], 2, i) for i in range(far)]

    state = shape((2, STATE, rows), F32)
    area = rows * rows
    held = call(first_kernel, state, (flags, tile, q_pair, both), 16 * area * HD, 4 * area)
    q_again = q_pair
    if small:
        side_own, q_again = lax.optimization_barrier((side_own, q_pair))
        side_other = swap_tiles(side_own)
        common_ready, _ = lax.optimization_barrier((common_weight, side_own))
        common = from_chip(common_ready, 1)
    held = call(
        second_kernel,
        state,
        (flags, tile, q_again, *nearest, held),
        32 * area * HD,
        8 * area,
        alias={5: 0},
    )
    if small:
        ready, held = lax.optimization_barrier((side_own, held))
        far_weights = [side_own, swap_cores(ready)]
        held, side_other = lax.optimization_barrier((held, side_other))
    block = (2, own_rows, HD)
    attended = call(
        functools.partial(third_kernel, far=far),
        (shape(block),) * 4 if small else (shape(one),) * 2,
        (flags, tile, head, q_pair, held, *farther),
        4 * area * HD,
        area,
        scratch=(pltpu.VMEM(state.shape, F32),),
    )
    if not small:
        mine, theirs = attended
        got = swap_tiles(theirs)
        even_tile = tile[0] % 2 == 0
        joined = jnp.concatenate(
            [jnp.where(even_tile, mine, got), jnp.where(even_tile, got, mine)], axis=1
        )
        return project_any(joined, out_weight, weight_pair, head_index)

    mine, mine_other, theirs, theirs_other = attended
    from_cross = swap_both(theirs_other)
    from_y = swap_tiles(theirs)
    from_core = swap_cores(mine_other)
    ready, _ = lax.optimization_barrier((side_other, mine))
    far_weights += [side_other, swap_cores(ready), common]
    from_cross, from_y, from_core, *far_weights = lax.optimization_barrier(
        (from_cross, from_y, from_core, *far_weights)
    )
    far_weights.append(swap_cores(far_weights[-1]))

    flops = 2 * own_rows * 2 * width * model
    near_weights = (out_weight, weight_pair)
    deep, gathered = 2 * width, 2 * SIDE + COMMON
    own_a, far_a = call(
        send_kernel,
        (shape((own_rows, deep)), shape((own_rows, deep + model - gathered))),
        (tile, head, mine, from_y, from_core, from_cross) + near_weights,
        flops // 4,
    )
    got = from_chip(far_a, 1)
    near = call(near_kernel, shape((own_rows, model), F32), (own_a,) + near_weights, flops)
    return call(
        last_kernel, shape((own_rows, model)), (tile, near, got, *far_weights), flops
    )


def solution(mesh):
    placed = (
        P("ctx", "head"),
        P("ctx", "head"),
        P("ctx", "head"),
        P("head", None),
        P("ctx", None),
        P("ctx"),
    )
    return jax.shard_map(
        local, mesh=mesh, in_specs=placed, out_specs=P(("ctx", "head"), None), check_vma=False
    )
```

profile of v0, /device:TPU:0, one launch (start us, length us, event | category | flops | bytes accessed | tf_op | source)
XLA Modules:
  0.0 66.9 jit_solution(11385006599369475065)
XLA Ops:
  0.0 0.0 copy-start
  0.8 3.6 %shard_map.64 = (bf16[1168,128]{1,0:T(8,128)(2,1)}, bf16[1168,128]{1,0:T(8,128)(2,1)}, bf16[256,768]{1,0:T(8,128)(2,1)}, bf16[256,1792]{1,0:T(8,128)(2,1)}) custom-call(s32[1]{0:T(128)} %bitcast.tile_ref, s32[1,7]{1,0:T(1,128)} %list_ref.1, s32[1]{0:T(128)S(6)} %copy.9.count_ref, bf16[384,256]{1,0:T(8,128)(2,1)} %q_ref.1, bf16[384,256]{1,0:T(8,128)(2,1)} %k_ref.1, ...), custom_call_target="tpu_custom_call" | custom-call | bytes 1048576 | tf_op jit(solution)/shard_map/pallas_call | solution.py:31
  4.4 0.0 copy-done
  4.4 0.5 collective-permute-start.1
  4.9 2.6 %collective-permute-start.2 = (bf16[256,768]{1,0:T(8,128)(2,1)}, bf16[256,768]{1,0:T(8,128)(2,1)}, u32[]{:S(2)}, u32[]{:S(2)}) collective-permute-start(bf16[256,768]{1,0:T(8,128)(2,1)} %get-tuple-element.46), channel_id=1, source_target_pairs={{2,0},{3,1},{0,2},{1,3},{6,4},{7,5},{4,6},{5,7},{10,8},{11,9},{8,1... | collective-permute-start | bytes 1179656 | tf_op jit(solution)/shard_map/ppermute | solution.py:266
  7.5 1.5 %collective-permute-start = (bf16[1168,128]{1,0:T(8,128)(2,1)}, bf16[1168,128]{1,0:T(8,128)(2,1)S(1)}, u32[]{:S(2)}, u32[]{:S(2)}) collective-permute-start(bf16[1168,128]{1,0:T(8,128)(2,1)} %get-tuple-element.41), channel_id=1, source_target_pairs={{0,4},{4,0},{8,12},{12,8},{16,20},{20,16},{24,28},{28,24},{1,5},{5... | collective-permute-start | bytes 897032 | tf_op jit(solution)/shard_map/ppermute | solution.py:250
  9.0 7.9 %collective-permute-done.came_ref = bf16[1168,128]{1,0:T(8,128)(2,1)S(1)} collective-permute-done((bf16[1168,128]{1,0:T(8,128)(2,1)}, bf16[1168,128]{1,0:T(8,128)(2,1)S(1)}, u32[]{:S(2)}, u32[]{:S(2)}) %collective-permute-start) | collective-permute-done | bytes 299040 | tf_op jit(solution)/shard_map/ppermute | solution.py:250
  16.9 0.0 collective-permute-done.1.wp_ref
  16.9 0.0 copy-start.1
  16.9 1.5 %copy-done.1 = bf16[256,5120]{1,0:T(8,128)(2,1)} copy-done((bf16[256,5120]{1,0:T(8,128)(2,1)}, bf16[256,5120]{1,0:T(8,128)(2,1)S(1)}, u32[]{:S(2)}) %copy-start.1) | copy-done | bytes 2621464
  18.4 0.0 copy-start.3
  18.4 1.0 %copy-done.3 = bf16[1168,128]{1,0:T(8,128)(2,1)S(1)} copy-done((bf16[1168,128]{1,0:T(8,128)(2,1)S(1)}, bf16[1168,128]{1,0:T(8,128)(2,1)}, u32[]{:S(2)}) %copy-start.3) | copy-done | bytes 299032
  19.3 0.9 %shard_map.65 = (s32[8,128]{1,0:T(8,128)S(1)}, bf16[2,384,128]{2,1,0:T(8,128)(2,1)S(1)}, bf16[1536,128]{1,0:T(8,128)(2,1)}, bf16[768,128]{1,0:T(8,128)(2,1)}) custom-call(s32[1]{0:T(128)} %bitcast.tile_ref, bf16[1168,128]{1,0:T(8,128)(2,1)S(1)} %copy-done.3, bf16[1168,128]{1,0:T(8,128)(2,1)S(1)} %collective-permute-done.came_ref), custom_call_target="tpu_custom_call" | custom-call | bytes 1048576 | tf_op jit(solution)/shard_map/pallas_call | solution.py:31
  20.2 0.0 copy-start.4
  20.2 0.7 %copy-done.4 = bf16[2,384,128]{2,1,0:T(8,128)(2,1)} copy-done((bf16[2,384,128]{2,1,0:T(8,128)(2,1)}, bf16[2,384,128]{2,1,0:T(8,128)(2,1)S(1)}, u32[]{:S(2)}) %copy-start.4) | copy-done | bytes 196632
  20.9 0.0 collective-permute-done.2.refs_0_
  20.9 0.3 collective-permute-start.12
  21.2 1.4 %collective-permute-start.4 = (bf16[1536,128]{1,0:T(8,128)(2,1)}, bf16[1536,128]{1,0:T(8,128)(2,1)}, u32[]{:S(2)}, u32[]{:S(2)}) collective-permute-start(bf16[1536,128]{1,0:T(8,128)(2,1)} %get-tuple-element.49.both_ref), channel_id=1, source_target_pairs={{8,16},{16,8},{12,20},{20,12},{9,17},{17,9},{13,21},{21,13},{10,18... | collective-permute-start | bytes 1179656 | tf_op jit(solution)/shard_map/ppermute | solution.py:246
  22.6 3.9 %collective-permute-start.3 = (bf16[1536,128]{1,0:T(8,128)(2,1)}, bf16[1536,128]{1,0:T(8,128)(2,1)}, u32[]{:S(2)}, u32[]{:S(2)}) collective-permute-start(bf16[1536,128]{1,0:T(8,128)(2,1)} %get-tuple-element.49.both_ref), channel_id=1, source_target_pairs={{0,8},{8,0},{4,12},{12,4},{16,24},{24,16},{20,28},{28,20},{1,9},{9... | collective-permute-start | bytes 1179656 | tf_op jit(solution)/shard_map/ppermute | solution.py:246
  26.6 1.5 %collective-permute-start.5 = (bf16[256,768]{1,0:T(8,128)(2,1)}, bf16[256,768]{1,0:T(8,128)(2,1)}, u32[]{:S(2)}, u32[]{:S(2)}) collective-permute-start(bf16[256,768]{1,0:T(8,128)(2,1)} %collective-permute-done.2.refs_0_), channel_id=1, source_target_pairs={{0,4},{4,0},{8,12},{12,8},{16,20},{20,16},{24,28},{28,24},{1,5},{5... | collective-permute-start | bytes 1179656 | tf_op jit(solution)/shard_map/ppermute | solution.py:250
  28.1 0.5 collective-permute-start.6
  28.6 0.0 copy-start.2
  28.6 0.0 copy-start.5
  28.6 1.1 %copy-done.5 = bf16[2,384,128]{2,1,0:T(8,128)(2,1)S(1)} copy-done((bf16[2,384,128]{2,1,0:T(8,128)(2,1)S(1)}, bf16[2,384,128]{2,1,0:T(8,128)(2,1)}, u32[]{:S(2)}) %copy-start.5) | copy-done | bytes 196632
  29.6 2.8 %shard_map.66._ = f32[2,136,384]{2,1,0:T(8,128)S(1)} custom-call(s32[8,128]{1,0:T(8,128)S(1)} %get-tuple-element.44.flag_ref, s32[1]{0:T(128)} %bitcast.tile_ref, bf16[2,384,128]{2,1,0:T(8,128)(2,1)S(1)} %copy-done.5, bf16[1536,128]{1,0:T(8,128)(2,1)} %get-tuple-element.49.both_ref), custom_call_target="tpu_custom_call" | custom-call | flops 301989888 | bytes 1048576 | tf_op jit(solution)/shard_map/pallas_call | solution.py:31
  32.4 0.0 collective-permute-done.4.second_ref
  32.4 4.0 %collective-permute-done.3.first_ref = bf16[1536,128]{1,0:T(8,128)(2,1)} collective-permute-done((bf16[1536,128]{1,0:T(8,128)(2,1)}, bf16[1536,128]{1,0:T(8,128)(2,1)}, u32[]{:S(2)}, u32[]{:S(2)}) %collective-permute-start.3) | collective-permute-done | bytes 393248 | tf_op jit(solution)/shard_map/ppermute | solution.py:246
  36.4 2.9 %shard_map.67.state_ref = f32[2,136,384]{2,1,0:T(8,128)S(1)} custom-call(s32[8,128]{1,0:T(8,128)S(1)} %get-tuple-element.44.flag_ref, s32[1]{0:T(128)} %bitcast.tile_ref, bf16[2,384,128]{2,1,0:T(8,128)(2,1)S(1)} %copy-done.5, bf16[1536,128]{1,0:T(8,128)(2,1)} %collective-permute-done.3.first_ref, ...), custom_call_target="tpu_custom_call", output_to_operand_aliasing={{}: (5, {})} | custom-call | flops 603979776 | bytes 1048576 | tf_op jit(solution)/shard_map/pallas_call | solution.py:31
  39.4 0.0 collective-permute-done.5.refs_2_
  39.4 3.9 %collective-permute-done.6.refs_0_ = bf16[768,128]{1,0:T(8,128)(2,1)} collective-permute-done((bf16[768,128]{1,0:T(8,128)(2,1)}, bf16[768,128]{1,0:T(8,128)(2,1)}, u32[]{:S(2)}, u32[]{:S(2)}) %collective-permute-start.6) | collective-permute-done | bytes 196640 | tf_op jit(solution)/shard_map/ppermute | solution.py:246
  43.3 1.7 %shard_map.68 = (bf16[2,96,128]{2,1,0:T(8,128)(2,1)S(1)}, bf16[2,96,128]{2,1,0:T(8,128)(2,1)S(1)}, bf16[2,96,128]{2,1,0:T(8,128)(2,1)S(1)}, bf16[2,96,128]{2,1,0:T(8,128)(2,1)S(1)}) custom-call(s32[8,128]{1,0:T(8,128)S(1)} %get-tuple-element.44.flag_ref, s32[1]{0:T(128)} %bitcast.tile_ref, s32[1]{0:T(128)} %bitcast.1.head_ref, ...), custom_call_target="tpu_custom_call" | custom-call | flops 75497472 | bytes 1048576 | tf_op jit(solution)/shard_map/pallas_call | solution.py:31
  45.0 0.1 collective-permute-start.11
  45.1 0.5 collective-permute-start.10
  45.6 1.2 %collective-permute-start.7 = (bf16[2,96,128]{2,1,0:T(8,128)(2,1)S(1)}, bf16[2,96,128]{2,1,0:T(8,128)(2,1)S(1)}, u32[]{:S(2)}, u32[]{:S(2)}) collective-permute-start(bf16[2,96,128]{2,1,0:T(8,128)(2,1)S(1)} %get-tuple-element.54), channel_id=1, source_target_pairs={{0,5},{1,4},{2,7},{3,6},{4,1},{5,0},{6,3},{7,2},{8,13},{9,12},{10,... | collective-permute-start | bytes 147464 | tf_op jit(solution)/shard_map/ppermute | solution.py:261
  46.8 0.5 collective-permute-start.8
  47.3 2.1 %collective-permute-done.7.cross_ref = bf16[2,96,128]{2,1,0:T(8,128)(2,1)S(1)} collective-permute-done((bf16[2,96,128]{2,1,0:T(8,128)(2,1)S(1)}, bf16[2,96,128]{2,1,0:T(8,128)(2,1)S(1)}, u32[]{:S(2)}, u32[]{:S(2)}) %collective-permute-start.7) | collective-permute-done | bytes 49184 | tf_op jit(solution)/shard_map/ppermute | solution.py:261
  49.3 0.1 collective-permute-start.9
  49.5 1.4 %collective-permute-done.8.y_ref = bf16[2,96,128]{2,1,0:T(8,128)(2,1)S(1)} collective-permute-done((bf16[2,96,128]{2,1,0:T(8,128)(2,1)S(1)}, bf16[2,96,128]{2,1,0:T(8,128)(2,1)S(1)}, u32[]{:S(2)}, u32[]{:S(2)}) %collective-permute-start.8) | collective-permute-done | bytes 49184 | tf_op jit(solution)/shard_map/ppermute | solution.py:250
  50.8 0.0 collective-permute-done.9.core_ref
  50.9 0.0 collective-permute-done.11.refs_3_
  50.9 0.0 collective-permute-done.10.refs_1_
  50.9 0.0 collective-permute-done.12.refs_4_
  50.9 0.1 collective-permute-start.14
  50.9 0.0 copy-done.2
  51.0 0.5 shard_map.69
  51.4 1.6 %collective-permute-start.13 = (bf16[96,2304]{1,0:T(8,128)(2,1)S(1)}, bf16[96,2304]{1,0:T(8,128)(2,1)S(1)}, u32[]{:S(2)}, u32[]{:S(2)}) collective-permute-start(bf16[96,2304]{1,0:T(8,128)(2,1)S(1)} %get-tuple-element.67), channel_id=1, source_target_pairs={{2,0},{3,1},{0,2},{1,3},{6,4},{7,5},{4,6},{5,7},{10,8},{11,9},{8,1... | collective-permute-start | bytes 1327112 | tf_op jit(solution)/shard_map/ppermute | solution.py:266
  53.0 1.0 %shard_map.70.near_ref = f32[96,5120]{1,0:T(8,128)S(1)} custom-call(bf16[96,512]{1,0:T(8,128)(2,1)S(1)} %get-tuple-element.66.a_ref, bf16[256,5120]{1,0:T(8,128)(2,1)S(1)} %copy-done, bf16[256,5120]{1,0:T(8,128)(2,1)S(1)} %copy-done.2), custom_call_target="tpu_custom_call" | custom-call | flops 503316480 | bytes 1048576 | tf_op jit(solution)/shard_map/pallas_call | solution.py:31
  54.0 10.0 %collective-permute-done.13.far_ref = bf16[96,2304]{1,0:T(8,128)(2,1)S(1)} collective-permute-done((bf16[96,2304]{1,0:T(8,128)(2,1)S(1)}, bf16[96,2304]{1,0:T(8,128)(2,1)S(1)}, u32[]{:S(2)}, u32[]{:S(2)}) %collective-permute-start.13) | collective-permute-done | bytes 442400 | tf_op jit(solution)/shard_map/ppermute | solution.py:266
  64.1 0.0 collective-permute-done.14.refs_5_
  64.1 2.9 %shard_map.71 = bf16[96,5120]{1,0:T(8,128)(2,1)} custom-call(s32[1]{0:T(128)} %bitcast.tile_ref, f32[96,5120]{1,0:T(8,128)S(1)} %shard_map.70.near_ref, bf16[96,2304]{1,0:T(8,128)(2,1)S(1)} %collective-permute-done.13.far_ref, bf16[256,768]{1,0:T(8,128)(2,1)} %collective-permute-done.2.refs_0_, bf16[256,768]{1,0:T(8,128)(2,1)S(1)} %collective-permute-done.10.refs_1_, ...), custom_call_target="tpu_custom_call" | custom-call | flops 503316480 | bytes 1048576 | tf_op jit(solution)/shard_map/pallas_call | solution.py:31
Async XLA Ops:
  0.0 4.4 %copy-start = (bf16[256,5120]{1,0:T(8,128)(2,1)S(1)}, bf16[256,5120]{1,0:T(8,128)(2,1)}, u32[]{:S(2)}) copy-start(bf16[256,5120]{1,0:T(8,128)(2,1)} %w_ref.5) | copy-start | bytes 7864324
  4.4 12.5 %collective-permute-start.1 = (bf16[256,5120]{1,0:T(8,128)(2,1)S(1)}, bf16[256,5120]{1,0:T(8,128)(2,1)S(1)}, u32[]{:S(2)}, u32[]{:S(2)}) collective-permute-start(bf16[256,5120]{1,0:T(8,128)(2,1)S(1)} %copy-done), channel_id=1, source_target_pairs={{0,1},{1,0},{2,3},{3,2},{4,5},{5,4},{6,7},{7,6},{8,9},{9,8},{10,11... | collective-permute-start | bytes 7864328 | tf_op jit(solution)/shard_map/ppermute | solution.py:254
  4.9 16.0 %collective-permute-start.2 = (bf16[256,768]{1,0:T(8,128)(2,1)}, bf16[256,768]{1,0:T(8,128)(2,1)}, u32[]{:S(2)}, u32[]{:S(2)}) collective-permute-start(bf16[256,768]{1,0:T(8,128)(2,1)} %get-tuple-element.46), channel_id=1, source_target_pairs={{2,0},{3,1},{0,2},{1,3},{6,4},{7,5},{4,6},{5,7},{10,8},{11,9},{8,1... | collective-permute-start | bytes 1179656 | tf_op jit(solution)/shard_map/ppermute | solution.py:266
  7.5 9.4 %collective-permute-start = (bf16[1168,128]{1,0:T(8,128)(2,1)}, bf16[1168,128]{1,0:T(8,128)(2,1)S(1)}, u32[]{:S(2)}, u32[]{:S(2)}) collective-permute-start(bf16[1168,128]{1,0:T(8,128)(2,1)} %get-tuple-element.41), channel_id=1, source_target_pairs={{0,4},{4,0},{8,12},{12,8},{16,20},{20,16},{24,28},{28,24},{1,5},{5... | collective-permute-start | bytes 897032 | tf_op jit(solution)/shard_map/ppermute | solution.py:250
  16.9 1.5 %copy-start.1 = (bf16[256,5120]{1,0:T(8,128)(2,1)}, bf16[256,5120]{1,0:T(8,128)(2,1)S(1)}, u32[]{:S(2)}) copy-start(bf16[256,5120]{1,0:T(8,128)(2,1)S(1)} %collective-permute-done.1.wp_ref) | copy-start | bytes 7864324
  18.4 1.0 %copy-start.3 = (bf16[1168,128]{1,0:T(8,128)(2,1)S(1)}, bf16[1168,128]{1,0:T(8,128)(2,1)}, u32[]{:S(2)}) copy-start(bf16[1168,128]{1,0:T(8,128)(2,1)} %get-tuple-element.40.keep_ref) | copy-start | bytes 897028
  20.2 0.7 %copy-start.4 = (bf16[2,384,128]{2,1,0:T(8,128)(2,1)}, bf16[2,384,128]{2,1,0:T(8,128)(2,1)S(1)}, u32[]{:S(2)}) copy-start(bf16[2,384,128]{2,1,0:T(8,128)(2,1)S(1)} %get-tuple-element.48.q_ref) | copy-start | bytes 589828
  20.9 29.9 %collective-permute-start.12 = (bf16[256,1792]{1,0:T(8,128)(2,1)}, bf16[256,1792]{1,0:T(8,128)(2,1)S(1)}, u32[]{:S(2)}, u32[]{:S(2)}) collective-permute-start(bf16[256,1792]{1,0:T(8,128)(2,1)} %get-tuple-element.61), channel_id=1, source_target_pairs={{2,0},{3,1},{0,2},{1,3},{6,4},{7,5},{4,6},{5,7},{10,8},{11,9},{8,1... | collective-permute-start | bytes 2752520 | tf_op jit(solution)/shard_map/ppermute | solution.py:266
  21.2 11.2 %collective-permute-start.4 = (bf16[1536,128]{1,0:T(8,128)(2,1)}, bf16[1536,128]{1,0:T(8,128)(2,1)}, u32[]{:S(2)}, u32[]{:S(2)}) collective-permute-start(bf16[1536,128]{1,0:T(8,128)(2,1)} %get-tuple-element.49.both_ref), channel_id=1, source_target_pairs={{8,16},{16,8},{12,20},{20,12},{9,17},{17,9},{13,21},{21,13},{10,18... | collective-permute-start | bytes 1179656 | tf_op jit(solution)/shard_map/ppermute | solution.py:246
  22.6 13.8 %collective-permute-start.3 = (bf16[1536,128]{1,0:T(8,128)(2,1)}, bf16[1536,128]{1,0:T(8,128)(2,1)}, u32[]{:S(2)}, u32[]{:S(2)}) collective-permute-start(bf16[1536,128]{1,0:T(8,128)(2,1)} %get-tuple-element.49.both_ref), channel_id=1, source_target_pairs={{0,8},{8,0},{4,12},{12,4},{16,24},{24,16},{20,28},{28,20},{1,9},{9... | collective-permute-start | bytes 1179656 | tf_op jit(solution)/shard_map/ppermute | solution.py:246
  26.6 12.8 %collective-permute-start.5 = (bf16[256,768]{1,0:T(8,128)(2,1)}, bf16[256,768]{1,0:T(8,128)(2,1)}, u32[]{:S(2)}, u32[]{:S(2)}) collective-permute-start(bf16[256,768]{1,0:T(8,128)(2,1)} %collective-permute-done.2.refs_0_), channel_id=1, source_target_pairs={{0,4},{4,0},{8,12},{12,8},{16,20},{20,16},{24,28},{28,24},{1,5},{5... | collective-permute-start | bytes 1179656 | tf_op jit(solution)/shard_map/ppermute | solution.py:250
  28.1 15.2 %collective-permute-start.6 = (bf16[768,128]{1,0:T(8,128)(2,1)}, bf16[768,128]{1,0:T(8,128)(2,1)}, u32[]{:S(2)}, u32[]{:S(2)}) collective-permute-start(bf16[768,128]{1,0:T(8,128)(2,1)} %get-tuple-element.52), channel_id=1, source_target_pairs={{0,16},{16,0},{4,20},{20,4},{8,24},{24,8},{12,28},{28,12},{1,17},{... | collective-permute-start | bytes 589832 | tf_op jit(solution)/shard_map/ppermute | solution.py:246
  28.6 22.4 %copy-start.2 = (bf16[256,5120]{1,0:T(8,128)(2,1)S(1)}, bf16[256,5120]{1,0:T(8,128)(2,1)}, u32[]{:S(2)}) copy-start(bf16[256,5120]{1,0:T(8,128)(2,1)} %copy-done.1) | copy-start | bytes 7864324
  28.6 1.1 %copy-start.5 = (bf16[2,384,128]{2,1,0:T(8,128)(2,1)S(1)}, bf16[2,384,128]{2,1,0:T(8,128)(2,1)}, u32[]{:S(2)}) copy-start(bf16[2,384,128]{2,1,0:T(8,128)(2,1)} %copy-done.4) | copy-start | bytes 589828
  45.0 5.9 %collective-permute-start.11 = (bf16[256,768]{1,0:T(8,128)(2,1)}, bf16[256,768]{1,0:T(8,128)(2,1)S(1)}, u32[]{:S(2)}, u32[]{:S(2)}) collective-permute-start(bf16[256,768]{1,0:T(8,128)(2,1)} %collective-permute-done.5.refs_2_), channel_id=1, source_target_pairs={{0,1},{1,0},{2,3},{3,2},{4,5},{5,4},{6,7},{7,6},{8,9},{9,8},{10,11... | collective-permute-start | bytes 1179656 | tf_op jit(solution)/shard_map/ppermute | solution.py:254
  45.1 5.8 %collective-permute-start.10 = (bf16[256,768]{1,0:T(8,128)(2,1)}, bf16[256,768]{1,0:T(8,128)(2,1)S(1)}, u32[]{:S(2)}, u32[]{:S(2)}) collective-permute-start(bf16[256,768]{1,0:T(8,128)(2,1)} %collective-permute-done.2.refs_0_), channel_id=1, source_target_pairs={{0,1},{1,0},{2,3},{3,2},{4,5},{5,4},{6,7},{7,6},{8,9},{9,8},{10,11... | collective-permute-start | bytes 1179656 | tf_op jit(solution)/shard_map/ppermute | solution.py:254
  45.6 3.8 %collective-permute-start.7 = (bf16[2,96,128]{2,1,0:T(8,128)(2,1)S(1)}, bf16[2,96,128]{2,1,0:T(8,128)(2,1)S(1)}, u32[]{:S(2)}, u32[]{:S(2)}) collective-permute-start(bf16[2,96,128]{2,1,0:T(8,128)(2,1)S(1)} %get-tuple-element.54), channel_id=1, source_target_pairs={{0,5},{1,4},{2,7},{3,6},{4,1},{5,0},{6,3},{7,2},{8,13},{9,12},{10,... | collective-permute-start | bytes 147464 | tf_op jit(solution)/shard_map/ppermute | solution.py:261
  46.8 4.1 %collective-permute-start.8 = (bf16[2,96,128]{2,1,0:T(8,128)(2,1)S(1)}, bf16[2,96,128]{2,1,0:T(8,128)(2,1)S(1)}, u32[]{:S(2)}, u32[]{:S(2)}) collective-permute-start(bf16[2,96,128]{2,1,0:T(8,128)(2,1)S(1)} %get-tuple-element.55), channel_id=1, source_target_pairs={{0,4},{4,0},{8,12},{12,8},{16,20},{20,16},{24,28},{28,24},{1,5},{5... | collective-permute-start | bytes 147464 | tf_op jit(solution)/shard_map/ppermute | solution.py:250
  49.3 1.5 %collective-permute-start.9 = (bf16[2,96,128]{2,1,0:T(8,128)(2,1)S(1)}, bf16[2,96,128]{2,1,0:T(8,128)(2,1)S(1)}, u32[]{:S(2)}, u32[]{:S(2)}) collective-permute-start(bf16[2,96,128]{2,1,0:T(8,128)(2,1)S(1)} %get-tuple-element.56), channel_id=1, source_target_pairs={{0,1},{1,0},{2,3},{3,2},{4,5},{5,4},{6,7},{7,6},{8,9},{9,8},{10,11... | collective-permute-start | bytes 147464 | tf_op jit(solution)/shard_map/ppermute | solution.py:254
  50.9 13.2 %collective-permute-start.14 = (bf16[256,1792]{1,0:T(8,128)(2,1)S(1)}, bf16[256,1792]{1,0:T(8,128)(2,1)S(1)}, u32[]{:S(2)}, u32[]{:S(2)}) collective-permute-start(bf16[256,1792]{1,0:T(8,128)(2,1)S(1)} %collective-permute-done.12.refs_4_), channel_id=1, source_target_pairs={{0,1},{1,0},{2,3},{3,2},{4,5},{5,4},{6,7},{7,6},{8,9},{9,8},{10,11... | collective-permute-start | bytes 2752520 | tf_op jit(solution)/shard_map/ppermute | solution.py:254
  51.4 12.6 %collective-permute-start.13 = (bf16[96,2304]{1,0:T(8,128)(2,1)S(1)}, bf16[96,2304]{1,0:T(8,128)(2,1)S(1)}, u32[]{:S(2)}, u32[]{:S(2)}) collective-permute-start(bf16[96,2304]{1,0:T(8,128)(2,1)S(1)} %get-tuple-element.67), channel_id=1, source_target_pairs={{2,0},{3,1},{0,2},{1,3},{6,4},{7,5},{4,6},{5,7},{10,8},{11,9},{8,1... | collective-permute-start | bytes 1327112 | tf_op jit(solution)/shard_map/ppermute | solution.py:266
where the time goes:
time: 67.5 us; the launch traced here: 66.9 us
  waiting for transfers between devices  29.3 us (43%)
  Pallas kernels  16.3 us (24%)
  starting transfers between devices  16.3 us (24%)
  local copies, waits for them, and re-layouts  4.23 us (6%)
  between operations  0.91 us (1%)
    pallas_call x8, Pallas kernels, call(): pl.pallas_call(kernel, out_shape=outs, in_specs=[SMEM if s else HBM if i...  16.3 us
    ppermute x3, waiting for transfers between devices, from_chip(): lax.ppermute(value, 'head', [((i + 2 * steps) % count, i) for i in range(...  10 us
    ppermute x3, waiting for transfers between devices, swap_tiles(): lax.ppermute(value, 'ctx', [(i, i ^ 1) for i in range(lax.axis_size('ctx'...  9.25 us
    ppermute x3, waiting for transfers between devices, swap_pairs(): return lax.ppermute(value, 'ctx', pairs)  7.9 us
    ppermute x3, starting transfers between devices, swap_pairs(): return lax.ppermute(value, 'ctx', pairs)  5.8 us
    ppermute x3, starting transfers between devices, from_chip(): lax.ppermute(value, 'head', [((i + 2 * steps) % count, i) for i in range(...  4.43 us
    unnamed x12, local copies, waits for them, and re-layouts  4.23 us
    ppermute x3, starting transfers between devices, swap_tiles(): lax.ppermute(value, 'ctx', [(i, i ^ 1) for i in range(lax.axis_size('ctx'...  3.55 us
  transfers between devices with their start and end apart: 15, of which 6 were waited for; matrix products, arithmetic and copies ran while one was open for 0% of the time, Pallas kernels for 15%

commit v1 on v0

--- a/solution.py
+++ b/solution.py
@@ -14,7 +14,6 @@
 FLAGS = 16
 SIDE = 768
 COMMON = 1792
-PACK = 58
 STATE = HD + 8
 EXPONENT = math.log2(math.e) / math.sqrt(HD)
 BF16, F32 = jnp.bfloat16, jnp.float32
@@ -46,7 +45,7 @@
 
 def pack_kernel(
     tile_ref, list_ref, count_ref, q_ref, k_ref, v_ref, w_ref,
-    keep_ref, send_ref, side_ref, common_ref, sems,
+    keep_q_ref, keep_kv_ref, send_ref, side_ref, sems,
 ):
     parity = tile_ref[0] & 1
     rows = q_ref.shape[0]
@@ -56,13 +55,15 @@
         copies.append(pltpu.make_async_copy(source, target, sems.at[len(copies)]))
         copies[-1].start()
 
-    for out, head in ((send_ref, 1 - parity), (keep_ref, parity)):
+    for head, kv_out, q_out, q_at in (
+        (1 - parity, send_ref, send_ref, 2 * rows),
+        (parity, keep_kv_ref, keep_q_ref, 0),
+    ):
         columns = pl.ds(pl.multiple_of(head * HD, HD), HD)
-        for i, ref in enumerate((k_ref, v_ref, q_ref)):
-            copy(ref.at[:, columns], out.at[pl.ds(i * rows, rows)])
+        for ref, out, at in ((k_ref, kv_out, 0), (v_ref, kv_out, rows), (q_ref, q_out, q_at)):
+            copy(ref.at[:, columns], out.at[pl.ds(at, rows)])
     side = side_ref.shape[1]
     copy(w_ref.at[:, pl.ds(pl.multiple_of(parity * side, HD), side)], side_ref)
-    copy(w_ref.at[:, pl.ds(2 * side, common_ref.shape[1])], common_ref)
     lane = lax.broadcasted_iota(jnp.int32, (FLAGS, HD), 1)
     flags = jnp.zeros((FLAGS, HD), F32)
     for offset in range(-REACH, REACH + 1):
@@ -71,23 +72,33 @@
             found = (list_ref[0, slot] == tile_ref[0] + offset) & (slot < count_ref[0])
             listed = jnp.where(found, 1, listed)
         flags = jnp.where(lane == offset + REACH, listed.astype(F32), flags)
-    keep_ref[3 * rows :, :] = flags.astype(BF16)
+    keep_q_ref[rows:, :] = flags.astype(BF16)
     send_ref[3 * rows :, :] = flags.astype(BF16)
     for each in copies:
         each.wait()
 
 
-def merge_kernel(tile_ref, keep_ref, came_ref, flag_ref, q_ref, both_ref, odd_ref, even_ref):
+def stage_kernel(keep_q_ref, keep_kv_ref, q_ref, kv_ref):
+    q_ref[...] = keep_q_ref[...]
+    kv_ref[...] = keep_kv_ref[...]
+
+
+def cut_kernel(w_ref, common_ref, *, first):
+    common_ref[...] = w_ref[:, first : first + common_ref.shape[1]]
+
+
+def merge_kernel(
+    tile_ref, keep_q_ref, keep_kv_ref, came_ref, flag_ref, q_ref, kv_ref, odd_ref, even_ref
+):
     parity = tile_ref[0] & 1
     rows = q_ref.shape[1]
-    both_ref[0 : 2 * rows, :] = keep_ref[0 : 2 * rows, :]
-    both_ref[2 * rows :, :] = came_ref[0 : 2 * rows, :]
+    kv_ref[...] = came_ref[0 : 2 * rows, :]
     up = (tile_ref[0] & 4) == 0
 
     def place(out, own):
         @pl.when(own)
         def _():
-            out[...] = keep_ref[0 : 2 * rows, :]
+            out[...] = keep_kv_ref[...]
 
         @pl.when(jnp.logical_not(own))
         def _():
@@ -96,9 +107,9 @@
     place(odd_ref, up == (parity == 1))
     if even_ref is not None:
         place(even_ref, up == (parity == 0))
-    q_ref[parity] = keep_ref[2 * rows : 3 * rows, :]
+    q_ref[parity] = keep_q_ref[0:rows, :]
     q_ref[1 - parity] = came_ref[2 * rows : 3 * rows, :]
-    own = keep_ref[3 * rows :, :].astype(F32)
+    own = keep_q_ref[rows:, :].astype(F32)
     other = came_ref[3 * rows :, :].astype(F32)
     even = jnp.where(parity == 0, own, other)[0:8]
     odd = jnp.where(parity == 0, other, own)[0:8]
@@ -125,32 +136,36 @@
 
 def visit(flag_ref, q_ref, state_ref, pairs):
     rows = q_ref.shape[1]
-    for a, tile, ref, at in pairs:
+    for a, tile, ref in pairs:
 
         @pl.when(flag_ref[a, tile - a + REACH] > 0)
         def _():
-            key, value = ref[at : at + rows, :], ref[at + rows : at + 2 * rows, :]
-            step(q_ref[a], key, value, state_ref, a)
-
-
-def visit_pair(flag_ref, tile_ref, q_ref, state_ref, base, ref):
-    parity = tile_ref[0] & 1
-    rows = q_ref.shape[1]
-    tiles = ((base + parity, 0), (base + 1 - parity, 2 * rows))
-    visit(flag_ref, q_ref, state_ref, [(a, t, ref, at) for t, at in tiles for a in range(2)])
-
-
-def first_kernel(flag_ref, tile_ref, q_ref, both_ref, state_ref):
+            step(q_ref[a], ref[0:rows, :], ref[rows : 2 * rows, :], state_ref, a)
+
+
+def visit_pairs(flag_ref, tile_ref, q_ref, state_ref, tiles):
+    parity = tile_ref[0] & 1
+    for base, own, ref in tiles:
+        tile = base + (parity if own else 1 - parity)
+        visit(flag_ref, q_ref, state_ref, [(a, tile, ref) for a in range(2)])
+
+
+def first_kernel(
+    flag_ref, tile_ref, q_ref, own_ref, came_ref, kept_first_ref, kept_second_ref, state_ref
+):
     state_ref[...] = jnp.zeros_like(state_ref)
     for a in range(2):
         state_ref[a, HD : HD + 1, :] = jnp.full((1, state_ref.shape[2]), NEG, F32)
-    visit_pair(flag_ref, tile_ref, q_ref, state_ref, 0, both_ref)
+    base = jnp.where((tile_ref[0] & 2) == 0, 2, -2)
+    tiles = [(0, True, own_ref), (0, False, came_ref)]
+    tiles += [(base, True, kept_first_ref), (-base, True, kept_second_ref)]
+    visit_pairs(flag_ref, tile_ref, q_ref, state_ref, tiles)
 
 
 def second_kernel(flag_ref, tile_ref, q_ref, first_ref, second_ref, _, state_ref):
     base = jnp.where((tile_ref[0] & 2) == 0, 2, -2)
-    visit_pair(flag_ref, tile_ref, q_ref, state_ref, base, first_ref)
-    visit_pair(flag_ref, tile_ref, q_ref, state_ref, -base, second_ref)
+    tiles = [(base, False, first_ref), (-base, False, second_ref)]
+    visit_pairs(flag_ref, tile_ref, q_ref, state_ref, tiles)
 
 
 def third_kernel(flag_ref, tile_ref, head_ref, q_ref, state_ref, *refs, far):
@@ -158,7 +173,7 @@
     last[...] = state_ref[...]
     for i in range(far):
         above = ((tile_ref[0] & 4) == 0) == (i == 0)
-        which = (jnp.where(above, 1, 0), jnp.where(above, 4, -3), refs[i], 0)
+        which = (jnp.where(above, 1, 0), jnp.where(above, 4, -3), refs[i])
         visit(flag_ref, q_ref, last, [which])
     parity = tile_ref[0] & 1
     core = head_ref[0] & 1
@@ -220,16 +235,13 @@
     weights, out_ref = refs[:-1], refs[-1]
     parity = tile_ref[0] & 1
     deep = 2 * weights[0].shape[0]
+    far = far_ref[:, 0:deep]
     side = weights[0].shape[1]
-    far = far_ref[:, 0:deep]
-    places = (parity * side, (1 - parity) * side, 2 * side)
-    for i, at in enumerate(places):
+    for i, first in enumerate((parity * side, (1 - parity) * side, 2 * side)):
         pair = weights[2 * i : 2 * i + 2]
         for start in range(0, pair[0].shape[1], CHUNK):
             stop = min(start + CHUNK, pair[0].shape[1])
-            columns = pl.ds(at + start, stop - start)
-            if i < 2:
-                columns = pl.ds(pl.multiple_of(at + start, HD), stop - start)
+            columns = pl.ds(pl.multiple_of(first + start, HD), stop - start)
             out_ref[:, columns] = (
                 near_ref[:, columns] + multiply(far, pair, start, stop)
             ).astype(BF16)
@@ -298,50 +310,60 @@
 
     one = (rows, HD)
     payload, kv_shape = shape((3 * rows + FLAGS, HD)), shape((2 * rows, HD))
-    keep, send, side_weight, common_weight = call(
+    weight_pair = swap_cores(out_weight)
+    keep_q, keep_kv, send, side_weight = call(
         pack_kernel,
-        (payload, payload, shape((width, SIDE)), shape((width, COMMON))),
+        (shape((rows + FLAGS, HD)), kv_shape, payload, shape((width, SIDE))),
         (tile, neighbours, counts, queries, keys, values, out_weight),
-        scratch=(pltpu.SemaphoreType.DMA((8,)),),
+        scratch=(pltpu.SemaphoreType.DMA((7,)),),
         in_hbm=(3, 4, 5, 6),
-        vmem=PACK,
+        vmem=58,
     )
     came = swap_tiles(send)
-    weight_ready, keep = lax.optimization_barrier((out_weight, keep))
-    weight_pair = swap_cores(weight_ready)
-    came, weight_pair = lax.optimization_barrier((came, weight_pair))
+    kept_near = [swap_pairs(keep_kv, 1, phase) for phase in range(2)]
     if small:
         side_own = from_chip(side_weight, 1)
 
+    held_q, held_kv = call(stage_kernel, (shape((rows + FLAGS, HD)), kv_shape), (keep_q, keep_kv))
+    came, weight_pair, held_q, held_kv, *kept_near = lax.optimization_barrier(
+        (came, weight_pair, held_q, held_kv, *kept_near)
+    )
     far = 1 if lax.axis_size("ctx") <= 8 else 2
-    flags, q_pair, both, *to_far = call(
+    flags, q_pair, came_kv, *to_far = call(
         merge_kernel if far == 2 else functools.partial(merge_kernel, even_ref=None),
-        (shape((8, HD), jnp.int32), shape((2,) + one), shape((4 * rows, HD))) + (kv_shape,) * far,
-        (tile, keep, came),
-    )
-    nearest = [swap_pairs(both, 1, phase) for phase in range(2)]
+        (shape((8, HD), jnp.int32), shape((2,) + one), kv_shape) + (kv_shape,) * far,
+        (tile, held_q, held_kv, came),
+    )
+    came_near = [swap_pairs(came_kv, 1, phase) for phase in range(2)]
     farther = [swap_pairs(to_far[i], 2, i) for i in range(far)]
 
     state = shape((2, STATE, rows), F32)
     area = rows * rows
-    held = call(first_kernel, state, (flags, tile, q_pair, both), 16 * area * HD, 4 * area)
+    held = call(
+        first_kernel,
+        state,
+        (flags, tile, q_pair, held_kv, came_kv, *kept_near),
+        32 * area * HD,
+        8 * area,
+    )
     q_again = q_pair
     if small:
         side_own, q_again = lax.optimization_barrier((side_own, q_pair))
         side_other = swap_tiles(side_own)
-        common_ready, _ = lax.optimization_barrier((common_weight, side_own))
-        common = from_chip(common_ready, 1)
+        ready, _ = lax.optimization_barrier((out_weight, side_own))
+        common_weight = call(
+            functools.partial(cut_kernel, first=2 * SIDE), shape((width, COMMON)), (ready,)
+        )
+        common = from_chip(common_weight, 1)
     held = call(
         second_kernel,
         state,
-        (flags, tile, q_again, *nearest, held),
-        32 * area * HD,
-        8 * area,
+        (flags, tile, q_again, *came_near, held),
+        16 * area * HD,
+        4 * area,
         alias={5: 0},
     )
     if small:
-        ready, held = lax.optimization_barrier((side_own, held))
-        far_weights = [side_own, swap_cores(ready)]
         held, side_other = lax.optimization_barrier((held, side_other))
     block = (2, own_rows, HD)
     attended = call(
@@ -365,12 +387,15 @@
     from_cross = swap_both(theirs_other)
     from_y = swap_tiles(theirs)
     from_core = swap_cores(mine_other)
-    ready, _ = lax.optimization_barrier((side_other, mine))
-    far_weights += [side_other, swap_cores(ready), common]
-    from_cross, from_y, from_core, *far_weights = lax.optimization_barrier(
-        (from_cross, from_y, from_core, *far_weights)
-    )
-    far_weights.append(swap_cores(far_weights[-1]))
+    pieces = [side_own, side_other]
+    *ready, _ = lax.optimization_barrier((*pieces, mine))
+    swapped = [swap_cores(piece) for piece in ready]
+    from_cross, from_y, from_core, common, *swapped = lax.optimization_barrier(
+        (from_cross, from_y, from_core, common, *swapped)
+    )
+    pieces.append(common)
+    swapped.append(swap_cores(common))
+    far_weights = [each for both in zip(pieces, swapped) for each in both]
 
     flops = 2 * own_rows * 2 * width * model
     near_weights = (out_weight, weight_pair)

time: 67.5 us -> 64.5 us (0.956)
  waiting for transfers between devices: 29.3 us -> 16.5 us
  Pallas kernels: 16.3 us -> 19.8 us
  starting transfers between devices: 16.3 us -> 19.7 us
  local copies, waits for them, and re-layouts: 4.23 us -> 6.97 us
    ppermute x3, waiting for transfers between devices: 9.25 us -> 1.4 us  [swap_tiles(): lax.ppermute(value, 'ctx', [(i, i ^ 1) for i in range(lax.axis_size('ctx'...]
    ppermute x3 -> x5, starting transfers between devices: 5.8 us -> 10.4 us  [swap_pairs(): return lax.ppermute(value, 'ctx', pairs)]
    pallas_call x8 -> x10, Pallas kernels: 16.3 us -> 19.8 us  [call(): pl.pallas_call(kernel, out_shape=outs, in_specs=[SMEM if s else HBM if i...]
    ppermute x3 -> x5, waiting for transfers between devices: 7.9 us -> 4.4 us  [swap_pairs(): return lax.ppermute(value, 'ctx', pairs)]
    unnamed x12 -> x22, local copies, waits for them, and re-layouts: 4.23 us -> 6.97 us
    ppermute x3, waiting for transfers between devices: 10 us -> 8.59 us  [from_chip(): lax.ppermute(value, 'head', [((i + 2 * steps) % count, i) for i in range(...]
    ppermute x3, starting transfers between devices: 3.55 us -> 2.54 us  [swap_tiles(): lax.ppermute(value, 'ctx', [(i, i ^ 1) for i in range(lax.axis_size('ctx'...]
  transfers between devices with their start and end apart: 15 -> 17, of which waited for: 6 -> 5; matrix products, arithmetic and copies ran while one was open for 0% -> 0% of each run, Pallas kernels for 15% -> 26%
where the time goes in v1:
time: 64.5 us; the launch traced here: 64 us
  Pallas kernels  19.8 us (31%)
  starting transfers between devices  19.7 us (31%)
  waiting for transfers between devices  16.5 us (26%)
  local copies, waits for them, and re-layouts  6.97 us (11%)
  between operations  1.04 us (2%)
    pallas_call x10, Pallas kernels, call(): pl.pallas_call(kernel, out_shape=outs, in_specs=[SMEM if s else HBM if i...  19.8 us
    ppermute x5, starting transfers between devices, swap_pairs(): return lax.ppermute(value, 'ctx', pairs)  10.4 us
    ppermute x3, waiting for transfers between devices, from_chip(): lax.ppermute(value, 'head', [((i + 2 * steps) % count, i) for i in range(...  8.59 us
    unnamed x22, local copies, waits for them, and re-layouts  6.97 us
    ppermute x5, waiting for transfers between devices, swap_pairs(): return lax.ppermute(value, 'ctx', pairs)  4.4 us
    ppermute x3, starting transfers between devices, from_chip(): lax.ppermute(value, 'head', [((i + 2 * steps) % count, i) for i in range(...  4.36 us
    ppermute x3, starting transfers between devices, swap_tiles(): lax.ppermute(value, 'ctx', [(i, i ^ 1) for i in range(lax.axis_size('ctx'...  2.54 us
    ppermute x1, waiting for transfers between devices, swap_both(): return lax.ppermute(value, ('ctx', 'head'), pairs)  2.07 us
  transfers between devices with their start and end apart: 17, of which 5 were waited for; matrix products, arithmetic and copies ran while one was open for 0% of the time, Pallas kernels for 26%

profile of v1, /device:TPU:0, one launch (start us, length us, event | category | flops | bytes accessed | tf_op | source)
XLA Modules:
  0.0 64.0 jit_solution(18000131429911088111)
XLA Ops:
  0.0 0.0 copy-start
  0.0 0.5 collective-permute-start.1
  1.3 3.0 %shard_map.64 = (bf16[400,128]{1,0:T(8,128)(2,1)}, bf16[768,128]{1,0:T(8,128)(2,1)}, bf16[1168,128]{1,0:T(8,128)(2,1)}, bf16[256,768]{1,0:T(8,128)(2,1)}) custom-call(s32[1]{0:T(128)} %bitcast.tile_ref, s32[1,7]{1,0:T(1,128)} %list_ref.1, s32[1]{0:T(128)S(6)} %copy.9.count_ref, bf16[384,256]{1,0:T(8,128)(2,1)} %q_ref.1, bf16[384,256]{1,0:T(8,128)(2,1)} %k_ref.1, ...), custom_call_target="tpu_custom_call" | custom-call | bytes 1048576 | tf_op jit(solution)/shard_map/pallas_call | solution.py:30
  4.3 2.5 %collective-permute-start.4 = (bf16[256,768]{1,0:T(8,128)(2,1)}, bf16[256,768]{1,0:T(8,128)(2,1)}, u32[]{:S(2)}, u32[]{:S(2)}) collective-permute-start(bf16[256,768]{1,0:T(8,128)(2,1)} %get-tuple-element.50), channel_id=1, source_target_pairs={{2,0},{3,1},{0,2},{1,3},{6,4},{7,5},{4,6},{5,7},{10,8},{11,9},{8,1... | collective-permute-start | bytes 1179656 | tf_op jit(solution)/shard_map/ppermute | solution.py:278
  6.8 1.5 %collective-permute-start = (bf16[1168,128]{1,0:T(8,128)(2,1)}, bf16[1168,128]{1,0:T(8,128)(2,1)S(1)}, u32[]{:S(2)}, u32[]{:S(2)}) collective-permute-start(bf16[1168,128]{1,0:T(8,128)(2,1)} %get-tuple-element.40), channel_id=1, source_target_pairs={{0,4},{4,0},{8,12},{12,8},{16,20},{20,16},{24,28},{28,24},{1,5},{5... | collective-permute-start | bytes 897032 | tf_op jit(solution)/shard_map/ppermute | solution.py:262
  8.3 0.7 %collective-permute-start.3 = (bf16[768,128]{1,0:T(8,128)(2,1)}, bf16[768,128]{1,0:T(8,128)(2,1)S(1)}, u32[]{:S(2)}, u32[]{:S(2)}) collective-permute-start(bf16[768,128]{1,0:T(8,128)(2,1)} %get-tuple-element.42.keep_kv_ref), channel_id=1, source_target_pairs={{8,16},{16,8},{12,20},{20,12},{9,17},{17,9},{13,21},{21,13},{10,18... | collective-permute-start | bytes 589832 | tf_op jit(solution)/shard_map/ppermute | solution.py:258
  9.0 4.5 %collective-permute-start.2 = (bf16[768,128]{1,0:T(8,128)(2,1)}, bf16[768,128]{1,0:T(8,128)(2,1)S(1)}, u32[]{:S(2)}, u32[]{:S(2)}) collective-permute-start(bf16[768,128]{1,0:T(8,128)(2,1)} %get-tuple-element.42.keep_kv_ref), channel_id=1, source_target_pairs={{0,8},{8,0},{4,12},{12,4},{16,24},{24,16},{20,28},{28,20},{1,9},{9... | collective-permute-start | bytes 589832 | tf_op jit(solution)/shard_map/ppermute | solution.py:258
  13.4 0.0 copy-start.3
  13.4 1.0 %copy-done.3 = bf16[768,128]{1,0:T(8,128)(2,1)S(1)} copy-done((bf16[768,128]{1,0:T(8,128)(2,1)S(1)}, bf16[768,128]{1,0:T(8,128)(2,1)}, u32[]{:S(2)}) %copy-start.3) | copy-done | bytes 196632
  14.4 0.0 copy-start.6
  14.4 0.9 %copy-done.6 = bf16[400,128]{1,0:T(8,128)(2,1)S(1)} copy-done((bf16[400,128]{1,0:T(8,128)(2,1)S(1)}, bf16[400,128]{1,0:T(8,128)(2,1)}, u32[]{:S(2)}) %copy-start.6) | copy-done | bytes 102424
  15.3 0.0 copy-start.4
  15.3 0.0 collective-permute-done.3.kept_second_ref
  15.3 0.0 copy-start.7
  15.3 0.7 %copy-done.7 = bf16[768,128]{1,0:T(8,128)(2,1)} copy-done((bf16[768,128]{1,0:T(8,128)(2,1)}, bf16[768,128]{1,0:T(8,128)(2,1)S(1)}, u32[]{:S(2)}) %copy-start.7) | copy-done | bytes 196632
  16.0 2.3 %collective-permute-done.2.kept_first_ref = bf16[768,128]{1,0:T(8,128)(2,1)S(1)} collective-permute-done((bf16[768,128]{1,0:T(8,128)(2,1)}, bf16[768,128]{1,0:T(8,128)(2,1)S(1)}, u32[]{:S(2)}, u32[]{:S(2)}) %collective-permute-start.2) | collective-permute-done | bytes 196640 | tf_op jit(solution)/shard_map/ppermute | solution.py:258
  18.3 0.0 copy-start.9
  18.3 0.7 %copy-done.9 = bf16[768,128]{1,0:T(8,128)(2,1)} copy-done((bf16[768,128]{1,0:T(8,128)(2,1)}, bf16[768,128]{1,0:T(8,128)(2,1)S(1)}, u32[]{:S(2)}) %copy-start.9) | copy-done | bytes 196632
  19.0 0.0 collective-permute-done.came_ref
  19.0 0.0 collective-permute-done.1.wp_ref
  19.0 0.8 %shard_map.66 = (s32[8,128]{1,0:T(8,128)S(1)}, bf16[2,384,128]{2,1,0:T(8,128)(2,1)S(1)}, bf16[768,128]{1,0:T(8,128)(2,1)}, bf16[768,128]{1,0:T(8,128)(2,1)}) custom-call(s32[1]{0:T(128)} %bitcast.tile_ref, bf16[400,128]{1,0:T(8,128)(2,1)S(1)} %get-tuple-element.45.keep_q_ref, bf16[768,128]{1,0:T(8,128)(2,1)S(1)} %get-tuple-element.46.keep_kv_ref.own_ref, ...), custom_call_target="tpu_custom_call" | custom-call | bytes 1048576 | tf_op jit(solution)/shard_map/pallas_call | solution.py:30
  19.9 0.0 copy-start.1
  19.9 0.0 collective-permute-done.4.refs_0_
  19.9 0.0 copy-done
  19.9 0.1 shard_map.70
  20.0 0.6 collective-permute-start.12
  20.6 0.0 copy-done.1
  20.6 0.5 collective-permute-start.7
  21.1 0.0 copy-done.4
  21.1 1.3 %collective-permute-start.6 = (bf16[768,128]{1,0:T(8,128)(2,1)}, bf16[768,128]{1,0:T(8,128)(2,1)}, u32[]{:S(2)}, u32[]{:S(2)}) collective-permute-start(bf16[768,128]{1,0:T(8,128)(2,1)} %get-tuple-element.52.came_ref), channel_id=1, source_target_pairs={{8,16},{16,8},{12,20},{20,12},{9,17},{17,9},{13,21},{21,13},{10,18... | collective-permute-start | bytes 589832 | tf_op jit(solution)/shard_map/ppermute | solution.py:258
  22.4 3.2 %collective-permute-start.5 = (bf16[768,128]{1,0:T(8,128)(2,1)}, bf16[768,128]{1,0:T(8,128)(2,1)}, u32[]{:S(2)}, u32[]{:S(2)}) collective-permute-start(bf16[768,128]{1,0:T(8,128)(2,1)} %get-tuple-element.52.came_ref), channel_id=1, source_target_pairs={{0,8},{8,0},{4,12},{12,4},{16,24},{24,16},{20,28},{28,20},{1,9},{9... | collective-permute-start | bytes 589832 | tf_op jit(solution)/shard_map/ppermute | solution.py:258
  25.7 0.7 %collective-permute-start.8 = (bf16[768,128]{1,0:T(8,128)(2,1)}, bf16[768,128]{1,0:T(8,128)(2,1)}, u32[]{:S(2)}, u32[]{:S(2)}) collective-permute-start(bf16[768,128]{1,0:T(8,128)(2,1)} %get-tuple-element.57), channel_id=1, source_target_pairs={{0,16},{16,0},{4,20},{20,4},{8,24},{24,8},{12,28},{28,12},{1,17},{... | collective-permute-start | bytes 589832 | tf_op jit(solution)/shard_map/ppermute | solution.py:258
  26.3 0.0 copy-start.2
  26.3 0.9 %copy-done.2 = bf16[2,384,128]{2,1,0:T(8,128)(2,1)S(1)} copy-done((bf16[2,384,128]{2,1,0:T(8,128)(2,1)S(1)}, bf16[2,384,128]{2,1,0:T(8,128)(2,1)}, u32[]{:S(2)}) %copy-start.2) | copy-done | bytes 196632
  27.3 0.9 %copy-done.5 = bf16[768,128]{1,0:T(8,128)(2,1)S(1)} copy-done((bf16[768,128]{1,0:T(8,128)(2,1)S(1)}, bf16[768,128]{1,0:T(8,128)(2,1)}, u32[]{:S(2)}) %copy-start.5) | copy-done | bytes 196632
  28.2 0.0 copy-start.8
  28.2 0.9 %copy-done.8 = bf16[768,128]{1,0:T(8,128)(2,1)S(1)} copy-done((bf16[768,128]{1,0:T(8,128)(2,1)S(1)}, bf16[768,128]{1,0:T(8,128)(2,1)}, u32[]{:S(2)}) %copy-start.8) | copy-done | bytes 196632
  29.1 0.0 copy-start.10
  29.1 0.9 %copy-done.10 = bf16[768,128]{1,0:T(8,128)(2,1)S(1)} copy-done((bf16[768,128]{1,0:T(8,128)(2,1)S(1)}, bf16[768,128]{1,0:T(8,128)(2,1)}, u32[]{:S(2)}) %copy-start.10) | copy-done | bytes 196632
  30.0 3.9 %shard_map.67._ = f32[2,136,384]{2,1,0:T(8,128)S(1)} custom-call(s32[8,128]{1,0:T(8,128)S(1)} %get-tuple-element.48.flag_ref, s32[1]{0:T(128)} %bitcast.tile_ref, bf16[2,384,128]{2,1,0:T(8,128)(2,1)S(1)} %copy-done.2, bf16[768,128]{1,0:T(8,128)(2,1)S(1)} %copy-done.5, bf16[768,128]{1,0:T(8,128)(2,1)} %get-tuple-element.52.came_ref, ...), custom_call_target="tpu_custom_call" | custom-call | flops 603979776 | bytes 1048576 | tf_op jit(solution)/shard_map/pallas_call | solution.py:30
  33.9 0.0 collective-permute-done.6.second_ref
  33.9 0.0 collective-permute-done.5.first_ref
  34.0 2.2 %shard_map.68.state_ref = f32[2,136,384]{2,1,0:T(8,128)S(1)} custom-call(s32[8,128]{1,0:T(8,128)S(1)} %get-tuple-element.48.flag_ref, s32[1]{0:T(128)} %bitcast.tile_ref, bf16[2,384,128]{2,1,0:T(8,128)(2,1)S(1)} %copy-done.2, bf16[768,128]{1,0:T(8,128)(2,1)} %collective-permute-done.5.first_ref, ...), custom_call_target="tpu_custom_call", output_to_operand_aliasing={{}: (5, {})} | custom-call | flops 301989888 | bytes 1048576 | tf_op jit(solution)/shard_map/pallas_call | solution.py:30
  36.2 0.0 collective-permute-done.7.refs_2_
  36.2 2.1 %collective-permute-done.8.refs_0_ = bf16[768,128]{1,0:T(8,128)(2,1)} collective-permute-done((bf16[768,128]{1,0:T(8,128)(2,1)}, bf16[768,128]{1,0:T(8,128)(2,1)}, u32[]{:S(2)}, u32[]{:S(2)}) %collective-permute-start.8) | collective-permute-done | bytes 196640 | tf_op jit(solution)/shard_map/ppermute | solution.py:258
  38.3 1.7 %shard_map.69 = (bf16[2,96,128]{2,1,0:T(8,128)(2,1)S(1)}, bf16[2,96,128]{2,1,0:T(8,128)(2,1)S(1)}, bf16[2,96,128]{2,1,0:T(8,128)(2,1)S(1)}, bf16[2,96,128]{2,1,0:T(8,128)(2,1)S(1)}) custom-call(s32[8,128]{1,0:T(8,128)S(1)} %get-tuple-element.48.flag_ref, s32[1]{0:T(128)} %bitcast.tile_ref, s32[1]{0:T(128)} %bitcast.1.head_ref, ...), custom_call_target="tpu_custom_call" | custom-call | flops 75497472 | bytes 1048576 | tf_op jit(solution)/shard_map/pallas_call | solution.py:30
  40.0 0.1 collective-permute-start.13
  40.1 0.5 collective-permute-start.14
  40.6 1.2 %collective-permute-start.9 = (bf16[2,96,128]{2,1,0:T(8,128)(2,1)S(1)}, bf16[2,96,128]{2,1,0:T(8,128)(2,1)S(1)}, u32[]{:S(2)}, u32[]{:S(2)}) collective-permute-start(bf16[2,96,128]{2,1,0:T(8,128)(2,1)S(1)} %get-tuple-element.59), channel_id=1, source_target_pairs={{0,5},{1,4},{2,7},{3,6},{4,1},{5,0},{6,3},{7,2},{8,13},{9,12},{10,... | collective-permute-start | bytes 147464 | tf_op jit(solution)/shard_map/ppermute | solution.py:273
  41.8 0.5 collective-permute-start.10
  42.3 2.1 %collective-permute-done.9.cross_ref = bf16[2,96,128]{2,1,0:T(8,128)(2,1)S(1)} collective-permute-done((bf16[2,96,128]{2,1,0:T(8,128)(2,1)S(1)}, bf16[2,96,128]{2,1,0:T(8,128)(2,1)S(1)}, u32[]{:S(2)}, u32[]{:S(2)}) %collective-permute-start.9) | collective-permute-done | bytes 49184 | tf_op jit(solution)/shard_map/ppermute | solution.py:273
  44.4 0.1 collective-permute-start.11
  44.5 1.4 %collective-permute-done.10.y_ref = bf16[2,96,128]{2,1,0:T(8,128)(2,1)S(1)} collective-permute-done((bf16[2,96,128]{2,1,0:T(8,128)(2,1)S(1)}, bf16[2,96,128]{2,1,0:T(8,128)(2,1)S(1)}, u32[]{:S(2)}, u32[]{:S(2)}) %collective-permute-start.10) | collective-permute-done | bytes 49184 | tf_op jit(solution)/shard_map/ppermute | solution.py:262
  45.9 0.0 collective-permute-done.11.core_ref
  45.9 0.0 collective-permute-done.13.refs_1_
  45.9 0.0 collective-permute-done.14.refs_3_
  45.9 0.0 collective-permute-done.12.refs_4_
  45.9 0.1 collective-permute-start.16
  46.0 2.2 %shard_map.71 = (bf16[96,512]{1,0:T(8,128)(2,1)S(1)}, bf16[96,2304]{1,0:T(8,128)(2,1)S(1)}) custom-call(s32[1]{0:T(128)} %bitcast.tile_ref, s32[1]{0:T(128)} %bitcast.1.head_ref, bf16[2,96,128]{2,1,0:T(8,128)(2,1)S(1)} %get-tuple-element.58.own_ref, bf16[2,96,128]{2,1,0:T(8,128)(2,1)S(1)} %collective-permute-done.10.y_ref, ...), custom_call_target="tpu_custom_call" | custom-call | flops 125829120 | bytes 1048576 | tf_op jit(solution)/shard_map/pallas_call | solution.py:30
  48.2 1.3 %collective-permute-start.15 = (bf16[96,2304]{1,0:T(8,128)(2,1)S(1)}, bf16[96,2304]{1,0:T(8,128)(2,1)S(1)}, u32[]{:S(2)}, u32[]{:S(2)}) collective-permute-start(bf16[96,2304]{1,0:T(8,128)(2,1)S(1)} %get-tuple-element.71), channel_id=1, source_target_pairs={{2,0},{3,1},{0,2},{1,3},{6,4},{7,5},{4,6},{5,7},{10,8},{11,9},{8,1... | collective-permute-start | bytes 1327112 | tf_op jit(solution)/shard_map/ppermute | solution.py:278
  49.5 2.8 %shard_map.72.near_ref = f32[96,5120]{1,0:T(8,128)S(1)} custom-call(bf16[96,512]{1,0:T(8,128)(2,1)S(1)} %get-tuple-element.70.a_ref, bf16[256,5120]{1,0:T(8,128)(2,1)S(1)} %copy-done, bf16[256,5120]{1,0:T(8,128)(2,1)} %collective-permute-done.1.wp_ref), custom_call_target="tpu_custom_call" | custom-call | flops 503316480 | bytes 1048576 | tf_op jit(solution)/shard_map/pallas_call | solution.py:30
  52.2 8.6 %collective-permute-done.15.far_ref = bf16[96,2304]{1,0:T(8,128)(2,1)S(1)} collective-permute-done((bf16[96,2304]{1,0:T(8,128)(2,1)S(1)}, bf16[96,2304]{1,0:T(8,128)(2,1)S(1)}, u32[]{:S(2)}, u32[]{:S(2)}) %collective-permute-start.15) | collective-permute-done | bytes 442400 | tf_op jit(solution)/shard_map/ppermute | solution.py:278
  60.8 0.0 collective-permute-done.16.refs_5_
  60.8 3.2 %shard_map.73 = bf16[96,5120]{1,0:T(8,128)(2,1)} custom-call(s32[1]{0:T(128)} %bitcast.tile_ref, f32[96,5120]{1,0:T(8,128)S(1)} %shard_map.72.near_ref, bf16[96,2304]{1,0:T(8,128)(2,1)S(1)} %collective-permute-done.15.far_ref, bf16[256,768]{1,0:T(8,128)(2,1)} %collective-permute-done.4.refs_0_, bf16[256,768]{1,0:T(8,128)(2,1)S(1)} %collective-permute-done.13.refs_1_, ...), custom_call_target="tpu_custom_call" | custom-call | flops 503316480 | bytes 1048576 | tf_op jit(solution)/shard_map/pallas_call | solution.py:30
  (2 shorter events, 0.0 us)
Async XLA Ops:
  0.0 19.9 %copy-start = (bf16[256,5120]{1,0:T(8,128)(2,1)S(1)}, bf16[256,5120]{1,0:T(8,128)(2,1)}, u32[]{:S(2)}) copy-start(bf16[256,5120]{1,0:T(8,128)(2,1)} %w_ref.6) | copy-start | bytes 7864324
  0.0 19.0 %collective-permute-start.1 = (bf16[256,5120]{1,0:T(8,128)(2,1)}, bf16[256,5120]{1,0:T(8,128)(2,1)}, u32[]{:S(2)}, u32[]{:S(2)}) collective-permute-start(bf16[256,5120]{1,0:T(8,128)(2,1)} %w_ref.6), channel_id=1, source_target_pairs={{0,1},{1,0},{2,3},{3,2},{4,5},{5,4},{6,7},{7,6},{8,9},{9,8},{10,11... | collective-permute-start | bytes 7864328 | tf_op jit(solution)/shard_map/ppermute | solution.py:266
  4.3 15.6 %collective-permute-start.4 = (bf16[256,768]{1,0:T(8,128)(2,1)}, bf16[256,768]{1,0:T(8,128)(2,1)}, u32[]{:S(2)}, u32[]{:S(2)}) collective-permute-start(bf16[256,768]{1,0:T(8,128)(2,1)} %get-tuple-element.50), channel_id=1, source_target_pairs={{2,0},{3,1},{0,2},{1,3},{6,4},{7,5},{4,6},{5,7},{10,8},{11,9},{8,1... | collective-permute-start | bytes 1179656 | tf_op jit(solution)/shard_map/ppermute | solution.py:278
  6.8 12.3 %collective-permute-start = (bf16[1168,128]{1,0:T(8,128)(2,1)}, bf16[1168,128]{1,0:T(8,128)(2,1)S(1)}, u32[]{:S(2)}, u32[]{:S(2)}) collective-permute-start(bf16[1168,128]{1,0:T(8,128)(2,1)} %get-tuple-element.40), channel_id=1, source_target_pairs={{0,4},{4,0},{8,12},{12,8},{16,20},{20,16},{24,28},{28,24},{1,5},{5... | collective-permute-start | bytes 897032 | tf_op jit(solution)/shard_map/ppermute | solution.py:262
  8.3 7.0 %collective-permute-start.3 = (bf16[768,128]{1,0:T(8,128)(2,1)}, bf16[768,128]{1,0:T(8,128)(2,1)S(1)}, u32[]{:S(2)}, u32[]{:S(2)}) collective-permute-start(bf16[768,128]{1,0:T(8,128)(2,1)} %get-tuple-element.42.keep_kv_ref), channel_id=1, source_target_pairs={{8,16},{16,8},{12,20},{20,12},{9,17},{17,9},{13,21},{21,13},{10,18... | collective-permute-start | bytes 589832 | tf_op jit(solution)/shard_map/ppermute | solution.py:258
  9.0 9.4 %collective-permute-start.2 = (bf16[768,128]{1,0:T(8,128)(2,1)}, bf16[768,128]{1,0:T(8,128)(2,1)S(1)}, u32[]{:S(2)}, u32[]{:S(2)}) collective-permute-start(bf16[768,128]{1,0:T(8,128)(2,1)} %get-tuple-element.42.keep_kv_ref), channel_id=1, source_target_pairs={{0,8},{8,0},{4,12},{12,4},{16,24},{24,16},{20,28},{28,20},{1,9},{9... | collective-permute-start | bytes 589832 | tf_op jit(solution)/shard_map/ppermute | solution.py:258
  13.4 1.0 %copy-start.3 = (bf16[768,128]{1,0:T(8,128)(2,1)S(1)}, bf16[768,128]{1,0:T(8,128)(2,1)}, u32[]{:S(2)}) copy-start(bf16[768,128]{1,0:T(8,128)(2,1)} %get-tuple-element.42.keep_kv_ref) | copy-start | bytes 589828
  14.4 0.9 %copy-start.6 = (bf16[400,128]{1,0:T(8,128)(2,1)S(1)}, bf16[400,128]{1,0:T(8,128)(2,1)}, u32[]{:S(2)}) copy-start(bf16[400,128]{1,0:T(8,128)(2,1)} %get-tuple-element.41.keep_q_ref) | copy-start | bytes 307204
  15.3 5.8 %copy-start.4 = (bf16[768,128]{1,0:T(8,128)(2,1)}, bf16[768,128]{1,0:T(8,128)(2,1)S(1)}, u32[]{:S(2)}) copy-start(bf16[768,128]{1,0:T(8,128)(2,1)S(1)} %get-tuple-element.46.keep_kv_ref.own_ref) | copy-start | bytes 589828
  15.3 0.7 %copy-start.7 = (bf16[768,128]{1,0:T(8,128)(2,1)}, bf16[768,128]{1,0:T(8,128)(2,1)S(1)}, u32[]{:S(2)}) copy-start(bf16[768,128]{1,0:T(8,128)(2,1)S(1)} %collective-permute-done.3.kept_second_ref) | copy-start | bytes 589828
  18.3 0.7 %copy-start.9 = (bf16[768,128]{1,0:T(8,128)(2,1)}, bf16[768,128]{1,0:T(8,128)(2,1)S(1)}, u32[]{:S(2)}) copy-start(bf16[768,128]{1,0:T(8,128)(2,1)S(1)} %collective-permute-done.2.kept_first_ref) | copy-start | bytes 589828
  19.9 0.7 %copy-start.1 = (bf16[2,384,128]{2,1,0:T(8,128)(2,1)}, bf16[2,384,128]{2,1,0:T(8,128)(2,1)S(1)}, u32[]{:S(2)}) copy-start(bf16[2,384,128]{2,1,0:T(8,128)(2,1)S(1)} %get-tuple-element.51.q_ref) | copy-start | bytes 589828
  20.0 25.9 %collective-permute-start.12 = (bf16[256,1792]{1,0:T(8,128)(2,1)S(1)}, bf16[256,1792]{1,0:T(8,128)(2,1)}, u32[]{:S(2)}, u32[]{:S(2)}) collective-permute-start(bf16[256,1792]{1,0:T(8,128)(2,1)S(1)} %shard_map.70), channel_id=1, source_target_pairs={{2,0},{3,1},{0,2},{1,3},{6,4},{7,5},{4,6},{5,7},{10,8},{11,9},{8,1... | collective-permute-start | bytes 2752520 | tf_op jit(solution)/shard_map/ppermute | solution.py:278
  20.6 15.6 %collective-permute-start.7 = (bf16[256,768]{1,0:T(8,128)(2,1)}, bf16[256,768]{1,0:T(8,128)(2,1)}, u32[]{:S(2)}, u32[]{:S(2)}) collective-permute-start(bf16[256,768]{1,0:T(8,128)(2,1)} %collective-permute-done.4.refs_0_), channel_id=1, source_target_pairs={{0,4},{4,0},{8,12},{12,8},{16,20},{20,16},{24,28},{28,24},{1,5},{5... | collective-permute-start | bytes 1179656 | tf_op jit(solution)/shard_map/ppermute | solution.py:262
  21.1 12.9 %collective-permute-start.6 = (bf16[768,128]{1,0:T(8,128)(2,1)}, bf16[768,128]{1,0:T(8,128)(2,1)}, u32[]{:S(2)}, u32[]{:S(2)}) collective-permute-start(bf16[768,128]{1,0:T(8,128)(2,1)} %get-tuple-element.52.came_ref), channel_id=1, source_target_pairs={{8,16},{16,8},{12,20},{20,12},{9,17},{17,9},{13,21},{21,13},{10,18... | collective-permute-start | bytes 589832 | tf_op jit(solution)/shard_map/ppermute | solution.py:258
  22.4 11.5 %collective-permute-start.5 = (bf16[768,128]{1,0:T(8,128)(2,1)}, bf16[768,128]{1,0:T(8,128)(2,1)}, u32[]{:S(2)}, u32[]{:S(2)}) collective-permute-start(bf16[768,128]{1,0:T(8,128)(2,1)} %get-tuple-element.52.came_ref), channel_id=1, source_target_pairs={{0,8},{8,0},{4,12},{12,4},{16,24},{24,16},{20,28},{28,20},{1,9},{9... | collective-permute-start | bytes 589832 | tf_op jit(solution)/shard_map/ppermute | solution.py:258
  25.7 12.6 %collective-permute-start.8 = (bf16[768,128]{1,0:T(8,128)(2,1)}, bf16[768,128]{1,0:T(8,128)(2,1)}, u32[]{:S(2)}, u32[]{:S(2)}) collective-permute-start(bf16[768,128]{1,0:T(8,128)(2,1)} %get-tuple-element.57), channel_id=1, source_target_pairs={{0,16},{16,0},{4,20},{20,4},{8,24},{24,8},{12,28},{28,12},{1,17},{... | collective-permute-start | bytes 589832 | tf_op jit(solution)/shard_map/ppermute | solution.py:258
  26.3 0.9 %copy-start.2 = (bf16[2,384,128]{2,1,0:T(8,128)(2,1)S(1)}, bf16[2,384,128]{2,1,0:T(8,128)(2,1)}, u32[]{:S(2)}) copy-start(bf16[2,384,128]{2,1,0:T(8,128)(2,1)} %copy-done.1) | copy-start | bytes 589828
  27.3 0.9 %copy-start.5 = (bf16[768,128]{1,0:T(8,128)(2,1)S(1)}, bf16[768,128]{1,0:T(8,128)(2,1)}, u32[]{:S(2)}) copy-start(bf16[768,128]{1,0:T(8,128)(2,1)} %copy-done.4) | copy-start | bytes 589828
  28.2 0.9 %copy-start.8 = (bf16[768,128]{1,0:T(8,128)(2,1)S(1)}, bf16[768,128]{1,0:T(8,128)(2,1)}, u32[]{:S(2)}) copy-start(bf16[768,128]{1,0:T(8,128)(2,1)} %copy-done.7) | copy-start | bytes 589828
  29.1 0.9 %copy-start.10 = (bf16[768,128]{1,0:T(8,128)(2,1)S(1)}, bf16[768,128]{1,0:T(8,128)(2,1)}, u32[]{:S(2)}) copy-start(bf16[768,128]{1,0:T(8,128)(2,1)} %copy-done.9) | copy-start | bytes 589828
  40.0 5.9 %collective-permute-start.13 = (bf16[256,768]{1,0:T(8,128)(2,1)}, bf16[256,768]{1,0:T(8,128)(2,1)S(1)}, u32[]{:S(2)}, u32[]{:S(2)}) collective-permute-start(bf16[256,768]{1,0:T(8,128)(2,1)} %collective-permute-done.4.refs_0_), channel_id=1, source_target_pairs={{0,1},{1,0},{2,3},{3,2},{4,5},{5,4},{6,7},{7,6},{8,9},{9,8},{10,11... | collective-permute-start | bytes 1179656 | tf_op jit(solution)/shard_map/ppermute | solution.py:266
  40.1 5.8 %collective-permute-start.14 = (bf16[256,768]{1,0:T(8,128)(2,1)}, bf16[256,768]{1,0:T(8,128)(2,1)S(1)}, u32[]{:S(2)}, u32[]{:S(2)}) collective-permute-start(bf16[256,768]{1,0:T(8,128)(2,1)} %collective-permute-done.7.refs_2_), channel_id=1, source_target_pairs={{0,1},{1,0},{2,3},{3,2},{4,5},{5,4},{6,7},{7,6},{8,9},{9,8},{10,11... | collective-permute-start | bytes 1179656 | tf_op jit(solution)/shard_map/ppermute | solution.py:266
  40.6 3.8 %collective-permute-start.9 = (bf16[2,96,128]{2,1,0:T(8,128)(2,1)S(1)}, bf16[2,96,128]{2,1,0:T(8,128)(2,1)S(1)}, u32[]{:S(2)}, u32[]{:S(2)}) collective-permute-start(bf16[2,96,128]{2,1,0:T(8,128)(2,1)S(1)} %get-tuple-element.59), channel_id=1, source_target_pairs={{0,5},{1,4},{2,7},{3,6},{4,1},{5,0},{6,3},{7,2},{8,13},{9,12},{10,... | collective-permute-start | bytes 147464 | tf_op jit(solution)/shard_map/ppermute | solution.py:273
  41.8 4.1 %collective-permute-start.10 = (bf16[2,96,128]{2,1,0:T(8,128)(2,1)S(1)}, bf16[2,96,128]{2,1,0:T(8,128)(2,1)S(1)}, u32[]{:S(2)}, u32[]{:S(2)}) collective-permute-start(bf16[2,96,128]{2,1,0:T(8,128)(2,1)S(1)} %get-tuple-element.60), channel_id=1, source_target_pairs={{0,4},{4,0},{8,12},{12,8},{16,20},{20,16},{24,28},{28,24},{1,5},{5... | collective-permute-start | bytes 147464 | tf_op jit(solution)/shard_map/ppermute | solution.py:262
  44.4 1.5 %collective-permute-start.11 = (bf16[2,96,128]{2,1,0:T(8,128)(2,1)S(1)}, bf16[2,96,128]{2,1,0:T(8,128)(2,1)S(1)}, u32[]{:S(2)}, u32[]{:S(2)}) collective-permute-start(bf16[2,96,128]{2,1,0:T(8,128)(2,1)S(1)} %get-tuple-element.61), channel_id=1, source_target_pairs={{0,1},{1,0},{2,3},{3,2},{4,5},{5,4},{6,7},{7,6},{8,9},{9,8},{10,11... | collective-permute-start | bytes 147464 | tf_op jit(solution)/shard_map/ppermute | solution.py:266
  45.9 14.9 %collective-permute-start.16 = (bf16[256,1792]{1,0:T(8,128)(2,1)}, bf16[256,1792]{1,0:T(8,128)(2,1)S(1)}, u32[]{:S(2)}, u32[]{:S(2)}) collective-permute-start(bf16[256,1792]{1,0:T(8,128)(2,1)} %collective-permute-done.12.refs_4_), channel_id=1, source_target_pairs={{0,1},{1,0},{2,3},{3,2},{4,5},{5,4},{6,7},{7,6},{8,9},{9,8},{10,11... | collective-permute-start | bytes 2752520 | tf_op jit(solution)/shard_map/ppermute | solution.py:266
  48.2 12.6 %collective-permute-start.15 = (bf16[96,2304]{1,0:T(8,128)(2,1)S(1)}, bf16[96,2304]{1,0:T(8,128)(2,1)S(1)}, u32[]{:S(2)}, u32[]{:S(2)}) collective-permute-start(bf16[96,2304]{1,0:T(8,128)(2,1)S(1)} %get-tuple-element.71), channel_id=1, source_target_pairs={{2,0},{3,1},{0,2},{1,3},{6,4},{7,5},{4,6},{5,7},{10,8},{11,9},{8,1... | collective-permute-start | bytes 1327112 | tf_op jit(solution)/shard_map/ppermute | solution.py:278

commit v2 on v1

--- a/solution.py
+++ b/solution.py
@@ -12,8 +12,8 @@
 REACH = 3
 NEG = -1e30
 FLAGS = 16
-SIDE = 768
-COMMON = 1792
+SIDE = 1024
+COMMON = 1536
 STATE = HD + 8
 EXPONENT = math.log2(math.e) / math.sqrt(HD)
 BF16, F32 = jnp.bfloat16, jnp.float32
@@ -24,7 +24,7 @@
 
 
 def call(
-    kernel, outs, ins, flops=0, exps=0, moved=1 << 20, scratch=(), alias=None, in_hbm=(), out_hbm=False, vmem=24
+    kernel, outs, ins, flops=0, exps=0, moved=1 << 20, scratch=(), alias=None, in_hbm=(), out_hbm=False, vmem=8
 ):
     scalars = [x.dtype == jnp.int32 for x in ins]
     return pl.pallas_call(
@@ -310,7 +310,6 @@
 
     one = (rows, HD)
     payload, kv_shape = shape((3 * rows + FLAGS, HD)), shape((2 * rows, HD))
-    weight_pair = swap_cores(out_weight)
     keep_q, keep_kv, send, side_weight = call(
         pack_kernel,
         (shape((rows + FLAGS, HD)), kv_shape, payload, shape((width, SIDE))),
@@ -319,6 +318,8 @@
         in_hbm=(3, 4, 5, 6),
         vmem=58,
     )
+    weight_ready, _ = lax.optimization_barrier((out_weight, keep_kv))
+    weight_pair = swap_cores(weight_ready)
     came = swap_tiles(send)
     kept_near = [swap_pairs(keep_kv, 1, phase) for phase in range(2)]
     if small:
@@ -387,15 +388,9 @@
     from_cross = swap_both(theirs_other)
     from_y = swap_tiles(theirs)
     from_core = swap_cores(mine_other)
-    pieces = [side_own, side_other]
-    *ready, _ = lax.optimization_barrier((*pieces, mine))
-    swapped = [swap_cores(piece) for piece in ready]
-    from_cross, from_y, from_core, common, *swapped = lax.optimization_barrier(
-        (from_cross, from_y, from_core, common, *swapped)
-    )
-    pieces.append(common)
-    swapped.append(swap_cores(common))
-    far_weights = [each for both in zip(pieces, swapped) for each in both]
+    from_cross, from_y, from_core, common = lax.optimization_barrier(
+        (from_cross, from_y, from_core, common)
+    )
 
     flops = 2 * own_rows * 2 * width * model
     near_weights = (out_weight, weight_pair)
@@ -405,11 +400,15 @@
         (shape((own_rows, deep)), shape((own_rows, deep + model - gathered))),
         (tile, head, mine, from_y, from_core, from_cross) + near_weights,
         flops // 4,
+        vmem=16,
     )
     got = from_chip(far_a, 1)
-    near = call(near_kernel, shape((own_rows, model), F32), (own_a,) + near_weights, flops)
+    pieces = [side_own, side_other, common]
+    *ready, _ = lax.optimization_barrier((*pieces, own_a))
+    far_weights = [each for piece, to in zip(pieces, ready) for each in (piece, swap_cores(to))]
+    near = call(near_kernel, shape((own_rows, model), F32), (own_a,) + near_weights, flops, vmem=16)
     return call(
-        last_kernel, shape((own_rows, model)), (tile, near, got, *far_weights), flops
+        last_kernel, shape((own_rows, model)), (tile, near, got, *far_weights), flops, vmem=20
     )
 
 

time: 64.5 us -> 63.5 us (0.984)
  Pallas kernels: 19.8 us -> 17.6 us
  waiting for transfers between devices: 16.5 us -> 18 us
    pallas_call x10, Pallas kernels: 19.8 us -> 17.6 us  [call(): pl.pallas_call(kernel, out_shape=outs, in_specs=[SMEM if s else HBM if i...]
    ppermute x5, waiting for transfers between devices: 4.4 us -> 5.61 us  [swap_pairs(): return lax.ppermute(value, 'ctx', pairs)]
    ppermute x1, starting transfers between devices: 1.2 us -> 0.07 us  [swap_both(): return lax.ppermute(value, ('ctx', 'head'), pairs)]
    ppermute x3, waiting for transfers between devices: 8.59 us -> 9.57 us  [from_chip(): lax.ppermute(value, 'head', [((i + 2 * steps) % count, i) for i in range(...]
    ppermute x3, starting transfers between devices: 2.54 us -> 3.48 us  [swap_tiles(): lax.ppermute(value, 'ctx', [(i, i ^ 1) for i in range(lax.axis_size('ctx'...]
    ppermute x5, starting transfers between devices: 1.21 us -> 2.03 us  [swap_cores(): lax.ppermute(value, 'head', [(i, i ^ 1) for i in range(lax.axis_size('hea...]
    unnamed x22 -> x18, local copies, waits for them, and re-layouts: 6.97 us -> 6.72 us
  transfers between devices with their start and end apart: 17 -> 17, of which waited for: 5 -> 5; matrix products, arithmetic and copies ran while one was open for 0% -> 0% of each run, Pallas kernels for 26% -> 16%
where the time goes in v2:
time: 63.5 us
  starting transfers between devices  20.2 us (32%)
  waiting for transfers between devices  18 us (28%)
  Pallas kernels  17.6 us (28%)
  local copies, waits for them, and re-layouts  6.72 us (11%)
  between operations  0.94 us (1%)
    pallas_call x10, Pallas kernels, call(): pl.pallas_call(kernel, out_shape=outs, in_specs=[SMEM if s else HBM if i...  17.6 us
    ppermute x5, starting transfers between devices, swap_pairs(): return lax.ppermute(value, 'ctx', pairs)  10.6 us
    ppermute x3, waiting for transfers between devices, from_chip(): lax.ppermute(value, 'head', [((i + 2 * steps) % count, i) for i in range(...  9.57 us
    unnamed x18, local copies, waits for them, and re-layouts  6.72 us
    ppermute x5, waiting for transfers between devices, swap_pairs(): return lax.ppermute(value, 'ctx', pairs)  5.61 us
    ppermute x3, starting transfers between devices, from_chip(): lax.ppermute(value, 'head', [((i + 2 * steps) % count, i) for i in range(...  4.02 us
    ppermute x3, starting transfers between devices, swap_tiles(): lax.ppermute(value, 'ctx', [(i, i ^ 1) for i in range(lax.axis_size('ctx'...  3.48 us
    ppermute x5, starting transfers between devices, swap_cores(): lax.ppermute(value, 'head', [(i, i ^ 1) for i in range(lax.axis_size('hea...  2.03 us
  transfers between devices with their start and end apart: 17, of which 5 were waited for; matrix products, arithmetic and copies ran while one was open for 0% of the time, Pallas kernels for 16%

profile of v2, /device:TPU:0, one launch (start us, length us, event | category | flops | bytes accessed | tf_op | source)
XLA Modules:
  0.0 63.5 jit_solution(15756002180615059198)
XLA Ops:
  0.0 0.0 copy-start
  0.8 3.1 %shard_map.64 = (bf16[400,128]{1,0:T(8,128)(2,1)}, bf16[768,128]{1,0:T(8,128)(2,1)}, bf16[1168,128]{1,0:T(8,128)(2,1)}, bf16[256,1024]{1,0:T(8,128)(2,1)}) custom-call(s32[1]{0:T(128)} %bitcast.tile_ref, s32[1,7]{1,0:T(1,128)} %list_ref.1, s32[1]{0:T(128)S(6)} %copy.9.count_ref, bf16[384,256]{1,0:T(8,128)(2,1)} %q_ref.1, bf16[384,256]{1,0:T(8,128)(2,1)} %k_ref.1, ...), custom_call_target="tpu_custom_call" | custom-call | bytes 1048576 | tf_op jit(solution)/shard_map/pallas_call | solution.py:30
  3.9 0.0 copy-done
  3.9 0.5 collective-permute-start.1
  4.4 2.6 %collective-permute-start.4 = (bf16[256,1024]{1,0:T(8,128)(2,1)}, bf16[256,1024]{1,0:T(8,128)(2,1)S(1)}, u32[]{:S(2)}, u32[]{:S(2)}) collective-permute-start(bf16[256,1024]{1,0:T(8,128)(2,1)} %get-tuple-element.51), channel_id=1, source_target_pairs={{2,0},{3,1},{0,2},{1,3},{6,4},{7,5},{4,6},{5,7},{10,8},{11,9},{8,1... | collective-permute-start | bytes 1572872 | tf_op jit(solution)/shard_map/ppermute | solution.py:278
  7.0 1.5 %collective-permute-start = (bf16[1168,128]{1,0:T(8,128)(2,1)}, bf16[1168,128]{1,0:T(8,128)(2,1)S(1)}, u32[]{:S(2)}, u32[]{:S(2)}) collective-permute-start(bf16[1168,128]{1,0:T(8,128)(2,1)} %get-tuple-element.40), channel_id=1, source_target_pairs={{0,4},{4,0},{8,12},{12,8},{16,20},{20,16},{24,28},{28,24},{1,5},{5... | collective-permute-start | bytes 897032 | tf_op jit(solution)/shard_map/ppermute | solution.py:262
  8.5 0.7 %collective-permute-start.3 = (bf16[768,128]{1,0:T(8,128)(2,1)}, bf16[768,128]{1,0:T(8,128)(2,1)S(1)}, u32[]{:S(2)}, u32[]{:S(2)}) collective-permute-start(bf16[768,128]{1,0:T(8,128)(2,1)} %get-tuple-element.41.keep_kv_ref), channel_id=1, source_target_pairs={{8,16},{16,8},{12,20},{20,12},{9,17},{17,9},{13,21},{21,13},{10,18... | collective-permute-start | bytes 589832 | tf_op jit(solution)/shard_map/ppermute | solution.py:258
  9.1 4.5 %collective-permute-start.2 = (bf16[768,128]{1,0:T(8,128)(2,1)}, bf16[768,128]{1,0:T(8,128)(2,1)S(1)}, u32[]{:S(2)}, u32[]{:S(2)}) collective-permute-start(bf16[768,128]{1,0:T(8,128)(2,1)} %get-tuple-element.41.keep_kv_ref), channel_id=1, source_target_pairs={{0,8},{8,0},{4,12},{12,4},{16,24},{24,16},{20,28},{28,20},{1,9},{9... | collective-permute-start | bytes 589832 | tf_op jit(solution)/shard_map/ppermute | solution.py:258
  13.6 0.0 copy-start.3
  13.6 1.0 %copy-done.3 = bf16[768,128]{1,0:T(8,128)(2,1)S(1)} copy-done((bf16[768,128]{1,0:T(8,128)(2,1)S(1)}, bf16[768,128]{1,0:T(8,128)(2,1)}, u32[]{:S(2)}) %copy-start.3) | copy-done | bytes 196632
  14.6 0.0 copy-start.4
  14.6 0.9 %copy-done.4 = bf16[400,128]{1,0:T(8,128)(2,1)S(1)} copy-done((bf16[400,128]{1,0:T(8,128)(2,1)S(1)}, bf16[400,128]{1,0:T(8,128)(2,1)}, u32[]{:S(2)}) %copy-start.4) | copy-done | bytes 102424
  15.5 0.0 collective-permute-done.3.kept_second_ref
  15.5 0.0 copy-start.5
  15.5 0.7 %copy-done.5 = bf16[768,128]{1,0:T(8,128)(2,1)} copy-done((bf16[768,128]{1,0:T(8,128)(2,1)}, bf16[768,128]{1,0:T(8,128)(2,1)S(1)}, u32[]{:S(2)}) %copy-start.5) | copy-done | bytes 196632
  16.2 2.3 %collective-permute-done.2.kept_first_ref = bf16[768,128]{1,0:T(8,128)(2,1)S(1)} collective-permute-done((bf16[768,128]{1,0:T(8,128)(2,1)}, bf16[768,128]{1,0:T(8,128)(2,1)S(1)}, u32[]{:S(2)}, u32[]{:S(2)}) %collective-permute-start.2) | collective-permute-done | bytes 196640 | tf_op jit(solution)/shard_map/ppermute | solution.py:258
  18.5 0.0 copy-start.7
  18.5 0.7 %copy-done.7 = bf16[768,128]{1,0:T(8,128)(2,1)} copy-done((bf16[768,128]{1,0:T(8,128)(2,1)}, bf16[768,128]{1,0:T(8,128)(2,1)S(1)}, u32[]{:S(2)}) %copy-start.7) | copy-done | bytes 196632
  19.2 0.0 collective-permute-done.came_ref
  19.2 0.0 collective-permute-done.1.wp_ref
  19.2 0.0 copy-start.1
  19.2 1.5 %copy-done.1 = bf16[256,5120]{1,0:T(8,128)(2,1)} copy-done((bf16[256,5120]{1,0:T(8,128)(2,1)}, bf16[256,5120]{1,0:T(8,128)(2,1)S(1)}, u32[]{:S(2)}) %copy-start.1) | copy-done | bytes 2621464
  20.7 0.8 %shard_map.66 = (s32[8,128]{1,0:T(8,128)S(1)}, bf16[2,384,128]{2,1,0:T(8,128)(2,1)S(1)}, bf16[768,128]{1,0:T(8,128)(2,1)}, bf16[768,128]{1,0:T(8,128)(2,1)}) custom-call(s32[1]{0:T(128)} %bitcast.tile_ref, bf16[400,128]{1,0:T(8,128)(2,1)S(1)} %get-tuple-element.46.keep_q_ref, bf16[768,128]{1,0:T(8,128)(2,1)S(1)} %get-tuple-element.47.keep_kv_ref.own_ref, ...), custom_call_target="tpu_custom_call" | custom-call | bytes 1048576 | tf_op jit(solution)/shard_map/pallas_call | solution.py:30
  21.5 0.0 collective-permute-done.4.refs_0_
  21.5 0.9 %shard_map.70 = bf16[256,1536]{1,0:T(8,128)(2,1)} custom-call(bf16[256,5120]{1,0:T(8,128)(2,1)S(1)} %copy-done), custom_call_target="tpu_custom_call" | custom-call | bytes 1048576 | tf_op jit(solution)/shard_map/pallas_call | solution.py:30
  22.4 0.5 collective-permute-start.12
  23.0 0.9 %collective-permute-start.7 = (bf16[256,1024]{1,0:T(8,128)(2,1)S(1)}, bf16[256,1024]{1,0:T(8,128)(2,1)}, u32[]{:S(2)}, u32[]{:S(2)}) collective-permute-start(bf16[256,1024]{1,0:T(8,128)(2,1)S(1)} %collective-permute-done.4.refs_0_), channel_id=1, source_target_pairs={{0,4},{4,0},{8,12},{12,8},{16,20},{20,16},{24,28},{28,24},{1,5},{5... | collective-permute-start | bytes 1572872 | tf_op jit(solution)/shard_map/ppermute | solution.py:262
  23.9 1.3 %collective-permute-start.6 = (bf16[768,128]{1,0:T(8,128)(2,1)}, bf16[768,128]{1,0:T(8,128)(2,1)}, u32[]{:S(2)}, u32[]{:S(2)}) collective-permute-start(bf16[768,128]{1,0:T(8,128)(2,1)} %get-tuple-element.53.came_ref), channel_id=1, source_target_pairs={{8,16},{16,8},{12,20},{20,12},{9,17},{17,9},{13,21},{21,13},{10,18... | collective-permute-start | bytes 589832 | tf_op jit(solution)/shard_map/ppermute | solution.py:258
  25.2 3.8 %collective-permute-start.5 = (bf16[768,128]{1,0:T(8,128)(2,1)}, bf16[768,128]{1,0:T(8,128)(2,1)}, u32[]{:S(2)}, u32[]{:S(2)}) collective-permute-start(bf16[768,128]{1,0:T(8,128)(2,1)} %get-tuple-element.53.came_ref), channel_id=1, source_target_pairs={{0,8},{8,0},{4,12},{12,4},{16,24},{24,16},{20,28},{28,20},{1,9},{9... | collective-permute-start | bytes 589832 | tf_op jit(solution)/shard_map/ppermute | solution.py:258
  29.0 0.4 collective-permute-start.8
  29.4 0.0 copy-start.2
  29.4 0.0 copy-start.6
  29.4 1.1 %copy-done.6 = bf16[768,128]{1,0:T(8,128)(2,1)S(1)} copy-done((bf16[768,128]{1,0:T(8,128)(2,1)S(1)}, bf16[768,128]{1,0:T(8,128)(2,1)}, u32[]{:S(2)}) %copy-start.6) | copy-done | bytes 196632
  30.5 0.0 copy-start.8
  30.5 0.9 %copy-done.8 = bf16[768,128]{1,0:T(8,128)(2,1)S(1)} copy-done((bf16[768,128]{1,0:T(8,128)(2,1)S(1)}, bf16[768,128]{1,0:T(8,128)(2,1)}, u32[]{:S(2)}) %copy-start.8) | copy-done | bytes 196632
  31.4 4.5 %shard_map.67._ = f32[2,136,384]{2,1,0:T(8,128)S(1)} custom-call(s32[8,128]{1,0:T(8,128)S(1)} %get-tuple-element.49.flag_ref, s32[1]{0:T(128)} %bitcast.tile_ref, bf16[2,384,128]{2,1,0:T(8,128)(2,1)S(1)} %get-tuple-element.52.q_ref, bf16[768,128]{1,0:T(8,128)(2,1)S(1)} %get-tuple-element.47.keep_kv_ref.own_ref, bf16[768,128]{1,0:T(8,128)(2,1)} %get-tuple-element.53.came_ref, ...), custom_call_target="tpu_custom_call" | custom-call | flops 603979776 | bytes 1048576 | tf_op jit(solution)/shard_map/pallas_call | solution.py:30
  35.9 0.0 collective-permute-done.6.second_ref
  35.9 0.0 collective-permute-done.5.first_ref
  35.9 2.2 %shard_map.68.state_ref = f32[2,136,384]{2,1,0:T(8,128)S(1)} custom-call(s32[8,128]{1,0:T(8,128)S(1)} %get-tuple-element.49.flag_ref, s32[1]{0:T(128)} %bitcast.tile_ref, bf16[2,384,128]{2,1,0:T(8,128)(2,1)S(1)} %get-tuple-element.52.q_ref, bf16[768,128]{1,0:T(8,128)(2,1)} %collective-permute-done.5.first_ref, ...), custom_call_target="tpu_custom_call", output_to_operand_aliasing={{}: (5, {})} | custom-call | flops 301989888 | bytes 1048576 | tf_op jit(solution)/shard_map/pallas_call | solution.py:30
  38.1 0.0 collective-permute-done.7.refs_2_
  38.1 3.3 %collective-permute-done.8.refs_0_ = bf16[768,128]{1,0:T(8,128)(2,1)} collective-permute-done((bf16[768,128]{1,0:T(8,128)(2,1)}, bf16[768,128]{1,0:T(8,128)(2,1)}, u32[]{:S(2)}, u32[]{:S(2)}) %collective-permute-start.8) | collective-permute-done | bytes 196640 | tf_op jit(solution)/shard_map/ppermute | solution.py:258
  41.4 1.7 %shard_map.69 = (bf16[2,96,128]{2,1,0:T(8,128)(2,1)S(1)}, bf16[2,96,128]{2,1,0:T(8,128)(2,1)S(1)}, bf16[2,96,128]{2,1,0:T(8,128)(2,1)S(1)}, bf16[2,96,128]{2,1,0:T(8,128)(2,1)S(1)}) custom-call(s32[8,128]{1,0:T(8,128)S(1)} %get-tuple-element.49.flag_ref, s32[1]{0:T(128)} %bitcast.tile_ref, s32[1]{0:T(128)} %bitcast.1.head_ref, ...), custom_call_target="tpu_custom_call" | custom-call | flops 75497472 | bytes 1048576 | tf_op jit(solution)/shard_map/pallas_call | solution.py:30
  43.1 0.1 collective-permute-start.9
  43.2 1.0 %collective-permute-start.10 = (bf16[2,96,128]{2,1,0:T(8,128)(2,1)S(1)}, bf16[2,96,128]{2,1,0:T(8,128)(2,1)S(1)}, u32[]{:S(2)}, u32[]{:S(2)}) collective-permute-start(bf16[2,96,128]{2,1,0:T(8,128)(2,1)S(1)} %get-tuple-element.61), channel_id=1, source_target_pairs={{0,4},{4,0},{8,12},{12,8},{16,20},{20,16},{24,28},{28,24},{1,5},{5... | collective-permute-start | bytes 147464 | tf_op jit(solution)/shard_map/ppermute | solution.py:262
  44.2 0.8 %collective-permute-start.11 = (bf16[2,96,128]{2,1,0:T(8,128)(2,1)S(1)}, bf16[2,96,128]{2,1,0:T(8,128)(2,1)S(1)}, u32[]{:S(2)}, u32[]{:S(2)}) collective-permute-start(bf16[2,96,128]{2,1,0:T(8,128)(2,1)S(1)} %get-tuple-element.62), channel_id=1, source_target_pairs={{0,1},{1,0},{2,3},{3,2},{4,5},{5,4},{6,7},{7,6},{8,9},{9,8},{10,11... | collective-permute-start | bytes 147464 | tf_op jit(solution)/shard_map/ppermute | solution.py:266
  45.1 1.7 %collective-permute-done.9.cross_ref = bf16[2,96,128]{2,1,0:T(8,128)(2,1)S(1)} collective-permute-done((bf16[2,96,128]{2,1,0:T(8,128)(2,1)S(1)}, bf16[2,96,128]{2,1,0:T(8,128)(2,1)S(1)}, u32[]{:S(2)}, u32[]{:S(2)}) %collective-permute-start.9) | collective-permute-done | bytes 49184 | tf_op jit(solution)/shard_map/ppermute | solution.py:273
  46.8 1.1 %collective-permute-done.10.y_ref = bf16[2,96,128]{2,1,0:T(8,128)(2,1)S(1)} collective-permute-done((bf16[2,96,128]{2,1,0:T(8,128)(2,1)S(1)}, bf16[2,96,128]{2,1,0:T(8,128)(2,1)S(1)}, u32[]{:S(2)}, u32[]{:S(2)}) %collective-permute-start.10) | collective-permute-done | bytes 49184 | tf_op jit(solution)/shard_map/ppermute | solution.py:262
  47.9 0.0 collective-permute-done.11.core_ref
  47.9 0.0 collective-permute-done.12.refs_4_
  47.9 0.0 copy-done.2
  47.9 0.4 shard_map.71
  48.3 0.2 collective-permute-start.16
  48.5 0.4 collective-permute-start.14
  48.9 0.1 collective-permute-start.15
  49.0 0.9 %collective-permute-start.13 = (bf16[96,2048]{1,0:T(8,128)(2,1)S(1)}, bf16[96,2048]{1,0:T(8,128)(2,1)S(1)}, u32[]{:S(2)}, u32[]{:S(2)}) collective-permute-start(bf16[96,2048]{1,0:T(8,128)(2,1)S(1)} %get-tuple-element.69), channel_id=1, source_target_pairs={{2,0},{3,1},{0,2},{1,3},{6,4},{7,5},{4,6},{5,7},{10,8},{11,9},{8,1... | collective-permute-start | bytes 1179656 | tf_op jit(solution)/shard_map/ppermute | solution.py:278
  49.9 1.0 %shard_map.72.near_ref = f32[96,5120]{1,0:T(8,128)S(1)} custom-call(bf16[96,512]{1,0:T(8,128)(2,1)S(1)} %get-tuple-element.68.a_ref, bf16[256,5120]{1,0:T(8,128)(2,1)S(1)} %copy-done, bf16[256,5120]{1,0:T(8,128)(2,1)S(1)} %copy-done.2), custom_call_target="tpu_custom_call" | custom-call | flops 503316480 | bytes 1048576 | tf_op jit(solution)/shard_map/pallas_call | solution.py:30
  50.9 9.6 %collective-permute-done.13.far_ref = bf16[96,2048]{1,0:T(8,128)(2,1)S(1)} collective-permute-done((bf16[96,2048]{1,0:T(8,128)(2,1)S(1)}, bf16[96,2048]{1,0:T(8,128)(2,1)S(1)}, u32[]{:S(2)}, u32[]{:S(2)}) %collective-permute-start.13) | collective-permute-done | bytes 393248 | tf_op jit(solution)/shard_map/ppermute | solution.py:278
  60.4 0.0 collective-permute-done.14.refs_1_
  60.4 0.0 collective-permute-done.15.refs_3_
  60.4 0.0 collective-permute-done.16.refs_5_
  60.4 3.0 %shard_map.73 = bf16[96,5120]{1,0:T(8,128)(2,1)} custom-call(s32[1]{0:T(128)} %bitcast.tile_ref, f32[96,5120]{1,0:T(8,128)S(1)} %shard_map.72.near_ref, bf16[96,2048]{1,0:T(8,128)(2,1)S(1)} %collective-permute-done.13.far_ref, bf16[256,1024]{1,0:T(8,128)(2,1)S(1)} %collective-permute-done.4.refs_0_, bf16[256,1024]{1,0:T(8,128)(2,1)S(1)} %collective-permute-done.14.refs_1_, ...), custom_call_target="tpu_custom_call" | custom-call | flops 503316480 | bytes 1048576 | tf_op jit(solution)/shard_map/pallas_call | solution.py:30
  (1 shorter events, 0.0 us)
Async XLA Ops:
  0.0 3.9 %copy-start = (bf16[256,5120]{1,0:T(8,128)(2,1)S(1)}, bf16[256,5120]{1,0:T(8,128)(2,1)}, u32[]{:S(2)}) copy-start(bf16[256,5120]{1,0:T(8,128)(2,1)} %w_ref.6) | copy-start | bytes 7864324
  3.9 15.3 %collective-permute-start.1 = (bf16[256,5120]{1,0:T(8,128)(2,1)S(1)}, bf16[256,5120]{1,0:T(8,128)(2,1)S(1)}, u32[]{:S(2)}, u32[]{:S(2)}) collective-permute-start(bf16[256,5120]{1,0:T(8,128)(2,1)S(1)} %copy-done), channel_id=1, source_target_pairs={{0,1},{1,0},{2,3},{3,2},{4,5},{5,4},{6,7},{7,6},{8,9},{9,8},{10,11... | collective-permute-start | bytes 7864328 | tf_op jit(solution)/shard_map/ppermute | solution.py:266
  4.4 17.1 %collective-permute-start.4 = (bf16[256,1024]{1,0:T(8,128)(2,1)}, bf16[256,1024]{1,0:T(8,128)(2,1)S(1)}, u32[]{:S(2)}, u32[]{:S(2)}) collective-permute-start(bf16[256,1024]{1,0:T(8,128)(2,1)} %get-tuple-element.51), channel_id=1, source_target_pairs={{2,0},{3,1},{0,2},{1,3},{6,4},{7,5},{4,6},{5,7},{10,8},{11,9},{8,1... | collective-permute-start | bytes 1572872 | tf_op jit(solution)/shard_map/ppermute | solution.py:278
  7.0 12.2 %collective-permute-start = (bf16[1168,128]{1,0:T(8,128)(2,1)}, bf16[1168,128]{1,0:T(8,128)(2,1)S(1)}, u32[]{:S(2)}, u32[]{:S(2)}) collective-permute-start(bf16[1168,128]{1,0:T(8,128)(2,1)} %get-tuple-element.40), channel_id=1, source_target_pairs={{0,4},{4,0},{8,12},{12,8},{16,20},{20,16},{24,28},{28,24},{1,5},{5... | collective-permute-start | bytes 897032 | tf_op jit(solution)/shard_map/ppermute | solution.py:262
  8.5 7.0 %collective-permute-start.3 = (bf16[768,128]{1,0:T(8,128)(2,1)}, bf16[768,128]{1,0:T(8,128)(2,1)S(1)}, u32[]{:S(2)}, u32[]{:S(2)}) collective-permute-start(bf16[768,128]{1,0:T(8,128)(2,1)} %get-tuple-element.41.keep_kv_ref), channel_id=1, source_target_pairs={{8,16},{16,8},{12,20},{20,12},{9,17},{17,9},{13,21},{21,13},{10,18... | collective-permute-start | bytes 589832 | tf_op jit(solution)/shard_map/ppermute | solution.py:258
  9.1 9.3 %collective-permute-start.2 = (bf16[768,128]{1,0:T(8,128)(2,1)}, bf16[768,128]{1,0:T(8,128)(2,1)S(1)}, u32[]{:S(2)}, u32[]{:S(2)}) collective-permute-start(bf16[768,128]{1,0:T(8,128)(2,1)} %get-tuple-element.41.keep_kv_ref), channel_id=1, source_target_pairs={{0,8},{8,0},{4,12},{12,4},{16,24},{24,16},{20,28},{28,20},{1,9},{9... | collective-permute-start | bytes 589832 | tf_op jit(solution)/shard_map/ppermute | solution.py:258
  13.6 1.0 %copy-start.3 = (bf16[768,128]{1,0:T(8,128)(2,1)S(1)}, bf16[768,128]{1,0:T(8,128)(2,1)}, u32[]{:S(2)}) copy-start(bf16[768,128]{1,0:T(8,128)(2,1)} %get-tuple-element.41.keep_kv_ref) | copy-start | bytes 589828
  14.6 0.9 %copy-start.4 = (bf16[400,128]{1,0:T(8,128)(2,1)S(1)}, bf16[400,128]{1,0:T(8,128)(2,1)}, u32[]{:S(2)}) copy-start(bf16[400,128]{1,0:T(8,128)(2,1)} %get-tuple-element.43.keep_q_ref) | copy-start | bytes 307204
  15.5 0.7 %copy-start.5 = (bf16[768,128]{1,0:T(8,128)(2,1)}, bf16[768,128]{1,0:T(8,128)(2,1)S(1)}, u32[]{:S(2)}) copy-start(bf16[768,128]{1,0:T(8,128)(2,1)S(1)} %collective-permute-done.3.kept_second_ref) | copy-start | bytes 589828
  18.5 0.7 %copy-start.7 = (bf16[768,128]{1,0:T(8,128)(2,1)}, bf16[768,128]{1,0:T(8,128)(2,1)S(1)}, u32[]{:S(2)}) copy-start(bf16[768,128]{1,0:T(8,128)(2,1)S(1)} %collective-permute-done.2.kept_first_ref) | copy-start | bytes 589828
  19.2 1.5 %copy-start.1 = (bf16[256,5120]{1,0:T(8,128)(2,1)}, bf16[256,5120]{1,0:T(8,128)(2,1)S(1)}, u32[]{:S(2)}) copy-start(bf16[256,5120]{1,0:T(8,128)(2,1)S(1)} %collective-permute-done.1.wp_ref) | copy-start | bytes 7864324
  22.4 25.4 %collective-permute-start.12 = (bf16[256,1536]{1,0:T(8,128)(2,1)}, bf16[256,1536]{1,0:T(8,128)(2,1)}, u32[]{:S(2)}, u32[]{:S(2)}) collective-permute-start(bf16[256,1536]{1,0:T(8,128)(2,1)} %shard_map.70), channel_id=1, source_target_pairs={{2,0},{3,1},{0,2},{1,3},{6,4},{7,5},{4,6},{5,7},{10,8},{11,9},{8,1... | collective-permute-start | bytes 2359304 | tf_op jit(solution)/shard_map/ppermute | solution.py:278
  23.0 15.2 %collective-permute-start.7 = (bf16[256,1024]{1,0:T(8,128)(2,1)S(1)}, bf16[256,1024]{1,0:T(8,128)(2,1)}, u32[]{:S(2)}, u32[]{:S(2)}) collective-permute-start(bf16[256,1024]{1,0:T(8,128)(2,1)S(1)} %collective-permute-done.4.refs_0_), channel_id=1, source_target_pairs={{0,4},{4,0},{8,12},{12,8},{16,20},{20,16},{24,28},{28,24},{1,5},{5... | collective-permute-start | bytes 1572872 | tf_op jit(solution)/shard_map/ppermute | solution.py:262
  23.9 12.0 %collective-permute-start.6 = (bf16[768,128]{1,0:T(8,128)(2,1)}, bf16[768,128]{1,0:T(8,128)(2,1)}, u32[]{:S(2)}, u32[]{:S(2)}) collective-permute-start(bf16[768,128]{1,0:T(8,128)(2,1)} %get-tuple-element.53.came_ref), channel_id=1, source_target_pairs={{8,16},{16,8},{12,20},{20,12},{9,17},{17,9},{13,21},{21,13},{10,18... | collective-permute-start | bytes 589832 | tf_op jit(solution)/shard_map/ppermute | solution.py:258
  25.2 10.7 %collective-permute-start.5 = (bf16[768,128]{1,0:T(8,128)(2,1)}, bf16[768,128]{1,0:T(8,128)(2,1)}, u32[]{:S(2)}, u32[]{:S(2)}) collective-permute-start(bf16[768,128]{1,0:T(8,128)(2,1)} %get-tuple-element.53.came_ref), channel_id=1, source_target_pairs={{0,8},{8,0},{4,12},{12,4},{16,24},{24,16},{20,28},{28,20},{1,9},{9... | collective-permute-start | bytes 589832 | tf_op jit(solution)/shard_map/ppermute | solution.py:258
  29.0 12.4 %collective-permute-start.8 = (bf16[768,128]{1,0:T(8,128)(2,1)}, bf16[768,128]{1,0:T(8,128)(2,1)}, u32[]{:S(2)}, u32[]{:S(2)}) collective-permute-start(bf16[768,128]{1,0:T(8,128)(2,1)} %get-tuple-element.58), channel_id=1, source_target_pairs={{0,16},{16,0},{4,20},{20,4},{8,24},{24,8},{12,28},{28,12},{1,17},{... | collective-permute-start | bytes 589832 | tf_op jit(solution)/shard_map/ppermute | solution.py:258
  29.4 18.5 %copy-start.2 = (bf16[256,5120]{1,0:T(8,128)(2,1)S(1)}, bf16[256,5120]{1,0:T(8,128)(2,1)}, u32[]{:S(2)}) copy-start(bf16[256,5120]{1,0:T(8,128)(2,1)} %copy-done.1) | copy-start | bytes 7864324
  29.4 1.1 %copy-start.6 = (bf16[768,128]{1,0:T(8,128)(2,1)S(1)}, bf16[768,128]{1,0:T(8,128)(2,1)}, u32[]{:S(2)}) copy-start(bf16[768,128]{1,0:T(8,128)(2,1)} %copy-done.5) | copy-start | bytes 589828
  30.5 0.9 %copy-start.8 = (bf16[768,128]{1,0:T(8,128)(2,1)S(1)}, bf16[768,128]{1,0:T(8,128)(2,1)}, u32[]{:S(2)}) copy-start(bf16[768,128]{1,0:T(8,128)(2,1)} %copy-done.7) | copy-start | bytes 589828
  43.1 3.6 %collective-permute-start.9 = (bf16[2,96,128]{2,1,0:T(8,128)(2,1)S(1)}, bf16[2,96,128]{2,1,0:T(8,128)(2,1)S(1)}, u32[]{:S(2)}, u32[]{:S(2)}) collective-permute-start(bf16[2,96,128]{2,1,0:T(8,128)(2,1)S(1)} %get-tuple-element.60), channel_id=1, source_target_pairs={{0,5},{1,4},{2,7},{3,6},{4,1},{5,0},{6,3},{7,2},{8,13},{9,12},{10,... | collective-permute-start | bytes 147464 | tf_op jit(solution)/shard_map/ppermute | solution.py:273
  43.2 4.6 %collective-permute-start.10 = (bf16[2,96,128]{2,1,0:T(8,128)(2,1)S(1)}, bf16[2,96,128]{2,1,0:T(8,128)(2,1)S(1)}, u32[]{:S(2)}, u32[]{:S(2)}) collective-permute-start(bf16[2,96,128]{2,1,0:T(8,128)(2,1)S(1)} %get-tuple-element.61), channel_id=1, source_target_pairs={{0,4},{4,0},{8,12},{12,8},{16,20},{20,16},{24,28},{28,24},{1,5},{5... | collective-permute-start | bytes 147464 | tf_op jit(solution)/shard_map/ppermute | solution.py:262
  44.2 3.6 %collective-permute-start.11 = (bf16[2,96,128]{2,1,0:T(8,128)(2,1)S(1)}, bf16[2,96,128]{2,1,0:T(8,128)(2,1)S(1)}, u32[]{:S(2)}, u32[]{:S(2)}) collective-permute-start(bf16[2,96,128]{2,1,0:T(8,128)(2,1)S(1)} %get-tuple-element.62), channel_id=1, source_target_pairs={{0,1},{1,0},{2,3},{3,2},{4,5},{5,4},{6,7},{7,6},{8,9},{9,8},{10,11... | collective-permute-start | bytes 147464 | tf_op jit(solution)/shard_map/ppermute | solution.py:266
  48.3 12.1 %collective-permute-start.16 = (bf16[256,1536]{1,0:T(8,128)(2,1)}, bf16[256,1536]{1,0:T(8,128)(2,1)S(1)}, u32[]{:S(2)}, u32[]{:S(2)}) collective-permute-start(bf16[256,1536]{1,0:T(8,128)(2,1)} %collective-permute-done.12.refs_4_), channel_id=1, source_target_pairs={{0,1},{1,0},{2,3},{3,2},{4,5},{5,4},{6,7},{7,6},{8,9},{9,8},{10,11... | collective-permute-start | bytes 2359304 | tf_op jit(solution)/shard_map/ppermute | solution.py:266
  48.5 12.0 %collective-permute-start.14 = (bf16[256,1024]{1,0:T(8,128)(2,1)S(1)}, bf16[256,1024]{1,0:T(8,128)(2,1)S(1)}, u32[]{:S(2)}, u32[]{:S(2)}) collective-permute-start(bf16[256,1024]{1,0:T(8,128)(2,1)S(1)} %collective-permute-done.4.refs_0_), channel_id=1, source_target_pairs={{0,1},{1,0},{2,3},{3,2},{4,5},{5,4},{6,7},{7,6},{8,9},{9,8},{10,11... | collective-permute-start | bytes 1572872 | tf_op jit(solution)/shard_map/ppermute | solution.py:266
  48.9 11.6 %collective-permute-start.15 = (bf16[256,1024]{1,0:T(8,128)(2,1)}, bf16[256,1024]{1,0:T(8,128)(2,1)S(1)}, u32[]{:S(2)}, u32[]{:S(2)}) collective-permute-start(bf16[256,1024]{1,0:T(8,128)(2,1)} %collective-permute-done.7.refs_2_), channel_id=1, source_target_pairs={{0,1},{1,0},{2,3},{3,2},{4,5},{5,4},{6,7},{7,6},{8,9},{9,8},{10,11... | collective-permute-start | bytes 1572872 | tf_op jit(solution)/shard_map/ppermute | solution.py:266
  49.0 11.4 %collective-permute-start.13 = (bf16[96,2048]{1,0:T(8,128)(2,1)S(1)}, bf16[96,2048]{1,0:T(8,128)(2,1)S(1)}, u32[]{:S(2)}, u32[]{:S(2)}) collective-permute-start(bf16[96,2048]{1,0:T(8,128)(2,1)S(1)} %get-tuple-element.69), channel_id=1, source_target_pairs={{2,0},{3,1},{0,2},{1,3},{6,4},{7,5},{4,6},{5,7},{10,8},{11,9},{8,1... | collective-permute-start | bytes 1179656 | tf_op jit(solution)/shard_map/ppermute | solution.py:278

commit v3 on v2

--- a/solution.py
+++ b/solution.py
@@ -44,10 +44,10 @@
 
 
 def pack_kernel(
-    tile_ref, list_ref, count_ref, q_ref, k_ref, v_ref, w_ref,
+    index_ref, list_ref, count_ref, q_ref, k_ref, v_ref, w_ref,
     keep_q_ref, keep_kv_ref, send_ref, side_ref, sems,
 ):
-    parity = tile_ref[0] & 1
+    parity = index_ref[0] & 1
     rows = q_ref.shape[0]
     copies = []
 
@@ -69,7 +69,7 @@
     for offset in range(-REACH, REACH + 1):
         listed = jnp.int32(0)
         for slot in range(list_ref.shape[1]):
-            found = (list_ref[0, slot] == tile_ref[0] + offset) & (slot < count_ref[0])
+            found = (list_ref[0, slot] == index_ref[0] + offset) & (slot < count_ref[0])
             listed = jnp.where(found, 1, listed)
         flags = jnp.where(lane == offset + REACH, listed.astype(F32), flags)
     keep_q_ref[rows:, :] = flags.astype(BF16)
@@ -88,12 +88,12 @@
 
 
 def merge_kernel(
-    tile_ref, keep_q_ref, keep_kv_ref, came_ref, flag_ref, q_ref, kv_ref, odd_ref, even_ref
+    index_ref, keep_q_ref, keep_kv_ref, came_ref, flag_ref, q_ref, kv_ref, odd_ref, even_ref
 ):
-    parity = tile_ref[0] & 1
+    parity = index_ref[0] & 1
     rows = q_ref.shape[1]
     kv_ref[...] = came_ref[0 : 2 * rows, :]
-    up = (tile_ref[0] & 4) == 0
+    up = (index_ref[0] & 4) == 0
 
     def place(out, own):
         @pl.when(own)
@@ -143,40 +143,40 @@
             step(q_ref[a], ref[0:rows, :], ref[rows : 2 * rows, :], state_ref, a)
 
 
-def visit_pairs(flag_ref, tile_ref, q_ref, state_ref, tiles):
-    parity = tile_ref[0] & 1
+def visit_pairs(flag_ref, index_ref, q_ref, state_ref, tiles):
+    parity = index_ref[0] & 1
     for base, own, ref in tiles:
         tile = base + (parity if own else 1 - parity)
         visit(flag_ref, q_ref, state_ref, [(a, tile, ref) for a in range(2)])
 
 
 def first_kernel(
-    flag_ref, tile_ref, q_ref, own_ref, came_ref, kept_first_ref, kept_second_ref, state_ref
+    flag_ref, index_ref, q_ref, own_ref, came_ref, kept_first_ref, kept_second_ref, state_ref
 ):
     state_ref[...] = jnp.zeros_like(state_ref)
     for a in range(2):
         state_ref[a, HD : HD + 1, :] = jnp.full((1, state_ref.shape[2]), NEG, F32)
-    base = jnp.where((tile_ref[0] & 2) == 0, 2, -2)
+    base = jnp.where((index_ref[0] & 2) == 0, 2, -2)
     tiles = [(0, True, own_ref), (0, False, came_ref)]
     tiles += [(base, True, kept_first_ref), (-base, True, kept_second_ref)]
-    visit_pairs(flag_ref, tile_ref, q_ref, state_ref, tiles)
-
-
-def second_kernel(flag_ref, tile_ref, q_ref, first_ref, second_ref, _, state_ref):
-    base = jnp.where((tile_ref[0] & 2) == 0, 2, -2)
+    visit_pairs(flag_ref, index_ref, q_ref, state_ref, tiles)
+
+
+def second_kernel(flag_ref, index_ref, q_ref, first_ref, second_ref, _, state_ref):
+    base = jnp.where((index_ref[0] & 2) == 0, 2, -2)
     tiles = [(base, False, first_ref), (-base, False, second_ref)]
-    visit_pairs(flag_ref, tile_ref, q_ref, state_ref, tiles)
-
-
-def third_kernel(flag_ref, tile_ref, head_ref, q_ref, state_ref, *refs, far):
+    visit_pairs(flag_ref, index_ref, q_ref, state_ref, tiles)
+
+
+def third_kernel(flag_ref, index_ref, q_ref, state_ref, *refs, far):
     outs, last = refs[far:-1], refs[-1]
     last[...] = state_ref[...]
     for i in range(far):
-        above = ((tile_ref[0] & 4) == 0) == (i == 0)
+        above = ((index_ref[0] & 4) == 0) == (i == 0)
         which = (jnp.where(above, 1, 0), jnp.where(above, 4, -3), refs[i])
         visit(flag_ref, q_ref, last, [which])
-    parity = tile_ref[0] & 1
-    core = head_ref[0] & 1
+    parity = index_ref[0] & 1
+    core = index_ref[1] & 1
     for i, a in enumerate((parity, 1 - parity)):
         done = last[a, 0:HD, :] / last[a, HD + 1 : HD + 2, :]
         rows = done.T.astype(BF16)
@@ -205,10 +205,10 @@
 
 
 def send_kernel(
-    tile_ref, head_ref, own_ref, y_ref, core_ref, cross_ref, w_ref, wp_ref, a_ref, far_ref
+    index_ref, own_ref, y_ref, core_ref, cross_ref, w_ref, wp_ref, a_ref, far_ref
 ):
-    parity = tile_ref[0] & 1
-    chip = head_ref[0] >> 1
+    parity = index_ref[0] & 1
+    chip = index_ref[1] >> 1
     deep = a_ref.shape[1]
     for out, which in ((a_ref, chip), (far_ref, 1 - chip)):
         for group, (mine, others) in enumerate(((own_ref, y_ref), (core_ref, cross_ref))):
@@ -231,9 +231,9 @@
         near_ref[:, start : start + CHUNK] = multiply(own, (w_ref, wp_ref), start, start + CHUNK)
 
 
-def last_kernel(tile_ref, near_ref, far_ref, *refs):
+def last_kernel(index_ref, near_ref, far_ref, *refs):
     weights, out_ref = refs[:-1], refs[-1]
-    parity = tile_ref[0] & 1
+    parity = index_ref[0] & 1
     deep = 2 * weights[0].shape[0]
     far = far_ref[:, 0:deep]
     side = weights[0].shape[1]
@@ -305,15 +305,14 @@
     model = out_weight.shape[1]
     small = n_head == 4 and own_rows % 16 == 0
     head_index = lax.axis_index("head").astype(jnp.int32)
-    head = head_index.reshape(1)
-    tile = lax.axis_index("ctx").astype(jnp.int32).reshape(1)
+    index = jnp.stack([lax.axis_index("ctx").astype(jnp.int32), head_index])
 
     one = (rows, HD)
     payload, kv_shape = shape((3 * rows + FLAGS, HD)), shape((2 * rows, HD))
     keep_q, keep_kv, send, side_weight = call(
         pack_kernel,
         (shape((rows + FLAGS, HD)), kv_shape, payload, shape((width, SIDE))),
-        (tile, neighbours, counts, queries, keys, values, out_weight),
+        (index, neighbours, counts, queries, keys, values, out_weight),
         scratch=(pltpu.SemaphoreType.DMA((7,)),),
         in_hbm=(3, 4, 5, 6),
         vmem=58,
@@ -326,14 +325,20 @@
         side_own = from_chip(side_weight, 1)
 
     held_q, held_kv = call(stage_kernel, (shape((rows + FLAGS, HD)), kv_shape), (keep_q, keep_kv))
-    came, weight_pair, held_q, held_kv, *kept_near = lax.optimization_barrier(
-        (came, weight_pair, held_q, held_kv, *kept_near)
+    cut = []
+    if small:
+        ready, _ = lax.optimization_barrier((out_weight, held_q))
+        cut.append(
+            call(functools.partial(cut_kernel, first=2 * SIDE), shape((width, COMMON)), (ready,))
+        )
+    came, weight_pair, held_q, held_kv, kept_near, cut = lax.optimization_barrier(
+        (came, weight_pair, held_q, held_kv, kept_near, cut)
     )
     far = 1 if lax.axis_size("ctx") <= 8 else 2
     flags, q_pair, came_kv, *to_far = call(
         merge_kernel if far == 2 else functools.partial(merge_kernel, even_ref=None),
         (shape((8, HD), jnp.int32), shape((2,) + one), kv_shape) + (kv_shape,) * far,
-        (tile, held_q, held_kv, came),
+        (index, held_q, held_kv, came),
     )
     came_near = [swap_pairs(came_kv, 1, phase) for phase in range(2)]
     farther = [swap_pairs(to_far[i], 2, i) for i in range(far)]
@@ -343,7 +348,7 @@
     held = call(
         first_kernel,
         state,
-        (flags, tile, q_pair, held_kv, came_kv, *kept_near),
+        (flags, index, q_pair, held_kv, came_kv, *kept_near),
         32 * area * HD,
         8 * area,
     )
@@ -351,15 +356,12 @@
     if small:
         side_own, q_again = lax.optimization_barrier((side_own, q_pair))
         side_other = swap_tiles(side_own)
-        ready, _ = lax.optimization_barrier((out_weight, side_own))
-        common_weight = call(
-            functools.partial(cut_kernel, first=2 * SIDE), shape((width, COMMON)), (ready,)
-        )
-        common = from_chip(common_weight, 1)
+        ready, _ = lax.optimization_barrier((cut[0], side_own))
+        common = from_chip(ready, 1)
     held = call(
         second_kernel,
         state,
-        (flags, tile, q_again, *came_near, held),
+        (flags, index, q_again, *came_near, held),
         16 * area * HD,
         4 * area,
         alias={5: 0},
@@ -370,7 +372,7 @@
     attended = call(
         functools.partial(third_kernel, far=far),
         (shape(block),) * 4 if small else (shape(one),) * 2,
-        (flags, tile, head, q_pair, held, *farther),
+        (flags, index, q_pair, held, *farther),
         4 * area * HD,
         area,
         scratch=(pltpu.VMEM(state.shape, F32),),
@@ -378,7 +380,7 @@
     if not small:
         mine, theirs = attended
         got = swap_tiles(theirs)
-        even_tile = tile[0] % 2 == 0
+        even_tile = index[0] % 2 == 0
         joined = jnp.concatenate(
             [jnp.where(even_tile, mine, got), jnp.where(even_tile, got, mine)], axis=1
         )
@@ -398,7 +400,7 @@
     own_a, far_a = call(
         send_kernel,
         (shape((own_rows, deep)), shape((own_rows, deep + model - gathered))),
-        (tile, head, mine, from_y, from_core, from_cross) + near_weights,
+        (index, mine, from_y, from_core, from_cross) + near_weights,
         flops // 4,
         vmem=16,
     )
@@ -408,7 +410,7 @@
     far_weights = [each for piece, to in zip(pieces, ready) for each in (piece, swap_cores(to))]
     near = call(near_kernel, shape((own_rows, model), F32), (own_a,) + near_weights, flops, vmem=16)
     return call(
-        last_kernel, shape((own_rows, model)), (tile, near, got, *far_weights), flops, vmem=20
+        last_kernel, shape((own_rows, model)), (index, near, got, *far_weights), flops, vmem=20
     )
 
 

time: 63.5 us -> 62.4 us (0.983)
  local copies, waits for them, and re-layouts: 6.72 us -> 1.86 us
  waiting for transfers between devices: 18 us -> 22.3 us
  Pallas kernels: 17.6 us -> 15.2 us
  starting transfers between devices: 20.2 us -> 21.2 us
  other arithmetic: 0 us -> 0.66 us
    unnamed x18 -> x8, local copies, waits for them, and re-layouts: 6.72 us -> 1.86 us
    ppermute x5, waiting for transfers between devices: 5.61 us -> 9.06 us  [swap_pairs(): return lax.ppermute(value, 'ctx', pairs)]
    pallas_call x10, Pallas kernels: 17.6 us -> 15.2 us  [call(): pl.pallas_call(kernel, out_shape=outs, in_specs=[SMEM if s else HBM if i...]
    ppermute x3, waiting for transfers between devices: 9.57 us -> 10.5 us  [from_chip(): lax.ppermute(value, 'head', [((i + 2 * steps) % count, i) for i in range(...]
    ppermute x3, starting transfers between devices: 4.02 us -> 4.86 us  [from_chip(): lax.ppermute(value, 'head', [((i + 2 * steps) % count, i) for i in range(...]
    another operation x0 -> x1, other arithmetic: none -> 0.66 us  [local(): index = jnp.stack([lax.axis_index('ctx').astype(jnp.int32), head_index])]
  transfers between devices with their start and end apart: 17 -> 17, of which waited for: 5 -> 7; matrix products, arithmetic and copies ran while one was open for 0% -> 0% of each run, Pallas kernels for 16% -> 14%
where the time goes in v3:
time: 62.4 us; the launch traced here: 62.2 us
  waiting for transfers between devices  22.3 us (36%)
  starting transfers between devices  21.2 us (34%)
  Pallas kernels  15.2 us (24%)
  local copies, waits for them, and re-layouts  1.86 us (3%)
  between operations  0.94 us (2%)
  other arithmetic  0.66 us (1%)
    pallas_call x10, Pallas kernels, call(): pl.pallas_call(kernel, out_shape=outs, in_specs=[SMEM if s else HBM if i...  15.2 us
    ppermute x3, waiting for transfers between devices, from_chip(): lax.ppermute(value, 'head', [((i + 2 * steps) % count, i) for i in range(...  10.5 us
    ppermute x5, starting transfers between devices, swap_pairs(): return lax.ppermute(value, 'ctx', pairs)  10.2 us
    ppermute x5, waiting for transfers between devices, swap_pairs(): return lax.ppermute(value, 'ctx', pairs)  9.06 us
    ppermute x3, starting transfers between devices, from_chip(): lax.ppermute(value, 'head', [((i + 2 * steps) % count, i) for i in range(...  4.86 us
    ppermute x3, starting transfers between devices, swap_tiles(): lax.ppermute(value, 'ctx', [(i, i ^ 1) for i in range(lax.axis_size('ctx'...  3.61 us
    ppermute x5, starting transfers between devices, swap_cores(): lax.ppermute(value, 'head', [(i, i ^ 1) for i in range(lax.axis_size('hea...  2.45 us
    unnamed x8, local copies, waits for them, and re-layouts  1.86 us
  transfers between devices with their start and end apart: 17, of which 7 were waited for; matrix products, arithmetic and copies ran while one was open for 0% of the time, Pallas kernels for 14%

profile of v3, /device:TPU:0, one launch (start us, length us, event | category | flops | bytes accessed | tf_op | source)
XLA Modules:
  0.0 62.2 jit_solution(8768018125698868507)
XLA Ops:
  0.0 0.0 copy-start
  0.8 0.7 %pad_add_fusion.index_ref = s32[2]{0:T(128)} fusion(s32[1]{0:T(128)} %bitcast.1, s32[1]{0:T(128)} %bitcast), kind=kLoop, calls=%fused_computation | loop fusion | flops 2 | bytes 16 | tf_op jit(solution)/shard_map/stack | solution.py:308
  1.5 3.1 %shard_map.64 = (bf16[400,128]{1,0:T(8,128)(2,1)}, bf16[768,128]{1,0:T(8,128)(2,1)}, bf16[1168,128]{1,0:T(8,128)(2,1)}, bf16[256,1024]{1,0:T(8,128)(2,1)}) custom-call(s32[2]{0:T(128)} %pad_add_fusion.index_ref, s32[1,7]{1,0:T(1,128)} %list_ref.1, s32[1]{0:T(128)S(6)} %copy.9.count_ref, bf16[384,256]{1,0:T(8,128)(2,1)} %q_ref.1, bf16[384,256]{1,0:T(8,128)(2,1)} %k_ref.1, ...), custom_call_target="tpu_custom_call" | custom-call | bytes 1048576 | tf_op jit(solution)/shard_map/pallas_call | solution.py:30
  4.5 0.0 copy-start.3
  4.5 0.0 copy-done
  4.6 0.5 collective-permute-start.1
  5.1 2.6 %collective-permute-start.4 = (bf16[256,1024]{1,0:T(8,128)(2,1)}, bf16[256,1024]{1,0:T(8,128)(2,1)S(1)}, u32[]{:S(2)}, u32[]{:S(2)}) collective-permute-start(bf16[256,1024]{1,0:T(8,128)(2,1)} %get-tuple-element.54), channel_id=1, source_target_pairs={{2,0},{3,1},{0,2},{1,3},{6,4},{7,5},{4,6},{5,7},{10,8},{11,9},{8,1... | collective-permute-start | bytes 1572872 | tf_op jit(solution)/shard_map/ppermute | solution.py:278
  7.6 1.5 %collective-permute-start = (bf16[1168,128]{1,0:T(8,128)(2,1)}, bf16[1168,128]{1,0:T(8,128)(2,1)S(1)}, u32[]{:S(2)}, u32[]{:S(2)}) collective-permute-start(bf16[1168,128]{1,0:T(8,128)(2,1)} %get-tuple-element.42), channel_id=1, source_target_pairs={{0,4},{4,0},{8,12},{12,8},{16,20},{20,16},{24,28},{28,24},{1,5},{5... | collective-permute-start | bytes 897032 | tf_op jit(solution)/shard_map/ppermute | solution.py:262
  9.2 0.7 %collective-permute-start.3 = (bf16[768,128]{1,0:T(8,128)(2,1)}, bf16[768,128]{1,0:T(8,128)(2,1)S(1)}, u32[]{:S(2)}, u32[]{:S(2)}) collective-permute-start(bf16[768,128]{1,0:T(8,128)(2,1)} %get-tuple-element.43.keep_kv_ref), channel_id=1, source_target_pairs={{8,16},{16,8},{12,20},{20,12},{9,17},{17,9},{13,21},{21,13},{10,18... | collective-permute-start | bytes 589832 | tf_op jit(solution)/shard_map/ppermute | solution.py:258
  9.8 4.5 %collective-permute-start.2 = (bf16[768,128]{1,0:T(8,128)(2,1)}, bf16[768,128]{1,0:T(8,128)(2,1)S(1)}, u32[]{:S(2)}, u32[]{:S(2)}) collective-permute-start(bf16[768,128]{1,0:T(8,128)(2,1)} %get-tuple-element.43.keep_kv_ref), channel_id=1, source_target_pairs={{0,8},{8,0},{4,12},{12,4},{16,24},{24,16},{20,28},{28,20},{1,9},{9... | collective-permute-start | bytes 589832 | tf_op jit(solution)/shard_map/ppermute | solution.py:258
  14.3 0.0 copy-start.1
  14.3 1.0 %copy-done.1 = bf16[768,128]{1,0:T(8,128)(2,1)S(1)} copy-done((bf16[768,128]{1,0:T(8,128)(2,1)S(1)}, bf16[768,128]{1,0:T(8,128)(2,1)}, u32[]{:S(2)}) %copy-start.1) | copy-done | bytes 196632
  15.2 0.0 copy-start.2
  15.2 0.9 %copy-done.2 = bf16[400,128]{1,0:T(8,128)(2,1)S(1)} copy-done((bf16[400,128]{1,0:T(8,128)(2,1)S(1)}, bf16[400,128]{1,0:T(8,128)(2,1)}, u32[]{:S(2)}) %copy-start.2) | copy-done | bytes 102424
  16.2 0.1 shard_map.66
  16.2 0.0 collective-permute-done.3.kept_second_ref
  16.2 2.9 %collective-permute-done.2.kept_first_ref = bf16[768,128]{1,0:T(8,128)(2,1)S(1)} collective-permute-done((bf16[768,128]{1,0:T(8,128)(2,1)}, bf16[768,128]{1,0:T(8,128)(2,1)S(1)}, u32[]{:S(2)}, u32[]{:S(2)}) %collective-permute-start.2) | collective-permute-done | bytes 196640 | tf_op jit(solution)/shard_map/ppermute | solution.py:258
  19.2 0.0 collective-permute-done.came_ref
  19.2 0.0 collective-permute-done.1.wp_ref
  19.2 0.0 copy-done.3
  19.2 0.6 shard_map.67
  19.8 0.6 collective-permute-done.4.refs_0_
  20.4 1.8 %collective-permute-start.12 = (bf16[256,1536]{1,0:T(8,128)(2,1)S(1)}, bf16[256,1536]{1,0:T(8,128)(2,1)S(1)}, u32[]{:S(2)}, u32[]{:S(2)}) collective-permute-start(bf16[256,1536]{1,0:T(8,128)(2,1)S(1)} %shard_map.66), channel_id=1, source_target_pairs={{2,0},{3,1},{0,2},{1,3},{6,4},{7,5},{4,6},{5,7},{10,8},{11,9},{8,1... | collective-permute-start | bytes 2359304 | tf_op jit(solution)/shard_map/ppermute | solution.py:278
  22.1 1.5 %collective-permute-start.7 = (bf16[256,1024]{1,0:T(8,128)(2,1)S(1)}, bf16[256,1024]{1,0:T(8,128)(2,1)S(1)}, u32[]{:S(2)}, u32[]{:S(2)}) collective-permute-start(bf16[256,1024]{1,0:T(8,128)(2,1)S(1)} %collective-permute-done.4.refs_0_), channel_id=1, source_target_pairs={{0,4},{4,0},{8,12},{12,8},{16,20},{20,16},{24,28},{28,24},{1,5},{5... | collective-permute-start | bytes 1572872 | tf_op jit(solution)/shard_map/ppermute | solution.py:262
  23.6 0.7 %collective-permute-start.6 = (bf16[768,128]{1,0:T(8,128)(2,1)S(1)}, bf16[768,128]{1,0:T(8,128)(2,1)S(1)}, u32[]{:S(2)}, u32[]{:S(2)}) collective-permute-start(bf16[768,128]{1,0:T(8,128)(2,1)S(1)} %get-tuple-element.56.came_ref), channel_id=1, source_target_pairs={{8,16},{16,8},{12,20},{20,12},{9,17},{17,9},{13,21},{21,13},{10,18... | collective-permute-start | bytes 589832 | tf_op jit(solution)/shard_map/ppermute | solution.py:258
  24.3 4.5 %collective-permute-start.5 = (bf16[768,128]{1,0:T(8,128)(2,1)S(1)}, bf16[768,128]{1,0:T(8,128)(2,1)S(1)}, u32[]{:S(2)}, u32[]{:S(2)}) collective-permute-start(bf16[768,128]{1,0:T(8,128)(2,1)S(1)} %get-tuple-element.56.came_ref), channel_id=1, source_target_pairs={{0,8},{8,0},{4,12},{12,4},{16,24},{24,16},{20,28},{28,20},{1,9},{9... | collective-permute-start | bytes 589832 | tf_op jit(solution)/shard_map/ppermute | solution.py:258
  28.8 0.0 collective-permute-start.8
  28.8 4.1 %shard_map.68._ = f32[2,136,384]{2,1,0:T(8,128)S(1)} custom-call(s32[8,128]{1,0:T(8,128)S(1)} %get-tuple-element.52.flag_ref, s32[2]{0:T(128)S(1)} %copy-done.3, bf16[2,384,128]{2,1,0:T(8,128)(2,1)S(1)} %get-tuple-element.55.q_ref, bf16[768,128]{1,0:T(8,128)(2,1)S(1)} %get-tuple-element.50.keep_kv_ref.own_ref, ...), custom_call_target="tpu_custom_call" | custom-call | flops 603979776 | bytes 1048576 | tf_op jit(solution)/shard_map/pallas_call | solution.py:30
  32.9 0.0 collective-permute-done.6.second_ref
  32.9 1.1 %collective-permute-done.5.first_ref = bf16[768,128]{1,0:T(8,128)(2,1)S(1)} collective-permute-done((bf16[768,128]{1,0:T(8,128)(2,1)S(1)}, bf16[768,128]{1,0:T(8,128)(2,1)S(1)}, u32[]{:S(2)}, u32[]{:S(2)}) %collective-permute-start.5) | collective-permute-done | bytes 196640 | tf_op jit(solution)/shard_map/ppermute | solution.py:258
  34.0 1.8 %shard_map.69.state_ref = f32[2,136,384]{2,1,0:T(8,128)S(1)} custom-call(s32[8,128]{1,0:T(8,128)S(1)} %get-tuple-element.52.flag_ref, s32[2]{0:T(128)S(1)} %copy-done.3, bf16[2,384,128]{2,1,0:T(8,128)(2,1)S(1)} %get-tuple-element.55.q_ref, bf16[768,128]{1,0:T(8,128)(2,1)S(1)} %collective-permute-done.5.first_ref, ...), custom_call_target="tpu_custom_call", output_to_operand_aliasing={{}: (5, {})} | custom-call | flops 301989888 | bytes 1048576 | tf_op jit(solution)/shard_map/pallas_call | solution.py:30
  35.8 0.0 collective-permute-done.7.refs_2_
  35.8 5.0 %collective-permute-done.8.refs_0_ = bf16[768,128]{1,0:T(8,128)(2,1)S(1)} collective-permute-done((bf16[768,128]{1,0:T(8,128)(2,1)S(1)}, bf16[768,128]{1,0:T(8,128)(2,1)S(1)}, u32[]{:S(2)}, u32[]{:S(2)}) %collective-permute-start.8) | collective-permute-done | bytes 196640 | tf_op jit(solution)/shard_map/ppermute | solution.py:258
  40.9 1.4 %shard_map.70 = (bf16[2,96,128]{2,1,0:T(8,128)(2,1)S(1)}, bf16[2,96,128]{2,1,0:T(8,128)(2,1)S(1)}, bf16[2,96,128]{2,1,0:T(8,128)(2,1)S(1)}, bf16[2,96,128]{2,1,0:T(8,128)(2,1)S(1)}) custom-call(s32[8,128]{1,0:T(8,128)S(1)} %get-tuple-element.52.flag_ref, s32[2]{0:T(128)S(1)} %copy-done.3, bf16[2,384,128]{2,1,0:T(8,128)(2,1)S(1)} %get-tuple-element.55.q_ref, ...), custom_call_target="tpu_custom_call" | custom-call | flops 75497472 | bytes 1048576 | tf_op jit(solution)/shard_map/pallas_call | solution.py:30
  42.2 0.1 collective-permute-start.9
  42.3 0.6 collective-permute-start.10
  42.9 1.3 %collective-permute-start.11 = (bf16[2,96,128]{2,1,0:T(8,128)(2,1)S(1)}, bf16[2,96,128]{2,1,0:T(8,128)(2,1)S(1)}, u32[]{:S(2)}, u32[]{:S(2)}) collective-permute-start(bf16[2,96,128]{2,1,0:T(8,128)(2,1)S(1)} %get-tuple-element.65), channel_id=1, source_target_pairs={{0,1},{1,0},{2,3},{3,2},{4,5},{5,4},{6,7},{7,6},{8,9},{9,8},{10,11... | collective-permute-start | bytes 147464 | tf_op jit(solution)/shard_map/ppermute | solution.py:266
  44.2 1.7 %collective-permute-done.9.cross_ref = bf16[2,96,128]{2,1,0:T(8,128)(2,1)S(1)} collective-permute-done((bf16[2,96,128]{2,1,0:T(8,128)(2,1)S(1)}, bf16[2,96,128]{2,1,0:T(8,128)(2,1)S(1)}, u32[]{:S(2)}, u32[]{:S(2)}) %collective-permute-start.9) | collective-permute-done | bytes 49184 | tf_op jit(solution)/shard_map/ppermute | solution.py:273
  45.8 1.1 %collective-permute-done.10.y_ref = bf16[2,96,128]{2,1,0:T(8,128)(2,1)S(1)} collective-permute-done((bf16[2,96,128]{2,1,0:T(8,128)(2,1)S(1)}, bf16[2,96,128]{2,1,0:T(8,128)(2,1)S(1)}, u32[]{:S(2)}, u32[]{:S(2)}) %collective-permute-start.10) | collective-permute-done | bytes 49184 | tf_op jit(solution)/shard_map/ppermute | solution.py:262
  46.9 0.0 collective-permute-done.11.core_ref
  46.9 0.0 collective-permute-done.12.refs_4_
  46.9 0.9 %shard_map.71 = (bf16[96,512]{1,0:T(8,128)(2,1)S(1)}, bf16[96,2048]{1,0:T(8,128)(2,1)S(1)}) custom-call(s32[2]{0:T(128)S(1)} %copy-done.3, bf16[2,96,128]{2,1,0:T(8,128)(2,1)S(1)} %get-tuple-element.62.own_ref, bf16[2,96,128]{2,1,0:T(8,128)(2,1)S(1)} %collective-permute-done.10.y_ref, bf16[2,96,128]{2,1,0:T(8,128)(2,1)S(1)} %collective-permute-done.11.core_ref, ...), custom_call_target="tpu_custom_call" | custom-call | flops 125829120 | bytes 1048576 | tf_op jit(solution)/shard_map/pallas_call | solution.py:30
  47.8 0.1 collective-permute-start.16
  47.9 0.5 collective-permute-start.14
  48.4 0.1 collective-permute-start.15
  48.5 0.5 collective-permute-start.13
  49.0 1.0 %shard_map.72.near_ref = f32[96,5120]{1,0:T(8,128)S(1)} custom-call(bf16[96,512]{1,0:T(8,128)(2,1)S(1)} %get-tuple-element.72.a_ref, bf16[256,5120]{1,0:T(8,128)(2,1)S(1)} %copy-done, bf16[256,5120]{1,0:T(8,128)(2,1)S(1)} %collective-permute-done.1.wp_ref), custom_call_target="tpu_custom_call" | custom-call | flops 503316480 | bytes 1048576 | tf_op jit(solution)/shard_map/pallas_call | solution.py:30
  50.0 9.9 %collective-permute-done.13.far_ref = bf16[96,2048]{1,0:T(8,128)(2,1)S(1)} collective-permute-done((bf16[96,2048]{1,0:T(8,128)(2,1)S(1)}, bf16[96,2048]{1,0:T(8,128)(2,1)S(1)}, u32[]{:S(2)}, u32[]{:S(2)}) %collective-permute-start.13) | collective-permute-done | bytes 393248 | tf_op jit(solution)/shard_map/ppermute | solution.py:278
  59.9 0.0 collective-permute-done.14.refs_1_
  59.9 0.0 collective-permute-done.15.refs_3_
  59.9 0.0 collective-permute-done.16.refs_5_
  60.0 2.3 %shard_map.73 = bf16[96,5120]{1,0:T(8,128)(2,1)} custom-call(s32[2]{0:T(128)S(1)} %copy-done.3, f32[96,5120]{1,0:T(8,128)S(1)} %shard_map.72.near_ref, bf16[96,2048]{1,0:T(8,128)(2,1)S(1)} %collective-permute-done.13.far_ref, bf16[256,1024]{1,0:T(8,128)(2,1)S(1)} %collective-permute-done.4.refs_0_, bf16[256,1024]{1,0:T(8,128)(2,1)S(1)} %collective-permute-done.14.refs_1_, ...), custom_call_target="tpu_custom_call" | custom-call | flops 503316480 | bytes 1048576 | tf_op jit(solution)/shard_map/pallas_call | solution.py:30
  (1 shorter events, 0.0 us)
Async XLA Ops:
  0.0 4.5 %copy-start = (bf16[256,5120]{1,0:T(8,128)(2,1)S(1)}, bf16[256,5120]{1,0:T(8,128)(2,1)}, u32[]{:S(2)}) copy-start(bf16[256,5120]{1,0:T(8,128)(2,1)} %w_ref.6) | copy-start | bytes 7864324
  4.5 14.6 %copy-start.3 = (s32[2]{0:T(128)S(1)}, s32[2]{0:T(128)}, u32[]{:S(2)}) copy-start(s32[2]{0:T(128)} %pad_add_fusion.index_ref) | copy-start | bytes 28
  4.6 14.6 %collective-permute-start.1 = (bf16[256,5120]{1,0:T(8,128)(2,1)S(1)}, bf16[256,5120]{1,0:T(8,128)(2,1)S(1)}, u32[]{:S(2)}, u32[]{:S(2)}) collective-permute-start(bf16[256,5120]{1,0:T(8,128)(2,1)S(1)} %copy-done), channel_id=1, source_target_pairs={{0,1},{1,0},{2,3},{3,2},{4,5},{5,4},{6,7},{7,6},{8,9},{9,8},{10,11... | collective-permute-start | bytes 7864328 | tf_op jit(solution)/shard_map/ppermute | solution.py:266
  5.1 15.3 %collective-permute-start.4 = (bf16[256,1024]{1,0:T(8,128)(2,1)}, bf16[256,1024]{1,0:T(8,128)(2,1)S(1)}, u32[]{:S(2)}, u32[]{:S(2)}) collective-permute-start(bf16[256,1024]{1,0:T(8,128)(2,1)} %get-tuple-element.54), channel_id=1, source_target_pairs={{2,0},{3,1},{0,2},{1,3},{6,4},{7,5},{4,6},{5,7},{10,8},{11,9},{8,1... | collective-permute-start | bytes 1572872 | tf_op jit(solution)/shard_map/ppermute | solution.py:278
  7.6 11.5 %collective-permute-start = (bf16[1168,128]{1,0:T(8,128)(2,1)}, bf16[1168,128]{1,0:T(8,128)(2,1)S(1)}, u32[]{:S(2)}, u32[]{:S(2)}) collective-permute-start(bf16[1168,128]{1,0:T(8,128)(2,1)} %get-tuple-element.42), channel_id=1, source_target_pairs={{0,4},{4,0},{8,12},{12,8},{16,20},{20,16},{24,28},{28,24},{1,5},{5... | collective-permute-start | bytes 897032 | tf_op jit(solution)/shard_map/ppermute | solution.py:262
  9.2 7.1 %collective-permute-start.3 = (bf16[768,128]{1,0:T(8,128)(2,1)}, bf16[768,128]{1,0:T(8,128)(2,1)S(1)}, u32[]{:S(2)}, u32[]{:S(2)}) collective-permute-start(bf16[768,128]{1,0:T(8,128)(2,1)} %get-tuple-element.43.keep_kv_ref), channel_id=1, source_target_pairs={{8,16},{16,8},{12,20},{20,12},{9,17},{17,9},{13,21},{21,13},{10,18... | collective-permute-start | bytes 589832 | tf_op jit(solution)/shard_map/ppermute | solution.py:258
  9.8 9.3 %collective-permute-start.2 = (bf16[768,128]{1,0:T(8,128)(2,1)}, bf16[768,128]{1,0:T(8,128)(2,1)S(1)}, u32[]{:S(2)}, u32[]{:S(2)}) collective-permute-start(bf16[768,128]{1,0:T(8,128)(2,1)} %get-tuple-element.43.keep_kv_ref), channel_id=1, source_target_pairs={{0,8},{8,0},{4,12},{12,4},{16,24},{24,16},{20,28},{28,20},{1,9},{9... | collective-permute-start | bytes 589832 | tf_op jit(solution)/shard_map/ppermute | solution.py:258
  14.3 1.0 %copy-start.1 = (bf16[768,128]{1,0:T(8,128)(2,1)S(1)}, bf16[768,128]{1,0:T(8,128)(2,1)}, u32[]{:S(2)}) copy-start(bf16[768,128]{1,0:T(8,128)(2,1)} %get-tuple-element.43.keep_kv_ref) | copy-start | bytes 589828
  15.2 0.9 %copy-start.2 = (bf16[400,128]{1,0:T(8,128)(2,1)S(1)}, bf16[400,128]{1,0:T(8,128)(2,1)}, u32[]{:S(2)}) copy-start(bf16[400,128]{1,0:T(8,128)(2,1)} %get-tuple-element.45.keep_q_ref) | copy-start | bytes 307204
  20.4 26.5 %collective-permute-start.12 = (bf16[256,1536]{1,0:T(8,128)(2,1)S(1)}, bf16[256,1536]{1,0:T(8,128)(2,1)S(1)}, u32[]{:S(2)}, u32[]{:S(2)}) collective-permute-start(bf16[256,1536]{1,0:T(8,128)(2,1)S(1)} %shard_map.66), channel_id=1, source_target_pairs={{2,0},{3,1},{0,2},{1,3},{6,4},{7,5},{4,6},{5,7},{10,8},{11,9},{8,1... | collective-permute-start | bytes 2359304 | tf_op jit(solution)/shard_map/ppermute | solution.py:278
  22.1 13.7 %collective-permute-start.7 = (bf16[256,1024]{1,0:T(8,128)(2,1)S(1)}, bf16[256,1024]{1,0:T(8,128)(2,1)S(1)}, u32[]{:S(2)}, u32[]{:S(2)}) collective-permute-start(bf16[256,1024]{1,0:T(8,128)(2,1)S(1)} %collective-permute-done.4.refs_0_), channel_id=1, source_target_pairs={{0,4},{4,0},{8,12},{12,8},{16,20},{20,16},{24,28},{28,24},{1,5},{5... | collective-permute-start | bytes 1572872 | tf_op jit(solution)/shard_map/ppermute | solution.py:262
  23.6 9.3 %collective-permute-start.6 = (bf16[768,128]{1,0:T(8,128)(2,1)S(1)}, bf16[768,128]{1,0:T(8,128)(2,1)S(1)}, u32[]{:S(2)}, u32[]{:S(2)}) collective-permute-start(bf16[768,128]{1,0:T(8,128)(2,1)S(1)} %get-tuple-element.56.came_ref), channel_id=1, source_target_pairs={{8,16},{16,8},{12,20},{20,12},{9,17},{17,9},{13,21},{21,13},{10,18... | collective-permute-start | bytes 589832 | tf_op jit(solution)/shard_map/ppermute | solution.py:258
  24.3 9.7 %collective-permute-start.5 = (bf16[768,128]{1,0:T(8,128)(2,1)S(1)}, bf16[768,128]{1,0:T(8,128)(2,1)S(1)}, u32[]{:S(2)}, u32[]{:S(2)}) collective-permute-start(bf16[768,128]{1,0:T(8,128)(2,1)S(1)} %get-tuple-element.56.came_ref), channel_id=1, source_target_pairs={{0,8},{8,0},{4,12},{12,4},{16,24},{24,16},{20,28},{28,20},{1,9},{9... | collective-permute-start | bytes 589832 | tf_op jit(solution)/shard_map/ppermute | solution.py:258
  28.8 12.1 %collective-permute-start.8 = (bf16[768,128]{1,0:T(8,128)(2,1)S(1)}, bf16[768,128]{1,0:T(8,128)(2,1)S(1)}, u32[]{:S(2)}, u32[]{:S(2)}) collective-permute-start(bf16[768,128]{1,0:T(8,128)(2,1)S(1)} %get-tuple-element.61), channel_id=1, source_target_pairs={{0,16},{16,0},{4,20},{20,4},{8,24},{24,8},{12,28},{28,12},{1,17},{... | collective-permute-start | bytes 589832 | tf_op jit(solution)/shard_map/ppermute | solution.py:258
  42.2 3.6 %collective-permute-start.9 = (bf16[2,96,128]{2,1,0:T(8,128)(2,1)S(1)}, bf16[2,96,128]{2,1,0:T(8,128)(2,1)S(1)}, u32[]{:S(2)}, u32[]{:S(2)}) collective-permute-start(bf16[2,96,128]{2,1,0:T(8,128)(2,1)S(1)} %get-tuple-element.63), channel_id=1, source_target_pairs={{0,5},{1,4},{2,7},{3,6},{4,1},{5,0},{6,3},{7,2},{8,13},{9,12},{10,... | collective-permute-start | bytes 147464 | tf_op jit(solution)/shard_map/ppermute | solution.py:273
  42.3 4.6 %collective-permute-start.10 = (bf16[2,96,128]{2,1,0:T(8,128)(2,1)S(1)}, bf16[2,96,128]{2,1,0:T(8,128)(2,1)S(1)}, u32[]{:S(2)}, u32[]{:S(2)}) collective-permute-start(bf16[2,96,128]{2,1,0:T(8,128)(2,1)S(1)} %get-tuple-element.64), channel_id=1, source_target_pairs={{0,4},{4,0},{8,12},{12,8},{16,20},{20,16},{24,28},{28,24},{1,5},{5... | collective-permute-start | bytes 147464 | tf_op jit(solution)/shard_map/ppermute | solution.py:262
  42.9 4.0 %collective-permute-start.11 = (bf16[2,96,128]{2,1,0:T(8,128)(2,1)S(1)}, bf16[2,96,128]{2,1,0:T(8,128)(2,1)S(1)}, u32[]{:S(2)}, u32[]{:S(2)}) collective-permute-start(bf16[2,96,128]{2,1,0:T(8,128)(2,1)S(1)} %get-tuple-element.65), channel_id=1, source_target_pairs={{0,1},{1,0},{2,3},{3,2},{4,5},{5,4},{6,7},{7,6},{8,9},{9,8},{10,11... | collective-permute-start | bytes 147464 | tf_op jit(solution)/shard_map/ppermute | solution.py:266
  47.8 12.1 %collective-permute-start.16 = (bf16[256,1536]{1,0:T(8,128)(2,1)S(1)}, bf16[256,1536]{1,0:T(8,128)(2,1)S(1)}, u32[]{:S(2)}, u32[]{:S(2)}) collective-permute-start(bf16[256,1536]{1,0:T(8,128)(2,1)S(1)} %collective-permute-done.12.refs_4_), channel_id=1, source_target_pairs={{0,1},{1,0},{2,3},{3,2},{4,5},{5,4},{6,7},{7,6},{8,9},{9,8},{10,11... | collective-permute-start | bytes 2359304 | tf_op jit(solution)/shard_map/ppermute | solution.py:266
  47.9 12.0 %collective-permute-start.14 = (bf16[256,1024]{1,0:T(8,128)(2,1)S(1)}, bf16[256,1024]{1,0:T(8,128)(2,1)S(1)}, u32[]{:S(2)}, u32[]{:S(2)}) collective-permute-start(bf16[256,1024]{1,0:T(8,128)(2,1)S(1)} %collective-permute-done.4.refs_0_), channel_id=1, source_target_pairs={{0,1},{1,0},{2,3},{3,2},{4,5},{5,4},{6,7},{7,6},{8,9},{9,8},{10,11... | collective-permute-start | bytes 1572872 | tf_op jit(solution)/shard_map/ppermute | solution.py:266
  48.4 11.6 %collective-permute-start.15 = (bf16[256,1024]{1,0:T(8,128)(2,1)S(1)}, bf16[256,1024]{1,0:T(8,128)(2,1)S(1)}, u32[]{:S(2)}, u32[]{:S(2)}) collective-permute-start(bf16[256,1024]{1,0:T(8,128)(2,1)S(1)} %collective-permute-done.7.refs_2_), channel_id=1, source_target_pairs={{0,1},{1,0},{2,3},{3,2},{4,5},{5,4},{6,7},{7,6},{8,9},{9,8},{10,11... | collective-permute-start | bytes 1572872 | tf_op jit(solution)/shard_map/ppermute | solution.py:266
  48.5 11.5 %collective-permute-start.13 = (bf16[96,2048]{1,0:T(8,128)(2,1)S(1)}, bf16[96,2048]{1,0:T(8,128)(2,1)S(1)}, u32[]{:S(2)}, u32[]{:S(2)}) collective-permute-start(bf16[96,2048]{1,0:T(8,128)(2,1)S(1)} %get-tuple-element.73), channel_id=1, source_target_pairs={{2,0},{3,1},{0,2},{1,3},{6,4},{7,5},{4,6},{5,7},{10,8},{11,9},{8,1... | collective-permute-start | bytes 1179656 | tf_op jit(solution)/shard_map/ppermute | solution.py:278

commit v4 on v2

--- a/solution.py
+++ b/solution.py
@@ -11,9 +11,10 @@
 HD = 128
 REACH = 3
 NEG = -1e30
+MERGE = 0
 FLAGS = 16
 SIDE = 1024
-COMMON = 1536
+COMMON = 1408
 STATE = HD + 8
 EXPONENT = math.log2(math.e) / math.sqrt(HD)
 BF16, F32 = jnp.bfloat16, jnp.float32
@@ -44,7 +45,7 @@
 
 
 def pack_kernel(
-    tile_ref, list_ref, count_ref, q_ref, k_ref, v_ref, w_ref,
+    tile_ref, _, list_ref, count_ref, q_ref, k_ref, v_ref, w_ref,
     keep_q_ref, keep_kv_ref, send_ref, side_ref, sems,
 ):
     parity = tile_ref[0] & 1
@@ -69,7 +70,7 @@
     for offset in range(-REACH, REACH + 1):
         listed = jnp.int32(0)
         for slot in range(list_ref.shape[1]):
-            found = (list_ref[0, slot] == tile_ref[0] + offset) & (slot < count_ref[0])
+            found = (list_ref[0, slot] == tile_ref[0] + offset) & (slot < count_ref[0, 0])
             listed = jnp.where(found, 1, listed)
         flags = jnp.where(lane == offset + REACH, listed.astype(F32), flags)
     keep_q_ref[rows:, :] = flags.astype(BF16)
@@ -305,17 +306,16 @@
     model = out_weight.shape[1]
     small = n_head == 4 and own_rows % 16 == 0
     head_index = lax.axis_index("head").astype(jnp.int32)
-    head = head_index.reshape(1)
-    tile = lax.axis_index("ctx").astype(jnp.int32).reshape(1)
+    tile, head = lax.axis_index("ctx").astype(jnp.int32).reshape(1), head_index.reshape(1)
 
     one = (rows, HD)
     payload, kv_shape = shape((3 * rows + FLAGS, HD)), shape((2 * rows, HD))
     keep_q, keep_kv, send, side_weight = call(
         pack_kernel,
         (shape((rows + FLAGS, HD)), kv_shape, payload, shape((width, SIDE))),
-        (tile, neighbours, counts, queries, keys, values, out_weight),
+        (tile, head, neighbours, counts.reshape(1, 1), queries, keys, values, out_weight),
         scratch=(pltpu.SemaphoreType.DMA((7,)),),
-        in_hbm=(3, 4, 5, 6),
+        in_hbm=(4, 5, 6, 7),
         vmem=58,
     )
     weight_ready, _ = lax.optimization_barrier((out_weight, keep_kv))
@@ -326,14 +326,21 @@
         side_own = from_chip(side_weight, 1)
 
     held_q, held_kv = call(stage_kernel, (shape((rows + FLAGS, HD)), kv_shape), (keep_q, keep_kv))
-    came, weight_pair, held_q, held_kv, *kept_near = lax.optimization_barrier(
-        (came, weight_pair, held_q, held_kv, *kept_near)
+    cut = []
+    if small:
+        ready, _ = lax.optimization_barrier((out_weight, held_q))
+        cut.append(
+            call(functools.partial(cut_kernel, first=2 * SIDE), shape((width, COMMON)), (ready,))
+        )
+    came, weight_pair, held_q, held_kv, kept_near, cut = lax.optimization_barrier(
+        (came, weight_pair, held_q, held_kv, kept_near, cut)
     )
     far = 1 if lax.axis_size("ctx") <= 8 else 2
     flags, q_pair, came_kv, *to_far = call(
         merge_kernel if far == 2 else functools.partial(merge_kernel, even_ref=None),
         (shape((8, HD), jnp.int32), shape((2,) + one), kv_shape) + (kv_shape,) * far,
         (tile, held_q, held_kv, came),
+        MERGE * rows * rows * HD,
     )
     came_near = [swap_pairs(came_kv, 1, phase) for phase in range(2)]
     farther = [swap_pairs(to_far[i], 2, i) for i in range(far)]
@@ -351,21 +358,16 @@
     if small:
         side_own, q_again = lax.optimization_barrier((side_own, q_pair))
         side_other = swap_tiles(side_own)
-        ready, _ = lax.optimization_barrier((out_weight, side_own))
-        common_weight = call(
-            functools.partial(cut_kernel, first=2 * SIDE), shape((width, COMMON)), (ready,)
-        )
-        common = from_chip(common_weight, 1)
+        ready, _ = lax.optimization_barrier((cut[0], side_own))
+        common = from_chip(ready, 1)
     held = call(
         second_kernel,
         state,
         (flags, tile, q_again, *came_near, held),
-        16 * area * HD,
-        4 * area,
+        1000 * area * HD,
+        0,
         alias={5: 0},
     )
-    if small:
-        held, side_other = lax.optimization_barrier((held, side_other))
     block = (2, own_rows, HD)
     attended = call(
         functools.partial(third_kernel, far=far),
@@ -388,8 +390,8 @@
     from_cross = swap_both(theirs_other)
     from_y = swap_tiles(theirs)
     from_core = swap_cores(mine_other)
-    from_cross, from_y, from_core, common = lax.optimization_barrier(
-        (from_cross, from_y, from_core, common)
+    from_cross, from_y, from_core, common, side_other = lax.optimization_barrier(
+        (from_cross, from_y, from_core, common, side_other)
     )
 
     flops = 2 * own_rows * 2 * width * model

time: 63.5 us -> 56.7 us (0.89)
  local copies, waits for them, and re-layouts: 6.72 us -> 1.86 us
  Pallas kernels: 17.6 us -> 13.6 us
  waiting for transfers between devices: 18 us -> 19.6 us
    unnamed x18 -> x6, local copies, waits for them, and re-layouts: 6.72 us -> 1.86 us
    pallas_call x10, Pallas kernels: 17.6 us -> 13.6 us  [call(): pl.pallas_call(kernel, out_shape=outs, in_specs=[SMEM if s else HBM if i...]
    ppermute x5, waiting for transfers between devices: 5.61 us -> 7 us  [swap_pairs(): return lax.ppermute(value, 'ctx', pairs)]
    ppermute x3, starting transfers between devices: 4.02 us -> 4.92 us  [from_chip(): lax.ppermute(value, 'head', [((i + 2 * steps) % count, i) for i in range(...]
    ppermute x3, starting transfers between devices: 3.48 us -> 2.73 us  [swap_tiles(): lax.ppermute(value, 'ctx', [(i, i ^ 1) for i in range(lax.axis_size('ctx'...]
  transfers between devices with their start and end apart: 17 -> 17, of which waited for: 5 -> 5; matrix products, arithmetic and copies ran while one was open for 0% -> 0% of each run, Pallas kernels for 16% -> 15%
where the time goes in v4:
time: 56.7 us; the launch traced here: 56.4 us
  starting transfers between devices  20.4 us (36%)
  waiting for transfers between devices  19.6 us (35%)
  Pallas kernels  13.6 us (24%)
  local copies, waits for them, and re-layouts  1.86 us (3%)
  between operations  0.94 us (2%)
    pallas_call x10, Pallas kernels, call(): pl.pallas_call(kernel, out_shape=outs, in_specs=[SMEM if s else HBM if i...  13.6 us
    ppermute x5, starting transfers between devices, swap_pairs(): return lax.ppermute(value, 'ctx', pairs)  10.4 us
    ppermute x3, waiting for transfers between devices, from_chip(): lax.ppermute(value, 'head', [((i + 2 * steps) % count, i) for i in range(...  9.92 us
    ppermute x5, waiting for transfers between devices, swap_pairs(): return lax.ppermute(value, 'ctx', pairs)  7 us
    ppermute x3, starting transfers between devices, from_chip(): lax.ppermute(value, 'head', [((i + 2 * steps) % count, i) for i in range(...  4.92 us
    ppermute x3, starting transfers between devices, swap_tiles(): lax.ppermute(value, 'ctx', [(i, i ^ 1) for i in range(lax.axis_size('ctx'...  2.73 us
    ppermute x5, starting transfers between devices, swap_cores(): lax.ppermute(value, 'head', [(i, i ^ 1) for i in range(lax.axis_size('hea...  2.32 us
    unnamed x6, local copies, waits for them, and re-layouts  1.86 us
  transfers between devices with their start and end apart: 17, of which 5 were waited for; matrix products, arithmetic and copies ran while one was open for 0% of the time, Pallas kernels for 15%

profile of v4, /device:TPU:0, one launch (start us, length us, event | category | flops | bytes accessed | tf_op | source)
XLA Modules:
  0.0 56.4 jit_solution(17431654203362127344)
XLA Ops:
  0.0 0.0 copy-start
  0.8 3.1 %shard_map.64 = (bf16[400,128]{1,0:T(8,128)(2,1)}, bf16[768,128]{1,0:T(8,128)(2,1)}, bf16[1168,128]{1,0:T(8,128)(2,1)}, bf16[256,1024]{1,0:T(8,128)(2,1)}) custom-call(s32[1]{0:T(128)} %bitcast.tile_ref, s32[1]{0:T(128)} %bitcast.1._.head_ref, s32[1,7]{1,0:T(1,128)} %list_ref.1, s32[1,1]{1,0:T(1,128)} %bitcast.3.count_ref, bf16[384,256]{1,0:T(8,128)(2,1)} %q_ref.1, ...), custom_call_target="tpu_custom_call" | custom-call | bytes 1048576 | tf_op jit(solution)/shard_map/pallas_call | solution.py:31
  3.9 0.0 copy-done
  3.9 0.5 collective-permute-start.1
  4.4 2.6 %collective-permute-start.4 = (bf16[256,1024]{1,0:T(8,128)(2,1)}, bf16[256,1024]{1,0:T(8,128)(2,1)S(1)}, u32[]{:S(2)}, u32[]{:S(2)}) collective-permute-start(bf16[256,1024]{1,0:T(8,128)(2,1)} %get-tuple-element.53), channel_id=1, source_target_pairs={{2,0},{3,1},{0,2},{1,3},{6,4},{7,5},{4,6},{5,7},{10,8},{11,9},{8,1... | collective-permute-start | bytes 1572872 | tf_op jit(solution)/shard_map/ppermute | solution.py:279
  7.0 1.5 %collective-permute-start = (bf16[1168,128]{1,0:T(8,128)(2,1)}, bf16[1168,128]{1,0:T(8,128)(2,1)S(1)}, u32[]{:S(2)}, u32[]{:S(2)}) collective-permute-start(bf16[1168,128]{1,0:T(8,128)(2,1)} %get-tuple-element.41), channel_id=1, source_target_pairs={{0,4},{4,0},{8,12},{12,8},{16,20},{20,16},{24,28},{28,24},{1,5},{5... | collective-permute-start | bytes 897032 | tf_op jit(solution)/shard_map/ppermute | solution.py:263
  8.5 0.7 %collective-permute-start.3 = (bf16[768,128]{1,0:T(8,128)(2,1)}, bf16[768,128]{1,0:T(8,128)(2,1)S(1)}, u32[]{:S(2)}, u32[]{:S(2)}) collective-permute-start(bf16[768,128]{1,0:T(8,128)(2,1)} %get-tuple-element.42.keep_kv_ref), channel_id=1, source_target_pairs={{8,16},{16,8},{12,20},{20,12},{9,17},{17,9},{13,21},{21,13},{10,18... | collective-permute-start | bytes 589832 | tf_op jit(solution)/shard_map/ppermute | solution.py:259
  9.1 4.5 %collective-permute-start.2 = (bf16[768,128]{1,0:T(8,128)(2,1)}, bf16[768,128]{1,0:T(8,128)(2,1)S(1)}, u32[]{:S(2)}, u32[]{:S(2)}) collective-permute-start(bf16[768,128]{1,0:T(8,128)(2,1)} %get-tuple-element.42.keep_kv_ref), channel_id=1, source_target_pairs={{0,8},{8,0},{4,12},{12,4},{16,24},{24,16},{20,28},{28,20},{1,9},{9... | collective-permute-start | bytes 589832 | tf_op jit(solution)/shard_map/ppermute | solution.py:259
  13.6 0.0 copy-start.1
  13.6 1.0 %copy-done.1 = bf16[768,128]{1,0:T(8,128)(2,1)S(1)} copy-done((bf16[768,128]{1,0:T(8,128)(2,1)S(1)}, bf16[768,128]{1,0:T(8,128)(2,1)}, u32[]{:S(2)}) %copy-start.1) | copy-done | bytes 196632
  14.6 0.0 copy-start.2
  14.6 0.9 %copy-done.2 = bf16[400,128]{1,0:T(8,128)(2,1)S(1)} copy-done((bf16[400,128]{1,0:T(8,128)(2,1)S(1)}, bf16[400,128]{1,0:T(8,128)(2,1)}, u32[]{:S(2)}) %copy-start.2) | copy-done | bytes 102424
  15.5 0.1 shard_map.66
  15.5 0.0 collective-permute-done.3.kept_second_ref
  15.5 2.9 %collective-permute-done.2.kept_first_ref = bf16[768,128]{1,0:T(8,128)(2,1)S(1)} collective-permute-done((bf16[768,128]{1,0:T(8,128)(2,1)}, bf16[768,128]{1,0:T(8,128)(2,1)S(1)}, u32[]{:S(2)}, u32[]{:S(2)}) %collective-permute-start.2) | collective-permute-done | bytes 196640 | tf_op jit(solution)/shard_map/ppermute | solution.py:259
  18.5 0.0 collective-permute-done.came_ref
  18.5 0.0 collective-permute-done.1.wp_ref
  18.5 0.7 %collective-permute-start.6 = (bf16[768,128]{1,0:T(8,128)(2,1)S(1)}, bf16[768,128]{1,0:T(8,128)(2,1)S(1)}, u32[]{:S(2)}, u32[]{:S(2)}) collective-permute-start(bf16[768,128]{1,0:T(8,128)(2,1)S(1)} %get-tuple-element.55.came_ref), channel_id=1, source_target_pairs={{8,16},{16,8},{12,20},{20,12},{9,17},{17,9},{13,21},{21,13},{10,18... | collective-permute-start | bytes 589832 | tf_op jit(solution)/shard_map/ppermute | solution.py:259
  19.2 3.5 %collective-permute-start.5 = (bf16[768,128]{1,0:T(8,128)(2,1)S(1)}, bf16[768,128]{1,0:T(8,128)(2,1)S(1)}, u32[]{:S(2)}, u32[]{:S(2)}) collective-permute-start(bf16[768,128]{1,0:T(8,128)(2,1)S(1)} %get-tuple-element.55.came_ref), channel_id=1, source_target_pairs={{0,8},{8,0},{4,12},{12,4},{16,24},{24,16},{20,28},{28,20},{1,9},{9... | collective-permute-start | bytes 589832 | tf_op jit(solution)/shard_map/ppermute | solution.py:259
  22.7 0.0 collective-permute-done.4.refs_0_
  22.7 0.5 collective-permute-start.12
  23.2 1.1 %collective-permute-start.7 = (bf16[768,128]{1,0:T(8,128)(2,1)S(1)}, bf16[768,128]{1,0:T(8,128)(2,1)S(1)}, u32[]{:S(2)}, u32[]{:S(2)}) collective-permute-start(bf16[768,128]{1,0:T(8,128)(2,1)S(1)} %get-tuple-element.58), channel_id=1, source_target_pairs={{0,16},{16,0},{4,20},{20,4},{8,24},{24,8},{12,28},{28,12},{1,17},{... | collective-permute-start | bytes 589832 | tf_op jit(solution)/shard_map/ppermute | solution.py:259
  24.3 1.2 %collective-permute-start.11 = (bf16[256,1408]{1,0:T(8,128)(2,1)S(1)}, bf16[256,1408]{1,0:T(8,128)(2,1)S(1)}, u32[]{:S(2)}, u32[]{:S(2)}) collective-permute-start(bf16[256,1408]{1,0:T(8,128)(2,1)S(1)} %shard_map.66), channel_id=1, source_target_pairs={{2,0},{3,1},{0,2},{1,3},{6,4},{7,5},{4,6},{5,7},{10,8},{11,9},{8,1... | collective-permute-start | bytes 2162696 | tf_op jit(solution)/shard_map/ppermute | solution.py:279
  25.6 4.1 %shard_map.68._ = f32[2,136,384]{2,1,0:T(8,128)S(1)} custom-call(s32[8,128]{1,0:T(8,128)S(1)} %get-tuple-element.51.flag_ref, s32[1]{0:T(128)} %bitcast.tile_ref, bf16[2,384,128]{2,1,0:T(8,128)(2,1)S(1)} %get-tuple-element.54.q_ref, bf16[768,128]{1,0:T(8,128)(2,1)S(1)} %get-tuple-element.49.keep_kv_ref.own_ref, ...), custom_call_target="tpu_custom_call" | custom-call | flops 603979776 | bytes 1048576 | tf_op jit(solution)/shard_map/pallas_call | solution.py:31
  29.7 0.0 collective-permute-done.6.second_ref
  29.7 0.0 collective-permute-done.5.first_ref
  29.7 1.8 %shard_map.69.state_ref = f32[2,136,384]{2,1,0:T(8,128)S(1)} custom-call(s32[8,128]{1,0:T(8,128)S(1)} %get-tuple-element.51.flag_ref, s32[1]{0:T(128)} %bitcast.tile_ref, bf16[2,384,128]{2,1,0:T(8,128)(2,1)S(1)} %get-tuple-element.54.q_ref, bf16[768,128]{1,0:T(8,128)(2,1)S(1)} %collective-permute-done.5.first_ref, ...), custom_call_target="tpu_custom_call", output_to_operand_aliasing={{}: (5, {})} | custom-call | flops 18874368000 | bytes 1048576 | tf_op jit(solution)/shard_map/pallas_call | solution.py:31
  31.5 4.1 %collective-permute-done.7.refs_0_ = bf16[768,128]{1,0:T(8,128)(2,1)S(1)} collective-permute-done((bf16[768,128]{1,0:T(8,128)(2,1)S(1)}, bf16[768,128]{1,0:T(8,128)(2,1)S(1)}, u32[]{:S(2)}, u32[]{:S(2)}) %collective-permute-start.7) | collective-permute-done | bytes 196640 | tf_op jit(solution)/shard_map/ppermute | solution.py:259
  35.6 1.4 %shard_map.70 = (bf16[2,96,128]{2,1,0:T(8,128)(2,1)S(1)}, bf16[2,96,128]{2,1,0:T(8,128)(2,1)S(1)}, bf16[2,96,128]{2,1,0:T(8,128)(2,1)S(1)}, bf16[2,96,128]{2,1,0:T(8,128)(2,1)S(1)}) custom-call(s32[8,128]{1,0:T(8,128)S(1)} %get-tuple-element.51.flag_ref, s32[1]{0:T(128)} %bitcast.tile_ref, s32[1]{0:T(128)} %bitcast.1._.head_ref, ...), custom_call_target="tpu_custom_call" | custom-call | flops 75497472 | bytes 1048576 | tf_op jit(solution)/shard_map/pallas_call | solution.py:31
  36.9 0.1 collective-permute-start.8
  37.0 0.7 %collective-permute-start.9 = (bf16[2,96,128]{2,1,0:T(8,128)(2,1)S(1)}, bf16[2,96,128]{2,1,0:T(8,128)(2,1)S(1)}, u32[]{:S(2)}, u32[]{:S(2)}) collective-permute-start(bf16[2,96,128]{2,1,0:T(8,128)(2,1)S(1)} %get-tuple-element.61), channel_id=1, source_target_pairs={{0,4},{4,0},{8,12},{12,8},{16,20},{20,16},{24,28},{28,24},{1,5},{5... | collective-permute-start | bytes 147464 | tf_op jit(solution)/shard_map/ppermute | solution.py:263
  37.7 1.1 %collective-permute-start.10 = (bf16[2,96,128]{2,1,0:T(8,128)(2,1)S(1)}, bf16[2,96,128]{2,1,0:T(8,128)(2,1)S(1)}, u32[]{:S(2)}, u32[]{:S(2)}) collective-permute-start(bf16[2,96,128]{2,1,0:T(8,128)(2,1)S(1)} %get-tuple-element.62), channel_id=1, source_target_pairs={{0,1},{1,0},{2,3},{3,2},{4,5},{5,4},{6,7},{7,6},{8,9},{9,8},{10,11... | collective-permute-start | bytes 147464 | tf_op jit(solution)/shard_map/ppermute | solution.py:267
  38.9 1.7 %collective-permute-done.8.cross_ref = bf16[2,96,128]{2,1,0:T(8,128)(2,1)S(1)} collective-permute-done((bf16[2,96,128]{2,1,0:T(8,128)(2,1)S(1)}, bf16[2,96,128]{2,1,0:T(8,128)(2,1)S(1)}, u32[]{:S(2)}, u32[]{:S(2)}) %collective-permute-start.8) | collective-permute-done | bytes 49184 | tf_op jit(solution)/shard_map/ppermute | solution.py:274
  40.5 1.1 %collective-permute-done.9.y_ref = bf16[2,96,128]{2,1,0:T(8,128)(2,1)S(1)} collective-permute-done((bf16[2,96,128]{2,1,0:T(8,128)(2,1)S(1)}, bf16[2,96,128]{2,1,0:T(8,128)(2,1)S(1)}, u32[]{:S(2)}, u32[]{:S(2)}) %collective-permute-start.9) | collective-permute-done | bytes 49184 | tf_op jit(solution)/shard_map/ppermute | solution.py:263
  41.6 0.0 collective-permute-done.10.core_ref
  41.6 0.0 collective-permute-done.12.refs_2_
  41.6 0.0 collective-permute-done.11.refs_4_
  41.6 0.4 shard_map.71
  42.0 0.1 collective-permute-start.16
  42.1 0.5 collective-permute-start.14
  42.6 0.1 collective-permute-start.15
  42.7 1.1 %collective-permute-start.13 = (bf16[96,2176]{1,0:T(8,128)(2,1)S(1)}, bf16[96,2176]{1,0:T(8,128)(2,1)S(1)}, u32[]{:S(2)}, u32[]{:S(2)}) collective-permute-start(bf16[96,2176]{1,0:T(8,128)(2,1)S(1)} %get-tuple-element.71), channel_id=1, source_target_pairs={{2,0},{3,1},{0,2},{1,3},{6,4},{7,5},{4,6},{5,7},{10,8},{11,9},{8,1... | collective-permute-start | bytes 1253384 | tf_op jit(solution)/shard_map/ppermute | solution.py:279
  43.8 1.0 %shard_map.72.near_ref = f32[96,5120]{1,0:T(8,128)S(1)} custom-call(bf16[96,512]{1,0:T(8,128)(2,1)S(1)} %get-tuple-element.70.a_ref, bf16[256,5120]{1,0:T(8,128)(2,1)S(1)} %copy-done, bf16[256,5120]{1,0:T(8,128)(2,1)S(1)} %collective-permute-done.1.wp_ref), custom_call_target="tpu_custom_call" | custom-call | flops 503316480 | bytes 1048576 | tf_op jit(solution)/shard_map/pallas_call | solution.py:31
  44.8 9.9 %collective-permute-done.13.far_ref = bf16[96,2176]{1,0:T(8,128)(2,1)S(1)} collective-permute-done((bf16[96,2176]{1,0:T(8,128)(2,1)S(1)}, bf16[96,2176]{1,0:T(8,128)(2,1)S(1)}, u32[]{:S(2)}, u32[]{:S(2)}) %collective-permute-start.13) | collective-permute-done | bytes 417824 | tf_op jit(solution)/shard_map/ppermute | solution.py:279
  54.7 0.0 collective-permute-done.14.refs_1_
  54.7 0.0 collective-permute-done.15.refs_3_
  54.7 0.0 collective-permute-done.16.refs_5_
  54.7 1.7 %shard_map.73 = bf16[96,5120]{1,0:T(8,128)(2,1)} custom-call(s32[1]{0:T(128)} %bitcast.tile_ref, f32[96,5120]{1,0:T(8,128)S(1)} %shard_map.72.near_ref, bf16[96,2176]{1,0:T(8,128)(2,1)S(1)} %collective-permute-done.13.far_ref, bf16[256,1024]{1,0:T(8,128)(2,1)S(1)} %collective-permute-done.4.refs_0_, bf16[256,1024]{1,0:T(8,128)(2,1)S(1)} %collective-permute-done.14.refs_1_, ...), custom_call_target="tpu_custom_call" | custom-call | flops 503316480 | bytes 1048576 | tf_op jit(solution)/shard_map/pallas_call | solution.py:31
  (2 shorter events, 0.1 us)
Async XLA Ops:
  0.0 3.9 %copy-start = (bf16[256,5120]{1,0:T(8,128)(2,1)S(1)}, bf16[256,5120]{1,0:T(8,128)(2,1)}, u32[]{:S(2)}) copy-start(bf16[256,5120]{1,0:T(8,128)(2,1)} %w_ref.6) | copy-start | bytes 7864324
  3.9 14.6 %collective-permute-start.1 = (bf16[256,5120]{1,0:T(8,128)(2,1)S(1)}, bf16[256,5120]{1,0:T(8,128)(2,1)S(1)}, u32[]{:S(2)}, u32[]{:S(2)}) collective-permute-start(bf16[256,5120]{1,0:T(8,128)(2,1)S(1)} %copy-done), channel_id=1, source_target_pairs={{0,1},{1,0},{2,3},{3,2},{4,5},{5,4},{6,7},{7,6},{8,9},{9,8},{10,11... | collective-permute-start | bytes 7864328 | tf_op jit(solution)/shard_map/ppermute | solution.py:267
  4.4 18.3 %collective-permute-start.4 = (bf16[256,1024]{1,0:T(8,128)(2,1)}, bf16[256,1024]{1,0:T(8,128)(2,1)S(1)}, u32[]{:S(2)}, u32[]{:S(2)}) collective-permute-start(bf16[256,1024]{1,0:T(8,128)(2,1)} %get-tuple-element.53), channel_id=1, source_target_pairs={{2,0},{3,1},{0,2},{1,3},{6,4},{7,5},{4,6},{5,7},{10,8},{11,9},{8,1... | collective-permute-start | bytes 1572872 | tf_op jit(solution)/shard_map/ppermute | solution.py:279
  7.0 11.5 %collective-permute-start = (bf16[1168,128]{1,0:T(8,128)(2,1)}, bf16[1168,128]{1,0:T(8,128)(2,1)S(1)}, u32[]{:S(2)}, u32[]{:S(2)}) collective-permute-start(bf16[1168,128]{1,0:T(8,128)(2,1)} %get-tuple-element.41), channel_id=1, source_target_pairs={{0,4},{4,0},{8,12},{12,8},{16,20},{20,16},{24,28},{28,24},{1,5},{5... | collective-permute-start | bytes 897032 | tf_op jit(solution)/shard_map/ppermute | solution.py:263
  8.5 7.1 %collective-permute-start.3 = (bf16[768,128]{1,0:T(8,128)(2,1)}, bf16[768,128]{1,0:T(8,128)(2,1)S(1)}, u32[]{:S(2)}, u32[]{:S(2)}) collective-permute-start(bf16[768,128]{1,0:T(8,128)(2,1)} %get-tuple-element.42.keep_kv_ref), channel_id=1, source_target_pairs={{8,16},{16,8},{12,20},{20,12},{9,17},{17,9},{13,21},{21,13},{10,18... | collective-permute-start | bytes 589832 | tf_op jit(solution)/shard_map/ppermute | solution.py:259
  9.1 9.3 %collective-permute-start.2 = (bf16[768,128]{1,0:T(8,128)(2,1)}, bf16[768,128]{1,0:T(8,128)(2,1)S(1)}, u32[]{:S(2)}, u32[]{:S(2)}) collective-permute-start(bf16[768,128]{1,0:T(8,128)(2,1)} %get-tuple-element.42.keep_kv_ref), channel_id=1, source_target_pairs={{0,8},{8,0},{4,12},{12,4},{16,24},{24,16},{20,28},{28,20},{1,9},{9... | collective-permute-start | bytes 589832 | tf_op jit(solution)/shard_map/ppermute | solution.py:259
  13.6 1.0 %copy-start.1 = (bf16[768,128]{1,0:T(8,128)(2,1)S(1)}, bf16[768,128]{1,0:T(8,128)(2,1)}, u32[]{:S(2)}) copy-start(bf16[768,128]{1,0:T(8,128)(2,1)} %get-tuple-element.42.keep_kv_ref) | copy-start | bytes 589828
  14.6 0.9 %copy-start.2 = (bf16[400,128]{1,0:T(8,128)(2,1)S(1)}, bf16[400,128]{1,0:T(8,128)(2,1)}, u32[]{:S(2)}) copy-start(bf16[400,128]{1,0:T(8,128)(2,1)} %get-tuple-element.44.keep_q_ref) | copy-start | bytes 307204
  18.5 11.2 %collective-permute-start.6 = (bf16[768,128]{1,0:T(8,128)(2,1)S(1)}, bf16[768,128]{1,0:T(8,128)(2,1)S(1)}, u32[]{:S(2)}, u32[]{:S(2)}) collective-permute-start(bf16[768,128]{1,0:T(8,128)(2,1)S(1)} %get-tuple-element.55.came_ref), channel_id=1, source_target_pairs={{8,16},{16,8},{12,20},{20,12},{9,17},{17,9},{13,21},{21,13},{10,18... | collective-permute-start | bytes 589832 | tf_op jit(solution)/shard_map/ppermute | solution.py:259
  19.2 10.5 %collective-permute-start.5 = (bf16[768,128]{1,0:T(8,128)(2,1)S(1)}, bf16[768,128]{1,0:T(8,128)(2,1)S(1)}, u32[]{:S(2)}, u32[]{:S(2)}) collective-permute-start(bf16[768,128]{1,0:T(8,128)(2,1)S(1)} %get-tuple-element.55.came_ref), channel_id=1, source_target_pairs={{0,8},{8,0},{4,12},{12,4},{16,24},{24,16},{20,28},{28,20},{1,9},{9... | collective-permute-start | bytes 589832 | tf_op jit(solution)/shard_map/ppermute | solution.py:259
  22.7 18.9 %collective-permute-start.12 = (bf16[256,1024]{1,0:T(8,128)(2,1)S(1)}, bf16[256,1024]{1,0:T(8,128)(2,1)S(1)}, u32[]{:S(2)}, u32[]{:S(2)}) collective-permute-start(bf16[256,1024]{1,0:T(8,128)(2,1)S(1)} %collective-permute-done.4.refs_0_), channel_id=1, source_target_pairs={{0,4},{4,0},{8,12},{12,8},{16,20},{20,16},{24,28},{28,24},{1,5},{5... | collective-permute-start | bytes 1572872 | tf_op jit(solution)/shard_map/ppermute | solution.py:263
  23.2 12.3 %collective-permute-start.7 = (bf16[768,128]{1,0:T(8,128)(2,1)S(1)}, bf16[768,128]{1,0:T(8,128)(2,1)S(1)}, u32[]{:S(2)}, u32[]{:S(2)}) collective-permute-start(bf16[768,128]{1,0:T(8,128)(2,1)S(1)} %get-tuple-element.58), channel_id=1, source_target_pairs={{0,16},{16,0},{4,20},{20,4},{8,24},{24,8},{12,28},{28,12},{1,17},{... | collective-permute-start | bytes 589832 | tf_op jit(solution)/shard_map/ppermute | solution.py:259
  24.3 17.3 %collective-permute-start.11 = (bf16[256,1408]{1,0:T(8,128)(2,1)S(1)}, bf16[256,1408]{1,0:T(8,128)(2,1)S(1)}, u32[]{:S(2)}, u32[]{:S(2)}) collective-permute-start(bf16[256,1408]{1,0:T(8,128)(2,1)S(1)} %shard_map.66), channel_id=1, source_target_pairs={{2,0},{3,1},{0,2},{1,3},{6,4},{7,5},{4,6},{5,7},{10,8},{11,9},{8,1... | collective-permute-start | bytes 2162696 | tf_op jit(solution)/shard_map/ppermute | solution.py:279
  36.9 3.6 %collective-permute-start.8 = (bf16[2,96,128]{2,1,0:T(8,128)(2,1)S(1)}, bf16[2,96,128]{2,1,0:T(8,128)(2,1)S(1)}, u32[]{:S(2)}, u32[]{:S(2)}) collective-permute-start(bf16[2,96,128]{2,1,0:T(8,128)(2,1)S(1)} %get-tuple-element.60), channel_id=1, source_target_pairs={{0,5},{1,4},{2,7},{3,6},{4,1},{5,0},{6,3},{7,2},{8,13},{9,12},{10,... | collective-permute-start | bytes 147464 | tf_op jit(solution)/shard_map/ppermute | solution.py:274
  37.0 4.6 %collective-permute-start.9 = (bf16[2,96,128]{2,1,0:T(8,128)(2,1)S(1)}, bf16[2,96,128]{2,1,0:T(8,128)(2,1)S(1)}, u32[]{:S(2)}, u32[]{:S(2)}) collective-permute-start(bf16[2,96,128]{2,1,0:T(8,128)(2,1)S(1)} %get-tuple-element.61), channel_id=1, source_target_pairs={{0,4},{4,0},{8,12},{12,8},{16,20},{20,16},{24,28},{28,24},{1,5},{5... | collective-permute-start | bytes 147464 | tf_op jit(solution)/shard_map/ppermute | solution.py:263
  37.7 3.9 %collective-permute-start.10 = (bf16[2,96,128]{2,1,0:T(8,128)(2,1)S(1)}, bf16[2,96,128]{2,1,0:T(8,128)(2,1)S(1)}, u32[]{:S(2)}, u32[]{:S(2)}) collective-permute-start(bf16[2,96,128]{2,1,0:T(8,128)(2,1)S(1)} %get-tuple-element.62), channel_id=1, source_target_pairs={{0,1},{1,0},{2,3},{3,2},{4,5},{5,4},{6,7},{7,6},{8,9},{9,8},{10,11... | collective-permute-start | bytes 147464 | tf_op jit(solution)/shard_map/ppermute | solution.py:267
  42.0 12.7 %collective-permute-start.16 = (bf16[256,1408]{1,0:T(8,128)(2,1)S(1)}, bf16[256,1408]{1,0:T(8,128)(2,1)S(1)}, u32[]{:S(2)}, u32[]{:S(2)}) collective-permute-start(bf16[256,1408]{1,0:T(8,128)(2,1)S(1)} %collective-permute-done.11.refs_4_), channel_id=1, source_target_pairs={{0,1},{1,0},{2,3},{3,2},{4,5},{5,4},{6,7},{7,6},{8,9},{9,8},{10,11... | collective-permute-start | bytes 2162696 | tf_op jit(solution)/shard_map/ppermute | solution.py:267
  42.1 12.5 %collective-permute-start.14 = (bf16[256,1024]{1,0:T(8,128)(2,1)S(1)}, bf16[256,1024]{1,0:T(8,128)(2,1)S(1)}, u32[]{:S(2)}, u32[]{:S(2)}) collective-permute-start(bf16[256,1024]{1,0:T(8,128)(2,1)S(1)} %collective-permute-done.4.refs_0_), channel_id=1, source_target_pairs={{0,1},{1,0},{2,3},{3,2},{4,5},{5,4},{6,7},{7,6},{8,9},{9,8},{10,11... | collective-permute-start | bytes 1572872 | tf_op jit(solution)/shard_map/ppermute | solution.py:267
  42.6 12.1 %collective-permute-start.15 = (bf16[256,1024]{1,0:T(8,128)(2,1)S(1)}, bf16[256,1024]{1,0:T(8,128)(2,1)S(1)}, u32[]{:S(2)}, u32[]{:S(2)}) collective-permute-start(bf16[256,1024]{1,0:T(8,128)(2,1)S(1)} %collective-permute-done.12.refs_2_), channel_id=1, source_target_pairs={{0,1},{1,0},{2,3},{3,2},{4,5},{5,4},{6,7},{7,6},{8,9},{9,8},{10,11... | collective-permute-start | bytes 1572872 | tf_op jit(solution)/shard_map/ppermute | solution.py:267
  42.7 12.0 %collective-permute-start.13 = (bf16[96,2176]{1,0:T(8,128)(2,1)S(1)}, bf16[96,2176]{1,0:T(8,128)(2,1)S(1)}, u32[]{:S(2)}, u32[]{:S(2)}) collective-permute-start(bf16[96,2176]{1,0:T(8,128)(2,1)S(1)} %get-tuple-element.71), channel_id=1, source_target_pairs={{2,0},{3,1},{0,2},{1,3},{6,4},{7,5},{4,6},{5,7},{10,8},{11,9},{8,1... | collective-permute-start | bytes 1253384 | tf_op jit(solution)/shard_map/ppermute | solution.py:279

commit v5 on v4

--- a/solution.py
+++ b/solution.py
@@ -11,10 +11,9 @@
 HD = 128
 REACH = 3
 NEG = -1e30
-MERGE = 0
 FLAGS = 16
-SIDE = 1024
-COMMON = 1408
+SIDE = 1152
+COMMON = 1280
 STATE = HD + 8
 EXPONENT = math.log2(math.e) / math.sqrt(HD)
 BF16, F32 = jnp.bfloat16, jnp.float32
@@ -340,7 +339,7 @@
         merge_kernel if far == 2 else functools.partial(merge_kernel, even_ref=None),
         (shape((8, HD), jnp.int32), shape((2,) + one), kv_shape) + (kv_shape,) * far,
         (tile, held_q, held_kv, came),
-        MERGE * rows * rows * HD,
+        0,
     )
     came_near = [swap_pairs(came_kv, 1, phase) for phase in range(2)]
     farther = [swap_pairs(to_far[i], 2, i) for i in range(far)]
@@ -364,7 +363,7 @@
         second_kernel,
         state,
         (flags, tile, q_again, *came_near, held),
-        1000 * area * HD,
+        16 * area * HD,
         0,
         alias={5: 0},
     )
@@ -373,8 +372,8 @@
         functools.partial(third_kernel, far=far),
         (shape(block),) * 4 if small else (shape(one),) * 2,
         (flags, tile, head, q_pair, held, *farther),
-        4 * area * HD,
-        area,
+        300 * area * HD,
+        0,
         scratch=(pltpu.VMEM(state.shape, F32),),
     )
     if not small:
@@ -408,7 +407,7 @@
     pieces = [side_own, side_other, common]
     *ready, _ = lax.optimization_barrier((*pieces, own_a))
     far_weights = [each for piece, to in zip(pieces, ready) for each in (piece, swap_cores(to))]
-    near = call(near_kernel, shape((own_rows, model), F32), (own_a,) + near_weights, flops, vmem=16)
+    near = call(near_kernel, shape((own_rows, model), F32), (own_a,) + near_weights, 300 * flops, vmem=16)
     return call(
         last_kernel, shape((own_rows, model)), (tile, near, got, *far_weights), flops, vmem=20
     )

time: 56.7 us -> 58.4 us (1.030)
  waiting for transfers between devices: 19.6 us -> 21.6 us
  starting transfers between devices: 20.4 us -> 19 us
  Pallas kernels: 13.6 us -> 14.8 us
    ppermute x5, waiting for transfers between devices: 7 us -> 9.51 us  [swap_pairs(): return lax.ppermute(value, 'ctx', pairs)]
    ppermute x3, starting transfers between devices: 4.92 us -> 3.64 us  [from_chip(): lax.ppermute(value, 'head', [((i + 2 * steps) % count, i) for i in range(...]
    pallas_call x10, Pallas kernels: 13.6 us -> 14.8 us  [call(): pl.pallas_call(kernel, out_shape=outs, in_specs=[SMEM if s else HBM if i...]
  transfers between devices with their start and end apart: 17 -> 17, of which waited for: 5 -> 5; matrix products, arithmetic and copies ran while one was open for 0% -> 0% of each run, Pallas kernels for 15% -> 11%
where the time goes in v5:
time: 58.4 us; the launch traced here: 58.1 us
  waiting for transfers between devices  21.6 us (37%)
  starting transfers between devices  19 us (33%)
  Pallas kernels  14.8 us (25%)
  local copies, waits for them, and re-layouts  1.86 us (3%)
  between operations  0.93 us (2%)
    pallas_call x10, Pallas kernels, call(): pl.pallas_call(kernel, out_shape=outs, in_specs=[SMEM if s else HBM if i...  14.8 us
    ppermute x5, starting transfers between devices, swap_pairs(): return lax.ppermute(value, 'ctx', pairs)  10.4 us
    ppermute x5, waiting for transfers between devices, swap_pairs(): return lax.ppermute(value, 'ctx', pairs)  9.51 us
    ppermute x3, waiting for transfers between devices, from_chip(): lax.ppermute(value, 'head', [((i + 2 * steps) % count, i) for i in range(...  9.36 us
    ppermute x3, starting transfers between devices, from_chip(): lax.ppermute(value, 'head', [((i + 2 * steps) % count, i) for i in range(...  3.64 us
    ppermute x3, starting transfers between devices, swap_tiles(): lax.ppermute(value, 'ctx', [(i, i ^ 1) for i in range(lax.axis_size('ctx'...  2.59 us
    ppermute x5, starting transfers between devices, swap_cores(): lax.ppermute(value, 'head', [(i, i ^ 1) for i in range(lax.axis_size('hea...  2.31 us
    unnamed x6, local copies, waits for them, and re-layouts  1.86 us
  transfers between devices with their start and end apart: 17, of which 5 were waited for; matrix products, arithmetic and copies ran while one was open for 0% of the time, Pallas kernels for 11%

profile of v5, /device:TPU:0, one launch (start us, length us, event | category | flops | bytes accessed | tf_op | source)
XLA Modules:
  0.0 58.1 jit_solution(3942711173058983722)
XLA Ops:
  0.0 0.0 copy-start
  0.8 3.1 %shard_map.64 = (bf16[400,128]{1,0:T(8,128)(2,1)}, bf16[768,128]{1,0:T(8,128)(2,1)}, bf16[1168,128]{1,0:T(8,128)(2,1)}, bf16[256,1152]{1,0:T(8,128)(2,1)}) custom-call(s32[1]{0:T(128)} %bitcast.tile_ref, s32[1]{0:T(128)} %bitcast.1._.head_ref, s32[1,7]{1,0:T(1,128)} %list_ref.1, s32[1,1]{1,0:T(1,128)} %bitcast.3.count_ref, bf16[384,256]{1,0:T(8,128)(2,1)} %q_ref.1, ...), custom_call_target="tpu_custom_call" | custom-call | bytes 1048576 | tf_op jit(solution)/shard_map/pallas_call | solution.py:30
  3.9 0.0 copy-done
  3.9 0.5 collective-permute-start.1
  4.4 2.6 %collective-permute-start.4 = (bf16[256,1152]{1,0:T(8,128)(2,1)}, bf16[256,1152]{1,0:T(8,128)(2,1)}, u32[]{:S(2)}, u32[]{:S(2)}) collective-permute-start(bf16[256,1152]{1,0:T(8,128)(2,1)} %get-tuple-element.53), channel_id=1, source_target_pairs={{2,0},{3,1},{0,2},{1,3},{6,4},{7,5},{4,6},{5,7},{10,8},{11,9},{8,1... | collective-permute-start | bytes 1769480 | tf_op jit(solution)/shard_map/ppermute | solution.py:278
  7.0 1.5 %collective-permute-start = (bf16[1168,128]{1,0:T(8,128)(2,1)}, bf16[1168,128]{1,0:T(8,128)(2,1)S(1)}, u32[]{:S(2)}, u32[]{:S(2)}) collective-permute-start(bf16[1168,128]{1,0:T(8,128)(2,1)} %get-tuple-element.41), channel_id=1, source_target_pairs={{0,4},{4,0},{8,12},{12,8},{16,20},{20,16},{24,28},{28,24},{1,5},{5... | collective-permute-start | bytes 897032 | tf_op jit(solution)/shard_map/ppermute | solution.py:262
  8.5 0.7 %collective-permute-start.3 = (bf16[768,128]{1,0:T(8,128)(2,1)}, bf16[768,128]{1,0:T(8,128)(2,1)S(1)}, u32[]{:S(2)}, u32[]{:S(2)}) collective-permute-start(bf16[768,128]{1,0:T(8,128)(2,1)} %get-tuple-element.42.keep_kv_ref), channel_id=1, source_target_pairs={{8,16},{16,8},{12,20},{20,12},{9,17},{17,9},{13,21},{21,13},{10,18... | collective-permute-start | bytes 589832 | tf_op jit(solution)/shard_map/ppermute | solution.py:258
  9.2 4.5 %collective-permute-start.2 = (bf16[768,128]{1,0:T(8,128)(2,1)}, bf16[768,128]{1,0:T(8,128)(2,1)S(1)}, u32[]{:S(2)}, u32[]{:S(2)}) collective-permute-start(bf16[768,128]{1,0:T(8,128)(2,1)} %get-tuple-element.42.keep_kv_ref), channel_id=1, source_target_pairs={{0,8},{8,0},{4,12},{12,4},{16,24},{24,16},{20,28},{28,20},{1,9},{9... | collective-permute-start | bytes 589832 | tf_op jit(solution)/shard_map/ppermute | solution.py:258
  13.6 0.0 copy-start.1
  13.6 1.0 %copy-done.1 = bf16[768,128]{1,0:T(8,128)(2,1)S(1)} copy-done((bf16[768,128]{1,0:T(8,128)(2,1)S(1)}, bf16[768,128]{1,0:T(8,128)(2,1)}, u32[]{:S(2)}) %copy-start.1) | copy-done | bytes 196632
  14.6 0.0 copy-start.2
  14.6 0.9 %copy-done.2 = bf16[400,128]{1,0:T(8,128)(2,1)S(1)} copy-done((bf16[400,128]{1,0:T(8,128)(2,1)S(1)}, bf16[400,128]{1,0:T(8,128)(2,1)}, u32[]{:S(2)}) %copy-start.2) | copy-done | bytes 102424
  15.6 0.0 collective-permute-done.3.kept_second_ref
  15.6 2.9 %collective-permute-done.2.kept_first_ref = bf16[768,128]{1,0:T(8,128)(2,1)S(1)} collective-permute-done((bf16[768,128]{1,0:T(8,128)(2,1)}, bf16[768,128]{1,0:T(8,128)(2,1)S(1)}, u32[]{:S(2)}, u32[]{:S(2)}) %collective-permute-start.2) | collective-permute-done | bytes 196640 | tf_op jit(solution)/shard_map/ppermute | solution.py:258
  18.5 0.0 collective-permute-done.came_ref
  18.5 0.0 collective-permute-done.1.wp_ref
  18.6 0.7 %collective-permute-start.6 = (bf16[768,128]{1,0:T(8,128)(2,1)S(1)}, bf16[768,128]{1,0:T(8,128)(2,1)S(1)}, u32[]{:S(2)}, u32[]{:S(2)}) collective-permute-start(bf16[768,128]{1,0:T(8,128)(2,1)S(1)} %get-tuple-element.55.came_ref), channel_id=1, source_target_pairs={{8,16},{16,8},{12,20},{20,12},{9,17},{17,9},{13,21},{21,13},{10,18... | collective-permute-start | bytes 589832 | tf_op jit(solution)/shard_map/ppermute | solution.py:258
  19.3 3.5 %collective-permute-start.5 = (bf16[768,128]{1,0:T(8,128)(2,1)S(1)}, bf16[768,128]{1,0:T(8,128)(2,1)S(1)}, u32[]{:S(2)}, u32[]{:S(2)}) collective-permute-start(bf16[768,128]{1,0:T(8,128)(2,1)S(1)} %get-tuple-element.55.came_ref), channel_id=1, source_target_pairs={{0,8},{8,0},{4,12},{12,4},{16,24},{24,16},{20,28},{28,20},{1,9},{9... | collective-permute-start | bytes 589832 | tf_op jit(solution)/shard_map/ppermute | solution.py:258
  22.8 1.1 %collective-permute-start.7 = (bf16[768,128]{1,0:T(8,128)(2,1)S(1)}, bf16[768,128]{1,0:T(8,128)(2,1)S(1)}, u32[]{:S(2)}, u32[]{:S(2)}) collective-permute-start(bf16[768,128]{1,0:T(8,128)(2,1)S(1)} %get-tuple-element.58), channel_id=1, source_target_pairs={{0,16},{16,0},{4,20},{20,4},{8,24},{24,8},{12,28},{28,12},{1,17},{... | collective-permute-start | bytes 589832 | tf_op jit(solution)/shard_map/ppermute | solution.py:258
  23.8 0.0 collective-permute-done.4.refs_0_
  23.9 0.5 collective-permute-start.12
  24.4 0.5 collective-permute-start.11
  24.9 3.0 %shard_map.68._ = f32[2,136,384]{2,1,0:T(8,128)S(1)} custom-call(s32[8,128]{1,0:T(8,128)S(1)} %get-tuple-element.51.flag_ref, s32[1]{0:T(128)} %bitcast.tile_ref, bf16[2,384,128]{2,1,0:T(8,128)(2,1)S(1)} %get-tuple-element.54.q_ref, bf16[768,128]{1,0:T(8,128)(2,1)S(1)} %get-tuple-element.49.keep_kv_ref.own_ref, ...), custom_call_target="tpu_custom_call" | custom-call | flops 603979776 | bytes 1048576 | tf_op jit(solution)/shard_map/pallas_call | solution.py:30
  27.9 0.0 collective-permute-done.6.second_ref
  27.9 0.0 collective-permute-done.5.first_ref
  27.9 1.2 %shard_map.69.state_ref = f32[2,136,384]{2,1,0:T(8,128)S(1)} custom-call(s32[8,128]{1,0:T(8,128)S(1)} %get-tuple-element.51.flag_ref, s32[1]{0:T(128)} %bitcast.tile_ref, bf16[2,384,128]{2,1,0:T(8,128)(2,1)S(1)} %get-tuple-element.54.q_ref, bf16[768,128]{1,0:T(8,128)(2,1)S(1)} %collective-permute-done.5.first_ref, ...), custom_call_target="tpu_custom_call", output_to_operand_aliasing={{}: (5, {})} | custom-call | flops 301989888 | bytes 1048576 | tf_op jit(solution)/shard_map/pallas_call | solution.py:30
  29.1 6.6 %collective-permute-done.7.refs_0_ = bf16[768,128]{1,0:T(8,128)(2,1)S(1)} collective-permute-done((bf16[768,128]{1,0:T(8,128)(2,1)S(1)}, bf16[768,128]{1,0:T(8,128)(2,1)S(1)}, u32[]{:S(2)}, u32[]{:S(2)}) %collective-permute-start.7) | collective-permute-done | bytes 196640 | tf_op jit(solution)/shard_map/ppermute | solution.py:258
  35.7 1.4 %shard_map.70 = (bf16[2,96,128]{2,1,0:T(8,128)(2,1)S(1)}, bf16[2,96,128]{2,1,0:T(8,128)(2,1)S(1)}, bf16[2,96,128]{2,1,0:T(8,128)(2,1)S(1)}, bf16[2,96,128]{2,1,0:T(8,128)(2,1)S(1)}) custom-call(s32[8,128]{1,0:T(8,128)S(1)} %get-tuple-element.51.flag_ref, s32[1]{0:T(128)} %bitcast.tile_ref, s32[1]{0:T(128)} %bitcast.1._.head_ref, ...), custom_call_target="tpu_custom_call" | custom-call | flops 5662310400 | bytes 1048576 | tf_op jit(solution)/shard_map/pallas_call | solution.py:30
  37.1 0.1 collective-permute-start.8
  37.1 0.6 collective-permute-start.9
  37.7 1.3 %collective-permute-start.10 = (bf16[2,96,128]{2,1,0:T(8,128)(2,1)S(1)}, bf16[2,96,128]{2,1,0:T(8,128)(2,1)S(1)}, u32[]{:S(2)}, u32[]{:S(2)}) collective-permute-start(bf16[2,96,128]{2,1,0:T(8,128)(2,1)S(1)} %get-tuple-element.62), channel_id=1, source_target_pairs={{0,1},{1,0},{2,3},{3,2},{4,5},{5,4},{6,7},{7,6},{8,9},{9,8},{10,11... | collective-permute-start | bytes 147464 | tf_op jit(solution)/shard_map/ppermute | solution.py:266
  39.0 1.7 %collective-permute-done.8.cross_ref = bf16[2,96,128]{2,1,0:T(8,128)(2,1)S(1)} collective-permute-done((bf16[2,96,128]{2,1,0:T(8,128)(2,1)S(1)}, bf16[2,96,128]{2,1,0:T(8,128)(2,1)S(1)}, u32[]{:S(2)}, u32[]{:S(2)}) %collective-permute-start.8) | collective-permute-done | bytes 49184 | tf_op jit(solution)/shard_map/ppermute | solution.py:273
  40.6 1.1 %collective-permute-done.9.y_ref = bf16[2,96,128]{2,1,0:T(8,128)(2,1)S(1)} collective-permute-done((bf16[2,96,128]{2,1,0:T(8,128)(2,1)S(1)}, bf16[2,96,128]{2,1,0:T(8,128)(2,1)S(1)}, u32[]{:S(2)}, u32[]{:S(2)}) %collective-permute-start.9) | collective-permute-done | bytes 49184 | tf_op jit(solution)/shard_map/ppermute | solution.py:262
  41.7 0.0 collective-permute-done.10.core_ref
  41.7 0.0 collective-permute-done.12.refs_2_
  41.7 0.0 collective-permute-done.11.refs_4_
  41.7 1.2 %shard_map.71 = (bf16[96,512]{1,0:T(8,128)(2,1)S(1)}, bf16[96,2048]{1,0:T(8,128)(2,1)}) custom-call(s32[1]{0:T(128)} %bitcast.tile_ref, s32[1]{0:T(128)} %bitcast.1._.head_ref, bf16[2,96,128]{2,1,0:T(8,128)(2,1)S(1)} %get-tuple-element.59.own_ref, bf16[2,96,128]{2,1,0:T(8,128)(2,1)S(1)} %collective-permute-done.9.y_ref, ...), custom_call_target="tpu_custom_call" | custom-call | flops 125829120 | bytes 1048576 | tf_op jit(solution)/shard_map/pallas_call | solution.py:30
  42.9 0.5 collective-permute-start.13
  43.4 0.0 collective-permute-start.14
  43.4 0.5 collective-permute-start.15
  43.9 0.0 collective-permute-start.16
  43.9 1.0 %shard_map.72.near_ref = f32[96,5120]{1,0:T(8,128)S(1)} custom-call(bf16[96,512]{1,0:T(8,128)(2,1)S(1)} %get-tuple-element.70.a_ref, bf16[256,5120]{1,0:T(8,128)(2,1)S(1)} %copy-done, bf16[256,5120]{1,0:T(8,128)(2,1)S(1)} %collective-permute-done.1.wp_ref), custom_call_target="tpu_custom_call" | custom-call | flops 150994944000 | bytes 1048576 | tf_op jit(solution)/shard_map/pallas_call | solution.py:30
  44.9 9.4 %collective-permute-done.13.far_ref = bf16[96,2048]{1,0:T(8,128)(2,1)} collective-permute-done((bf16[96,2048]{1,0:T(8,128)(2,1)}, bf16[96,2048]{1,0:T(8,128)(2,1)}, u32[]{:S(2)}, u32[]{:S(2)}) %collective-permute-start.13) | collective-permute-done | bytes 393248 | tf_op jit(solution)/shard_map/ppermute | solution.py:278
  54.2 0.0 collective-permute-done.14.refs_1_
  54.2 0.0 collective-permute-done.15.refs_3_
  54.2 0.0 collective-permute-done.16.refs_5_
  54.2 3.9 %shard_map.73 = bf16[96,5120]{1,0:T(8,128)(2,1)} custom-call(s32[1]{0:T(128)} %bitcast.tile_ref, f32[96,5120]{1,0:T(8,128)S(1)} %shard_map.72.near_ref, bf16[96,2048]{1,0:T(8,128)(2,1)} %collective-permute-done.13.far_ref, bf16[256,1152]{1,0:T(8,128)(2,1)} %collective-permute-done.4.refs_0_, bf16[256,1152]{1,0:T(8,128)(2,1)} %collective-permute-done.14.refs_1_, ...), custom_call_target="tpu_custom_call" | custom-call | flops 503316480 | bytes 1048576 | tf_op jit(solution)/shard_map/pallas_call | solution.py:30
  (3 shorter events, 0.1 us)
Async XLA Ops:
  0.0 3.9 %copy-start = (bf16[256,5120]{1,0:T(8,128)(2,1)S(1)}, bf16[256,5120]{1,0:T(8,128)(2,1)}, u32[]{:S(2)}) copy-start(bf16[256,5120]{1,0:T(8,128)(2,1)} %w_ref.6) | copy-start | bytes 7864324
  3.9 14.6 %collective-permute-start.1 = (bf16[256,5120]{1,0:T(8,128)(2,1)S(1)}, bf16[256,5120]{1,0:T(8,128)(2,1)S(1)}, u32[]{:S(2)}, u32[]{:S(2)}) collective-permute-start(bf16[256,5120]{1,0:T(8,128)(2,1)S(1)} %copy-done), channel_id=1, source_target_pairs={{0,1},{1,0},{2,3},{3,2},{4,5},{5,4},{6,7},{7,6},{8,9},{9,8},{10,11... | collective-permute-start | bytes 7864328 | tf_op jit(solution)/shard_map/ppermute | solution.py:266
  4.4 19.4 %collective-permute-start.4 = (bf16[256,1152]{1,0:T(8,128)(2,1)}, bf16[256,1152]{1,0:T(8,128)(2,1)}, u32[]{:S(2)}, u32[]{:S(2)}) collective-permute-start(bf16[256,1152]{1,0:T(8,128)(2,1)} %get-tuple-element.53), channel_id=1, source_target_pairs={{2,0},{3,1},{0,2},{1,3},{6,4},{7,5},{4,6},{5,7},{10,8},{11,9},{8,1... | collective-permute-start | bytes 1769480 | tf_op jit(solution)/shard_map/ppermute | solution.py:278
  7.0 11.5 %collective-permute-start = (bf16[1168,128]{1,0:T(8,128)(2,1)}, bf16[1168,128]{1,0:T(8,128)(2,1)S(1)}, u32[]{:S(2)}, u32[]{:S(2)}) collective-permute-start(bf16[1168,128]{1,0:T(8,128)(2,1)} %get-tuple-element.41), channel_id=1, source_target_pairs={{0,4},{4,0},{8,12},{12,8},{16,20},{20,16},{24,28},{28,24},{1,5},{5... | collective-permute-start | bytes 897032 | tf_op jit(solution)/shard_map/ppermute | solution.py:262
  8.5 7.1 %collective-permute-start.3 = (bf16[768,128]{1,0:T(8,128)(2,1)}, bf16[768,128]{1,0:T(8,128)(2,1)S(1)}, u32[]{:S(2)}, u32[]{:S(2)}) collective-permute-start(bf16[768,128]{1,0:T(8,128)(2,1)} %get-tuple-element.42.keep_kv_ref), channel_id=1, source_target_pairs={{8,16},{16,8},{12,20},{20,12},{9,17},{17,9},{13,21},{21,13},{10,18... | collective-permute-start | bytes 589832 | tf_op jit(solution)/shard_map/ppermute | solution.py:258
  9.2 9.3 %collective-permute-start.2 = (bf16[768,128]{1,0:T(8,128)(2,1)}, bf16[768,128]{1,0:T(8,128)(2,1)S(1)}, u32[]{:S(2)}, u32[]{:S(2)}) collective-permute-start(bf16[768,128]{1,0:T(8,128)(2,1)} %get-tuple-element.42.keep_kv_ref), channel_id=1, source_target_pairs={{0,8},{8,0},{4,12},{12,4},{16,24},{24,16},{20,28},{28,20},{1,9},{9... | collective-permute-start | bytes 589832 | tf_op jit(solution)/shard_map/ppermute | solution.py:258
  13.6 1.0 %copy-start.1 = (bf16[768,128]{1,0:T(8,128)(2,1)S(1)}, bf16[768,128]{1,0:T(8,128)(2,1)}, u32[]{:S(2)}) copy-start(bf16[768,128]{1,0:T(8,128)(2,1)} %get-tuple-element.42.keep_kv_ref) | copy-start | bytes 589828
  14.6 0.9 %copy-start.2 = (bf16[400,128]{1,0:T(8,128)(2,1)S(1)}, bf16[400,128]{1,0:T(8,128)(2,1)}, u32[]{:S(2)}) copy-start(bf16[400,128]{1,0:T(8,128)(2,1)} %get-tuple-element.44.keep_q_ref) | copy-start | bytes 307204
  18.6 9.3 %collective-permute-start.6 = (bf16[768,128]{1,0:T(8,128)(2,1)S(1)}, bf16[768,128]{1,0:T(8,128)(2,1)S(1)}, u32[]{:S(2)}, u32[]{:S(2)}) collective-permute-start(bf16[768,128]{1,0:T(8,128)(2,1)S(1)} %get-tuple-element.55.came_ref), channel_id=1, source_target_pairs={{8,16},{16,8},{12,20},{20,12},{9,17},{17,9},{13,21},{21,13},{10,18... | collective-permute-start | bytes 589832 | tf_op jit(solution)/shard_map/ppermute | solution.py:258
  19.3 8.6 %collective-permute-start.5 = (bf16[768,128]{1,0:T(8,128)(2,1)S(1)}, bf16[768,128]{1,0:T(8,128)(2,1)S(1)}, u32[]{:S(2)}, u32[]{:S(2)}) collective-permute-start(bf16[768,128]{1,0:T(8,128)(2,1)S(1)} %get-tuple-element.55.came_ref), channel_id=1, source_target_pairs={{0,8},{8,0},{4,12},{12,4},{16,24},{24,16},{20,28},{28,20},{1,9},{9... | collective-permute-start | bytes 589832 | tf_op jit(solution)/shard_map/ppermute | solution.py:258
  22.8 12.9 %collective-permute-start.7 = (bf16[768,128]{1,0:T(8,128)(2,1)S(1)}, bf16[768,128]{1,0:T(8,128)(2,1)S(1)}, u32[]{:S(2)}, u32[]{:S(2)}) collective-permute-start(bf16[768,128]{1,0:T(8,128)(2,1)S(1)} %get-tuple-element.58), channel_id=1, source_target_pairs={{0,16},{16,0},{4,20},{20,4},{8,24},{24,8},{12,28},{28,12},{1,17},{... | collective-permute-start | bytes 589832 | tf_op jit(solution)/shard_map/ppermute | solution.py:258
  23.9 17.8 %collective-permute-start.12 = (bf16[256,1152]{1,0:T(8,128)(2,1)}, bf16[256,1152]{1,0:T(8,128)(2,1)}, u32[]{:S(2)}, u32[]{:S(2)}) collective-permute-start(bf16[256,1152]{1,0:T(8,128)(2,1)} %collective-permute-done.4.refs_0_), channel_id=1, source_target_pairs={{0,4},{4,0},{8,12},{12,8},{16,20},{20,16},{24,28},{28,24},{1,5},{5... | collective-permute-start | bytes 1769480 | tf_op jit(solution)/shard_map/ppermute | solution.py:262
  24.4 17.3 %collective-permute-start.11 = (bf16[256,1280]{1,0:T(8,128)(2,1)S(1)}, bf16[256,1280]{1,0:T(8,128)(2,1)}, u32[]{:S(2)}, u32[]{:S(2)}) collective-permute-start(bf16[256,1280]{1,0:T(8,128)(2,1)S(1)} %shard_map.66), channel_id=1, source_target_pairs={{2,0},{3,1},{0,2},{1,3},{6,4},{7,5},{4,6},{5,7},{10,8},{11,9},{8,1... | collective-permute-start | bytes 1966088 | tf_op jit(solution)/shard_map/ppermute | solution.py:278
  37.1 3.6 %collective-permute-start.8 = (bf16[2,96,128]{2,1,0:T(8,128)(2,1)S(1)}, bf16[2,96,128]{2,1,0:T(8,128)(2,1)S(1)}, u32[]{:S(2)}, u32[]{:S(2)}) collective-permute-start(bf16[2,96,128]{2,1,0:T(8,128)(2,1)S(1)} %get-tuple-element.60), channel_id=1, source_target_pairs={{0,5},{1,4},{2,7},{3,6},{4,1},{5,0},{6,3},{7,2},{8,13},{9,12},{10,... | collective-permute-start | bytes 147464 | tf_op jit(solution)/shard_map/ppermute | solution.py:273
  37.1 4.6 %collective-permute-start.9 = (bf16[2,96,128]{2,1,0:T(8,128)(2,1)S(1)}, bf16[2,96,128]{2,1,0:T(8,128)(2,1)S(1)}, u32[]{:S(2)}, u32[]{:S(2)}) collective-permute-start(bf16[2,96,128]{2,1,0:T(8,128)(2,1)S(1)} %get-tuple-element.61), channel_id=1, source_target_pairs={{0,4},{4,0},{8,12},{12,8},{16,20},{20,16},{24,28},{28,24},{1,5},{5... | collective-permute-start | bytes 147464 | tf_op jit(solution)/shard_map/ppermute | solution.py:262
  37.7 4.0 %collective-permute-start.10 = (bf16[2,96,128]{2,1,0:T(8,128)(2,1)S(1)}, bf16[2,96,128]{2,1,0:T(8,128)(2,1)S(1)}, u32[]{:S(2)}, u32[]{:S(2)}) collective-permute-start(bf16[2,96,128]{2,1,0:T(8,128)(2,1)S(1)} %get-tuple-element.62), channel_id=1, source_target_pairs={{0,1},{1,0},{2,3},{3,2},{4,5},{5,4},{6,7},{7,6},{8,9},{9,8},{10,11... | collective-permute-start | bytes 147464 | tf_op jit(solution)/shard_map/ppermute | solution.py:266
  42.9 11.4 %collective-permute-start.13 = (bf16[96,2048]{1,0:T(8,128)(2,1)}, bf16[96,2048]{1,0:T(8,128)(2,1)}, u32[]{:S(2)}, u32[]{:S(2)}) collective-permute-start(bf16[96,2048]{1,0:T(8,128)(2,1)} %get-tuple-element.71), channel_id=1, source_target_pairs={{2,0},{3,1},{0,2},{1,3},{6,4},{7,5},{4,6},{5,7},{10,8},{11,9},{8,1... | collective-permute-start | bytes 1179656 | tf_op jit(solution)/shard_map/ppermute | solution.py:278
  43.4 10.8 %collective-permute-start.14 = (bf16[256,1152]{1,0:T(8,128)(2,1)}, bf16[256,1152]{1,0:T(8,128)(2,1)}, u32[]{:S(2)}, u32[]{:S(2)}) collective-permute-start(bf16[256,1152]{1,0:T(8,128)(2,1)} %collective-permute-done.4.refs_0_), channel_id=1, source_target_pairs={{0,1},{1,0},{2,3},{3,2},{4,5},{5,4},{6,7},{7,6},{8,9},{9,8},{10,11... | collective-permute-start | bytes 1769480 | tf_op jit(solution)/shard_map/ppermute | solution.py:266
  43.4 10.8 %collective-permute-start.15 = (bf16[256,1152]{1,0:T(8,128)(2,1)}, bf16[256,1152]{1,0:T(8,128)(2,1)}, u32[]{:S(2)}, u32[]{:S(2)}) collective-permute-start(bf16[256,1152]{1,0:T(8,128)(2,1)} %collective-permute-done.12.refs_2_), channel_id=1, source_target_pairs={{0,1},{1,0},{2,3},{3,2},{4,5},{5,4},{6,7},{7,6},{8,9},{9,8},{10,11... | collective-permute-start | bytes 1769480 | tf_op jit(solution)/shard_map/ppermute | solution.py:266
  43.9 10.3 %collective-permute-start.16 = (bf16[256,1280]{1,0:T(8,128)(2,1)}, bf16[256,1280]{1,0:T(8,128)(2,1)}, u32[]{:S(2)}, u32[]{:S(2)}) collective-permute-start(bf16[256,1280]{1,0:T(8,128)(2,1)} %collective-permute-done.11.refs_4_), channel_id=1, source_target_pairs={{0,1},{1,0},{2,3},{3,2},{4,5},{5,4},{6,7},{7,6},{8,9},{9,8},{10,11... | collective-permute-start | bytes 1966088 | tf_op jit(solution)/shard_map/ppermute | solution.py:266

commit v6 on v5

--- a/solution.py
+++ b/solution.py
@@ -12,8 +12,8 @@
 REACH = 3
 NEG = -1e30
 FLAGS = 16
-SIDE = 1152
-COMMON = 1280
+SIDE = 1280
+COMMON = 1152
 STATE = HD + 8
 EXPONENT = math.log2(math.e) / math.sqrt(HD)
 BF16, F32 = jnp.bfloat16, jnp.float32
@@ -407,7 +407,7 @@
     pieces = [side_own, side_other, common]
     *ready, _ = lax.optimization_barrier((*pieces, own_a))
     far_weights = [each for piece, to in zip(pieces, ready) for each in (piece, swap_cores(to))]
-    near = call(near_kernel, shape((own_rows, model), F32), (own_a,) + near_weights, 300 * flops, vmem=16)
+    near = call(near_kernel, shape((own_rows, model), F32), (own_a,) + near_weights, 30 * flops, vmem=16)
     return call(
         last_kernel, shape((own_rows, model)), (tile, near, got, *far_weights), flops, vmem=20
     )

time: 58.4 us -> 54.5 us (0.933)
  waiting for transfers between devices: 21.6 us -> 17 us
  starting transfers between devices: 19 us -> 21 us
  Pallas kernels: 14.8 us -> 13.2 us
    ppermute x5, waiting for transfers between devices: 9.51 us -> 6.76 us  [swap_pairs(): return lax.ppermute(value, 'ctx', pairs)]
    ppermute x3, starting transfers between devices: 3.64 us -> 5.7 us  [from_chip(): lax.ppermute(value, 'head', [((i + 2 * steps) % count, i) for i in range(...]
    ppermute x3, waiting for transfers between devices: 9.36 us -> 7.46 us  [from_chip(): lax.ppermute(value, 'head', [((i + 2 * steps) % count, i) for i in range(...]
    pallas_call x10, Pallas kernels: 14.8 us -> 13.2 us  [call(): pl.pallas_call(kernel, out_shape=outs, in_specs=[SMEM if s else HBM if i...]
  transfers between devices with their start and end apart: 17 -> 17, of which waited for: 5 -> 5; matrix products, arithmetic and copies ran while one was open for 0% -> 0% of each run, Pallas kernels for 11% -> 15%
where the time goes in v6:
time: 54.5 us; the launch traced here: 54 us
  starting transfers between devices  21 us (39%)
  waiting for transfers between devices  17 us (31%)
  Pallas kernels  13.2 us (24%)
  local copies, waits for them, and re-layouts  1.86 us (3%)
  between operations  0.94 us (2%)
    pallas_call x10, Pallas kernels, call(): pl.pallas_call(kernel, out_shape=outs, in_specs=[SMEM if s else HBM if i...  13.2 us
    ppermute x5, starting transfers between devices, swap_pairs(): return lax.ppermute(value, 'ctx', pairs)  10.4 us
    ppermute x3, waiting for transfers between devices, from_chip(): lax.ppermute(value, 'head', [((i + 2 * steps) % count, i) for i in range(...  7.46 us
    ppermute x5, waiting for transfers between devices, swap_pairs(): return lax.ppermute(value, 'ctx', pairs)  6.76 us
    ppermute x3, starting transfers between devices, from_chip(): lax.ppermute(value, 'head', [((i + 2 * steps) % count, i) for i in range(...  5.7 us
    ppermute x3, starting transfers between devices, swap_tiles(): lax.ppermute(value, 'ctx', [(i, i ^ 1) for i in range(lax.axis_size('ctx'...  2.59 us
    ppermute x5, starting transfers between devices, swap_cores(): lax.ppermute(value, 'head', [(i, i ^ 1) for i in range(lax.axis_size('hea...  2.31 us
    unnamed x6, local copies, waits for them, and re-layouts  1.86 us
  transfers between devices with their start and end apart: 17, of which 5 were waited for; matrix products, arithmetic and copies ran while one was open for 0% of the time, Pallas kernels for 15%

profile of v6, /device:TPU:0, one launch (start us, length us, event | category | flops | bytes accessed | tf_op | source)
XLA Modules:
  0.0 54.0 jit_solution(8195434459627573202)
XLA Ops:
  0.0 0.0 copy-start
  0.8 3.1 %shard_map.64 = (bf16[400,128]{1,0:T(8,128)(2,1)}, bf16[768,128]{1,0:T(8,128)(2,1)}, bf16[1168,128]{1,0:T(8,128)(2,1)}, bf16[256,1280]{1,0:T(8,128)(2,1)}) custom-call(s32[1]{0:T(128)} %bitcast.tile_ref, s32[1]{0:T(128)} %bitcast.1._.head_ref, s32[1,7]{1,0:T(1,128)} %list_ref.1, s32[1,1]{1,0:T(1,128)} %bitcast.3.count_ref, bf16[384,256]{1,0:T(8,128)(2,1)} %q_ref.1, ...), custom_call_target="tpu_custom_call" | custom-call | bytes 1048576 | tf_op jit(solution)/shard_map/pallas_call | solution.py:30
  4.0 0.0 copy-done
  4.0 0.5 collective-permute-start.1
  4.5 2.6 %collective-permute-start.4 = (bf16[256,1280]{1,0:T(8,128)(2,1)}, bf16[256,1280]{1,0:T(8,128)(2,1)S(1)}, u32[]{:S(2)}, u32[]{:S(2)}) collective-permute-start(bf16[256,1280]{1,0:T(8,128)(2,1)} %get-tuple-element.53), channel_id=1, source_target_pairs={{2,0},{3,1},{0,2},{1,3},{6,4},{7,5},{4,6},{5,7},{10,8},{11,9},{8,1... | collective-permute-start | bytes 1966088 | tf_op jit(solution)/shard_map/ppermute | solution.py:278
  7.0 1.5 %collective-permute-start = (bf16[1168,128]{1,0:T(8,128)(2,1)}, bf16[1168,128]{1,0:T(8,128)(2,1)S(1)}, u32[]{:S(2)}, u32[]{:S(2)}) collective-permute-start(bf16[1168,128]{1,0:T(8,128)(2,1)} %get-tuple-element.41), channel_id=1, source_target_pairs={{0,4},{4,0},{8,12},{12,8},{16,20},{20,16},{24,28},{28,24},{1,5},{5... | collective-permute-start | bytes 897032 | tf_op jit(solution)/shard_map/ppermute | solution.py:262
  8.6 0.7 %collective-permute-start.3 = (bf16[768,128]{1,0:T(8,128)(2,1)}, bf16[768,128]{1,0:T(8,128)(2,1)S(1)}, u32[]{:S(2)}, u32[]{:S(2)}) collective-permute-start(bf16[768,128]{1,0:T(8,128)(2,1)} %get-tuple-element.42.keep_kv_ref), channel_id=1, source_target_pairs={{8,16},{16,8},{12,20},{20,12},{9,17},{17,9},{13,21},{21,13},{10,18... | collective-permute-start | bytes 589832 | tf_op jit(solution)/shard_map/ppermute | solution.py:258
  9.2 4.5 %collective-permute-start.2 = (bf16[768,128]{1,0:T(8,128)(2,1)}, bf16[768,128]{1,0:T(8,128)(2,1)S(1)}, u32[]{:S(2)}, u32[]{:S(2)}) collective-permute-start(bf16[768,128]{1,0:T(8,128)(2,1)} %get-tuple-element.42.keep_kv_ref), channel_id=1, source_target_pairs={{0,8},{8,0},{4,12},{12,4},{16,24},{24,16},{20,28},{28,20},{1,9},{9... | collective-permute-start | bytes 589832 | tf_op jit(solution)/shard_map/ppermute | solution.py:258
  13.7 0.0 copy-start.1
  13.7 1.0 %copy-done.1 = bf16[768,128]{1,0:T(8,128)(2,1)S(1)} copy-done((bf16[768,128]{1,0:T(8,128)(2,1)S(1)}, bf16[768,128]{1,0:T(8,128)(2,1)}, u32[]{:S(2)}) %copy-start.1) | copy-done | bytes 196632
  14.7 0.0 copy-start.2
  14.7 0.9 %copy-done.2 = bf16[400,128]{1,0:T(8,128)(2,1)S(1)} copy-done((bf16[400,128]{1,0:T(8,128)(2,1)S(1)}, bf16[400,128]{1,0:T(8,128)(2,1)}, u32[]{:S(2)}) %copy-start.2) | copy-done | bytes 102424
  15.6 0.0 collective-permute-done.3.kept_second_ref
  15.6 2.9 %collective-permute-done.2.kept_first_ref = bf16[768,128]{1,0:T(8,128)(2,1)S(1)} collective-permute-done((bf16[768,128]{1,0:T(8,128)(2,1)}, bf16[768,128]{1,0:T(8,128)(2,1)S(1)}, u32[]{:S(2)}, u32[]{:S(2)}) %collective-permute-start.2) | collective-permute-done | bytes 196640 | tf_op jit(solution)/shard_map/ppermute | solution.py:258
  18.6 0.0 collective-permute-done.came_ref
  18.6 0.0 collective-permute-done.1.wp_ref
  18.6 0.7 %collective-permute-start.6 = (bf16[768,128]{1,0:T(8,128)(2,1)S(1)}, bf16[768,128]{1,0:T(8,128)(2,1)S(1)}, u32[]{:S(2)}, u32[]{:S(2)}) collective-permute-start(bf16[768,128]{1,0:T(8,128)(2,1)S(1)} %get-tuple-element.55.came_ref), channel_id=1, source_target_pairs={{8,16},{16,8},{12,20},{20,12},{9,17},{17,9},{13,21},{21,13},{10,18... | collective-permute-start | bytes 589832 | tf_op jit(solution)/shard_map/ppermute | solution.py:258
  19.3 3.5 %collective-permute-start.5 = (bf16[768,128]{1,0:T(8,128)(2,1)S(1)}, bf16[768,128]{1,0:T(8,128)(2,1)S(1)}, u32[]{:S(2)}, u32[]{:S(2)}) collective-permute-start(bf16[768,128]{1,0:T(8,128)(2,1)S(1)} %get-tuple-element.55.came_ref), channel_id=1, source_target_pairs={{0,8},{8,0},{4,12},{12,4},{16,24},{24,16},{20,28},{28,20},{1,9},{9... | collective-permute-start | bytes 589832 | tf_op jit(solution)/shard_map/ppermute | solution.py:258
  22.8 1.1 %collective-permute-start.7 = (bf16[768,128]{1,0:T(8,128)(2,1)S(1)}, bf16[768,128]{1,0:T(8,128)(2,1)S(1)}, u32[]{:S(2)}, u32[]{:S(2)}) collective-permute-start(bf16[768,128]{1,0:T(8,128)(2,1)S(1)} %get-tuple-element.58), channel_id=1, source_target_pairs={{0,16},{16,0},{4,20},{20,4},{8,24},{24,8},{12,28},{28,12},{1,17},{... | collective-permute-start | bytes 589832 | tf_op jit(solution)/shard_map/ppermute | solution.py:258
  23.9 0.0 collective-permute-done.4.refs_0_
  23.9 0.5 collective-permute-start.12
  24.4 1.5 %collective-permute-start.11 = (bf16[256,1152]{1,0:T(8,128)(2,1)S(1)}, bf16[256,1152]{1,0:T(8,128)(2,1)S(1)}, u32[]{:S(2)}, u32[]{:S(2)}) collective-permute-start(bf16[256,1152]{1,0:T(8,128)(2,1)S(1)} %shard_map.66), channel_id=1, source_target_pairs={{2,0},{3,1},{0,2},{1,3},{6,4},{7,5},{4,6},{5,7},{10,8},{11,9},{8,1... | collective-permute-start | bytes 1769480 | tf_op jit(solution)/shard_map/ppermute | solution.py:278
  25.9 4.1 %shard_map.68._ = f32[2,136,384]{2,1,0:T(8,128)S(1)} custom-call(s32[8,128]{1,0:T(8,128)S(1)} %get-tuple-element.51.flag_ref, s32[1]{0:T(128)} %bitcast.tile_ref, bf16[2,384,128]{2,1,0:T(8,128)(2,1)S(1)} %get-tuple-element.54.q_ref, bf16[768,128]{1,0:T(8,128)(2,1)S(1)} %get-tuple-element.49.keep_kv_ref.own_ref, ...), custom_call_target="tpu_custom_call" | custom-call | flops 603979776 | bytes 1048576 | tf_op jit(solution)/shard_map/pallas_call | solution.py:30
  30.0 0.0 collective-permute-done.6.second_ref
  30.0 0.0 collective-permute-done.5.first_ref
  30.0 1.8 %shard_map.69.state_ref = f32[2,136,384]{2,1,0:T(8,128)S(1)} custom-call(s32[8,128]{1,0:T(8,128)S(1)} %get-tuple-element.51.flag_ref, s32[1]{0:T(128)} %bitcast.tile_ref, bf16[2,384,128]{2,1,0:T(8,128)(2,1)S(1)} %get-tuple-element.54.q_ref, bf16[768,128]{1,0:T(8,128)(2,1)S(1)} %collective-permute-done.5.first_ref, ...), custom_call_target="tpu_custom_call", output_to_operand_aliasing={{}: (5, {})} | custom-call | flops 301989888 | bytes 1048576 | tf_op jit(solution)/shard_map/pallas_call | solution.py:30
  31.8 3.8 %collective-permute-done.7.refs_0_ = bf16[768,128]{1,0:T(8,128)(2,1)S(1)} collective-permute-done((bf16[768,128]{1,0:T(8,128)(2,1)S(1)}, bf16[768,128]{1,0:T(8,128)(2,1)S(1)}, u32[]{:S(2)}, u32[]{:S(2)}) %collective-permute-start.7) | collective-permute-done | bytes 196640 | tf_op jit(solution)/shard_map/ppermute | solution.py:258
  35.6 0.8 %shard_map.70 = (bf16[2,96,128]{2,1,0:T(8,128)(2,1)S(1)}, bf16[2,96,128]{2,1,0:T(8,128)(2,1)S(1)}, bf16[2,96,128]{2,1,0:T(8,128)(2,1)S(1)}, bf16[2,96,128]{2,1,0:T(8,128)(2,1)S(1)}) custom-call(s32[8,128]{1,0:T(8,128)S(1)} %get-tuple-element.51.flag_ref, s32[1]{0:T(128)} %bitcast.tile_ref, s32[1]{0:T(128)} %bitcast.1._.head_ref, ...), custom_call_target="tpu_custom_call" | custom-call | flops 5662310400 | bytes 1048576 | tf_op jit(solution)/shard_map/pallas_call | solution.py:30
  36.4 0.1 collective-permute-start.8
  36.5 0.6 %collective-permute-start.9 = (bf16[2,96,128]{2,1,0:T(8,128)(2,1)S(1)}, bf16[2,96,128]{2,1,0:T(8,128)(2,1)S(1)}, u32[]{:S(2)}, u32[]{:S(2)}) collective-permute-start(bf16[2,96,128]{2,1,0:T(8,128)(2,1)S(1)} %get-tuple-element.61), channel_id=1, source_target_pairs={{0,4},{4,0},{8,12},{12,8},{16,20},{20,16},{24,28},{28,24},{1,5},{5... | collective-permute-start | bytes 147464 | tf_op jit(solution)/shard_map/ppermute | solution.py:262
  37.1 1.3 %collective-permute-start.10 = (bf16[2,96,128]{2,1,0:T(8,128)(2,1)S(1)}, bf16[2,96,128]{2,1,0:T(8,128)(2,1)S(1)}, u32[]{:S(2)}, u32[]{:S(2)}) collective-permute-start(bf16[2,96,128]{2,1,0:T(8,128)(2,1)S(1)} %get-tuple-element.62), channel_id=1, source_target_pairs={{0,1},{1,0},{2,3},{3,2},{4,5},{5,4},{6,7},{7,6},{8,9},{9,8},{10,11... | collective-permute-start | bytes 147464 | tf_op jit(solution)/shard_map/ppermute | solution.py:266
  38.3 1.8 %collective-permute-done.8.cross_ref = bf16[2,96,128]{2,1,0:T(8,128)(2,1)S(1)} collective-permute-done((bf16[2,96,128]{2,1,0:T(8,128)(2,1)S(1)}, bf16[2,96,128]{2,1,0:T(8,128)(2,1)S(1)}, u32[]{:S(2)}, u32[]{:S(2)}) %collective-permute-start.8) | collective-permute-done | bytes 49184 | tf_op jit(solution)/shard_map/ppermute | solution.py:273
  40.1 1.0 %collective-permute-done.9.y_ref = bf16[2,96,128]{2,1,0:T(8,128)(2,1)S(1)} collective-permute-done((bf16[2,96,128]{2,1,0:T(8,128)(2,1)S(1)}, bf16[2,96,128]{2,1,0:T(8,128)(2,1)S(1)}, u32[]{:S(2)}, u32[]{:S(2)}) %collective-permute-start.9) | collective-permute-done | bytes 49184 | tf_op jit(solution)/shard_map/ppermute | solution.py:262
  41.1 0.0 collective-permute-done.10.core_ref
  41.1 0.0 collective-permute-done.11.refs_4_
  41.1 0.0 collective-permute-done.12.refs_2_
  41.1 0.4 shard_map.71
  41.5 1.7 %collective-permute-start.13 = (bf16[96,1920]{1,0:T(8,128)(2,1)S(1)}, bf16[96,1920]{1,0:T(8,128)(2,1)S(1)}, u32[]{:S(2)}, u32[]{:S(2)}) collective-permute-start(bf16[96,1920]{1,0:T(8,128)(2,1)S(1)} %get-tuple-element.71), channel_id=1, source_target_pairs={{2,0},{3,1},{0,2},{1,3},{6,4},{7,5},{4,6},{5,7},{10,8},{11,9},{8,1... | collective-permute-start | bytes 1105928 | tf_op jit(solution)/shard_map/ppermute | solution.py:278
  43.2 0.0 collective-permute-start.16
  43.2 0.5 collective-permute-start.14
  43.7 0.0 collective-permute-start.15
  43.7 1.0 %shard_map.72.near_ref = f32[96,5120]{1,0:T(8,128)S(1)} custom-call(bf16[96,512]{1,0:T(8,128)(2,1)S(1)} %get-tuple-element.70.a_ref, bf16[256,5120]{1,0:T(8,128)(2,1)S(1)} %copy-done, bf16[256,5120]{1,0:T(8,128)(2,1)S(1)} %collective-permute-done.1.wp_ref), custom_call_target="tpu_custom_call" | custom-call | flops 15099494400 | bytes 1048576 | tf_op jit(solution)/shard_map/pallas_call | solution.py:30
  44.8 7.5 %collective-permute-done.13.far_ref = bf16[96,1920]{1,0:T(8,128)(2,1)S(1)} collective-permute-done((bf16[96,1920]{1,0:T(8,128)(2,1)S(1)}, bf16[96,1920]{1,0:T(8,128)(2,1)S(1)}, u32[]{:S(2)}, u32[]{:S(2)}) %collective-permute-start.13) | collective-permute-done | bytes 368672 | tf_op jit(solution)/shard_map/ppermute | solution.py:278
  52.2 0.0 collective-permute-done.16.refs_5_
  52.2 0.0 collective-permute-done.14.refs_1_
  52.2 0.0 collective-permute-done.15.refs_3_
  52.2 1.8 %shard_map.73 = bf16[96,5120]{1,0:T(8,128)(2,1)} custom-call(s32[1]{0:T(128)} %bitcast.tile_ref, f32[96,5120]{1,0:T(8,128)S(1)} %shard_map.72.near_ref, bf16[96,1920]{1,0:T(8,128)(2,1)S(1)} %collective-permute-done.13.far_ref, bf16[256,1280]{1,0:T(8,128)(2,1)S(1)} %collective-permute-done.4.refs_0_, bf16[256,1280]{1,0:T(8,128)(2,1)S(1)} %collective-permute-done.14.refs_1_, ...), custom_call_target="tpu_custom_call" | custom-call | flops 503316480 | bytes 1048576 | tf_op jit(solution)/shard_map/pallas_call | solution.py:30
  (3 shorter events, 0.1 us)
Async XLA Ops:
  0.0 4.0 %copy-start = (bf16[256,5120]{1,0:T(8,128)(2,1)S(1)}, bf16[256,5120]{1,0:T(8,128)(2,1)}, u32[]{:S(2)}) copy-start(bf16[256,5120]{1,0:T(8,128)(2,1)} %w_ref.6) | copy-start | bytes 7864324
  4.0 14.6 %collective-permute-start.1 = (bf16[256,5120]{1,0:T(8,128)(2,1)S(1)}, bf16[256,5120]{1,0:T(8,128)(2,1)S(1)}, u32[]{:S(2)}, u32[]{:S(2)}) collective-permute-start(bf16[256,5120]{1,0:T(8,128)(2,1)S(1)} %copy-done), channel_id=1, source_target_pairs={{0,1},{1,0},{2,3},{3,2},{4,5},{5,4},{6,7},{7,6},{8,9},{9,8},{10,11... | collective-permute-start | bytes 7864328 | tf_op jit(solution)/shard_map/ppermute | solution.py:266
  4.5 19.4 %collective-permute-start.4 = (bf16[256,1280]{1,0:T(8,128)(2,1)}, bf16[256,1280]{1,0:T(8,128)(2,1)S(1)}, u32[]{:S(2)}, u32[]{:S(2)}) collective-permute-start(bf16[256,1280]{1,0:T(8,128)(2,1)} %get-tuple-element.53), channel_id=1, source_target_pairs={{2,0},{3,1},{0,2},{1,3},{6,4},{7,5},{4,6},{5,7},{10,8},{11,9},{8,1... | collective-permute-start | bytes 1966088 | tf_op jit(solution)/shard_map/ppermute | solution.py:278
  7.0 11.5 %collective-permute-start = (bf16[1168,128]{1,0:T(8,128)(2,1)}, bf16[1168,128]{1,0:T(8,128)(2,1)S(1)}, u32[]{:S(2)}, u32[]{:S(2)}) collective-permute-start(bf16[1168,128]{1,0:T(8,128)(2,1)} %get-tuple-element.41), channel_id=1, source_target_pairs={{0,4},{4,0},{8,12},{12,8},{16,20},{20,16},{24,28},{28,24},{1,5},{5... | collective-permute-start | bytes 897032 | tf_op jit(solution)/shard_map/ppermute | solution.py:262
  8.6 7.1 %collective-permute-start.3 = (bf16[768,128]{1,0:T(8,128)(2,1)}, bf16[768,128]{1,0:T(8,128)(2,1)S(1)}, u32[]{:S(2)}, u32[]{:S(2)}) collective-permute-start(bf16[768,128]{1,0:T(8,128)(2,1)} %get-tuple-element.42.keep_kv_ref), channel_id=1, source_target_pairs={{8,16},{16,8},{12,20},{20,12},{9,17},{17,9},{13,21},{21,13},{10,18... | collective-permute-start | bytes 589832 | tf_op jit(solution)/shard_map/ppermute | solution.py:258
  9.2 9.3 %collective-permute-start.2 = (bf16[768,128]{1,0:T(8,128)(2,1)}, bf16[768,128]{1,0:T(8,128)(2,1)S(1)}, u32[]{:S(2)}, u32[]{:S(2)}) collective-permute-start(bf16[768,128]{1,0:T(8,128)(2,1)} %get-tuple-element.42.keep_kv_ref), channel_id=1, source_target_pairs={{0,8},{8,0},{4,12},{12,4},{16,24},{24,16},{20,28},{28,20},{1,9},{9... | collective-permute-start | bytes 589832 | tf_op jit(solution)/shard_map/ppermute | solution.py:258
  13.7 1.0 %copy-start.1 = (bf16[768,128]{1,0:T(8,128)(2,1)S(1)}, bf16[768,128]{1,0:T(8,128)(2,1)}, u32[]{:S(2)}) copy-start(bf16[768,128]{1,0:T(8,128)(2,1)} %get-tuple-element.42.keep_kv_ref) | copy-start | bytes 589828
  14.7 0.9 %copy-start.2 = (bf16[400,128]{1,0:T(8,128)(2,1)S(1)}, bf16[400,128]{1,0:T(8,128)(2,1)}, u32[]{:S(2)}) copy-start(bf16[400,128]{1,0:T(8,128)(2,1)} %get-tuple-element.44.keep_q_ref) | copy-start | bytes 307204
  18.6 11.4 %collective-permute-start.6 = (bf16[768,128]{1,0:T(8,128)(2,1)S(1)}, bf16[768,128]{1,0:T(8,128)(2,1)S(1)}, u32[]{:S(2)}, u32[]{:S(2)}) collective-permute-start(bf16[768,128]{1,0:T(8,128)(2,1)S(1)} %get-tuple-element.55.came_ref), channel_id=1, source_target_pairs={{8,16},{16,8},{12,20},{20,12},{9,17},{17,9},{13,21},{21,13},{10,18... | collective-permute-start | bytes 589832 | tf_op jit(solution)/shard_map/ppermute | solution.py:258
  19.3 10.7 %collective-permute-start.5 = (bf16[768,128]{1,0:T(8,128)(2,1)S(1)}, bf16[768,128]{1,0:T(8,128)(2,1)S(1)}, u32[]{:S(2)}, u32[]{:S(2)}) collective-permute-start(bf16[768,128]{1,0:T(8,128)(2,1)S(1)} %get-tuple-element.55.came_ref), channel_id=1, source_target_pairs={{0,8},{8,0},{4,12},{12,4},{16,24},{24,16},{20,28},{28,20},{1,9},{9... | collective-permute-start | bytes 589832 | tf_op jit(solution)/shard_map/ppermute | solution.py:258
  22.8 12.8 %collective-permute-start.7 = (bf16[768,128]{1,0:T(8,128)(2,1)S(1)}, bf16[768,128]{1,0:T(8,128)(2,1)S(1)}, u32[]{:S(2)}, u32[]{:S(2)}) collective-permute-start(bf16[768,128]{1,0:T(8,128)(2,1)S(1)} %get-tuple-element.58), channel_id=1, source_target_pairs={{0,16},{16,0},{4,20},{20,4},{8,24},{24,8},{12,28},{28,12},{1,17},{... | collective-permute-start | bytes 589832 | tf_op jit(solution)/shard_map/ppermute | solution.py:258
  23.9 17.2 %collective-permute-start.12 = (bf16[256,1280]{1,0:T(8,128)(2,1)S(1)}, bf16[256,1280]{1,0:T(8,128)(2,1)S(1)}, u32[]{:S(2)}, u32[]{:S(2)}) collective-permute-start(bf16[256,1280]{1,0:T(8,128)(2,1)S(1)} %collective-permute-done.4.refs_0_), channel_id=1, source_target_pairs={{0,4},{4,0},{8,12},{12,8},{16,20},{20,16},{24,28},{28,24},{1,5},{5... | collective-permute-start | bytes 1966088 | tf_op jit(solution)/shard_map/ppermute | solution.py:262
  24.4 16.7 %collective-permute-start.11 = (bf16[256,1152]{1,0:T(8,128)(2,1)S(1)}, bf16[256,1152]{1,0:T(8,128)(2,1)S(1)}, u32[]{:S(2)}, u32[]{:S(2)}) collective-permute-start(bf16[256,1152]{1,0:T(8,128)(2,1)S(1)} %shard_map.66), channel_id=1, source_target_pairs={{2,0},{3,1},{0,2},{1,3},{6,4},{7,5},{4,6},{5,7},{10,8},{11,9},{8,1... | collective-permute-start | bytes 1769480 | tf_op jit(solution)/shard_map/ppermute | solution.py:278
  36.4 3.7 %collective-permute-start.8 = (bf16[2,96,128]{2,1,0:T(8,128)(2,1)S(1)}, bf16[2,96,128]{2,1,0:T(8,128)(2,1)S(1)}, u32[]{:S(2)}, u32[]{:S(2)}) collective-permute-start(bf16[2,96,128]{2,1,0:T(8,128)(2,1)S(1)} %get-tuple-element.60), channel_id=1, source_target_pairs={{0,5},{1,4},{2,7},{3,6},{4,1},{5,0},{6,3},{7,2},{8,13},{9,12},{10,... | collective-permute-start | bytes 147464 | tf_op jit(solution)/shard_map/ppermute | solution.py:273
  36.5 4.6 %collective-permute-start.9 = (bf16[2,96,128]{2,1,0:T(8,128)(2,1)S(1)}, bf16[2,96,128]{2,1,0:T(8,128)(2,1)S(1)}, u32[]{:S(2)}, u32[]{:S(2)}) collective-permute-start(bf16[2,96,128]{2,1,0:T(8,128)(2,1)S(1)} %get-tuple-element.61), channel_id=1, source_target_pairs={{0,4},{4,0},{8,12},{12,8},{16,20},{20,16},{24,28},{28,24},{1,5},{5... | collective-permute-start | bytes 147464 | tf_op jit(solution)/shard_map/ppermute | solution.py:262
  37.1 4.1 %collective-permute-start.10 = (bf16[2,96,128]{2,1,0:T(8,128)(2,1)S(1)}, bf16[2,96,128]{2,1,0:T(8,128)(2,1)S(1)}, u32[]{:S(2)}, u32[]{:S(2)}) collective-permute-start(bf16[2,96,128]{2,1,0:T(8,128)(2,1)S(1)} %get-tuple-element.62), channel_id=1, source_target_pairs={{0,1},{1,0},{2,3},{3,2},{4,5},{5,4},{6,7},{7,6},{8,9},{9,8},{10,11... | collective-permute-start | bytes 147464 | tf_op jit(solution)/shard_map/ppermute | solution.py:266
  41.5 10.7 %collective-permute-start.13 = (bf16[96,1920]{1,0:T(8,128)(2,1)S(1)}, bf16[96,1920]{1,0:T(8,128)(2,1)S(1)}, u32[]{:S(2)}, u32[]{:S(2)}) collective-permute-start(bf16[96,1920]{1,0:T(8,128)(2,1)S(1)} %get-tuple-element.71), channel_id=1, source_target_pairs={{2,0},{3,1},{0,2},{1,3},{6,4},{7,5},{4,6},{5,7},{10,8},{11,9},{8,1... | collective-permute-start | bytes 1105928 | tf_op jit(solution)/shard_map/ppermute | solution.py:278
  43.2 9.0 %collective-permute-start.16 = (bf16[256,1152]{1,0:T(8,128)(2,1)S(1)}, bf16[256,1152]{1,0:T(8,128)(2,1)S(1)}, u32[]{:S(2)}, u32[]{:S(2)}) collective-permute-start(bf16[256,1152]{1,0:T(8,128)(2,1)S(1)} %collective-permute-done.11.refs_4_), channel_id=1, source_target_pairs={{0,1},{1,0},{2,3},{3,2},{4,5},{5,4},{6,7},{7,6},{8,9},{9,8},{10,11... | collective-permute-start | bytes 1769480 | tf_op jit(solution)/shard_map/ppermute | solution.py:266
  43.2 9.0 %collective-permute-start.14 = (bf16[256,1280]{1,0:T(8,128)(2,1)S(1)}, bf16[256,1280]{1,0:T(8,128)(2,1)S(1)}, u32[]{:S(2)}, u32[]{:S(2)}) collective-permute-start(bf16[256,1280]{1,0:T(8,128)(2,1)S(1)} %collective-permute-done.4.refs_0_), channel_id=1, source_target_pairs={{0,1},{1,0},{2,3},{3,2},{4,5},{5,4},{6,7},{7,6},{8,9},{9,8},{10,11... | collective-permute-start | bytes 1966088 | tf_op jit(solution)/shard_map/ppermute | solution.py:266
  43.7 8.5 %collective-permute-start.15 = (bf16[256,1280]{1,0:T(8,128)(2,1)S(1)}, bf16[256,1280]{1,0:T(8,128)(2,1)S(1)}, u32[]{:S(2)}, u32[]{:S(2)}) collective-permute-start(bf16[256,1280]{1,0:T(8,128)(2,1)S(1)} %collective-permute-done.12.refs_2_), channel_id=1, source_target_pairs={{0,1},{1,0},{2,3},{3,2},{4,5},{5,4},{6,7},{7,6},{8,9},{9,8},{10,11... | collective-permute-start | bytes 1966088 | tf_op jit(solution)/shard_map/ppermute | solution.py:266

commit v7 on v5

--- a/solution.py
+++ b/solution.py
@@ -170,7 +170,6 @@
 
 def third_kernel(flag_ref, tile_ref, head_ref, q_ref, state_ref, *refs, far):
     outs, last = refs[far:-1], refs[-1]
-    last[...] = state_ref[...]
     for i in range(far):
         above = ((tile_ref[0] & 4) == 0) == (i == 0)
         which = (jnp.where(above, 1, 0), jnp.where(above, 4, -3), refs[i])
@@ -232,21 +231,36 @@
 
 
 def last_kernel(tile_ref, near_ref, far_ref, *refs):
-    weights, out_ref = refs[:-1], refs[-1]
+    weights, (out_ref, done_ref, sems) = refs[:6], refs[6:]
     parity = tile_ref[0] & 1
     deep = 2 * weights[0].shape[0]
+    side = weights[0].shape[1]
     far = far_ref[:, 0:deep]
-    side = weights[0].shape[1]
-    for i, first in enumerate((parity * side, (1 - parity) * side, 2 * side)):
-        pair = weights[2 * i : 2 * i + 2]
-        for start in range(0, pair[0].shape[1], CHUNK):
-            stop = min(start + CHUNK, pair[0].shape[1])
+    gathered = 2 * side + weights[4].shape[1]
+    copies = []
+
+    def write(columns):
+        copies.append(
+            pltpu.make_async_copy(
+                done_ref.at[:, columns], out_ref.at[:, columns], sems.at[len(copies)]
+            )
+        )
+        copies[-1].start()
+
+    done_ref[:, gathered:] = (near_ref[:, gathered:] + far_ref[:, deep:].astype(F32)).astype(BF16)
+    write(pl.ds(gathered, near_ref.shape[1] - gathered))
+    for i, first in enumerate((2 * side, parity * side, (1 - parity) * side)):
+        pair = weights[4:6] if i == 0 else weights[2 * i - 2 : 2 * i]
+        width = pair[0].shape[1]
+        for start in range(0, width, CHUNK):
+            stop = min(start + CHUNK, width)
             columns = pl.ds(pl.multiple_of(first + start, HD), stop - start)
-            out_ref[:, columns] = (
+            done_ref[:, columns] = (
                 near_ref[:, columns] + multiply(far, pair, start, stop)
             ).astype(BF16)
-    gathered = 2 * side + weights[4].shape[1]
-    out_ref[:, gathered:] = (near_ref[:, gathered:] + far_ref[:, deep:].astype(F32)).astype(BF16)
+        write(pl.ds(pl.multiple_of(first, HD), width))
+    for each in copies:
+        each.wait()
 
 
 def swap_pairs(value, distance, phase):
@@ -370,12 +384,12 @@
     block = (2, own_rows, HD)
     attended = call(
         functools.partial(third_kernel, far=far),
-        (shape(block),) * 4 if small else (shape(one),) * 2,
+        ((shape(block),) * 4 if small else (shape(one),) * 2) + (state,),
         (flags, tile, head, q_pair, held, *farther),
         300 * area * HD,
         0,
-        scratch=(pltpu.VMEM(state.shape, F32),),
-    )
+        alias={4: 4 if small else 2},
+    )[:-1]
     if not small:
         mine, theirs = attended
         got = swap_tiles(theirs)
@@ -407,9 +421,15 @@
     pieces = [side_own, side_other, common]
     *ready, _ = lax.optimization_barrier((*pieces, own_a))
     far_weights = [each for piece, to in zip(pieces, ready) for each in (piece, swap_cores(to))]
-    near = call(near_kernel, shape((own_rows, model), F32), (own_a,) + near_weights, 300 * flops, vmem=16)
+    near = call(near_kernel, shape((own_rows, model), F32), (own_a,) + near_weights, 30 * flops, vmem=16)
     return call(
-        last_kernel, shape((own_rows, model)), (tile, near, got, *far_weights), flops, vmem=20
+        last_kernel,
+        shape((own_rows, model)),
+        (tile, near, got, *far_weights),
+        flops,
+        scratch=(pltpu.VMEM((own_rows, model), BF16), pltpu.SemaphoreType.DMA((4,))),
+        out_hbm=True,
+        vmem=20,
     )
 
 

time: 58.4 us -> 54.6 us (0.935)
  Pallas kernels: 14.8 us -> 12.2 us
  waiting for transfers between devices: 21.6 us -> 20 us
    pallas_call x10, Pallas kernels: 14.8 us -> 12.2 us  [call(): pl.pallas_call(kernel, out_shape=outs, in_specs=[SMEM if s else HBM if i...]
    ppermute x5, waiting for transfers between devices: 9.51 us -> 8.25 us  [swap_pairs(): return lax.ppermute(value, 'ctx', pairs)]
  transfers between devices with their start and end apart: 17 -> 17, of which waited for: 5 -> 5; matrix products, arithmetic and copies ran while one was open for 0% -> 0% of each run, Pallas kernels for 11% -> 13%
where the time goes in v7:
time: 54.6 us; the launch traced here: 54.1 us
  waiting for transfers between devices  20 us (37%)
  starting transfers between devices  19 us (35%)
  Pallas kernels  12.2 us (22%)
  local copies, waits for them, and re-layouts  1.86 us (3%)
  between operations  0.94 us (2%)
    pallas_call x10, Pallas kernels, call(): pl.pallas_call(kernel, out_shape=outs, in_specs=[SMEM if s else HBM if i...  12.2 us
    ppermute x5, starting transfers between devices, swap_pairs(): return lax.ppermute(value, 'ctx', pairs)  10.4 us
    ppermute x3, waiting for transfers between devices, from_chip(): lax.ppermute(value, 'head', [((i + 2 * steps) % count, i) for i in range(...  9.04 us
    ppermute x5, waiting for transfers between devices, swap_pairs(): return lax.ppermute(value, 'ctx', pairs)  8.25 us
    ppermute x3, starting transfers between devices, from_chip(): lax.ppermute(value, 'head', [((i + 2 * steps) % count, i) for i in range(...  3.7 us
    ppermute x3, starting transfers between devices, swap_tiles(): lax.ppermute(value, 'ctx', [(i, i ^ 1) for i in range(lax.axis_size('ctx'...  2.59 us
    ppermute x5, starting transfers between devices, swap_cores(): lax.ppermute(value, 'head', [(i, i ^ 1) for i in range(lax.axis_size('hea...  2.31 us
    unnamed x6, local copies, waits for them, and re-layouts  1.86 us
  transfers between devices with their start and end apart: 17, of which 5 were waited for; matrix products, arithmetic and copies ran while one was open for 0% of the time, Pallas kernels for 13%

profile of v7, /device:TPU:0, one launch (start us, length us, event | category | flops | bytes accessed | tf_op | source)
XLA Modules:
  0.0 54.1 jit_solution(12580159287637043585)
XLA Ops:
  0.0 0.0 copy-start
  0.8 3.1 %shard_map.64 = (bf16[400,128]{1,0:T(8,128)(2,1)}, bf16[768,128]{1,0:T(8,128)(2,1)}, bf16[1168,128]{1,0:T(8,128)(2,1)}, bf16[256,1152]{1,0:T(8,128)(2,1)}) custom-call(s32[1]{0:T(128)} %bitcast.tile_ref, s32[1]{0:T(128)} %bitcast.1._.head_ref, s32[1,7]{1,0:T(1,128)} %list_ref.1, s32[1,1]{1,0:T(1,128)} %bitcast.3.count_ref, bf16[384,256]{1,0:T(8,128)(2,1)} %q_ref.1, ...), custom_call_target="tpu_custom_call" | custom-call | bytes 1048576 | tf_op jit(solution)/shard_map/pallas_call | solution.py:30
  3.9 0.0 copy-done
  3.9 0.5 collective-permute-start.1
  4.4 2.6 %collective-permute-start.4 = (bf16[256,1152]{1,0:T(8,128)(2,1)}, bf16[256,1152]{1,0:T(8,128)(2,1)S(1)}, u32[]{:S(2)}, u32[]{:S(2)}) collective-permute-start(bf16[256,1152]{1,0:T(8,128)(2,1)} %get-tuple-element.53), channel_id=1, source_target_pairs={{2,0},{3,1},{0,2},{1,3},{6,4},{7,5},{4,6},{5,7},{10,8},{11,9},{8,1... | collective-permute-start | bytes 1769480 | tf_op jit(solution)/shard_map/ppermute | solution.py:292
  7.0 1.5 %collective-permute-start = (bf16[1168,128]{1,0:T(8,128)(2,1)}, bf16[1168,128]{1,0:T(8,128)(2,1)S(1)}, u32[]{:S(2)}, u32[]{:S(2)}) collective-permute-start(bf16[1168,128]{1,0:T(8,128)(2,1)} %get-tuple-element.41), channel_id=1, source_target_pairs={{0,4},{4,0},{8,12},{12,8},{16,20},{20,16},{24,28},{28,24},{1,5},{5... | collective-permute-start | bytes 897032 | tf_op jit(solution)/shard_map/ppermute | solution.py:276
  8.5 0.7 %collective-permute-start.3 = (bf16[768,128]{1,0:T(8,128)(2,1)}, bf16[768,128]{1,0:T(8,128)(2,1)S(1)}, u32[]{:S(2)}, u32[]{:S(2)}) collective-permute-start(bf16[768,128]{1,0:T(8,128)(2,1)} %get-tuple-element.42.keep_kv_ref), channel_id=1, source_target_pairs={{8,16},{16,8},{12,20},{20,12},{9,17},{17,9},{13,21},{21,13},{10,18... | collective-permute-start | bytes 589832 | tf_op jit(solution)/shard_map/ppermute | solution.py:272
  9.2 4.5 %collective-permute-start.2 = (bf16[768,128]{1,0:T(8,128)(2,1)}, bf16[768,128]{1,0:T(8,128)(2,1)S(1)}, u32[]{:S(2)}, u32[]{:S(2)}) collective-permute-start(bf16[768,128]{1,0:T(8,128)(2,1)} %get-tuple-element.42.keep_kv_ref), channel_id=1, source_target_pairs={{0,8},{8,0},{4,12},{12,4},{16,24},{24,16},{20,28},{28,20},{1,9},{9... | collective-permute-start | bytes 589832 | tf_op jit(solution)/shard_map/ppermute | solution.py:272
  13.6 0.0 copy-start.1
  13.6 1.0 %copy-done.1 = bf16[768,128]{1,0:T(8,128)(2,1)S(1)} copy-done((bf16[768,128]{1,0:T(8,128)(2,1)S(1)}, bf16[768,128]{1,0:T(8,128)(2,1)}, u32[]{:S(2)}) %copy-start.1) | copy-done | bytes 196632
  14.6 0.0 copy-start.2
  14.6 0.9 %copy-done.2 = bf16[400,128]{1,0:T(8,128)(2,1)S(1)} copy-done((bf16[400,128]{1,0:T(8,128)(2,1)S(1)}, bf16[400,128]{1,0:T(8,128)(2,1)}, u32[]{:S(2)}) %copy-start.2) | copy-done | bytes 102424
  15.6 0.0 collective-permute-done.3.kept_second_ref
  15.6 2.9 %collective-permute-done.2.kept_first_ref = bf16[768,128]{1,0:T(8,128)(2,1)S(1)} collective-permute-done((bf16[768,128]{1,0:T(8,128)(2,1)}, bf16[768,128]{1,0:T(8,128)(2,1)S(1)}, u32[]{:S(2)}, u32[]{:S(2)}) %collective-permute-start.2) | collective-permute-done | bytes 196640 | tf_op jit(solution)/shard_map/ppermute | solution.py:272
  18.5 0.0 collective-permute-done.came_ref
  18.5 0.0 collective-permute-done.1.wp_ref
  18.6 0.7 %collective-permute-start.6 = (bf16[768,128]{1,0:T(8,128)(2,1)S(1)}, bf16[768,128]{1,0:T(8,128)(2,1)S(1)}, u32[]{:S(2)}, u32[]{:S(2)}) collective-permute-start(bf16[768,128]{1,0:T(8,128)(2,1)S(1)} %get-tuple-element.55.came_ref), channel_id=1, source_target_pairs={{8,16},{16,8},{12,20},{20,12},{9,17},{17,9},{13,21},{21,13},{10,18... | collective-permute-start | bytes 589832 | tf_op jit(solution)/shard_map/ppermute | solution.py:272
  19.3 3.5 %collective-permute-start.5 = (bf16[768,128]{1,0:T(8,128)(2,1)S(1)}, bf16[768,128]{1,0:T(8,128)(2,1)S(1)}, u32[]{:S(2)}, u32[]{:S(2)}) collective-permute-start(bf16[768,128]{1,0:T(8,128)(2,1)S(1)} %get-tuple-element.55.came_ref), channel_id=1, source_target_pairs={{0,8},{8,0},{4,12},{12,4},{16,24},{24,16},{20,28},{28,20},{1,9},{9... | collective-permute-start | bytes 589832 | tf_op jit(solution)/shard_map/ppermute | solution.py:272
  22.8 1.1 %collective-permute-start.7 = (bf16[768,128]{1,0:T(8,128)(2,1)S(1)}, bf16[768,128]{1,0:T(8,128)(2,1)S(1)}, u32[]{:S(2)}, u32[]{:S(2)}) collective-permute-start(bf16[768,128]{1,0:T(8,128)(2,1)S(1)} %get-tuple-element.58), channel_id=1, source_target_pairs={{0,16},{16,0},{4,20},{20,4},{8,24},{24,8},{12,28},{28,12},{1,17},{... | collective-permute-start | bytes 589832 | tf_op jit(solution)/shard_map/ppermute | solution.py:272
  23.8 0.0 collective-permute-done.4.refs_0_
  23.9 0.5 collective-permute-start.12
  24.4 0.5 collective-permute-start.11
  24.9 3.6 %shard_map.68._ = f32[2,136,384]{2,1,0:T(8,128)S(1)} custom-call(s32[8,128]{1,0:T(8,128)S(1)} %get-tuple-element.51.flag_ref, s32[1]{0:T(128)} %bitcast.tile_ref, bf16[2,384,128]{2,1,0:T(8,128)(2,1)S(1)} %get-tuple-element.54.q_ref, bf16[768,128]{1,0:T(8,128)(2,1)S(1)} %get-tuple-element.49.keep_kv_ref.own_ref, ...), custom_call_target="tpu_custom_call" | custom-call | flops 603979776 | bytes 1048576 | tf_op jit(solution)/shard_map/pallas_call | solution.py:30
  28.5 0.0 collective-permute-done.6.second_ref
  28.5 0.0 collective-permute-done.5.first_ref
  28.5 1.8 %shard_map.69.state_ref = f32[2,136,384]{2,1,0:T(8,128)S(1)} custom-call(s32[8,128]{1,0:T(8,128)S(1)} %get-tuple-element.51.flag_ref, s32[1]{0:T(128)} %bitcast.tile_ref, bf16[2,384,128]{2,1,0:T(8,128)(2,1)S(1)} %get-tuple-element.54.q_ref, bf16[768,128]{1,0:T(8,128)(2,1)S(1)} %collective-permute-done.5.first_ref, ...), custom_call_target="tpu_custom_call", output_to_operand_aliasing={{}: (5, {})} | custom-call | flops 301989888 | bytes 1048576 | tf_op jit(solution)/shard_map/pallas_call | solution.py:30
  30.3 5.3 %collective-permute-done.7.refs_0_ = bf16[768,128]{1,0:T(8,128)(2,1)S(1)} collective-permute-done((bf16[768,128]{1,0:T(8,128)(2,1)S(1)}, bf16[768,128]{1,0:T(8,128)(2,1)S(1)}, u32[]{:S(2)}, u32[]{:S(2)}) %collective-permute-start.7) | collective-permute-done | bytes 196640 | tf_op jit(solution)/shard_map/ppermute | solution.py:272
  35.6 0.8 %shard_map.70 = (bf16[2,96,128]{2,1,0:T(8,128)(2,1)S(1)}, bf16[2,96,128]{2,1,0:T(8,128)(2,1)S(1)}, bf16[2,96,128]{2,1,0:T(8,128)(2,1)S(1)}, bf16[2,96,128]{2,1,0:T(8,128)(2,1)S(1)}, f32[2,136,384]{2,1,0:T(8,128)S(1)}) custom-call(s32[8,128]{1,0:T(8,128)S(1)} %get-tuple-element.51.flag_ref, s32[1]{0:T(128)} %bitcast.tile_ref, ...), custom_call_target="tpu_custom_call", output_to_operand_aliasing={{4}: (4, {})} | custom-call | flops 5662310400 | bytes 1048576 | tf_op jit(solution)/shard_map/pallas_call | solution.py:30
  36.4 0.1 collective-permute-start.8
  36.4 0.6 %collective-permute-start.9 = (bf16[2,96,128]{2,1,0:T(8,128)(2,1)S(1)}, bf16[2,96,128]{2,1,0:T(8,128)(2,1)S(1)}, u32[]{:S(2)}, u32[]{:S(2)}) collective-permute-start(bf16[2,96,128]{2,1,0:T(8,128)(2,1)S(1)} %get-tuple-element.61), channel_id=1, source_target_pairs={{0,4},{4,0},{8,12},{12,8},{16,20},{20,16},{24,28},{28,24},{1,5},{5... | collective-permute-start | bytes 147464 | tf_op jit(solution)/shard_map/ppermute | solution.py:276
  37.0 1.3 %collective-permute-start.10 = (bf16[2,96,128]{2,1,0:T(8,128)(2,1)S(1)}, bf16[2,96,128]{2,1,0:T(8,128)(2,1)S(1)}, u32[]{:S(2)}, u32[]{:S(2)}) collective-permute-start(bf16[2,96,128]{2,1,0:T(8,128)(2,1)S(1)} %get-tuple-element.62), channel_id=1, source_target_pairs={{0,1},{1,0},{2,3},{3,2},{4,5},{5,4},{6,7},{7,6},{8,9},{9,8},{10,11... | collective-permute-start | bytes 147464 | tf_op jit(solution)/shard_map/ppermute | solution.py:280
  38.3 1.7 %collective-permute-done.8.cross_ref = bf16[2,96,128]{2,1,0:T(8,128)(2,1)S(1)} collective-permute-done((bf16[2,96,128]{2,1,0:T(8,128)(2,1)S(1)}, bf16[2,96,128]{2,1,0:T(8,128)(2,1)S(1)}, u32[]{:S(2)}, u32[]{:S(2)}) %collective-permute-start.8) | collective-permute-done | bytes 49184 | tf_op jit(solution)/shard_map/ppermute | solution.py:287
  39.9 1.1 %collective-permute-done.9.y_ref = bf16[2,96,128]{2,1,0:T(8,128)(2,1)S(1)} collective-permute-done((bf16[2,96,128]{2,1,0:T(8,128)(2,1)S(1)}, bf16[2,96,128]{2,1,0:T(8,128)(2,1)S(1)}, u32[]{:S(2)}, u32[]{:S(2)}) %collective-permute-start.9) | collective-permute-done | bytes 49184 | tf_op jit(solution)/shard_map/ppermute | solution.py:276
  41.0 0.0 collective-permute-done.10.core_ref
  41.0 0.0 collective-permute-done.12.refs_2_
  41.0 0.0 collective-permute-done.11.refs_4_
  41.0 0.4 shard_map.71
  41.4 0.6 %collective-permute-start.13 = (bf16[96,2048]{1,0:T(8,128)(2,1)S(1)}, bf16[96,2048]{1,0:T(8,128)(2,1)S(1)}, u32[]{:S(2)}, u32[]{:S(2)}) collective-permute-start(bf16[96,2048]{1,0:T(8,128)(2,1)S(1)} %get-tuple-element.71), channel_id=1, source_target_pairs={{2,0},{3,1},{0,2},{1,3},{6,4},{7,5},{4,6},{5,7},{10,8},{11,9},{8,1... | collective-permute-start | bytes 1179656 | tf_op jit(solution)/shard_map/ppermute | solution.py:292
  42.0 0.0 collective-permute-start.14
  42.0 0.5 collective-permute-start.15
  42.5 0.0 collective-permute-start.16
  42.5 1.0 %shard_map.72.near_ref = f32[96,5120]{1,0:T(8,128)S(1)} custom-call(bf16[96,512]{1,0:T(8,128)(2,1)S(1)} %get-tuple-element.70.a_ref, bf16[256,5120]{1,0:T(8,128)(2,1)S(1)} %copy-done, bf16[256,5120]{1,0:T(8,128)(2,1)S(1)} %collective-permute-done.1.wp_ref), custom_call_target="tpu_custom_call" | custom-call | flops 15099494400 | bytes 1048576 | tf_op jit(solution)/shard_map/pallas_call | solution.py:30
  43.5 9.0 %collective-permute-done.13.far_ref = bf16[96,2048]{1,0:T(8,128)(2,1)S(1)} collective-permute-done((bf16[96,2048]{1,0:T(8,128)(2,1)S(1)}, bf16[96,2048]{1,0:T(8,128)(2,1)S(1)}, u32[]{:S(2)}, u32[]{:S(2)}) %collective-permute-start.13) | collective-permute-done | bytes 393248 | tf_op jit(solution)/shard_map/ppermute | solution.py:292
  52.5 0.0 collective-permute-done.14.refs_1_
  52.5 0.0 collective-permute-done.15.refs_3_
  52.5 0.0 collective-permute-done.16.refs_5_
  52.5 1.5 %shard_map.73 = bf16[96,5120]{1,0:T(8,128)(2,1)} custom-call(s32[1]{0:T(128)} %bitcast.tile_ref, f32[96,5120]{1,0:T(8,128)S(1)} %shard_map.72.near_ref, bf16[96,2048]{1,0:T(8,128)(2,1)S(1)} %collective-permute-done.13.far_ref, bf16[256,1152]{1,0:T(8,128)(2,1)S(1)} %collective-permute-done.4.refs_0_, bf16[256,1152]{1,0:T(8,128)(2,1)S(1)} %collective-permute-done.14.refs_1_, ...), custom_call_target="tpu_custom_call" | custom-call | flops 503316480 | bytes 1048576 | tf_op jit(solution)/shard_map/pallas_call | solution.py:30
  (3 shorter events, 0.1 us)
Async XLA Ops:
  0.0 3.9 %copy-start = (bf16[256,5120]{1,0:T(8,128)(2,1)S(1)}, bf16[256,5120]{1,0:T(8,128)(2,1)}, u32[]{:S(2)}) copy-start(bf16[256,5120]{1,0:T(8,128)(2,1)} %w_ref.6) | copy-start | bytes 7864324
  3.9 14.6 %collective-permute-start.1 = (bf16[256,5120]{1,0:T(8,128)(2,1)S(1)}, bf16[256,5120]{1,0:T(8,128)(2,1)S(1)}, u32[]{:S(2)}, u32[]{:S(2)}) collective-permute-start(bf16[256,5120]{1,0:T(8,128)(2,1)S(1)} %copy-done), channel_id=1, source_target_pairs={{0,1},{1,0},{2,3},{3,2},{4,5},{5,4},{6,7},{7,6},{8,9},{9,8},{10,11... | collective-permute-start | bytes 7864328 | tf_op jit(solution)/shard_map/ppermute | solution.py:280
  4.4 19.4 %collective-permute-start.4 = (bf16[256,1152]{1,0:T(8,128)(2,1)}, bf16[256,1152]{1,0:T(8,128)(2,1)S(1)}, u32[]{:S(2)}, u32[]{:S(2)}) collective-permute-start(bf16[256,1152]{1,0:T(8,128)(2,1)} %get-tuple-element.53), channel_id=1, source_target_pairs={{2,0},{3,1},{0,2},{1,3},{6,4},{7,5},{4,6},{5,7},{10,8},{11,9},{8,1... | collective-permute-start | bytes 1769480 | tf_op jit(solution)/shard_map/ppermute | solution.py:292
  7.0 11.5 %collective-permute-start = (bf16[1168,128]{1,0:T(8,128)(2,1)}, bf16[1168,128]{1,0:T(8,128)(2,1)S(1)}, u32[]{:S(2)}, u32[]{:S(2)}) collective-permute-start(bf16[1168,128]{1,0:T(8,128)(2,1)} %get-tuple-element.41), channel_id=1, source_target_pairs={{0,4},{4,0},{8,12},{12,8},{16,20},{20,16},{24,28},{28,24},{1,5},{5... | collective-permute-start | bytes 897032 | tf_op jit(solution)/shard_map/ppermute | solution.py:276
  8.5 7.1 %collective-permute-start.3 = (bf16[768,128]{1,0:T(8,128)(2,1)}, bf16[768,128]{1,0:T(8,128)(2,1)S(1)}, u32[]{:S(2)}, u32[]{:S(2)}) collective-permute-start(bf16[768,128]{1,0:T(8,128)(2,1)} %get-tuple-element.42.keep_kv_ref), channel_id=1, source_target_pairs={{8,16},{16,8},{12,20},{20,12},{9,17},{17,9},{13,21},{21,13},{10,18... | collective-permute-start | bytes 589832 | tf_op jit(solution)/shard_map/ppermute | solution.py:272
  9.2 9.3 %collective-permute-start.2 = (bf16[768,128]{1,0:T(8,128)(2,1)}, bf16[768,128]{1,0:T(8,128)(2,1)S(1)}, u32[]{:S(2)}, u32[]{:S(2)}) collective-permute-start(bf16[768,128]{1,0:T(8,128)(2,1)} %get-tuple-element.42.keep_kv_ref), channel_id=1, source_target_pairs={{0,8},{8,0},{4,12},{12,4},{16,24},{24,16},{20,28},{28,20},{1,9},{9... | collective-permute-start | bytes 589832 | tf_op jit(solution)/shard_map/ppermute | solution.py:272
  13.6 1.0 %copy-start.1 = (bf16[768,128]{1,0:T(8,128)(2,1)S(1)}, bf16[768,128]{1,0:T(8,128)(2,1)}, u32[]{:S(2)}) copy-start(bf16[768,128]{1,0:T(8,128)(2,1)} %get-tuple-element.42.keep_kv_ref) | copy-start | bytes 589828
  14.6 0.9 %copy-start.2 = (bf16[400,128]{1,0:T(8,128)(2,1)S(1)}, bf16[400,128]{1,0:T(8,128)(2,1)}, u32[]{:S(2)}) copy-start(bf16[400,128]{1,0:T(8,128)(2,1)} %get-tuple-element.44.keep_q_ref) | copy-start | bytes 307204
  18.6 9.9 %collective-permute-start.6 = (bf16[768,128]{1,0:T(8,128)(2,1)S(1)}, bf16[768,128]{1,0:T(8,128)(2,1)S(1)}, u32[]{:S(2)}, u32[]{:S(2)}) collective-permute-start(bf16[768,128]{1,0:T(8,128)(2,1)S(1)} %get-tuple-element.55.came_ref), channel_id=1, source_target_pairs={{8,16},{16,8},{12,20},{20,12},{9,17},{17,9},{13,21},{21,13},{10,18... | collective-permute-start | bytes 589832 | tf_op jit(solution)/shard_map/ppermute | solution.py:272
  19.3 9.2 %collective-permute-start.5 = (bf16[768,128]{1,0:T(8,128)(2,1)S(1)}, bf16[768,128]{1,0:T(8,128)(2,1)S(1)}, u32[]{:S(2)}, u32[]{:S(2)}) collective-permute-start(bf16[768,128]{1,0:T(8,128)(2,1)S(1)} %get-tuple-element.55.came_ref), channel_id=1, source_target_pairs={{0,8},{8,0},{4,12},{12,4},{16,24},{24,16},{20,28},{28,20},{1,9},{9... | collective-permute-start | bytes 589832 | tf_op jit(solution)/shard_map/ppermute | solution.py:272
  22.8 12.8 %collective-permute-start.7 = (bf16[768,128]{1,0:T(8,128)(2,1)S(1)}, bf16[768,128]{1,0:T(8,128)(2,1)S(1)}, u32[]{:S(2)}, u32[]{:S(2)}) collective-permute-start(bf16[768,128]{1,0:T(8,128)(2,1)S(1)} %get-tuple-element.58), channel_id=1, source_target_pairs={{0,16},{16,0},{4,20},{20,4},{8,24},{24,8},{12,28},{28,12},{1,17},{... | collective-permute-start | bytes 589832 | tf_op jit(solution)/shard_map/ppermute | solution.py:272
  23.9 17.2 %collective-permute-start.12 = (bf16[256,1152]{1,0:T(8,128)(2,1)S(1)}, bf16[256,1152]{1,0:T(8,128)(2,1)S(1)}, u32[]{:S(2)}, u32[]{:S(2)}) collective-permute-start(bf16[256,1152]{1,0:T(8,128)(2,1)S(1)} %collective-permute-done.4.refs_0_), channel_id=1, source_target_pairs={{0,4},{4,0},{8,12},{12,8},{16,20},{20,16},{24,28},{28,24},{1,5},{5... | collective-permute-start | bytes 1769480 | tf_op jit(solution)/shard_map/ppermute | solution.py:276
  24.4 16.7 %collective-permute-start.11 = (bf16[256,1280]{1,0:T(8,128)(2,1)S(1)}, bf16[256,1280]{1,0:T(8,128)(2,1)S(1)}, u32[]{:S(2)}, u32[]{:S(2)}) collective-permute-start(bf16[256,1280]{1,0:T(8,128)(2,1)S(1)} %shard_map.66), channel_id=1, source_target_pairs={{2,0},{3,1},{0,2},{1,3},{6,4},{7,5},{4,6},{5,7},{10,8},{11,9},{8,1... | collective-permute-start | bytes 1966088 | tf_op jit(solution)/shard_map/ppermute | solution.py:292
  36.4 3.6 %collective-permute-start.8 = (bf16[2,96,128]{2,1,0:T(8,128)(2,1)S(1)}, bf16[2,96,128]{2,1,0:T(8,128)(2,1)S(1)}, u32[]{:S(2)}, u32[]{:S(2)}) collective-permute-start(bf16[2,96,128]{2,1,0:T(8,128)(2,1)S(1)} %get-tuple-element.60), channel_id=1, source_target_pairs={{0,5},{1,4},{2,7},{3,6},{4,1},{5,0},{6,3},{7,2},{8,13},{9,12},{10,... | collective-permute-start | bytes 147464 | tf_op jit(solution)/shard_map/ppermute | solution.py:287
  36.4 4.6 %collective-permute-start.9 = (bf16[2,96,128]{2,1,0:T(8,128)(2,1)S(1)}, bf16[2,96,128]{2,1,0:T(8,128)(2,1)S(1)}, u32[]{:S(2)}, u32[]{:S(2)}) collective-permute-start(bf16[2,96,128]{2,1,0:T(8,128)(2,1)S(1)} %get-tuple-element.61), channel_id=1, source_target_pairs={{0,4},{4,0},{8,12},{12,8},{16,20},{20,16},{24,28},{28,24},{1,5},{5... | collective-permute-start | bytes 147464 | tf_op jit(solution)/shard_map/ppermute | solution.py:276
  37.0 4.0 %collective-permute-start.10 = (bf16[2,96,128]{2,1,0:T(8,128)(2,1)S(1)}, bf16[2,96,128]{2,1,0:T(8,128)(2,1)S(1)}, u32[]{:S(2)}, u32[]{:S(2)}) collective-permute-start(bf16[2,96,128]{2,1,0:T(8,128)(2,1)S(1)} %get-tuple-element.62), channel_id=1, source_target_pairs={{0,1},{1,0},{2,3},{3,2},{4,5},{5,4},{6,7},{7,6},{8,9},{9,8},{10,11... | collective-permute-start | bytes 147464 | tf_op jit(solution)/shard_map/ppermute | solution.py:280
  41.4 11.1 %collective-permute-start.13 = (bf16[96,2048]{1,0:T(8,128)(2,1)S(1)}, bf16[96,2048]{1,0:T(8,128)(2,1)S(1)}, u32[]{:S(2)}, u32[]{:S(2)}) collective-permute-start(bf16[96,2048]{1,0:T(8,128)(2,1)S(1)} %get-tuple-element.71), channel_id=1, source_target_pairs={{2,0},{3,1},{0,2},{1,3},{6,4},{7,5},{4,6},{5,7},{10,8},{11,9},{8,1... | collective-permute-start | bytes 1179656 | tf_op jit(solution)/shard_map/ppermute | solution.py:292
  42.0 10.5 %collective-permute-start.14 = (bf16[256,1152]{1,0:T(8,128)(2,1)S(1)}, bf16[256,1152]{1,0:T(8,128)(2,1)S(1)}, u32[]{:S(2)}, u32[]{:S(2)}) collective-permute-start(bf16[256,1152]{1,0:T(8,128)(2,1)S(1)} %collective-permute-done.4.refs_0_), channel_id=1, source_target_pairs={{0,1},{1,0},{2,3},{3,2},{4,5},{5,4},{6,7},{7,6},{8,9},{9,8},{10,11... | collective-permute-start | bytes 1769480 | tf_op jit(solution)/shard_map/ppermute | solution.py:280
  42.0 10.5 %collective-permute-start.15 = (bf16[256,1152]{1,0:T(8,128)(2,1)S(1)}, bf16[256,1152]{1,0:T(8,128)(2,1)S(1)}, u32[]{:S(2)}, u32[]{:S(2)}) collective-permute-start(bf16[256,1152]{1,0:T(8,128)(2,1)S(1)} %collective-permute-done.12.refs_2_), channel_id=1, source_target_pairs={{0,1},{1,0},{2,3},{3,2},{4,5},{5,4},{6,7},{7,6},{8,9},{9,8},{10,11... | collective-permute-start | bytes 1769480 | tf_op jit(solution)/shard_map/ppermute | solution.py:280
  42.5 10.0 %collective-permute-start.16 = (bf16[256,1280]{1,0:T(8,128)(2,1)S(1)}, bf16[256,1280]{1,0:T(8,128)(2,1)S(1)}, u32[]{:S(2)}, u32[]{:S(2)}) collective-permute-start(bf16[256,1280]{1,0:T(8,128)(2,1)S(1)} %collective-permute-done.11.refs_4_), channel_id=1, source_target_pairs={{0,1},{1,0},{2,3},{3,2},{4,5},{5,4},{6,7},{7,6},{8,9},{9,8},{10,11... | collective-permute-start | bytes 1966088 | tf_op jit(solution)/shard_map/ppermute | solution.py:280

commit v8 on v7

--- a/solution.py
+++ b/solution.py
@@ -12,8 +12,8 @@
 REACH = 3
 NEG = -1e30
 FLAGS = 16
-SIDE = 1152
-COMMON = 1280
+SIDE = 1408
+COMMON = 1152
 STATE = HD + 8
 EXPONENT = math.log2(math.e) / math.sqrt(HD)
 BF16, F32 = jnp.bfloat16, jnp.float32
@@ -403,8 +403,8 @@
     from_cross = swap_both(theirs_other)
     from_y = swap_tiles(theirs)
     from_core = swap_cores(mine_other)
-    from_cross, from_y, from_core, common, side_other = lax.optimization_barrier(
-        (from_cross, from_y, from_core, common, side_other)
+    from_cross, from_y, from_core, common = lax.optimization_barrier(
+        (from_cross, from_y, from_core, common)
     )
 
     flops = 2 * own_rows * 2 * width * model

time: 54.6 us -> 55.1 us (level)
  starting transfers between devices: 19 us -> 22.3 us
  waiting for transfers between devices: 20 us -> 18.5 us
  Pallas kernels: 12.2 us -> 11.2 us
    ppermute x3, waiting for transfers between devices: 9.04 us -> 5.74 us  [from_chip(): lax.ppermute(value, 'head', [((i + 2 * steps) % count, i) for i in range(...]
    ppermute x1, waiting for transfers between devices: 1.65 us -> 4.24 us  [swap_both(): return lax.ppermute(value, ('ctx', 'head'), pairs)]
    ppermute x3, starting transfers between devices: 3.7 us -> 5.68 us  [from_chip(): lax.ppermute(value, 'head', [((i + 2 * steps) % count, i) for i in range(...]
    ppermute x3, starting transfers between devices: 2.59 us -> 3.87 us  [swap_tiles(): lax.ppermute(value, 'ctx', [(i, i ^ 1) for i in range(lax.axis_size('ctx'...]
    ppermute x5, waiting for transfers between devices: 8.25 us -> 7.08 us  [swap_pairs(): return lax.ppermute(value, 'ctx', pairs)]
    pallas_call x10, Pallas kernels: 12.2 us -> 11.2 us  [call(): pl.pallas_call(kernel, out_shape=outs, in_specs=[SMEM if s else HBM if i...]
  transfers between devices with their start and end apart: 17 -> 17, of which waited for: 5 -> 6; matrix products, arithmetic and copies ran while one was open for 0% -> 0% of each run, Pallas kernels for 13% -> 12%
where the time goes in v8:
time: 55.1 us; the launch traced here: 54.8 us
  starting transfers between devices  22.3 us (40%)
  waiting for transfers between devices  18.5 us (34%)
  Pallas kernels  11.2 us (20%)
  local copies, waits for them, and re-layouts  1.86 us (3%)
  between operations  0.94 us (2%)
    pallas_call x10, Pallas kernels, call(): pl.pallas_call(kernel, out_shape=outs, in_specs=[SMEM if s else HBM if i...  11.2 us
    ppermute x5, starting transfers between devices, swap_pairs(): return lax.ppermute(value, 'ctx', pairs)  10.4 us
    ppermute x5, waiting for transfers between devices, swap_pairs(): return lax.ppermute(value, 'ctx', pairs)  7.08 us
    ppermute x3, waiting for transfers between devices, from_chip(): lax.ppermute(value, 'head', [((i + 2 * steps) % count, i) for i in range(...  5.74 us
    ppermute x3, starting transfers between devices, from_chip(): lax.ppermute(value, 'head', [((i + 2 * steps) % count, i) for i in range(...  5.68 us
    ppermute x1, waiting for transfers between devices, swap_both(): return lax.ppermute(value, ('ctx', 'head'), pairs)  4.24 us
    ppermute x3, starting transfers between devices, swap_tiles(): lax.ppermute(value, 'ctx', [(i, i ^ 1) for i in range(lax.axis_size('ctx'...  3.87 us
    ppermute x5, starting transfers between devices, swap_cores(): lax.ppermute(value, 'head', [(i, i ^ 1) for i in range(lax.axis_size('hea...  2.31 us
  transfers between devices with their start and end apart: 17, of which 6 were waited for; matrix products, arithmetic and copies ran while one was open for 0% of the time, Pallas kernels for 12%

profile of v8, /device:TPU:0, one launch (start us, length us, event | category | flops | bytes accessed | tf_op | source)
XLA Modules:
  0.0 54.8 jit_solution(726735042420442972)
XLA Ops:
  0.0 0.0 copy-start
  0.8 3.2 %shard_map.64 = (bf16[400,128]{1,0:T(8,128)(2,1)}, bf16[768,128]{1,0:T(8,128)(2,1)}, bf16[1168,128]{1,0:T(8,128)(2,1)}, bf16[256,1408]{1,0:T(8,128)(2,1)}) custom-call(s32[1]{0:T(128)} %bitcast.tile_ref, s32[1]{0:T(128)} %bitcast.1._.head_ref, s32[1,7]{1,0:T(1,128)} %list_ref.1, s32[1,1]{1,0:T(1,128)} %bitcast.3.count_ref, bf16[384,256]{1,0:T(8,128)(2,1)} %q_ref.1, ...), custom_call_target="tpu_custom_call" | custom-call | bytes 1048576 | tf_op jit(solution)/shard_map/pallas_call | solution.py:30
  4.0 0.0 copy-done
  4.0 0.5 collective-permute-start.1
  4.5 2.6 %collective-permute-start.4 = (bf16[256,1408]{1,0:T(8,128)(2,1)}, bf16[256,1408]{1,0:T(8,128)(2,1)S(1)}, u32[]{:S(2)}, u32[]{:S(2)}) collective-permute-start(bf16[256,1408]{1,0:T(8,128)(2,1)} %get-tuple-element.52), channel_id=1, source_target_pairs={{2,0},{3,1},{0,2},{1,3},{6,4},{7,5},{4,6},{5,7},{10,8},{11,9},{8,1... | collective-permute-start | bytes 2162696 | tf_op jit(solution)/shard_map/ppermute | solution.py:292
  7.1 1.5 %collective-permute-start = (bf16[1168,128]{1,0:T(8,128)(2,1)}, bf16[1168,128]{1,0:T(8,128)(2,1)S(1)}, u32[]{:S(2)}, u32[]{:S(2)}) collective-permute-start(bf16[1168,128]{1,0:T(8,128)(2,1)} %get-tuple-element.40), channel_id=1, source_target_pairs={{0,4},{4,0},{8,12},{12,8},{16,20},{20,16},{24,28},{28,24},{1,5},{5... | collective-permute-start | bytes 897032 | tf_op jit(solution)/shard_map/ppermute | solution.py:276
  8.6 0.7 %collective-permute-start.3 = (bf16[768,128]{1,0:T(8,128)(2,1)}, bf16[768,128]{1,0:T(8,128)(2,1)S(1)}, u32[]{:S(2)}, u32[]{:S(2)}) collective-permute-start(bf16[768,128]{1,0:T(8,128)(2,1)} %get-tuple-element.41.keep_kv_ref), channel_id=1, source_target_pairs={{8,16},{16,8},{12,20},{20,12},{9,17},{17,9},{13,21},{21,13},{10,18... | collective-permute-start | bytes 589832 | tf_op jit(solution)/shard_map/ppermute | solution.py:272
  9.3 4.5 %collective-permute-start.2 = (bf16[768,128]{1,0:T(8,128)(2,1)}, bf16[768,128]{1,0:T(8,128)(2,1)S(1)}, u32[]{:S(2)}, u32[]{:S(2)}) collective-permute-start(bf16[768,128]{1,0:T(8,128)(2,1)} %get-tuple-element.41.keep_kv_ref), channel_id=1, source_target_pairs={{0,8},{8,0},{4,12},{12,4},{16,24},{24,16},{20,28},{28,20},{1,9},{9... | collective-permute-start | bytes 589832 | tf_op jit(solution)/shard_map/ppermute | solution.py:272
  13.7 0.0 copy-start.1
  13.7 1.0 %copy-done.1 = bf16[768,128]{1,0:T(8,128)(2,1)S(1)} copy-done((bf16[768,128]{1,0:T(8,128)(2,1)S(1)}, bf16[768,128]{1,0:T(8,128)(2,1)}, u32[]{:S(2)}) %copy-start.1) | copy-done | bytes 196632
  14.7 0.0 copy-start.2
  14.7 0.9 %copy-done.2 = bf16[400,128]{1,0:T(8,128)(2,1)S(1)} copy-done((bf16[400,128]{1,0:T(8,128)(2,1)S(1)}, bf16[400,128]{1,0:T(8,128)(2,1)}, u32[]{:S(2)}) %copy-start.2) | copy-done | bytes 102424
  15.7 0.0 collective-permute-done.3.kept_second_ref
  15.7 2.9 %collective-permute-done.2.kept_first_ref = bf16[768,128]{1,0:T(8,128)(2,1)S(1)} collective-permute-done((bf16[768,128]{1,0:T(8,128)(2,1)}, bf16[768,128]{1,0:T(8,128)(2,1)S(1)}, u32[]{:S(2)}, u32[]{:S(2)}) %collective-permute-start.2) | collective-permute-done | bytes 196640 | tf_op jit(solution)/shard_map/ppermute | solution.py:272
  18.6 0.0 collective-permute-done.came_ref
  18.6 0.0 collective-permute-done.1.wp_ref
  18.7 0.7 %collective-permute-start.6 = (bf16[768,128]{1,0:T(8,128)(2,1)S(1)}, bf16[768,128]{1,0:T(8,128)(2,1)S(1)}, u32[]{:S(2)}, u32[]{:S(2)}) collective-permute-start(bf16[768,128]{1,0:T(8,128)(2,1)S(1)} %get-tuple-element.54.came_ref), channel_id=1, source_target_pairs={{8,16},{16,8},{12,20},{20,12},{9,17},{17,9},{13,21},{21,13},{10,18... | collective-permute-start | bytes 589832 | tf_op jit(solution)/shard_map/ppermute | solution.py:272
  19.4 3.5 %collective-permute-start.5 = (bf16[768,128]{1,0:T(8,128)(2,1)S(1)}, bf16[768,128]{1,0:T(8,128)(2,1)S(1)}, u32[]{:S(2)}, u32[]{:S(2)}) collective-permute-start(bf16[768,128]{1,0:T(8,128)(2,1)S(1)} %get-tuple-element.54.came_ref), channel_id=1, source_target_pairs={{0,8},{8,0},{4,12},{12,4},{16,24},{24,16},{20,28},{28,20},{1,9},{9... | collective-permute-start | bytes 589832 | tf_op jit(solution)/shard_map/ppermute | solution.py:272
  22.8 1.1 %collective-permute-start.7 = (bf16[768,128]{1,0:T(8,128)(2,1)S(1)}, bf16[768,128]{1,0:T(8,128)(2,1)S(1)}, u32[]{:S(2)}, u32[]{:S(2)}) collective-permute-start(bf16[768,128]{1,0:T(8,128)(2,1)S(1)} %get-tuple-element.57), channel_id=1, source_target_pairs={{0,16},{16,0},{4,20},{20,4},{8,24},{24,8},{12,28},{28,12},{1,17},{... | collective-permute-start | bytes 589832 | tf_op jit(solution)/shard_map/ppermute | solution.py:272
  23.9 0.1 collective-permute-done.4.refs_0_
  24.0 1.8 %collective-permute-start.13 = (bf16[256,1408]{1,0:T(8,128)(2,1)S(1)}, bf16[256,1408]{1,0:T(8,128)(2,1)S(1)}, u32[]{:S(2)}, u32[]{:S(2)}) collective-permute-start(bf16[256,1408]{1,0:T(8,128)(2,1)S(1)} %collective-permute-done.4.refs_0_), channel_id=1, source_target_pairs={{0,4},{4,0},{8,12},{12,8},{16,20},{20,16},{24,28},{28,24},{1,5},{5... | collective-permute-start | bytes 2162696 | tf_op jit(solution)/shard_map/ppermute | solution.py:276
  25.8 1.5 %collective-permute-start.11 = (bf16[256,1152]{1,0:T(8,128)(2,1)S(1)}, bf16[256,1152]{1,0:T(8,128)(2,1)S(1)}, u32[]{:S(2)}, u32[]{:S(2)}) collective-permute-start(bf16[256,1152]{1,0:T(8,128)(2,1)S(1)} %shard_map.66), channel_id=1, source_target_pairs={{2,0},{3,1},{0,2},{1,3},{6,4},{7,5},{4,6},{5,7},{10,8},{11,9},{8,1... | collective-permute-start | bytes 1769480 | tf_op jit(solution)/shard_map/ppermute | solution.py:292
  27.3 3.0 %shard_map.68._ = f32[2,136,384]{2,1,0:T(8,128)S(1)} custom-call(s32[8,128]{1,0:T(8,128)S(1)} %get-tuple-element.50.flag_ref, s32[1]{0:T(128)} %bitcast.tile_ref, bf16[2,384,128]{2,1,0:T(8,128)(2,1)S(1)} %get-tuple-element.53.q_ref, bf16[768,128]{1,0:T(8,128)(2,1)S(1)} %get-tuple-element.48.keep_kv_ref.own_ref, ...), custom_call_target="tpu_custom_call" | custom-call | flops 603979776 | bytes 1048576 | tf_op jit(solution)/shard_map/pallas_call | solution.py:30
  30.3 0.0 collective-permute-done.6.second_ref
  30.3 0.0 collective-permute-done.5.first_ref
  30.3 1.2 %shard_map.69.state_ref = f32[2,136,384]{2,1,0:T(8,128)S(1)} custom-call(s32[8,128]{1,0:T(8,128)S(1)} %get-tuple-element.50.flag_ref, s32[1]{0:T(128)} %bitcast.tile_ref, bf16[2,384,128]{2,1,0:T(8,128)(2,1)S(1)} %get-tuple-element.53.q_ref, bf16[768,128]{1,0:T(8,128)(2,1)S(1)} %collective-permute-done.5.first_ref, ...), custom_call_target="tpu_custom_call", output_to_operand_aliasing={{}: (5, {})} | custom-call | flops 301989888 | bytes 1048576 | tf_op jit(solution)/shard_map/pallas_call | solution.py:30
  31.6 4.1 %collective-permute-done.7.refs_0_ = bf16[768,128]{1,0:T(8,128)(2,1)S(1)} collective-permute-done((bf16[768,128]{1,0:T(8,128)(2,1)S(1)}, bf16[768,128]{1,0:T(8,128)(2,1)S(1)}, u32[]{:S(2)}, u32[]{:S(2)}) %collective-permute-start.7) | collective-permute-done | bytes 196640 | tf_op jit(solution)/shard_map/ppermute | solution.py:272
  35.7 0.8 %shard_map.70 = (bf16[2,96,128]{2,1,0:T(8,128)(2,1)S(1)}, bf16[2,96,128]{2,1,0:T(8,128)(2,1)S(1)}, bf16[2,96,128]{2,1,0:T(8,128)(2,1)S(1)}, bf16[2,96,128]{2,1,0:T(8,128)(2,1)S(1)}, f32[2,136,384]{2,1,0:T(8,128)S(1)}) custom-call(s32[8,128]{1,0:T(8,128)S(1)} %get-tuple-element.50.flag_ref, s32[1]{0:T(128)} %bitcast.tile_ref, ...), custom_call_target="tpu_custom_call", output_to_operand_aliasing={{4}: (4, {})} | custom-call | flops 5662310400 | bytes 1048576 | tf_op jit(solution)/shard_map/pallas_call | solution.py:30
  36.5 0.1 collective-permute-start.8
  36.5 0.6 %collective-permute-start.9 = (bf16[2,96,128]{2,1,0:T(8,128)(2,1)S(1)}, bf16[2,96,128]{2,1,0:T(8,128)(2,1)S(1)}, u32[]{:S(2)}, u32[]{:S(2)}) collective-permute-start(bf16[2,96,128]{2,1,0:T(8,128)(2,1)S(1)} %get-tuple-element.60), channel_id=1, source_target_pairs={{0,4},{4,0},{8,12},{12,8},{16,20},{20,16},{24,28},{28,24},{1,5},{5... | collective-permute-start | bytes 147464 | tf_op jit(solution)/shard_map/ppermute | solution.py:276
  37.1 1.3 %collective-permute-start.10 = (bf16[2,96,128]{2,1,0:T(8,128)(2,1)S(1)}, bf16[2,96,128]{2,1,0:T(8,128)(2,1)S(1)}, u32[]{:S(2)}, u32[]{:S(2)}) collective-permute-start(bf16[2,96,128]{2,1,0:T(8,128)(2,1)S(1)} %get-tuple-element.61), channel_id=1, source_target_pairs={{0,1},{1,0},{2,3},{3,2},{4,5},{5,4},{6,7},{7,6},{8,9},{9,8},{10,11... | collective-permute-start | bytes 147464 | tf_op jit(solution)/shard_map/ppermute | solution.py:280
  38.4 4.2 %collective-permute-done.8.cross_ref = bf16[2,96,128]{2,1,0:T(8,128)(2,1)S(1)} collective-permute-done((bf16[2,96,128]{2,1,0:T(8,128)(2,1)S(1)}, bf16[2,96,128]{2,1,0:T(8,128)(2,1)S(1)}, u32[]{:S(2)}, u32[]{:S(2)}) %collective-permute-start.8) | collective-permute-done | bytes 49184 | tf_op jit(solution)/shard_map/ppermute | solution.py:287
  42.6 1.4 %collective-permute-done.9.y_ref = bf16[2,96,128]{2,1,0:T(8,128)(2,1)S(1)} collective-permute-done((bf16[2,96,128]{2,1,0:T(8,128)(2,1)S(1)}, bf16[2,96,128]{2,1,0:T(8,128)(2,1)S(1)}, u32[]{:S(2)}, u32[]{:S(2)}) %collective-permute-start.9) | collective-permute-done | bytes 49184 | tf_op jit(solution)/shard_map/ppermute | solution.py:276
  44.0 0.0 collective-permute-done.10.core_ref
  44.0 0.0 collective-permute-done.11.refs_4_
  44.0 0.4 shard_map.71
  44.4 1.6 %collective-permute-start.12 = (bf16[96,1664]{1,0:T(8,128)(2,1)S(1)}, bf16[96,1664]{1,0:T(8,128)(2,1)S(1)}, u32[]{:S(2)}, u32[]{:S(2)}) collective-permute-start(bf16[96,1664]{1,0:T(8,128)(2,1)S(1)} %get-tuple-element.70), channel_id=1, source_target_pairs={{2,0},{3,1},{0,2},{1,3},{6,4},{7,5},{4,6},{5,7},{10,8},{11,9},{8,1... | collective-permute-start | bytes 958472 | tf_op jit(solution)/shard_map/ppermute | solution.py:292
  46.0 0.0 collective-permute-done.13.refs_2_
  46.0 0.0 collective-permute-start.16
  46.0 0.5 collective-permute-start.14
  46.5 0.0 collective-permute-start.15
  46.5 1.0 %shard_map.72.near_ref = f32[96,5120]{1,0:T(8,128)S(1)} custom-call(bf16[96,512]{1,0:T(8,128)(2,1)S(1)} %get-tuple-element.69.a_ref, bf16[256,5120]{1,0:T(8,128)(2,1)S(1)} %copy-done, bf16[256,5120]{1,0:T(8,128)(2,1)S(1)} %collective-permute-done.1.wp_ref), custom_call_target="tpu_custom_call" | custom-call | flops 15099494400 | bytes 1048576 | tf_op jit(solution)/shard_map/pallas_call | solution.py:30
  47.6 5.6 %collective-permute-done.12.far_ref = bf16[96,1664]{1,0:T(8,128)(2,1)S(1)} collective-permute-done((bf16[96,1664]{1,0:T(8,128)(2,1)S(1)}, bf16[96,1664]{1,0:T(8,128)(2,1)S(1)}, u32[]{:S(2)}, u32[]{:S(2)}) %collective-permute-start.12) | collective-permute-done | bytes 319520 | tf_op jit(solution)/shard_map/ppermute | solution.py:292
  53.2 0.0 collective-permute-done.16.refs_5_
  53.2 0.0 collective-permute-done.14.refs_1_
  53.2 0.0 collective-permute-done.15.refs_3_
  53.2 1.6 %shard_map.73 = bf16[96,5120]{1,0:T(8,128)(2,1)} custom-call(s32[1]{0:T(128)} %bitcast.tile_ref, f32[96,5120]{1,0:T(8,128)S(1)} %shard_map.72.near_ref, bf16[96,1664]{1,0:T(8,128)(2,1)S(1)} %collective-permute-done.12.far_ref, bf16[256,1408]{1,0:T(8,128)(2,1)S(1)} %collective-permute-done.4.refs_0_, bf16[256,1408]{1,0:T(8,128)(2,1)S(1)} %collective-permute-done.14.refs_1_, ...), custom_call_target="tpu_custom_call" | custom-call | flops 503316480 | bytes 1048576 | tf_op jit(solution)/shard_map/pallas_call | solution.py:30
  (3 shorter events, 0.1 us)
Async XLA Ops:
  0.0 4.0 %copy-start = (bf16[256,5120]{1,0:T(8,128)(2,1)S(1)}, bf16[256,5120]{1,0:T(8,128)(2,1)}, u32[]{:S(2)}) copy-start(bf16[256,5120]{1,0:T(8,128)(2,1)} %w_ref.6) | copy-start | bytes 7864324
  4.0 14.6 %collective-permute-start.1 = (bf16[256,5120]{1,0:T(8,128)(2,1)S(1)}, bf16[256,5120]{1,0:T(8,128)(2,1)S(1)}, u32[]{:S(2)}, u32[]{:S(2)}) collective-permute-start(bf16[256,5120]{1,0:T(8,128)(2,1)S(1)} %copy-done), channel_id=1, source_target_pairs={{0,1},{1,0},{2,3},{3,2},{4,5},{5,4},{6,7},{7,6},{8,9},{9,8},{10,11... | collective-permute-start | bytes 7864328 | tf_op jit(solution)/shard_map/ppermute | solution.py:280
  4.5 19.5 %collective-permute-start.4 = (bf16[256,1408]{1,0:T(8,128)(2,1)}, bf16[256,1408]{1,0:T(8,128)(2,1)S(1)}, u32[]{:S(2)}, u32[]{:S(2)}) collective-permute-start(bf16[256,1408]{1,0:T(8,128)(2,1)} %get-tuple-element.52), channel_id=1, source_target_pairs={{2,0},{3,1},{0,2},{1,3},{6,4},{7,5},{4,6},{5,7},{10,8},{11,9},{8,1... | collective-permute-start | bytes 2162696 | tf_op jit(solution)/shard_map/ppermute | solution.py:292
  7.1 11.5 %collective-permute-start = (bf16[1168,128]{1,0:T(8,128)(2,1)}, bf16[1168,128]{1,0:T(8,128)(2,1)S(1)}, u32[]{:S(2)}, u32[]{:S(2)}) collective-permute-start(bf16[1168,128]{1,0:T(8,128)(2,1)} %get-tuple-element.40), channel_id=1, source_target_pairs={{0,4},{4,0},{8,12},{12,8},{16,20},{20,16},{24,28},{28,24},{1,5},{5... | collective-permute-start | bytes 897032 | tf_op jit(solution)/shard_map/ppermute | solution.py:276
  8.6 7.1 %collective-permute-start.3 = (bf16[768,128]{1,0:T(8,128)(2,1)}, bf16[768,128]{1,0:T(8,128)(2,1)S(1)}, u32[]{:S(2)}, u32[]{:S(2)}) collective-permute-start(bf16[768,128]{1,0:T(8,128)(2,1)} %get-tuple-element.41.keep_kv_ref), channel_id=1, source_target_pairs={{8,16},{16,8},{12,20},{20,12},{9,17},{17,9},{13,21},{21,13},{10,18... | collective-permute-start | bytes 589832 | tf_op jit(solution)/shard_map/ppermute | solution.py:272
  9.3 9.3 %collective-permute-start.2 = (bf16[768,128]{1,0:T(8,128)(2,1)}, bf16[768,128]{1,0:T(8,128)(2,1)S(1)}, u32[]{:S(2)}, u32[]{:S(2)}) collective-permute-start(bf16[768,128]{1,0:T(8,128)(2,1)} %get-tuple-element.41.keep_kv_ref), channel_id=1, source_target_pairs={{0,8},{8,0},{4,12},{12,4},{16,24},{24,16},{20,28},{28,20},{1,9},{9... | collective-permute-start | bytes 589832 | tf_op jit(solution)/shard_map/ppermute | solution.py:272
  13.7 1.0 %copy-start.1 = (bf16[768,128]{1,0:T(8,128)(2,1)S(1)}, bf16[768,128]{1,0:T(8,128)(2,1)}, u32[]{:S(2)}) copy-start(bf16[768,128]{1,0:T(8,128)(2,1)} %get-tuple-element.41.keep_kv_ref) | copy-start | bytes 589828
  14.7 0.9 %copy-start.2 = (bf16[400,128]{1,0:T(8,128)(2,1)S(1)}, bf16[400,128]{1,0:T(8,128)(2,1)}, u32[]{:S(2)}) copy-start(bf16[400,128]{1,0:T(8,128)(2,1)} %get-tuple-element.43.keep_q_ref) | copy-start | bytes 307204
  18.7 11.6 %collective-permute-start.6 = (bf16[768,128]{1,0:T(8,128)(2,1)S(1)}, bf16[768,128]{1,0:T(8,128)(2,1)S(1)}, u32[]{:S(2)}, u32[]{:S(2)}) collective-permute-start(bf16[768,128]{1,0:T(8,128)(2,1)S(1)} %get-tuple-element.54.came_ref), channel_id=1, source_target_pairs={{8,16},{16,8},{12,20},{20,12},{9,17},{17,9},{13,21},{21,13},{10,18... | collective-permute-start | bytes 589832 | tf_op jit(solution)/shard_map/ppermute | solution.py:272
  19.4 11.0 %collective-permute-start.5 = (bf16[768,128]{1,0:T(8,128)(2,1)S(1)}, bf16[768,128]{1,0:T(8,128)(2,1)S(1)}, u32[]{:S(2)}, u32[]{:S(2)}) collective-permute-start(bf16[768,128]{1,0:T(8,128)(2,1)S(1)} %get-tuple-element.54.came_ref), channel_id=1, source_target_pairs={{0,8},{8,0},{4,12},{12,4},{16,24},{24,16},{20,28},{28,20},{1,9},{9... | collective-permute-start | bytes 589832 | tf_op jit(solution)/shard_map/ppermute | solution.py:272
  22.8 12.8 %collective-permute-start.7 = (bf16[768,128]{1,0:T(8,128)(2,1)S(1)}, bf16[768,128]{1,0:T(8,128)(2,1)S(1)}, u32[]{:S(2)}, u32[]{:S(2)}) collective-permute-start(bf16[768,128]{1,0:T(8,128)(2,1)S(1)} %get-tuple-element.57), channel_id=1, source_target_pairs={{0,16},{16,0},{4,20},{20,4},{8,24},{24,8},{12,28},{28,12},{1,17},{... | collective-permute-start | bytes 589832 | tf_op jit(solution)/shard_map/ppermute | solution.py:272
  24.0 22.0 %collective-permute-start.13 = (bf16[256,1408]{1,0:T(8,128)(2,1)S(1)}, bf16[256,1408]{1,0:T(8,128)(2,1)S(1)}, u32[]{:S(2)}, u32[]{:S(2)}) collective-permute-start(bf16[256,1408]{1,0:T(8,128)(2,1)S(1)} %collective-permute-done.4.refs_0_), channel_id=1, source_target_pairs={{0,4},{4,0},{8,12},{12,8},{16,20},{20,16},{24,28},{28,24},{1,5},{5... | collective-permute-start | bytes 2162696 | tf_op jit(solution)/shard_map/ppermute | solution.py:276
  25.8 18.2 %collective-permute-start.11 = (bf16[256,1152]{1,0:T(8,128)(2,1)S(1)}, bf16[256,1152]{1,0:T(8,128)(2,1)S(1)}, u32[]{:S(2)}, u32[]{:S(2)}) collective-permute-start(bf16[256,1152]{1,0:T(8,128)(2,1)S(1)} %shard_map.66), channel_id=1, source_target_pairs={{2,0},{3,1},{0,2},{1,3},{6,4},{7,5},{4,6},{5,7},{10,8},{11,9},{8,1... | collective-permute-start | bytes 1769480 | tf_op jit(solution)/shard_map/ppermute | solution.py:292
  36.5 6.2 %collective-permute-start.8 = (bf16[2,96,128]{2,1,0:T(8,128)(2,1)S(1)}, bf16[2,96,128]{2,1,0:T(8,128)(2,1)S(1)}, u32[]{:S(2)}, u32[]{:S(2)}) collective-permute-start(bf16[2,96,128]{2,1,0:T(8,128)(2,1)S(1)} %get-tuple-element.59), channel_id=1, source_target_pairs={{0,5},{1,4},{2,7},{3,6},{4,1},{5,0},{6,3},{7,2},{8,13},{9,12},{10,... | collective-permute-start | bytes 147464 | tf_op jit(solution)/shard_map/ppermute | solution.py:287
  36.5 7.5 %collective-permute-start.9 = (bf16[2,96,128]{2,1,0:T(8,128)(2,1)S(1)}, bf16[2,96,128]{2,1,0:T(8,128)(2,1)S(1)}, u32[]{:S(2)}, u32[]{:S(2)}) collective-permute-start(bf16[2,96,128]{2,1,0:T(8,128)(2,1)S(1)} %get-tuple-element.60), channel_id=1, source_target_pairs={{0,4},{4,0},{8,12},{12,8},{16,20},{20,16},{24,28},{28,24},{1,5},{5... | collective-permute-start | bytes 147464 | tf_op jit(solution)/shard_map/ppermute | solution.py:276
  37.1 6.9 %collective-permute-start.10 = (bf16[2,96,128]{2,1,0:T(8,128)(2,1)S(1)}, bf16[2,96,128]{2,1,0:T(8,128)(2,1)S(1)}, u32[]{:S(2)}, u32[]{:S(2)}) collective-permute-start(bf16[2,96,128]{2,1,0:T(8,128)(2,1)S(1)} %get-tuple-element.61), channel_id=1, source_target_pairs={{0,1},{1,0},{2,3},{3,2},{4,5},{5,4},{6,7},{7,6},{8,9},{9,8},{10,11... | collective-permute-start | bytes 147464 | tf_op jit(solution)/shard_map/ppermute | solution.py:280
  44.4 8.8 %collective-permute-start.12 = (bf16[96,1664]{1,0:T(8,128)(2,1)S(1)}, bf16[96,1664]{1,0:T(8,128)(2,1)S(1)}, u32[]{:S(2)}, u32[]{:S(2)}) collective-permute-start(bf16[96,1664]{1,0:T(8,128)(2,1)S(1)} %get-tuple-element.70), channel_id=1, source_target_pairs={{2,0},{3,1},{0,2},{1,3},{6,4},{7,5},{4,6},{5,7},{10,8},{11,9},{8,1... | collective-permute-start | bytes 958472 | tf_op jit(solution)/shard_map/ppermute | solution.py:292
  46.0 7.2 %collective-permute-start.16 = (bf16[256,1152]{1,0:T(8,128)(2,1)S(1)}, bf16[256,1152]{1,0:T(8,128)(2,1)S(1)}, u32[]{:S(2)}, u32[]{:S(2)}) collective-permute-start(bf16[256,1152]{1,0:T(8,128)(2,1)S(1)} %collective-permute-done.11.refs_4_), channel_id=1, source_target_pairs={{0,1},{1,0},{2,3},{3,2},{4,5},{5,4},{6,7},{7,6},{8,9},{9,8},{10,11... | collective-permute-start | bytes 1769480 | tf_op jit(solution)/shard_map/ppermute | solution.py:280
  46.0 7.2 %collective-permute-start.14 = (bf16[256,1408]{1,0:T(8,128)(2,1)S(1)}, bf16[256,1408]{1,0:T(8,128)(2,1)S(1)}, u32[]{:S(2)}, u32[]{:S(2)}) collective-permute-start(bf16[256,1408]{1,0:T(8,128)(2,1)S(1)} %collective-permute-done.4.refs_0_), channel_id=1, source_target_pairs={{0,1},{1,0},{2,3},{3,2},{4,5},{5,4},{6,7},{7,6},{8,9},{9,8},{10,11... | collective-permute-start | bytes 2162696 | tf_op jit(solution)/shard_map/ppermute | solution.py:280
  46.5 6.7 %collective-permute-start.15 = (bf16[256,1408]{1,0:T(8,128)(2,1)S(1)}, bf16[256,1408]{1,0:T(8,128)(2,1)S(1)}, u32[]{:S(2)}, u32[]{:S(2)}) collective-permute-start(bf16[256,1408]{1,0:T(8,128)(2,1)S(1)} %collective-permute-done.13.refs_2_), channel_id=1, source_target_pairs={{0,1},{1,0},{2,3},{3,2},{4,5},{5,4},{6,7},{7,6},{8,9},{9,8},{10,11... | collective-permute-start | bytes 2162696 | tf_op jit(solution)/shard_map/ppermute | solution.py:280

commit v9 on v8

--- a/solution.py
+++ b/solution.py
@@ -12,8 +12,8 @@
 REACH = 3
 NEG = -1e30
 FLAGS = 16
-SIDE = 1408
-COMMON = 1152
+SIDE = 1280
+COMMON = 1280
 STATE = HD + 8
 EXPONENT = math.log2(math.e) / math.sqrt(HD)
 BF16, F32 = jnp.bfloat16, jnp.float32

time: 55.1 us -> 53.7 us (0.975)
  waiting for transfers between devices: 18.5 us -> 16.5 us
  Pallas kernels: 11.2 us -> 12.9 us
  starting transfers between devices: 22.3 us -> 21.1 us
    ppermute x1, waiting for transfers between devices: 4.24 us -> 1.84 us  [swap_both(): return lax.ppermute(value, ('ctx', 'head'), pairs)]
    pallas_call x10, Pallas kernels: 11.2 us -> 12.9 us  [call(): pl.pallas_call(kernel, out_shape=outs, in_specs=[SMEM if s else HBM if i...]
    ppermute x3, starting transfers between devices: 3.87 us -> 2.59 us  [swap_tiles(): lax.ppermute(value, 'ctx', [(i, i ^ 1) for i in range(lax.axis_size('ctx'...]
    ppermute x3, waiting for transfers between devices: 5.74 us -> 6.92 us  [from_chip(): lax.ppermute(value, 'head', [((i + 2 * steps) % count, i) for i in range(...]
  transfers between devices with their start and end apart: 17 -> 17, of which waited for: 6 -> 5; matrix products, arithmetic and copies ran while one was open for 0% -> 0% of each run, Pallas kernels for 12% -> 15%
where the time goes in v9:
time: 53.7 us; the launch traced here: 53.2 us
  starting transfers between devices  21.1 us (39%)
  waiting for transfers between devices  16.5 us (31%)
  Pallas kernels  12.9 us (24%)
  local copies, waits for them, and re-layouts  1.86 us (3%)
  between operations  0.93 us (2%)
    pallas_call x10, Pallas kernels, call(): pl.pallas_call(kernel, out_shape=outs, in_specs=[SMEM if s else HBM if i...  12.9 us
    ppermute x5, starting transfers between devices, swap_pairs(): return lax.ppermute(value, 'ctx', pairs)  10.4 us
    ppermute x3, waiting for transfers between devices, from_chip(): lax.ppermute(value, 'head', [((i + 2 * steps) % count, i) for i in range(...  6.92 us
    ppermute x5, waiting for transfers between devices, swap_pairs(): return lax.ppermute(value, 'ctx', pairs)  6.76 us
    ppermute x3, starting transfers between devices, from_chip(): lax.ppermute(value, 'head', [((i + 2 * steps) % count, i) for i in range(...  5.71 us
    ppermute x3, starting transfers between devices, swap_tiles(): lax.ppermute(value, 'ctx', [(i, i ^ 1) for i in range(lax.axis_size('ctx'...  2.59 us
    ppermute x5, starting transfers between devices, swap_cores(): lax.ppermute(value, 'head', [(i, i ^ 1) for i in range(lax.axis_size('hea...  2.31 us
    unnamed x6, local copies, waits for them, and re-layouts  1.86 us
  transfers between devices with their start and end apart: 17, of which 5 were waited for; matrix products, arithmetic and copies ran while one was open for 0% of the time, Pallas kernels for 15%

profile of v9, /device:TPU:0, one launch (start us, length us, event | category | flops | bytes accessed | tf_op | source)
XLA Modules:
  0.0 53.2 jit_solution(12209227461180390262)
XLA Ops:
  0.0 0.0 copy-start
  0.8 3.1 %shard_map.64 = (bf16[400,128]{1,0:T(8,128)(2,1)}, bf16[768,128]{1,0:T(8,128)(2,1)}, bf16[1168,128]{1,0:T(8,128)(2,1)}, bf16[256,1280]{1,0:T(8,128)(2,1)}) custom-call(s32[1]{0:T(128)} %bitcast.tile_ref, s32[1]{0:T(128)} %bitcast.1._.head_ref, s32[1,7]{1,0:T(1,128)} %list_ref.1, s32[1,1]{1,0:T(1,128)} %bitcast.3.count_ref, bf16[384,256]{1,0:T(8,128)(2,1)} %q_ref.1, ...), custom_call_target="tpu_custom_call" | custom-call | bytes 1048576 | tf_op jit(solution)/shard_map/pallas_call | solution.py:30
  4.0 0.0 copy-done
  4.0 0.5 collective-permute-start.1
  4.5 2.6 %collective-permute-start.4 = (bf16[256,1280]{1,0:T(8,128)(2,1)}, bf16[256,1280]{1,0:T(8,128)(2,1)S(1)}, u32[]{:S(2)}, u32[]{:S(2)}) collective-permute-start(bf16[256,1280]{1,0:T(8,128)(2,1)} %get-tuple-element.52), channel_id=1, source_target_pairs={{2,0},{3,1},{0,2},{1,3},{6,4},{7,5},{4,6},{5,7},{10,8},{11,9},{8,1... | collective-permute-start | bytes 1966088 | tf_op jit(solution)/shard_map/ppermute | solution.py:292
  7.0 1.5 %collective-permute-start = (bf16[1168,128]{1,0:T(8,128)(2,1)}, bf16[1168,128]{1,0:T(8,128)(2,1)S(1)}, u32[]{:S(2)}, u32[]{:S(2)}) collective-permute-start(bf16[1168,128]{1,0:T(8,128)(2,1)} %get-tuple-element.40), channel_id=1, source_target_pairs={{0,4},{4,0},{8,12},{12,8},{16,20},{20,16},{24,28},{28,24},{1,5},{5... | collective-permute-start | bytes 897032 | tf_op jit(solution)/shard_map/ppermute | solution.py:276
  8.6 0.7 %collective-permute-start.3 = (bf16[768,128]{1,0:T(8,128)(2,1)}, bf16[768,128]{1,0:T(8,128)(2,1)S(1)}, u32[]{:S(2)}, u32[]{:S(2)}) collective-permute-start(bf16[768,128]{1,0:T(8,128)(2,1)} %get-tuple-element.41.keep_kv_ref), channel_id=1, source_target_pairs={{8,16},{16,8},{12,20},{20,12},{9,17},{17,9},{13,21},{21,13},{10,18... | collective-permute-start | bytes 589832 | tf_op jit(solution)/shard_map/ppermute | solution.py:272
  9.2 4.5 %collective-permute-start.2 = (bf16[768,128]{1,0:T(8,128)(2,1)}, bf16[768,128]{1,0:T(8,128)(2,1)S(1)}, u32[]{:S(2)}, u32[]{:S(2)}) collective-permute-start(bf16[768,128]{1,0:T(8,128)(2,1)} %get-tuple-element.41.keep_kv_ref), channel_id=1, source_target_pairs={{0,8},{8,0},{4,12},{12,4},{16,24},{24,16},{20,28},{28,20},{1,9},{9... | collective-permute-start | bytes 589832 | tf_op jit(solution)/shard_map/ppermute | solution.py:272
  13.7 0.0 copy-start.1
  13.7 1.0 %copy-done.1 = bf16[768,128]{1,0:T(8,128)(2,1)S(1)} copy-done((bf16[768,128]{1,0:T(8,128)(2,1)S(1)}, bf16[768,128]{1,0:T(8,128)(2,1)}, u32[]{:S(2)}) %copy-start.1) | copy-done | bytes 196632
  14.7 0.0 copy-start.2
  14.7 0.9 %copy-done.2 = bf16[400,128]{1,0:T(8,128)(2,1)S(1)} copy-done((bf16[400,128]{1,0:T(8,128)(2,1)S(1)}, bf16[400,128]{1,0:T(8,128)(2,1)}, u32[]{:S(2)}) %copy-start.2) | copy-done | bytes 102424
  15.6 0.0 collective-permute-done.3.kept_second_ref
  15.6 2.9 %collective-permute-done.2.kept_first_ref = bf16[768,128]{1,0:T(8,128)(2,1)S(1)} collective-permute-done((bf16[768,128]{1,0:T(8,128)(2,1)}, bf16[768,128]{1,0:T(8,128)(2,1)S(1)}, u32[]{:S(2)}, u32[]{:S(2)}) %collective-permute-start.2) | collective-permute-done | bytes 196640 | tf_op jit(solution)/shard_map/ppermute | solution.py:272
  18.6 0.0 collective-permute-done.came_ref
  18.6 0.0 collective-permute-done.1.wp_ref
  18.6 0.7 %collective-permute-start.6 = (bf16[768,128]{1,0:T(8,128)(2,1)S(1)}, bf16[768,128]{1,0:T(8,128)(2,1)S(1)}, u32[]{:S(2)}, u32[]{:S(2)}) collective-permute-start(bf16[768,128]{1,0:T(8,128)(2,1)S(1)} %get-tuple-element.54.came_ref), channel_id=1, source_target_pairs={{8,16},{16,8},{12,20},{20,12},{9,17},{17,9},{13,21},{21,13},{10,18... | collective-permute-start | bytes 589832 | tf_op jit(solution)/shard_map/ppermute | solution.py:272
  19.3 3.5 %collective-permute-start.5 = (bf16[768,128]{1,0:T(8,128)(2,1)S(1)}, bf16[768,128]{1,0:T(8,128)(2,1)S(1)}, u32[]{:S(2)}, u32[]{:S(2)}) collective-permute-start(bf16[768,128]{1,0:T(8,128)(2,1)S(1)} %get-tuple-element.54.came_ref), channel_id=1, source_target_pairs={{0,8},{8,0},{4,12},{12,4},{16,24},{24,16},{20,28},{28,20},{1,9},{9... | collective-permute-start | bytes 589832 | tf_op jit(solution)/shard_map/ppermute | solution.py:272
  22.8 1.1 %collective-permute-start.7 = (bf16[768,128]{1,0:T(8,128)(2,1)S(1)}, bf16[768,128]{1,0:T(8,128)(2,1)S(1)}, u32[]{:S(2)}, u32[]{:S(2)}) collective-permute-start(bf16[768,128]{1,0:T(8,128)(2,1)S(1)} %get-tuple-element.57), channel_id=1, source_target_pairs={{0,16},{16,0},{4,20},{20,4},{8,24},{24,8},{12,28},{28,12},{1,17},{... | collective-permute-start | bytes 589832 | tf_op jit(solution)/shard_map/ppermute | solution.py:272
  23.9 0.0 collective-permute-done.4.refs_0_
  23.9 0.5 collective-permute-start.13
  24.4 1.5 %collective-permute-start.11 = (bf16[256,1280]{1,0:T(8,128)(2,1)S(1)}, bf16[256,1280]{1,0:T(8,128)(2,1)S(1)}, u32[]{:S(2)}, u32[]{:S(2)}) collective-permute-start(bf16[256,1280]{1,0:T(8,128)(2,1)S(1)} %shard_map.66), channel_id=1, source_target_pairs={{2,0},{3,1},{0,2},{1,3},{6,4},{7,5},{4,6},{5,7},{10,8},{11,9},{8,1... | collective-permute-start | bytes 1966088 | tf_op jit(solution)/shard_map/ppermute | solution.py:292
  25.9 4.1 %shard_map.68._ = f32[2,136,384]{2,1,0:T(8,128)S(1)} custom-call(s32[8,128]{1,0:T(8,128)S(1)} %get-tuple-element.50.flag_ref, s32[1]{0:T(128)} %bitcast.tile_ref, bf16[2,384,128]{2,1,0:T(8,128)(2,1)S(1)} %get-tuple-element.53.q_ref, bf16[768,128]{1,0:T(8,128)(2,1)S(1)} %get-tuple-element.48.keep_kv_ref.own_ref, ...), custom_call_target="tpu_custom_call" | custom-call | flops 603979776 | bytes 1048576 | tf_op jit(solution)/shard_map/pallas_call | solution.py:30
  30.0 0.0 collective-permute-done.6.second_ref
  30.0 0.0 collective-permute-done.5.first_ref
  30.0 1.8 %shard_map.69.state_ref = f32[2,136,384]{2,1,0:T(8,128)S(1)} custom-call(s32[8,128]{1,0:T(8,128)S(1)} %get-tuple-element.50.flag_ref, s32[1]{0:T(128)} %bitcast.tile_ref, bf16[2,384,128]{2,1,0:T(8,128)(2,1)S(1)} %get-tuple-element.53.q_ref, bf16[768,128]{1,0:T(8,128)(2,1)S(1)} %collective-permute-done.5.first_ref, ...), custom_call_target="tpu_custom_call", output_to_operand_aliasing={{}: (5, {})} | custom-call | flops 301989888 | bytes 1048576 | tf_op jit(solution)/shard_map/pallas_call | solution.py:30
  31.8 3.8 %collective-permute-done.7.refs_0_ = bf16[768,128]{1,0:T(8,128)(2,1)S(1)} collective-permute-done((bf16[768,128]{1,0:T(8,128)(2,1)S(1)}, bf16[768,128]{1,0:T(8,128)(2,1)S(1)}, u32[]{:S(2)}, u32[]{:S(2)}) %collective-permute-start.7) | collective-permute-done | bytes 196640 | tf_op jit(solution)/shard_map/ppermute | solution.py:272
  35.6 0.8 %shard_map.70 = (bf16[2,96,128]{2,1,0:T(8,128)(2,1)S(1)}, bf16[2,96,128]{2,1,0:T(8,128)(2,1)S(1)}, bf16[2,96,128]{2,1,0:T(8,128)(2,1)S(1)}, bf16[2,96,128]{2,1,0:T(8,128)(2,1)S(1)}, f32[2,136,384]{2,1,0:T(8,128)S(1)}) custom-call(s32[8,128]{1,0:T(8,128)S(1)} %get-tuple-element.50.flag_ref, s32[1]{0:T(128)} %bitcast.tile_ref, ...), custom_call_target="tpu_custom_call", output_to_operand_aliasing={{4}: (4, {})} | custom-call | flops 5662310400 | bytes 1048576 | tf_op jit(solution)/shard_map/pallas_call | solution.py:30
  36.4 0.1 collective-permute-start.8
  36.5 0.6 %collective-permute-start.9 = (bf16[2,96,128]{2,1,0:T(8,128)(2,1)S(1)}, bf16[2,96,128]{2,1,0:T(8,128)(2,1)S(1)}, u32[]{:S(2)}, u32[]{:S(2)}) collective-permute-start(bf16[2,96,128]{2,1,0:T(8,128)(2,1)S(1)} %get-tuple-element.60), channel_id=1, source_target_pairs={{0,4},{4,0},{8,12},{12,8},{16,20},{20,16},{24,28},{28,24},{1,5},{5... | collective-permute-start | bytes 147464 | tf_op jit(solution)/shard_map/ppermute | solution.py:276
  37.1 1.3 %collective-permute-start.10 = (bf16[2,96,128]{2,1,0:T(8,128)(2,1)S(1)}, bf16[2,96,128]{2,1,0:T(8,128)(2,1)S(1)}, u32[]{:S(2)}, u32[]{:S(2)}) collective-permute-start(bf16[2,96,128]{2,1,0:T(8,128)(2,1)S(1)} %get-tuple-element.61), channel_id=1, source_target_pairs={{0,1},{1,0},{2,3},{3,2},{4,5},{5,4},{6,7},{7,6},{8,9},{9,8},{10,11... | collective-permute-start | bytes 147464 | tf_op jit(solution)/shard_map/ppermute | solution.py:280
  38.3 1.8 %collective-permute-done.8.cross_ref = bf16[2,96,128]{2,1,0:T(8,128)(2,1)S(1)} collective-permute-done((bf16[2,96,128]{2,1,0:T(8,128)(2,1)S(1)}, bf16[2,96,128]{2,1,0:T(8,128)(2,1)S(1)}, u32[]{:S(2)}, u32[]{:S(2)}) %collective-permute-start.8) | collective-permute-done | bytes 49184 | tf_op jit(solution)/shard_map/ppermute | solution.py:287
  40.2 0.9 %collective-permute-done.9.y_ref = bf16[2,96,128]{2,1,0:T(8,128)(2,1)S(1)} collective-permute-done((bf16[2,96,128]{2,1,0:T(8,128)(2,1)S(1)}, bf16[2,96,128]{2,1,0:T(8,128)(2,1)S(1)}, u32[]{:S(2)}, u32[]{:S(2)}) %collective-permute-start.9) | collective-permute-done | bytes 49184 | tf_op jit(solution)/shard_map/ppermute | solution.py:276
  41.1 0.0 collective-permute-done.10.core_ref
  41.1 0.0 collective-permute-done.11.refs_4_
  41.1 0.4 shard_map.71
  41.5 1.7 %collective-permute-start.12 = (bf16[96,1792]{1,0:T(8,128)(2,1)S(1)}, bf16[96,1792]{1,0:T(8,128)(2,1)S(1)}, u32[]{:S(2)}, u32[]{:S(2)}) collective-permute-start(bf16[96,1792]{1,0:T(8,128)(2,1)S(1)} %get-tuple-element.70), channel_id=1, source_target_pairs={{2,0},{3,1},{0,2},{1,3},{6,4},{7,5},{4,6},{5,7},{10,8},{11,9},{8,1... | collective-permute-start | bytes 1032200 | tf_op jit(solution)/shard_map/ppermute | solution.py:292
  43.2 0.0 collective-permute-done.13.refs_2_
  43.2 0.0 collective-permute-start.14
  43.2 0.5 collective-permute-start.15
  43.7 0.0 collective-permute-start.16
  43.7 1.0 %shard_map.72.near_ref = f32[96,5120]{1,0:T(8,128)S(1)} custom-call(bf16[96,512]{1,0:T(8,128)(2,1)S(1)} %get-tuple-element.69.a_ref, bf16[256,5120]{1,0:T(8,128)(2,1)S(1)} %copy-done, bf16[256,5120]{1,0:T(8,128)(2,1)S(1)} %collective-permute-done.1.wp_ref), custom_call_target="tpu_custom_call" | custom-call | flops 15099494400 | bytes 1048576 | tf_op jit(solution)/shard_map/pallas_call | solution.py:30
  44.7 6.9 %collective-permute-done.12.far_ref = bf16[96,1792]{1,0:T(8,128)(2,1)S(1)} collective-permute-done((bf16[96,1792]{1,0:T(8,128)(2,1)S(1)}, bf16[96,1792]{1,0:T(8,128)(2,1)S(1)}, u32[]{:S(2)}, u32[]{:S(2)}) %collective-permute-start.12) | collective-permute-done | bytes 344096 | tf_op jit(solution)/shard_map/ppermute | solution.py:292
  51.7 0.0 collective-permute-done.14.refs_1_
  51.7 0.0 collective-permute-done.15.refs_3_
  51.7 0.0 collective-permute-done.16.refs_5_
  51.7 1.6 %shard_map.73 = bf16[96,5120]{1,0:T(8,128)(2,1)} custom-call(s32[1]{0:T(128)} %bitcast.tile_ref, f32[96,5120]{1,0:T(8,128)S(1)} %shard_map.72.near_ref, bf16[96,1792]{1,0:T(8,128)(2,1)S(1)} %collective-permute-done.12.far_ref, bf16[256,1280]{1,0:T(8,128)(2,1)S(1)} %collective-permute-done.4.refs_0_, bf16[256,1280]{1,0:T(8,128)(2,1)S(1)} %collective-permute-done.14.refs_1_, ...), custom_call_target="tpu_custom_call" | custom-call | flops 503316480 | bytes 1048576 | tf_op jit(solution)/shard_map/pallas_call | solution.py:30
  (3 shorter events, 0.1 us)
Async XLA Ops:
  0.0 4.0 %copy-start = (bf16[256,5120]{1,0:T(8,128)(2,1)S(1)}, bf16[256,5120]{1,0:T(8,128)(2,1)}, u32[]{:S(2)}) copy-start(bf16[256,5120]{1,0:T(8,128)(2,1)} %w_ref.6) | copy-start | bytes 7864324
  4.0 14.6 %collective-permute-start.1 = (bf16[256,5120]{1,0:T(8,128)(2,1)S(1)}, bf16[256,5120]{1,0:T(8,128)(2,1)S(1)}, u32[]{:S(2)}, u32[]{:S(2)}) collective-permute-start(bf16[256,5120]{1,0:T(8,128)(2,1)S(1)} %copy-done), channel_id=1, source_target_pairs={{0,1},{1,0},{2,3},{3,2},{4,5},{5,4},{6,7},{7,6},{8,9},{9,8},{10,11... | collective-permute-start | bytes 7864328 | tf_op jit(solution)/shard_map/ppermute | solution.py:280
  4.5 19.4 %collective-permute-start.4 = (bf16[256,1280]{1,0:T(8,128)(2,1)}, bf16[256,1280]{1,0:T(8,128)(2,1)S(1)}, u32[]{:S(2)}, u32[]{:S(2)}) collective-permute-start(bf16[256,1280]{1,0:T(8,128)(2,1)} %get-tuple-element.52), channel_id=1, source_target_pairs={{2,0},{3,1},{0,2},{1,3},{6,4},{7,5},{4,6},{5,7},{10,8},{11,9},{8,1... | collective-permute-start | bytes 1966088 | tf_op jit(solution)/shard_map/ppermute | solution.py:292
  7.0 11.5 %collective-permute-start = (bf16[1168,128]{1,0:T(8,128)(2,1)}, bf16[1168,128]{1,0:T(8,128)(2,1)S(1)}, u32[]{:S(2)}, u32[]{:S(2)}) collective-permute-start(bf16[1168,128]{1,0:T(8,128)(2,1)} %get-tuple-element.40), channel_id=1, source_target_pairs={{0,4},{4,0},{8,12},{12,8},{16,20},{20,16},{24,28},{28,24},{1,5},{5... | collective-permute-start | bytes 897032 | tf_op jit(solution)/shard_map/ppermute | solution.py:276
  8.6 7.1 %collective-permute-start.3 = (bf16[768,128]{1,0:T(8,128)(2,1)}, bf16[768,128]{1,0:T(8,128)(2,1)S(1)}, u32[]{:S(2)}, u32[]{:S(2)}) collective-permute-start(bf16[768,128]{1,0:T(8,128)(2,1)} %get-tuple-element.41.keep_kv_ref), channel_id=1, source_target_pairs={{8,16},{16,8},{12,20},{20,12},{9,17},{17,9},{13,21},{21,13},{10,18... | collective-permute-start | bytes 589832 | tf_op jit(solution)/shard_map/ppermute | solution.py:272
  9.2 9.3 %collective-permute-start.2 = (bf16[768,128]{1,0:T(8,128)(2,1)}, bf16[768,128]{1,0:T(8,128)(2,1)S(1)}, u32[]{:S(2)}, u32[]{:S(2)}) collective-permute-start(bf16[768,128]{1,0:T(8,128)(2,1)} %get-tuple-element.41.keep_kv_ref), channel_id=1, source_target_pairs={{0,8},{8,0},{4,12},{12,4},{16,24},{24,16},{20,28},{28,20},{1,9},{9... | collective-permute-start | bytes 589832 | tf_op jit(solution)/shard_map/ppermute | solution.py:272
  13.7 1.0 %copy-start.1 = (bf16[768,128]{1,0:T(8,128)(2,1)S(1)}, bf16[768,128]{1,0:T(8,128)(2,1)}, u32[]{:S(2)}) copy-start(bf16[768,128]{1,0:T(8,128)(2,1)} %get-tuple-element.41.keep_kv_ref) | copy-start | bytes 589828
  14.7 0.9 %copy-start.2 = (bf16[400,128]{1,0:T(8,128)(2,1)S(1)}, bf16[400,128]{1,0:T(8,128)(2,1)}, u32[]{:S(2)}) copy-start(bf16[400,128]{1,0:T(8,128)(2,1)} %get-tuple-element.43.keep_q_ref) | copy-start | bytes 307204
  18.6 11.4 %collective-permute-start.6 = (bf16[768,128]{1,0:T(8,128)(2,1)S(1)}, bf16[768,128]{1,0:T(8,128)(2,1)S(1)}, u32[]{:S(2)}, u32[]{:S(2)}) collective-permute-start(bf16[768,128]{1,0:T(8,128)(2,1)S(1)} %get-tuple-element.54.came_ref), channel_id=1, source_target_pairs={{8,16},{16,8},{12,20},{20,12},{9,17},{17,9},{13,21},{21,13},{10,18... | collective-permute-start | bytes 589832 | tf_op jit(solution)/shard_map/ppermute | solution.py:272
  19.3 10.7 %collective-permute-start.5 = (bf16[768,128]{1,0:T(8,128)(2,1)S(1)}, bf16[768,128]{1,0:T(8,128)(2,1)S(1)}, u32[]{:S(2)}, u32[]{:S(2)}) collective-permute-start(bf16[768,128]{1,0:T(8,128)(2,1)S(1)} %get-tuple-element.54.came_ref), channel_id=1, source_target_pairs={{0,8},{8,0},{4,12},{12,4},{16,24},{24,16},{20,28},{28,20},{1,9},{9... | collective-permute-start | bytes 589832 | tf_op jit(solution)/shard_map/ppermute | solution.py:272
  22.8 12.8 %collective-permute-start.7 = (bf16[768,128]{1,0:T(8,128)(2,1)S(1)}, bf16[768,128]{1,0:T(8,128)(2,1)S(1)}, u32[]{:S(2)}, u32[]{:S(2)}) collective-permute-start(bf16[768,128]{1,0:T(8,128)(2,1)S(1)} %get-tuple-element.57), channel_id=1, source_target_pairs={{0,16},{16,0},{4,20},{20,4},{8,24},{24,8},{12,28},{28,12},{1,17},{... | collective-permute-start | bytes 589832 | tf_op jit(solution)/shard_map/ppermute | solution.py:272
  23.9 19.3 %collective-permute-start.13 = (bf16[256,1280]{1,0:T(8,128)(2,1)S(1)}, bf16[256,1280]{1,0:T(8,128)(2,1)S(1)}, u32[]{:S(2)}, u32[]{:S(2)}) collective-permute-start(bf16[256,1280]{1,0:T(8,128)(2,1)S(1)} %collective-permute-done.4.refs_0_), channel_id=1, source_target_pairs={{0,4},{4,0},{8,12},{12,8},{16,20},{20,16},{24,28},{28,24},{1,5},{5... | collective-permute-start | bytes 1966088 | tf_op jit(solution)/shard_map/ppermute | solution.py:276
  24.4 16.7 %collective-permute-start.11 = (bf16[256,1280]{1,0:T(8,128)(2,1)S(1)}, bf16[256,1280]{1,0:T(8,128)(2,1)S(1)}, u32[]{:S(2)}, u32[]{:S(2)}) collective-permute-start(bf16[256,1280]{1,0:T(8,128)(2,1)S(1)} %shard_map.66), channel_id=1, source_target_pairs={{2,0},{3,1},{0,2},{1,3},{6,4},{7,5},{4,6},{5,7},{10,8},{11,9},{8,1... | collective-permute-start | bytes 1966088 | tf_op jit(solution)/shard_map/ppermute | solution.py:292
  36.4 3.8 %collective-permute-start.8 = (bf16[2,96,128]{2,1,0:T(8,128)(2,1)S(1)}, bf16[2,96,128]{2,1,0:T(8,128)(2,1)S(1)}, u32[]{:S(2)}, u32[]{:S(2)}) collective-permute-start(bf16[2,96,128]{2,1,0:T(8,128)(2,1)S(1)} %get-tuple-element.59), channel_id=1, source_target_pairs={{0,5},{1,4},{2,7},{3,6},{4,1},{5,0},{6,3},{7,2},{8,13},{9,12},{10,... | collective-permute-start | bytes 147464 | tf_op jit(solution)/shard_map/ppermute | solution.py:287
  36.5 4.6 %collective-permute-start.9 = (bf16[2,96,128]{2,1,0:T(8,128)(2,1)S(1)}, bf16[2,96,128]{2,1,0:T(8,128)(2,1)S(1)}, u32[]{:S(2)}, u32[]{:S(2)}) collective-permute-start(bf16[2,96,128]{2,1,0:T(8,128)(2,1)S(1)} %get-tuple-element.60), channel_id=1, source_target_pairs={{0,4},{4,0},{8,12},{12,8},{16,20},{20,16},{24,28},{28,24},{1,5},{5... | collective-permute-start | bytes 147464 | tf_op jit(solution)/shard_map/ppermute | solution.py:276
  37.1 4.1 %collective-permute-start.10 = (bf16[2,96,128]{2,1,0:T(8,128)(2,1)S(1)}, bf16[2,96,128]{2,1,0:T(8,128)(2,1)S(1)}, u32[]{:S(2)}, u32[]{:S(2)}) collective-permute-start(bf16[2,96,128]{2,1,0:T(8,128)(2,1)S(1)} %get-tuple-element.61), channel_id=1, source_target_pairs={{0,1},{1,0},{2,3},{3,2},{4,5},{5,4},{6,7},{7,6},{8,9},{9,8},{10,11... | collective-permute-start | bytes 147464 | tf_op jit(solution)/shard_map/ppermute | solution.py:280
  41.5 10.1 %collective-permute-start.12 = (bf16[96,1792]{1,0:T(8,128)(2,1)S(1)}, bf16[96,1792]{1,0:T(8,128)(2,1)S(1)}, u32[]{:S(2)}, u32[]{:S(2)}) collective-permute-start(bf16[96,1792]{1,0:T(8,128)(2,1)S(1)} %get-tuple-element.70), channel_id=1, source_target_pairs={{2,0},{3,1},{0,2},{1,3},{6,4},{7,5},{4,6},{5,7},{10,8},{11,9},{8,1... | collective-permute-start | bytes 1032200 | tf_op jit(solution)/shard_map/ppermute | solution.py:292
  43.2 8.5 %collective-permute-start.14 = (bf16[256,1280]{1,0:T(8,128)(2,1)S(1)}, bf16[256,1280]{1,0:T(8,128)(2,1)S(1)}, u32[]{:S(2)}, u32[]{:S(2)}) collective-permute-start(bf16[256,1280]{1,0:T(8,128)(2,1)S(1)} %collective-permute-done.4.refs_0_), channel_id=1, source_target_pairs={{0,1},{1,0},{2,3},{3,2},{4,5},{5,4},{6,7},{7,6},{8,9},{9,8},{10,11... | collective-permute-start | bytes 1966088 | tf_op jit(solution)/shard_map/ppermute | solution.py:280
  43.2 8.5 %collective-permute-start.15 = (bf16[256,1280]{1,0:T(8,128)(2,1)S(1)}, bf16[256,1280]{1,0:T(8,128)(2,1)S(1)}, u32[]{:S(2)}, u32[]{:S(2)}) collective-permute-start(bf16[256,1280]{1,0:T(8,128)(2,1)S(1)} %collective-permute-done.13.refs_2_), channel_id=1, source_target_pairs={{0,1},{1,0},{2,3},{3,2},{4,5},{5,4},{6,7},{7,6},{8,9},{9,8},{10,11... | collective-permute-start | bytes 1966088 | tf_op jit(solution)/shard_map/ppermute | solution.py:280
  43.7 8.0 %collective-permute-start.16 = (bf16[256,1280]{1,0:T(8,128)(2,1)S(1)}, bf16[256,1280]{1,0:T(8,128)(2,1)S(1)}, u32[]{:S(2)}, u32[]{:S(2)}) collective-permute-start(bf16[256,1280]{1,0:T(8,128)(2,1)S(1)} %collective-permute-done.11.refs_4_), channel_id=1, source_target_pairs={{0,1},{1,0},{2,3},{3,2},{4,5},{5,4},{6,7},{7,6},{8,9},{9,8},{10,11... | collective-permute-start | bytes 1966088 | tf_op jit(solution)/shard_map/ppermute | solution.py:280

commit v10 on v9

--- a/solution.py
+++ b/solution.py
@@ -45,25 +45,30 @@
 
 def pack_kernel(
     tile_ref, _, list_ref, count_ref, q_ref, k_ref, v_ref, w_ref,
-    keep_q_ref, keep_kv_ref, send_ref, side_ref, sems,
+    keep_q_ref, keep_kv_ref, send_ref, side_ref,
+    keep_q, keep_kv, send, side, in_sems, out_sems,
 ):
     parity = tile_ref[0] & 1
     rows = q_ref.shape[0]
-    copies = []
-
-    def copy(source, target):
-        copies.append(pltpu.make_async_copy(source, target, sems.at[len(copies)]))
-        copies[-1].start()
-
-    for head, kv_out, q_out, q_at in (
-        (1 - parity, send_ref, send_ref, 2 * rows),
-        (parity, keep_kv_ref, keep_q_ref, 0),
-    ):
+    reads, writes = [], []
+
+    def read(source, target):
+        reads.append(pltpu.make_async_copy(source, target, in_sems.at[len(reads)]))
+        reads[-1].start()
+
+    def write(count, source, target):
+        for each in reads[len(reads) - left[0] :][:count]:
+            each.wait()
+        left[0] -= count
+        writes.append(pltpu.make_async_copy(source, target, out_sems.at[len(writes)]))
+        writes[-1].start()
+
+    for head, kv_out, q_out, q_at in ((1 - parity, send, send, 2 * rows), (parity, keep_kv, keep_q, 0)):
         columns = pl.ds(pl.multiple_of(head * HD, HD), HD)
         for ref, out, at in ((k_ref, kv_out, 0), (v_ref, kv_out, rows), (q_ref, q_out, q_at)):
-            copy(ref.at[:, columns], out.at[pl.ds(at, rows)])
-    side = side_ref.shape[1]
-    copy(w_ref.at[:, pl.ds(pl.multiple_of(parity * side, HD), side)], side_ref)
+            read(ref.at[:, columns], out.at[pl.ds(at, rows)])
+    width = side.shape[1]
+    read(w_ref.at[:, pl.ds(pl.multiple_of(parity * width, HD), width)], side)
     lane = lax.broadcasted_iota(jnp.int32, (FLAGS, HD), 1)
     flags = jnp.zeros((FLAGS, HD), F32)
     for offset in range(-REACH, REACH + 1):
@@ -72,9 +77,14 @@
             found = (list_ref[0, slot] == tile_ref[0] + offset) & (slot < count_ref[0, 0])
             listed = jnp.where(found, 1, listed)
         flags = jnp.where(lane == offset + REACH, listed.astype(F32), flags)
-    keep_q_ref[rows:, :] = flags.astype(BF16)
-    send_ref[3 * rows :, :] = flags.astype(BF16)
-    for each in copies:
+    keep_q[rows:, :] = flags.astype(BF16)
+    send[3 * rows :, :] = flags.astype(BF16)
+    left = [len(reads)]
+    write(3, send, send_ref)
+    write(2, keep_kv, keep_kv_ref)
+    write(1, keep_q, keep_q_ref)
+    write(1, side, side_ref)
+    for each in writes:
         each.wait()
 
 
@@ -323,12 +333,15 @@
 
     one = (rows, HD)
     payload, kv_shape = shape((3 * rows + FLAGS, HD)), shape((2 * rows, HD))
+    packed = (shape((rows + FLAGS, HD)), kv_shape, payload, shape((width, SIDE)))
     keep_q, keep_kv, send, side_weight = call(
         pack_kernel,
-        (shape((rows + FLAGS, HD)), kv_shape, payload, shape((width, SIDE))),
+        packed,
         (tile, head, neighbours, counts.reshape(1, 1), queries, keys, values, out_weight),
-        scratch=(pltpu.SemaphoreType.DMA((7,)),),
+        scratch=[pltpu.VMEM(each.shape, each.dtype) for each in packed]
+        + [pltpu.SemaphoreType.DMA((7,)), pltpu.SemaphoreType.DMA((4,))],
         in_hbm=(4, 5, 6, 7),
+        out_hbm=True,
         vmem=58,
     )
     weight_ready, _ = lax.optimization_barrier((out_weight, keep_kv))

time: 53.7 us -> 53.5 us (level)
  waiting for transfers between devices: 16.5 us -> 18.5 us
  Pallas kernels: 12.9 us -> 11.6 us
    ppermute x5, waiting for transfers between devices: 6.76 us -> 8.48 us  [swap_pairs(): return lax.ppermute(value, 'ctx', pairs)]
    pallas_call x10, Pallas kernels: 12.9 us -> 11.6 us  [call(): pl.pallas_call(kernel, out_shape=outs, in_specs=[SMEM if s else HBM if i...]
  transfers between devices with their start and end apart: 17 -> 17, of which waited for: 5 -> 5; matrix products, arithmetic and copies ran while one was open for 0% -> 0% of each run, Pallas kernels for 15% -> 13%
where the time goes in v10:
time: 53.5 us
  starting transfers between devices  20.6 us (39%)
  waiting for transfers between devices  18.5 us (35%)
  Pallas kernels  11.6 us (22%)
  local copies, waits for them, and re-layouts  1.86 us (3%)
  between operations  0.93 us (2%)
    pallas_call x10, Pallas kernels, call(): pl.pallas_call(kernel, out_shape=outs, in_specs=[SMEM if s else HBM if i...  11.6 us
    ppermute x5, starting transfers between devices, swap_pairs(): return lax.ppermute(value, 'ctx', pairs)  10.4 us
    ppermute x5, waiting for transfers between devices, swap_pairs(): return lax.ppermute(value, 'ctx', pairs)  8.48 us
    ppermute x3, waiting for transfers between devices, from_chip(): lax.ppermute(value, 'head', [((i + 2 * steps) % count, i) for i in range(...  7.34 us
    ppermute x3, starting transfers between devices, from_chip(): lax.ppermute(value, 'head', [((i + 2 * steps) % count, i) for i in range(...  5.21 us
    ppermute x3, starting transfers between devices, swap_tiles(): lax.ppermute(value, 'ctx', [(i, i ^ 1) for i in range(lax.axis_size('ctx'...  2.59 us
    ppermute x5, starting transfers between devices, swap_cores(): lax.ppermute(value, 'head', [(i, i ^ 1) for i in range(lax.axis_size('hea...  2.31 us
    unnamed x6, local copies, waits for them, and re-layouts  1.86 us
  transfers between devices with their start and end apart: 17, of which 5 were waited for; matrix products, arithmetic and copies ran while one was open for 0% of the time, Pallas kernels for 13%

profile of v10, /device:TPU:0, one launch (start us, length us, event | category | flops | bytes accessed | tf_op | source)
XLA Modules:
  0.0 53.5 jit_solution(6320670031979175051)
XLA Ops:
  0.0 0.0 copy-start
  0.8 3.0 %shard_map.64 = (bf16[400,128]{1,0:T(8,128)(2,1)}, bf16[768,128]{1,0:T(8,128)(2,1)}, bf16[1168,128]{1,0:T(8,128)(2,1)}, bf16[256,1280]{1,0:T(8,128)(2,1)}) custom-call(s32[1]{0:T(128)} %bitcast.tile_ref, s32[1]{0:T(128)} %bitcast.1._.head_ref, s32[1,7]{1,0:T(1,128)} %list_ref.1, s32[1,1]{1,0:T(1,128)} %bitcast.3.count_ref, bf16[384,256]{1,0:T(8,128)(2,1)} %q_ref.1, ...), custom_call_target="tpu_custom_call" | custom-call | bytes 1048576 | tf_op jit(solution)/shard_map/pallas_call | solution.py:30
  3.8 0.0 copy-done
  3.8 0.5 collective-permute-start.1
  4.3 2.6 %collective-permute-start.4 = (bf16[256,1280]{1,0:T(8,128)(2,1)}, bf16[256,1280]{1,0:T(8,128)(2,1)S(1)}, u32[]{:S(2)}, u32[]{:S(2)}) collective-permute-start(bf16[256,1280]{1,0:T(8,128)(2,1)} %get-tuple-element.52), channel_id=1, source_target_pairs={{2,0},{3,1},{0,2},{1,3},{6,4},{7,5},{4,6},{5,7},{10,8},{11,9},{8,1... | collective-permute-start | bytes 1966088 | tf_op jit(solution)/shard_map/ppermute | solution.py:302
  6.9 1.5 %collective-permute-start = (bf16[1168,128]{1,0:T(8,128)(2,1)}, bf16[1168,128]{1,0:T(8,128)(2,1)S(1)}, u32[]{:S(2)}, u32[]{:S(2)}) collective-permute-start(bf16[1168,128]{1,0:T(8,128)(2,1)} %get-tuple-element.40), channel_id=1, source_target_pairs={{0,4},{4,0},{8,12},{12,8},{16,20},{20,16},{24,28},{28,24},{1,5},{5... | collective-permute-start | bytes 897032 | tf_op jit(solution)/shard_map/ppermute | solution.py:286
  8.4 0.7 %collective-permute-start.3 = (bf16[768,128]{1,0:T(8,128)(2,1)}, bf16[768,128]{1,0:T(8,128)(2,1)S(1)}, u32[]{:S(2)}, u32[]{:S(2)}) collective-permute-start(bf16[768,128]{1,0:T(8,128)(2,1)} %get-tuple-element.41.keep_kv_ref), channel_id=1, source_target_pairs={{8,16},{16,8},{12,20},{20,12},{9,17},{17,9},{13,21},{21,13},{10,18... | collective-permute-start | bytes 589832 | tf_op jit(solution)/shard_map/ppermute | solution.py:282
  9.1 4.5 %collective-permute-start.2 = (bf16[768,128]{1,0:T(8,128)(2,1)}, bf16[768,128]{1,0:T(8,128)(2,1)S(1)}, u32[]{:S(2)}, u32[]{:S(2)}) collective-permute-start(bf16[768,128]{1,0:T(8,128)(2,1)} %get-tuple-element.41.keep_kv_ref), channel_id=1, source_target_pairs={{0,8},{8,0},{4,12},{12,4},{16,24},{24,16},{20,28},{28,20},{1,9},{9... | collective-permute-start | bytes 589832 | tf_op jit(solution)/shard_map/ppermute | solution.py:282
  13.5 0.0 copy-start.1
  13.5 1.0 %copy-done.1 = bf16[768,128]{1,0:T(8,128)(2,1)S(1)} copy-done((bf16[768,128]{1,0:T(8,128)(2,1)S(1)}, bf16[768,128]{1,0:T(8,128)(2,1)}, u32[]{:S(2)}) %copy-start.1) | copy-done | bytes 196632
  14.5 0.0 copy-start.2
  14.5 0.9 %copy-done.2 = bf16[400,128]{1,0:T(8,128)(2,1)S(1)} copy-done((bf16[400,128]{1,0:T(8,128)(2,1)S(1)}, bf16[400,128]{1,0:T(8,128)(2,1)}, u32[]{:S(2)}) %copy-start.2) | copy-done | bytes 102424
  15.5 0.0 collective-permute-done.3.kept_second_ref
  15.5 2.9 %collective-permute-done.2.kept_first_ref = bf16[768,128]{1,0:T(8,128)(2,1)S(1)} collective-permute-done((bf16[768,128]{1,0:T(8,128)(2,1)}, bf16[768,128]{1,0:T(8,128)(2,1)S(1)}, u32[]{:S(2)}, u32[]{:S(2)}) %collective-permute-start.2) | collective-permute-done | bytes 196640 | tf_op jit(solution)/shard_map/ppermute | solution.py:282
  18.4 0.0 collective-permute-done.came_ref
  18.4 0.0 collective-permute-done.1.wp_ref
  18.5 0.7 %collective-permute-start.6 = (bf16[768,128]{1,0:T(8,128)(2,1)S(1)}, bf16[768,128]{1,0:T(8,128)(2,1)S(1)}, u32[]{:S(2)}, u32[]{:S(2)}) collective-permute-start(bf16[768,128]{1,0:T(8,128)(2,1)S(1)} %get-tuple-element.54.came_ref), channel_id=1, source_target_pairs={{8,16},{16,8},{12,20},{20,12},{9,17},{17,9},{13,21},{21,13},{10,18... | collective-permute-start | bytes 589832 | tf_op jit(solution)/shard_map/ppermute | solution.py:282
  19.1 3.5 %collective-permute-start.5 = (bf16[768,128]{1,0:T(8,128)(2,1)S(1)}, bf16[768,128]{1,0:T(8,128)(2,1)S(1)}, u32[]{:S(2)}, u32[]{:S(2)}) collective-permute-start(bf16[768,128]{1,0:T(8,128)(2,1)S(1)} %get-tuple-element.54.came_ref), channel_id=1, source_target_pairs={{0,8},{8,0},{4,12},{12,4},{16,24},{24,16},{20,28},{28,20},{1,9},{9... | collective-permute-start | bytes 589832 | tf_op jit(solution)/shard_map/ppermute | solution.py:282
  22.6 1.1 %collective-permute-start.7 = (bf16[768,128]{1,0:T(8,128)(2,1)S(1)}, bf16[768,128]{1,0:T(8,128)(2,1)S(1)}, u32[]{:S(2)}, u32[]{:S(2)}) collective-permute-start(bf16[768,128]{1,0:T(8,128)(2,1)S(1)} %get-tuple-element.57), channel_id=1, source_target_pairs={{0,16},{16,0},{4,20},{20,4},{8,24},{24,8},{12,28},{28,12},{1,17},{... | collective-permute-start | bytes 589832 | tf_op jit(solution)/shard_map/ppermute | solution.py:282
  23.7 0.0 collective-permute-done.4.refs_0_
  23.7 0.5 collective-permute-start.13
  24.2 1.5 %collective-permute-start.11 = (bf16[256,1280]{1,0:T(8,128)(2,1)S(1)}, bf16[256,1280]{1,0:T(8,128)(2,1)S(1)}, u32[]{:S(2)}, u32[]{:S(2)}) collective-permute-start(bf16[256,1280]{1,0:T(8,128)(2,1)S(1)} %shard_map.66), channel_id=1, source_target_pairs={{2,0},{3,1},{0,2},{1,3},{6,4},{7,5},{4,6},{5,7},{10,8},{11,9},{8,1... | collective-permute-start | bytes 1966088 | tf_op jit(solution)/shard_map/ppermute | solution.py:302
  25.7 3.0 %shard_map.68._ = f32[2,136,384]{2,1,0:T(8,128)S(1)} custom-call(s32[8,128]{1,0:T(8,128)S(1)} %get-tuple-element.50.flag_ref, s32[1]{0:T(128)} %bitcast.tile_ref, bf16[2,384,128]{2,1,0:T(8,128)(2,1)S(1)} %get-tuple-element.53.q_ref, bf16[768,128]{1,0:T(8,128)(2,1)S(1)} %get-tuple-element.48.keep_kv_ref.own_ref, ...), custom_call_target="tpu_custom_call" | custom-call | flops 603979776 | bytes 1048576 | tf_op jit(solution)/shard_map/pallas_call | solution.py:30
  28.7 0.0 collective-permute-done.6.second_ref
  28.7 0.0 collective-permute-done.5.first_ref
  28.7 1.2 %shard_map.69.state_ref = f32[2,136,384]{2,1,0:T(8,128)S(1)} custom-call(s32[8,128]{1,0:T(8,128)S(1)} %get-tuple-element.50.flag_ref, s32[1]{0:T(128)} %bitcast.tile_ref, bf16[2,384,128]{2,1,0:T(8,128)(2,1)S(1)} %get-tuple-element.53.q_ref, bf16[768,128]{1,0:T(8,128)(2,1)S(1)} %collective-permute-done.5.first_ref, ...), custom_call_target="tpu_custom_call", output_to_operand_aliasing={{}: (5, {})} | custom-call | flops 301989888 | bytes 1048576 | tf_op jit(solution)/shard_map/pallas_call | solution.py:30
  29.9 5.5 %collective-permute-done.7.refs_0_ = bf16[768,128]{1,0:T(8,128)(2,1)S(1)} collective-permute-done((bf16[768,128]{1,0:T(8,128)(2,1)S(1)}, bf16[768,128]{1,0:T(8,128)(2,1)S(1)}, u32[]{:S(2)}, u32[]{:S(2)}) %collective-permute-start.7) | collective-permute-done | bytes 196640 | tf_op jit(solution)/shard_map/ppermute | solution.py:282
  35.5 1.3 %shard_map.70 = (bf16[2,96,128]{2,1,0:T(8,128)(2,1)S(1)}, bf16[2,96,128]{2,1,0:T(8,128)(2,1)S(1)}, bf16[2,96,128]{2,1,0:T(8,128)(2,1)S(1)}, bf16[2,96,128]{2,1,0:T(8,128)(2,1)S(1)}, f32[2,136,384]{2,1,0:T(8,128)S(1)}) custom-call(s32[8,128]{1,0:T(8,128)S(1)} %get-tuple-element.50.flag_ref, s32[1]{0:T(128)} %bitcast.tile_ref, ...), custom_call_target="tpu_custom_call", output_to_operand_aliasing={{4}: (4, {})} | custom-call | flops 5662310400 | bytes 1048576 | tf_op jit(solution)/shard_map/pallas_call | solution.py:30
  36.8 0.1 collective-permute-start.8
  36.9 0.6 %collective-permute-start.9 = (bf16[2,96,128]{2,1,0:T(8,128)(2,1)S(1)}, bf16[2,96,128]{2,1,0:T(8,128)(2,1)S(1)}, u32[]{:S(2)}, u32[]{:S(2)}) collective-permute-start(bf16[2,96,128]{2,1,0:T(8,128)(2,1)S(1)} %get-tuple-element.60), channel_id=1, source_target_pairs={{0,4},{4,0},{8,12},{12,8},{16,20},{20,16},{24,28},{28,24},{1,5},{5... | collective-permute-start | bytes 147464 | tf_op jit(solution)/shard_map/ppermute | solution.py:286
  37.5 1.3 %collective-permute-start.10 = (bf16[2,96,128]{2,1,0:T(8,128)(2,1)S(1)}, bf16[2,96,128]{2,1,0:T(8,128)(2,1)S(1)}, u32[]{:S(2)}, u32[]{:S(2)}) collective-permute-start(bf16[2,96,128]{2,1,0:T(8,128)(2,1)S(1)} %get-tuple-element.61), channel_id=1, source_target_pairs={{0,1},{1,0},{2,3},{3,2},{4,5},{5,4},{6,7},{7,6},{8,9},{9,8},{10,11... | collective-permute-start | bytes 147464 | tf_op jit(solution)/shard_map/ppermute | solution.py:290
  38.8 1.7 %collective-permute-done.8.cross_ref = bf16[2,96,128]{2,1,0:T(8,128)(2,1)S(1)} collective-permute-done((bf16[2,96,128]{2,1,0:T(8,128)(2,1)S(1)}, bf16[2,96,128]{2,1,0:T(8,128)(2,1)S(1)}, u32[]{:S(2)}, u32[]{:S(2)}) %collective-permute-start.8) | collective-permute-done | bytes 49184 | tf_op jit(solution)/shard_map/ppermute | solution.py:297
  40.4 1.1 %collective-permute-done.9.y_ref = bf16[2,96,128]{2,1,0:T(8,128)(2,1)S(1)} collective-permute-done((bf16[2,96,128]{2,1,0:T(8,128)(2,1)S(1)}, bf16[2,96,128]{2,1,0:T(8,128)(2,1)S(1)}, u32[]{:S(2)}, u32[]{:S(2)}) %collective-permute-start.9) | collective-permute-done | bytes 49184 | tf_op jit(solution)/shard_map/ppermute | solution.py:286
  41.5 0.0 collective-permute-done.10.core_ref
  41.5 0.0 collective-permute-done.11.refs_4_
  41.5 0.4 shard_map.71
  41.8 1.2 %collective-permute-start.12 = (bf16[96,1792]{1,0:T(8,128)(2,1)S(1)}, bf16[96,1792]{1,0:T(8,128)(2,1)S(1)}, u32[]{:S(2)}, u32[]{:S(2)}) collective-permute-start(bf16[96,1792]{1,0:T(8,128)(2,1)S(1)} %get-tuple-element.70), channel_id=1, source_target_pairs={{2,0},{3,1},{0,2},{1,3},{6,4},{7,5},{4,6},{5,7},{10,8},{11,9},{8,1... | collective-permute-start | bytes 1032200 | tf_op jit(solution)/shard_map/ppermute | solution.py:302
  43.0 0.0 collective-permute-done.13.refs_2_
  43.0 0.0 collective-permute-start.14
  43.0 0.5 collective-permute-start.15
  43.5 0.0 collective-permute-start.16
  43.5 1.0 %shard_map.72.near_ref = f32[96,5120]{1,0:T(8,128)S(1)} custom-call(bf16[96,512]{1,0:T(8,128)(2,1)S(1)} %get-tuple-element.69.a_ref, bf16[256,5120]{1,0:T(8,128)(2,1)S(1)} %copy-done, bf16[256,5120]{1,0:T(8,128)(2,1)S(1)} %collective-permute-done.1.wp_ref), custom_call_target="tpu_custom_call" | custom-call | flops 15099494400 | bytes 1048576 | tf_op jit(solution)/shard_map/pallas_call | solution.py:30
  44.6 7.3 %collective-permute-done.12.far_ref = bf16[96,1792]{1,0:T(8,128)(2,1)S(1)} collective-permute-done((bf16[96,1792]{1,0:T(8,128)(2,1)S(1)}, bf16[96,1792]{1,0:T(8,128)(2,1)S(1)}, u32[]{:S(2)}, u32[]{:S(2)}) %collective-permute-start.12) | collective-permute-done | bytes 344096 | tf_op jit(solution)/shard_map/ppermute | solution.py:302
  51.9 0.0 collective-permute-done.14.refs_1_
  51.9 0.0 collective-permute-done.15.refs_3_
  51.9 0.0 collective-permute-done.16.refs_5_
  51.9 1.6 %shard_map.73 = bf16[96,5120]{1,0:T(8,128)(2,1)} custom-call(s32[1]{0:T(128)} %bitcast.tile_ref, f32[96,5120]{1,0:T(8,128)S(1)} %shard_map.72.near_ref, bf16[96,1792]{1,0:T(8,128)(2,1)S(1)} %collective-permute-done.12.far_ref, bf16[256,1280]{1,0:T(8,128)(2,1)S(1)} %collective-permute-done.4.refs_0_, bf16[256,1280]{1,0:T(8,128)(2,1)S(1)} %collective-permute-done.14.refs_1_, ...), custom_call_target="tpu_custom_call" | custom-call | flops 503316480 | bytes 1048576 | tf_op jit(solution)/shard_map/pallas_call | solution.py:30
  (3 shorter events, 0.1 us)
Async XLA Ops:
  0.0 3.8 %copy-start = (bf16[256,5120]{1,0:T(8,128)(2,1)S(1)}, bf16[256,5120]{1,0:T(8,128)(2,1)}, u32[]{:S(2)}) copy-start(bf16[256,5120]{1,0:T(8,128)(2,1)} %w_ref.6) | copy-start | bytes 7864324
  3.8 14.6 %collective-permute-start.1 = (bf16[256,5120]{1,0:T(8,128)(2,1)S(1)}, bf16[256,5120]{1,0:T(8,128)(2,1)S(1)}, u32[]{:S(2)}, u32[]{:S(2)}) collective-permute-start(bf16[256,5120]{1,0:T(8,128)(2,1)S(1)} %copy-done), channel_id=1, source_target_pairs={{0,1},{1,0},{2,3},{3,2},{4,5},{5,4},{6,7},{7,6},{8,9},{9,8},{10,11... | collective-permute-start | bytes 7864328 | tf_op jit(solution)/shard_map/ppermute | solution.py:290
  4.3 19.4 %collective-permute-start.4 = (bf16[256,1280]{1,0:T(8,128)(2,1)}, bf16[256,1280]{1,0:T(8,128)(2,1)S(1)}, u32[]{:S(2)}, u32[]{:S(2)}) collective-permute-start(bf16[256,1280]{1,0:T(8,128)(2,1)} %get-tuple-element.52), channel_id=1, source_target_pairs={{2,0},{3,1},{0,2},{1,3},{6,4},{7,5},{4,6},{5,7},{10,8},{11,9},{8,1... | collective-permute-start | bytes 1966088 | tf_op jit(solution)/shard_map/ppermute | solution.py:302
  6.9 11.5 %collective-permute-start = (bf16[1168,128]{1,0:T(8,128)(2,1)}, bf16[1168,128]{1,0:T(8,128)(2,1)S(1)}, u32[]{:S(2)}, u32[]{:S(2)}) collective-permute-start(bf16[1168,128]{1,0:T(8,128)(2,1)} %get-tuple-element.40), channel_id=1, source_target_pairs={{0,4},{4,0},{8,12},{12,8},{16,20},{20,16},{24,28},{28,24},{1,5},{5... | collective-permute-start | bytes 897032 | tf_op jit(solution)/shard_map/ppermute | solution.py:286
  8.4 7.1 %collective-permute-start.3 = (bf16[768,128]{1,0:T(8,128)(2,1)}, bf16[768,128]{1,0:T(8,128)(2,1)S(1)}, u32[]{:S(2)}, u32[]{:S(2)}) collective-permute-start(bf16[768,128]{1,0:T(8,128)(2,1)} %get-tuple-element.41.keep_kv_ref), channel_id=1, source_target_pairs={{8,16},{16,8},{12,20},{20,12},{9,17},{17,9},{13,21},{21,13},{10,18... | collective-permute-start | bytes 589832 | tf_op jit(solution)/shard_map/ppermute | solution.py:282
  9.1 9.3 %collective-permute-start.2 = (bf16[768,128]{1,0:T(8,128)(2,1)}, bf16[768,128]{1,0:T(8,128)(2,1)S(1)}, u32[]{:S(2)}, u32[]{:S(2)}) collective-permute-start(bf16[768,128]{1,0:T(8,128)(2,1)} %get-tuple-element.41.keep_kv_ref), channel_id=1, source_target_pairs={{0,8},{8,0},{4,12},{12,4},{16,24},{24,16},{20,28},{28,20},{1,9},{9... | collective-permute-start | bytes 589832 | tf_op jit(solution)/shard_map/ppermute | solution.py:282
  13.5 1.0 %copy-start.1 = (bf16[768,128]{1,0:T(8,128)(2,1)S(1)}, bf16[768,128]{1,0:T(8,128)(2,1)}, u32[]{:S(2)}) copy-start(bf16[768,128]{1,0:T(8,128)(2,1)} %get-tuple-element.41.keep_kv_ref) | copy-start | bytes 589828
  14.5 0.9 %copy-start.2 = (bf16[400,128]{1,0:T(8,128)(2,1)S(1)}, bf16[400,128]{1,0:T(8,128)(2,1)}, u32[]{:S(2)}) copy-start(bf16[400,128]{1,0:T(8,128)(2,1)} %get-tuple-element.43.keep_q_ref) | copy-start | bytes 307204
  18.5 10.2 %collective-permute-start.6 = (bf16[768,128]{1,0:T(8,128)(2,1)S(1)}, bf16[768,128]{1,0:T(8,128)(2,1)S(1)}, u32[]{:S(2)}, u32[]{:S(2)}) collective-permute-start(bf16[768,128]{1,0:T(8,128)(2,1)S(1)} %get-tuple-element.54.came_ref), channel_id=1, source_target_pairs={{8,16},{16,8},{12,20},{20,12},{9,17},{17,9},{13,21},{21,13},{10,18... | collective-permute-start | bytes 589832 | tf_op jit(solution)/shard_map/ppermute | solution.py:282
  19.1 9.6 %collective-permute-start.5 = (bf16[768,128]{1,0:T(8,128)(2,1)S(1)}, bf16[768,128]{1,0:T(8,128)(2,1)S(1)}, u32[]{:S(2)}, u32[]{:S(2)}) collective-permute-start(bf16[768,128]{1,0:T(8,128)(2,1)S(1)} %get-tuple-element.54.came_ref), channel_id=1, source_target_pairs={{0,8},{8,0},{4,12},{12,4},{16,24},{24,16},{20,28},{28,20},{1,9},{9... | collective-permute-start | bytes 589832 | tf_op jit(solution)/shard_map/ppermute | solution.py:282
  22.6 12.8 %collective-permute-start.7 = (bf16[768,128]{1,0:T(8,128)(2,1)S(1)}, bf16[768,128]{1,0:T(8,128)(2,1)S(1)}, u32[]{:S(2)}, u32[]{:S(2)}) collective-permute-start(bf16[768,128]{1,0:T(8,128)(2,1)S(1)} %get-tuple-element.57), channel_id=1, source_target_pairs={{0,16},{16,0},{4,20},{20,4},{8,24},{24,8},{12,28},{28,12},{1,17},{... | collective-permute-start | bytes 589832 | tf_op jit(solution)/shard_map/ppermute | solution.py:282
  23.7 19.3 %collective-permute-start.13 = (bf16[256,1280]{1,0:T(8,128)(2,1)S(1)}, bf16[256,1280]{1,0:T(8,128)(2,1)S(1)}, u32[]{:S(2)}, u32[]{:S(2)}) collective-permute-start(bf16[256,1280]{1,0:T(8,128)(2,1)S(1)} %collective-permute-done.4.refs_0_), channel_id=1, source_target_pairs={{0,4},{4,0},{8,12},{12,8},{16,20},{20,16},{24,28},{28,24},{1,5},{5... | collective-permute-start | bytes 1966088 | tf_op jit(solution)/shard_map/ppermute | solution.py:286
  24.2 17.2 %collective-permute-start.11 = (bf16[256,1280]{1,0:T(8,128)(2,1)S(1)}, bf16[256,1280]{1,0:T(8,128)(2,1)S(1)}, u32[]{:S(2)}, u32[]{:S(2)}) collective-permute-start(bf16[256,1280]{1,0:T(8,128)(2,1)S(1)} %shard_map.66), channel_id=1, source_target_pairs={{2,0},{3,1},{0,2},{1,3},{6,4},{7,5},{4,6},{5,7},{10,8},{11,9},{8,1... | collective-permute-start | bytes 1966088 | tf_op jit(solution)/shard_map/ppermute | solution.py:302
  36.8 3.6 %collective-permute-start.8 = (bf16[2,96,128]{2,1,0:T(8,128)(2,1)S(1)}, bf16[2,96,128]{2,1,0:T(8,128)(2,1)S(1)}, u32[]{:S(2)}, u32[]{:S(2)}) collective-permute-start(bf16[2,96,128]{2,1,0:T(8,128)(2,1)S(1)} %get-tuple-element.59), channel_id=1, source_target_pairs={{0,5},{1,4},{2,7},{3,6},{4,1},{5,0},{6,3},{7,2},{8,13},{9,12},{10,... | collective-permute-start | bytes 147464 | tf_op jit(solution)/shard_map/ppermute | solution.py:297
  36.9 4.6 %collective-permute-start.9 = (bf16[2,96,128]{2,1,0:T(8,128)(2,1)S(1)}, bf16[2,96,128]{2,1,0:T(8,128)(2,1)S(1)}, u32[]{:S(2)}, u32[]{:S(2)}) collective-permute-start(bf16[2,96,128]{2,1,0:T(8,128)(2,1)S(1)} %get-tuple-element.60), channel_id=1, source_target_pairs={{0,4},{4,0},{8,12},{12,8},{16,20},{20,16},{24,28},{28,24},{1,5},{5... | collective-permute-start | bytes 147464 | tf_op jit(solution)/shard_map/ppermute | solution.py:286
  37.5 4.0 %collective-permute-start.10 = (bf16[2,96,128]{2,1,0:T(8,128)(2,1)S(1)}, bf16[2,96,128]{2,1,0:T(8,128)(2,1)S(1)}, u32[]{:S(2)}, u32[]{:S(2)}) collective-permute-start(bf16[2,96,128]{2,1,0:T(8,128)(2,1)S(1)} %get-tuple-element.61), channel_id=1, source_target_pairs={{0,1},{1,0},{2,3},{3,2},{4,5},{5,4},{6,7},{7,6},{8,9},{9,8},{10,11... | collective-permute-start | bytes 147464 | tf_op jit(solution)/shard_map/ppermute | solution.py:290
  41.8 10.1 %collective-permute-start.12 = (bf16[96,1792]{1,0:T(8,128)(2,1)S(1)}, bf16[96,1792]{1,0:T(8,128)(2,1)S(1)}, u32[]{:S(2)}, u32[]{:S(2)}) collective-permute-start(bf16[96,1792]{1,0:T(8,128)(2,1)S(1)} %get-tuple-element.70), channel_id=1, source_target_pairs={{2,0},{3,1},{0,2},{1,3},{6,4},{7,5},{4,6},{5,7},{10,8},{11,9},{8,1... | collective-permute-start | bytes 1032200 | tf_op jit(solution)/shard_map/ppermute | solution.py:302
  43.0 8.9 %collective-permute-start.14 = (bf16[256,1280]{1,0:T(8,128)(2,1)S(1)}, bf16[256,1280]{1,0:T(8,128)(2,1)S(1)}, u32[]{:S(2)}, u32[]{:S(2)}) collective-permute-start(bf16[256,1280]{1,0:T(8,128)(2,1)S(1)} %collective-permute-done.4.refs_0_), channel_id=1, source_target_pairs={{0,1},{1,0},{2,3},{3,2},{4,5},{5,4},{6,7},{7,6},{8,9},{9,8},{10,11... | collective-permute-start | bytes 1966088 | tf_op jit(solution)/shard_map/ppermute | solution.py:290
  43.0 8.9 %collective-permute-start.15 = (bf16[256,1280]{1,0:T(8,128)(2,1)S(1)}, bf16[256,1280]{1,0:T(8,128)(2,1)S(1)}, u32[]{:S(2)}, u32[]{:S(2)}) collective-permute-start(bf16[256,1280]{1,0:T(8,128)(2,1)S(1)} %collective-permute-done.13.refs_2_), channel_id=1, source_target_pairs={{0,1},{1,0},{2,3},{3,2},{4,5},{5,4},{6,7},{7,6},{8,9},{9,8},{10,11... | collective-permute-start | bytes 1966088 | tf_op jit(solution)/shard_map/ppermute | solution.py:290
  43.5 8.4 %collective-permute-start.16 = (bf16[256,1280]{1,0:T(8,128)(2,1)S(1)}, bf16[256,1280]{1,0:T(8,128)(2,1)S(1)}, u32[]{:S(2)}, u32[]{:S(2)}) collective-permute-start(bf16[256,1280]{1,0:T(8,128)(2,1)S(1)} %collective-permute-done.11.refs_4_), channel_id=1, source_target_pairs={{0,1},{1,0},{2,3},{3,2},{4,5},{5,4},{6,7},{7,6},{8,9},{9,8},{10,11... | collective-permute-start | bytes 1966088 | tf_op jit(solution)/shard_map/ppermute | solution.py:290

commit v11 on v10

--- a/solution.py
+++ b/solution.py
@@ -44,9 +44,9 @@
 
 
 def pack_kernel(
-    tile_ref, _, list_ref, count_ref, q_ref, k_ref, v_ref, w_ref,
-    keep_q_ref, keep_kv_ref, send_ref, side_ref,
-    keep_q, keep_kv, send, side, in_sems, out_sems,
+    tile_ref, _, list_ref, count_ref, q_ref, k_ref, v_ref, __,
+    keep_q_ref, keep_kv_ref, send_ref,
+    keep_q, keep_kv, send, in_sems, out_sems,
 ):
     parity = tile_ref[0] & 1
     rows = q_ref.shape[0]
@@ -67,8 +67,6 @@
         columns = pl.ds(pl.multiple_of(head * HD, HD), HD)
         for ref, out, at in ((k_ref, kv_out, 0), (v_ref, kv_out, rows), (q_ref, q_out, q_at)):
             read(ref.at[:, columns], out.at[pl.ds(at, rows)])
-    width = side.shape[1]
-    read(w_ref.at[:, pl.ds(pl.multiple_of(parity * width, HD), width)], side)
     lane = lax.broadcasted_iota(jnp.int32, (FLAGS, HD), 1)
     flags = jnp.zeros((FLAGS, HD), F32)
     for offset in range(-REACH, REACH + 1):
@@ -83,7 +81,6 @@
     write(3, send, send_ref)
     write(2, keep_kv, keep_kv_ref)
     write(1, keep_q, keep_q_ref)
-    write(1, side, side_ref)
     for each in writes:
         each.wait()
 
@@ -91,6 +88,11 @@
 def stage_kernel(keep_q_ref, keep_kv_ref, q_ref, kv_ref):
     q_ref[...] = keep_q_ref[...]
     kv_ref[...] = keep_kv_ref[...]
+
+
+def side_kernel(tile_ref, w_ref, side_ref):
+    side = side_ref.shape[1]
+    side_ref[...] = w_ref[:, pl.ds(pl.multiple_of((tile_ref[0] & 1) * side, HD), side)]
 
 
 def cut_kernel(w_ref, common_ref, *, first):
@@ -333,13 +335,13 @@
 
     one = (rows, HD)
     payload, kv_shape = shape((3 * rows + FLAGS, HD)), shape((2 * rows, HD))
-    packed = (shape((rows + FLAGS, HD)), kv_shape, payload, shape((width, SIDE)))
-    keep_q, keep_kv, send, side_weight = call(
+    packed = (shape((rows + FLAGS, HD)), kv_shape, payload)
+    keep_q, keep_kv, send = call(
         pack_kernel,
         packed,
         (tile, head, neighbours, counts.reshape(1, 1), queries, keys, values, out_weight),
         scratch=[pltpu.VMEM(each.shape, each.dtype) for each in packed]
-        + [pltpu.SemaphoreType.DMA((7,)), pltpu.SemaphoreType.DMA((4,))],
+        + [pltpu.SemaphoreType.DMA((6,)), pltpu.SemaphoreType.DMA((3,))],
         in_hbm=(4, 5, 6, 7),
         out_hbm=True,
         vmem=58,
@@ -349,6 +351,7 @@
     came = swap_tiles(send)
     kept_near = [swap_pairs(keep_kv, 1, phase) for phase in range(2)]
     if small:
+        side_weight = call(side_kernel, shape((width, SIDE)), (tile, weight_ready))
         side_own = from_chip(side_weight, 1)
 
     held_q, held_kv = call(stage_kernel, (shape((rows + FLAGS, HD)), kv_shape), (keep_q, keep_kv))

time: 53.5 us -> 53.2 us (level)
  local copies, waits for them, and re-layouts: 1.86 us -> 0.02 us
  waiting for transfers between devices: 18.5 us -> 20.3 us
    unnamed x6 -> x8, local copies, waits for them, and re-layouts: 1.86 us -> 0.02 us
    ppermute x5, waiting for transfers between devices: 8.48 us -> 10.2 us  [swap_pairs(): return lax.ppermute(value, 'ctx', pairs)]
    pallas_call x10 -> x11, Pallas kernels: 11.6 us -> 11.2 us  [call(): pl.pallas_call(kernel, out_shape=outs, in_specs=[SMEM if s else HBM if i...]
where the time goes in v11:
time: 53.2 us; the launch traced here: 53 us
  starting transfers between devices  20.6 us (39%)
  waiting for transfers between devices  20.3 us (38%)
  Pallas kernels  11.2 us (21%)
  between operations  0.95 us (2%)
    pallas_call x11, Pallas kernels, call(): pl.pallas_call(kernel, out_shape=outs, in_specs=[SMEM if s else HBM if i...  11.2 us
    ppermute x5, starting transfers between devices, swap_pairs(): return lax.ppermute(value, 'ctx', pairs)  10.4 us
    ppermute x5, waiting for transfers between devices, swap_pairs(): return lax.ppermute(value, 'ctx', pairs)  10.2 us
    ppermute x3, waiting for transfers between devices, from_chip(): lax.ppermute(value, 'head', [((i + 2 * steps) % count, i) for i in range(...  7.32 us
    ppermute x3, starting transfers between devices, from_chip(): lax.ppermute(value, 'head', [((i + 2 * steps) % count, i) for i in range(...  5.21 us
    ppermute x3, starting transfers between devices, swap_tiles(): lax.ppermute(value, 'ctx', [(i, i ^ 1) for i in range(lax.axis_size('ctx'...  2.59 us
    ppermute x5, starting transfers between devices, swap_cores(): lax.ppermute(value, 'head', [(i, i ^ 1) for i in range(lax.axis_size('hea...  2.31 us
    ppermute x1, waiting for transfers between devices, swap_both(): return lax.ppermute(value, ('ctx', 'head'), pairs)  1.65 us
  transfers between devices with their start and end apart: 17, of which 5 were waited for; matrix products, arithmetic and copies ran while one was open for 0% of the time, Pallas kernels for 13%

profile of v11, /device:TPU:0, one launch (start us, length us, event | category | flops | bytes accessed | tf_op | source)
XLA Modules:
  0.0 53.0 jit_solution(10153011572011326664)
XLA Ops:
  0.0 0.0 copy-start
  0.8 2.5 %shard_map.64 = (bf16[400,128]{1,0:T(8,128)(2,1)}, bf16[768,128]{1,0:T(8,128)(2,1)}, bf16[1168,128]{1,0:T(8,128)(2,1)}) custom-call(s32[1]{0:T(128)} %bitcast.tile_ref, s32[1]{0:T(128)} %bitcast.1._.head_ref, s32[1,7]{1,0:T(1,128)} %list_ref.1, s32[1,1]{1,0:T(1,128)} %bitcast.3.count_ref, bf16[384,256]{1,0:T(8,128)(2,1)} %q_ref.1, bf16[384,256]{1,0:T(8,128)(2,1)} %k_ref.1, ...), custom_call_target="tpu_custom_call" | custom-call | bytes 1048576 | tf_op jit(solution)/shard_map/pallas_call | solution.py:30
  3.3 0.0 copy-start.3
  3.3 0.0 copy-start.1
  3.4 0.0 copy-start.2
  3.4 0.0 copy-done
  3.4 0.5 collective-permute-start.1
  3.9 2.6 %collective-permute-start.4 = (bf16[256,1280]{1,0:T(8,128)(2,1)S(1)}, bf16[256,1280]{1,0:T(8,128)(2,1)S(1)}, u32[]{:S(2)}, u32[]{:S(2)}) collective-permute-start(bf16[256,1280]{1,0:T(8,128)(2,1)S(1)} %shard_map.68), channel_id=1, source_target_pairs={{2,0},{3,1},{0,2},{1,3},{6,4},{7,5},{4,6},{5,7},{10,8},{11,9},{8,1... | collective-permute-start | bytes 1966088 | tf_op jit(solution)/shard_map/ppermute | solution.py:304
  6.5 0.0 copy-done.3
  6.5 1.5 %collective-permute-start = (bf16[1168,128]{1,0:T(8,128)(2,1)S(1)}, bf16[1168,128]{1,0:T(8,128)(2,1)S(1)}, u32[]{:S(2)}, u32[]{:S(2)}) collective-permute-start(bf16[1168,128]{1,0:T(8,128)(2,1)S(1)} %copy-done.3), channel_id=1, source_target_pairs={{0,4},{4,0},{8,12},{12,8},{16,20},{20,16},{24,28},{28,24},{1,5},{5... | collective-permute-start | bytes 897032 | tf_op jit(solution)/shard_map/ppermute | solution.py:288
  8.0 0.0 copy-done.1
  8.0 0.7 %collective-permute-start.3 = (bf16[768,128]{1,0:T(8,128)(2,1)S(1)}, bf16[768,128]{1,0:T(8,128)(2,1)S(1)}, u32[]{:S(2)}, u32[]{:S(2)}) collective-permute-start(bf16[768,128]{1,0:T(8,128)(2,1)S(1)} %copy-done.1), channel_id=1, source_target_pairs={{8,16},{16,8},{12,20},{20,12},{9,17},{17,9},{13,21},{21,13},{10,18... | collective-permute-start | bytes 589832 | tf_op jit(solution)/shard_map/ppermute | solution.py:284
  8.7 4.5 %collective-permute-start.2 = (bf16[768,128]{1,0:T(8,128)(2,1)S(1)}, bf16[768,128]{1,0:T(8,128)(2,1)S(1)}, u32[]{:S(2)}, u32[]{:S(2)}) collective-permute-start(bf16[768,128]{1,0:T(8,128)(2,1)S(1)} %copy-done.1), channel_id=1, source_target_pairs={{0,8},{8,0},{4,12},{12,4},{16,24},{24,16},{20,28},{28,20},{1,9},{9... | collective-permute-start | bytes 589832 | tf_op jit(solution)/shard_map/ppermute | solution.py:284
  13.2 0.0 copy-done.2
  13.2 0.0 collective-permute-done.3.kept_second_ref
  13.3 4.6 %collective-permute-done.2.kept_first_ref = bf16[768,128]{1,0:T(8,128)(2,1)S(1)} collective-permute-done((bf16[768,128]{1,0:T(8,128)(2,1)S(1)}, bf16[768,128]{1,0:T(8,128)(2,1)S(1)}, u32[]{:S(2)}, u32[]{:S(2)}) %collective-permute-start.2) | collective-permute-done | bytes 196640 | tf_op jit(solution)/shard_map/ppermute | solution.py:284
  17.9 0.0 collective-permute-done.came_ref
  17.9 0.0 collective-permute-done.1.wp_ref
  17.9 0.7 %collective-permute-start.6 = (bf16[768,128]{1,0:T(8,128)(2,1)S(1)}, bf16[768,128]{1,0:T(8,128)(2,1)S(1)}, u32[]{:S(2)}, u32[]{:S(2)}) collective-permute-start(bf16[768,128]{1,0:T(8,128)(2,1)S(1)} %get-tuple-element.52.came_ref), channel_id=1, source_target_pairs={{8,16},{16,8},{12,20},{20,12},{9,17},{17,9},{13,21},{21,13},{10,18... | collective-permute-start | bytes 589832 | tf_op jit(solution)/shard_map/ppermute | solution.py:284
  18.6 3.5 %collective-permute-start.5 = (bf16[768,128]{1,0:T(8,128)(2,1)S(1)}, bf16[768,128]{1,0:T(8,128)(2,1)S(1)}, u32[]{:S(2)}, u32[]{:S(2)}) collective-permute-start(bf16[768,128]{1,0:T(8,128)(2,1)S(1)} %get-tuple-element.52.came_ref), channel_id=1, source_target_pairs={{0,8},{8,0},{4,12},{12,4},{16,24},{24,16},{20,28},{28,20},{1,9},{9... | collective-permute-start | bytes 589832 | tf_op jit(solution)/shard_map/ppermute | solution.py:284
  22.1 1.1 %collective-permute-start.7 = (bf16[768,128]{1,0:T(8,128)(2,1)S(1)}, bf16[768,128]{1,0:T(8,128)(2,1)S(1)}, u32[]{:S(2)}, u32[]{:S(2)}) collective-permute-start(bf16[768,128]{1,0:T(8,128)(2,1)S(1)} %get-tuple-element.55), channel_id=1, source_target_pairs={{0,16},{16,0},{4,20},{20,4},{8,24},{24,8},{12,28},{28,12},{1,17},{... | collective-permute-start | bytes 589832 | tf_op jit(solution)/shard_map/ppermute | solution.py:284
  23.2 0.0 collective-permute-done.4.refs_0_
  23.2 0.5 collective-permute-start.13
  23.7 1.5 %collective-permute-start.11 = (bf16[256,1280]{1,0:T(8,128)(2,1)S(1)}, bf16[256,1280]{1,0:T(8,128)(2,1)S(1)}, u32[]{:S(2)}, u32[]{:S(2)}) collective-permute-start(bf16[256,1280]{1,0:T(8,128)(2,1)S(1)} %shard_map.66), channel_id=1, source_target_pairs={{2,0},{3,1},{0,2},{1,3},{6,4},{7,5},{4,6},{5,7},{10,8},{11,9},{8,1... | collective-permute-start | bytes 1966088 | tf_op jit(solution)/shard_map/ppermute | solution.py:304
  25.2 3.6 %shard_map.69._ = f32[2,136,384]{2,1,0:T(8,128)S(1)} custom-call(s32[8,128]{1,0:T(8,128)S(1)} %get-tuple-element.49.flag_ref, s32[1]{0:T(128)} %bitcast.tile_ref, bf16[2,384,128]{2,1,0:T(8,128)(2,1)S(1)} %get-tuple-element.51.q_ref, bf16[768,128]{1,0:T(8,128)(2,1)S(1)} %get-tuple-element.47.keep_kv_ref.own_ref, ...), custom_call_target="tpu_custom_call" | custom-call | flops 603979776 | bytes 1048576 | tf_op jit(solution)/shard_map/pallas_call | solution.py:30
  28.7 0.0 collective-permute-done.6.second_ref
  28.7 0.0 collective-permute-done.5.first_ref
  28.7 0.6 %shard_map.70.state_ref = f32[2,136,384]{2,1,0:T(8,128)S(1)} custom-call(s32[8,128]{1,0:T(8,128)S(1)} %get-tuple-element.49.flag_ref, s32[1]{0:T(128)} %bitcast.tile_ref, bf16[2,384,128]{2,1,0:T(8,128)(2,1)S(1)} %get-tuple-element.51.q_ref, bf16[768,128]{1,0:T(8,128)(2,1)S(1)} %collective-permute-done.5.first_ref, ...), custom_call_target="tpu_custom_call", output_to_operand_aliasing={{}: (5, {})} | custom-call | flops 301989888 | bytes 1048576 | tf_op jit(solution)/shard_map/pallas_call | solution.py:30
  29.4 5.6 %collective-permute-done.7.refs_0_ = bf16[768,128]{1,0:T(8,128)(2,1)S(1)} collective-permute-done((bf16[768,128]{1,0:T(8,128)(2,1)S(1)}, bf16[768,128]{1,0:T(8,128)(2,1)S(1)}, u32[]{:S(2)}, u32[]{:S(2)}) %collective-permute-start.7) | collective-permute-done | bytes 196640 | tf_op jit(solution)/shard_map/ppermute | solution.py:284
  35.0 1.3 %shard_map.71 = (bf16[2,96,128]{2,1,0:T(8,128)(2,1)S(1)}, bf16[2,96,128]{2,1,0:T(8,128)(2,1)S(1)}, bf16[2,96,128]{2,1,0:T(8,128)(2,1)S(1)}, bf16[2,96,128]{2,1,0:T(8,128)(2,1)S(1)}, f32[2,136,384]{2,1,0:T(8,128)S(1)}) custom-call(s32[8,128]{1,0:T(8,128)S(1)} %get-tuple-element.49.flag_ref, s32[1]{0:T(128)} %bitcast.tile_ref, ...), custom_call_target="tpu_custom_call", output_to_operand_aliasing={{4}: (4, {})} | custom-call | flops 5662310400 | bytes 1048576 | tf_op jit(solution)/shard_map/pallas_call | solution.py:30
  36.3 0.1 collective-permute-start.8
  36.4 0.6 %collective-permute-start.9 = (bf16[2,96,128]{2,1,0:T(8,128)(2,1)S(1)}, bf16[2,96,128]{2,1,0:T(8,128)(2,1)S(1)}, u32[]{:S(2)}, u32[]{:S(2)}) collective-permute-start(bf16[2,96,128]{2,1,0:T(8,128)(2,1)S(1)} %get-tuple-element.58), channel_id=1, source_target_pairs={{0,4},{4,0},{8,12},{12,8},{16,20},{20,16},{24,28},{28,24},{1,5},{5... | collective-permute-start | bytes 147464 | tf_op jit(solution)/shard_map/ppermute | solution.py:288
  37.0 1.3 %collective-permute-start.10 = (bf16[2,96,128]{2,1,0:T(8,128)(2,1)S(1)}, bf16[2,96,128]{2,1,0:T(8,128)(2,1)S(1)}, u32[]{:S(2)}, u32[]{:S(2)}) collective-permute-start(bf16[2,96,128]{2,1,0:T(8,128)(2,1)S(1)} %get-tuple-element.59), channel_id=1, source_target_pairs={{0,1},{1,0},{2,3},{3,2},{4,5},{5,4},{6,7},{7,6},{8,9},{9,8},{10,11... | collective-permute-start | bytes 147464 | tf_op jit(solution)/shard_map/ppermute | solution.py:292
  38.3 1.7 %collective-permute-done.8.cross_ref = bf16[2,96,128]{2,1,0:T(8,128)(2,1)S(1)} collective-permute-done((bf16[2,96,128]{2,1,0:T(8,128)(2,1)S(1)}, bf16[2,96,128]{2,1,0:T(8,128)(2,1)S(1)}, u32[]{:S(2)}, u32[]{:S(2)}) %collective-permute-start.8) | collective-permute-done | bytes 49184 | tf_op jit(solution)/shard_map/ppermute | solution.py:299
  39.9 1.1 %collective-permute-done.9.y_ref = bf16[2,96,128]{2,1,0:T(8,128)(2,1)S(1)} collective-permute-done((bf16[2,96,128]{2,1,0:T(8,128)(2,1)S(1)}, bf16[2,96,128]{2,1,0:T(8,128)(2,1)S(1)}, u32[]{:S(2)}, u32[]{:S(2)}) %collective-permute-start.9) | collective-permute-done | bytes 49184 | tf_op jit(solution)/shard_map/ppermute | solution.py:288
  41.0 0.0 collective-permute-done.10.core_ref
  41.0 0.0 collective-permute-done.11.refs_4_
  41.0 0.4 shard_map.72
  41.4 1.2 %collective-permute-start.12 = (bf16[96,1792]{1,0:T(8,128)(2,1)S(1)}, bf16[96,1792]{1,0:T(8,128)(2,1)S(1)}, u32[]{:S(2)}, u32[]{:S(2)}) collective-permute-start(bf16[96,1792]{1,0:T(8,128)(2,1)S(1)} %get-tuple-element.68), channel_id=1, source_target_pairs={{2,0},{3,1},{0,2},{1,3},{6,4},{7,5},{4,6},{5,7},{10,8},{11,9},{8,1... | collective-permute-start | bytes 1032200 | tf_op jit(solution)/shard_map/ppermute | solution.py:304
  42.5 0.0 collective-permute-done.13.refs_2_
  42.5 0.0 collective-permute-start.14
  42.5 0.5 collective-permute-start.15
  43.1 0.0 collective-permute-start.16
  43.1 1.0 %shard_map.73.near_ref = f32[96,5120]{1,0:T(8,128)S(1)} custom-call(bf16[96,512]{1,0:T(8,128)(2,1)S(1)} %get-tuple-element.67.a_ref, bf16[256,5120]{1,0:T(8,128)(2,1)S(1)} %copy-done, bf16[256,5120]{1,0:T(8,128)(2,1)S(1)} %collective-permute-done.1.wp_ref), custom_call_target="tpu_custom_call" | custom-call | flops 15099494400 | bytes 1048576 | tf_op jit(solution)/shard_map/pallas_call | solution.py:30
  44.1 7.3 %collective-permute-done.12.far_ref = bf16[96,1792]{1,0:T(8,128)(2,1)S(1)} collective-permute-done((bf16[96,1792]{1,0:T(8,128)(2,1)S(1)}, bf16[96,1792]{1,0:T(8,128)(2,1)S(1)}, u32[]{:S(2)}, u32[]{:S(2)}) %collective-permute-start.12) | collective-permute-done | bytes 344096 | tf_op jit(solution)/shard_map/ppermute | solution.py:304
  51.4 0.0 collective-permute-done.14.refs_1_
  51.4 0.0 collective-permute-done.15.refs_3_
  51.4 0.0 collective-permute-done.16.refs_5_
  51.4 1.6 %shard_map.74 = bf16[96,5120]{1,0:T(8,128)(2,1)} custom-call(s32[1]{0:T(128)} %bitcast.tile_ref, f32[96,5120]{1,0:T(8,128)S(1)} %shard_map.73.near_ref, bf16[96,1792]{1,0:T(8,128)(2,1)S(1)} %collective-permute-done.12.far_ref, bf16[256,1280]{1,0:T(8,128)(2,1)S(1)} %collective-permute-done.4.refs_0_, bf16[256,1280]{1,0:T(8,128)(2,1)S(1)} %collective-permute-done.14.refs_1_, ...), custom_call_target="tpu_custom_call" | custom-call | flops 503316480 | bytes 1048576 | tf_op jit(solution)/shard_map/pallas_call | solution.py:30
  (4 shorter events, 0.2 us)
Async XLA Ops:
  0.0 3.4 %copy-start = (bf16[256,5120]{1,0:T(8,128)(2,1)S(1)}, bf16[256,5120]{1,0:T(8,128)(2,1)}, u32[]{:S(2)}) copy-start(bf16[256,5120]{1,0:T(8,128)(2,1)} %w_ref.5) | copy-start | bytes 7864324
  3.3 3.2 %copy-start.3 = (bf16[1168,128]{1,0:T(8,128)(2,1)S(1)}, bf16[1168,128]{1,0:T(8,128)(2,1)}, u32[]{:S(2)}) copy-start(bf16[1168,128]{1,0:T(8,128)(2,1)} %get-tuple-element.39) | copy-start | bytes 897028
  3.3 4.7 %copy-start.1 = (bf16[768,128]{1,0:T(8,128)(2,1)S(1)}, bf16[768,128]{1,0:T(8,128)(2,1)}, u32[]{:S(2)}) copy-start(bf16[768,128]{1,0:T(8,128)(2,1)} %get-tuple-element.40.keep_kv_ref) | copy-start | bytes 589828
  3.4 9.8 %copy-start.2 = (bf16[400,128]{1,0:T(8,128)(2,1)S(1)}, bf16[400,128]{1,0:T(8,128)(2,1)}, u32[]{:S(2)}) copy-start(bf16[400,128]{1,0:T(8,128)(2,1)} %get-tuple-element.42.keep_q_ref) | copy-start | bytes 307204
  3.4 14.5 %collective-permute-start.1 = (bf16[256,5120]{1,0:T(8,128)(2,1)S(1)}, bf16[256,5120]{1,0:T(8,128)(2,1)S(1)}, u32[]{:S(2)}, u32[]{:S(2)}) collective-permute-start(bf16[256,5120]{1,0:T(8,128)(2,1)S(1)} %copy-done), channel_id=1, source_target_pairs={{0,1},{1,0},{2,3},{3,2},{4,5},{5,4},{6,7},{7,6},{8,9},{9,8},{10,11... | collective-permute-start | bytes 7864328 | tf_op jit(solution)/shard_map/ppermute | solution.py:292
  3.9 19.3 %collective-permute-start.4 = (bf16[256,1280]{1,0:T(8,128)(2,1)S(1)}, bf16[256,1280]{1,0:T(8,128)(2,1)S(1)}, u32[]{:S(2)}, u32[]{:S(2)}) collective-permute-start(bf16[256,1280]{1,0:T(8,128)(2,1)S(1)} %shard_map.68), channel_id=1, source_target_pairs={{2,0},{3,1},{0,2},{1,3},{6,4},{7,5},{4,6},{5,7},{10,8},{11,9},{8,1... | collective-permute-start | bytes 1966088 | tf_op jit(solution)/shard_map/ppermute | solution.py:304
  6.5 11.4 %collective-permute-start = (bf16[1168,128]{1,0:T(8,128)(2,1)S(1)}, bf16[1168,128]{1,0:T(8,128)(2,1)S(1)}, u32[]{:S(2)}, u32[]{:S(2)}) collective-permute-start(bf16[1168,128]{1,0:T(8,128)(2,1)S(1)} %copy-done.3), channel_id=1, source_target_pairs={{0,4},{4,0},{8,12},{12,8},{16,20},{20,16},{24,28},{28,24},{1,5},{5... | collective-permute-start | bytes 897032 | tf_op jit(solution)/shard_map/ppermute | solution.py:288
  8.0 5.2 %collective-permute-start.3 = (bf16[768,128]{1,0:T(8,128)(2,1)S(1)}, bf16[768,128]{1,0:T(8,128)(2,1)S(1)}, u32[]{:S(2)}, u32[]{:S(2)}) collective-permute-start(bf16[768,128]{1,0:T(8,128)(2,1)S(1)} %copy-done.1), channel_id=1, source_target_pairs={{8,16},{16,8},{12,20},{20,12},{9,17},{17,9},{13,21},{21,13},{10,18... | collective-permute-start | bytes 589832 | tf_op jit(solution)/shard_map/ppermute | solution.py:284
  8.7 9.2 %collective-permute-start.2 = (bf16[768,128]{1,0:T(8,128)(2,1)S(1)}, bf16[768,128]{1,0:T(8,128)(2,1)S(1)}, u32[]{:S(2)}, u32[]{:S(2)}) collective-permute-start(bf16[768,128]{1,0:T(8,128)(2,1)S(1)} %copy-done.1), channel_id=1, source_target_pairs={{0,8},{8,0},{4,12},{12,4},{16,24},{24,16},{20,28},{28,20},{1,9},{9... | collective-permute-start | bytes 589832 | tf_op jit(solution)/shard_map/ppermute | solution.py:284
  17.9 10.8 %collective-permute-start.6 = (bf16[768,128]{1,0:T(8,128)(2,1)S(1)}, bf16[768,128]{1,0:T(8,128)(2,1)S(1)}, u32[]{:S(2)}, u32[]{:S(2)}) collective-permute-start(bf16[768,128]{1,0:T(8,128)(2,1)S(1)} %get-tuple-element.52.came_ref), channel_id=1, source_target_pairs={{8,16},{16,8},{12,20},{20,12},{9,17},{17,9},{13,21},{21,13},{10,18... | collective-permute-start | bytes 589832 | tf_op jit(solution)/shard_map/ppermute | solution.py:284
  18.6 10.1 %collective-permute-start.5 = (bf16[768,128]{1,0:T(8,128)(2,1)S(1)}, bf16[768,128]{1,0:T(8,128)(2,1)S(1)}, u32[]{:S(2)}, u32[]{:S(2)}) collective-permute-start(bf16[768,128]{1,0:T(8,128)(2,1)S(1)} %get-tuple-element.52.came_ref), channel_id=1, source_target_pairs={{0,8},{8,0},{4,12},{12,4},{16,24},{24,16},{20,28},{28,20},{1,9},{9... | collective-permute-start | bytes 589832 | tf_op jit(solution)/shard_map/ppermute | solution.py:284
  22.1 12.9 %collective-permute-start.7 = (bf16[768,128]{1,0:T(8,128)(2,1)S(1)}, bf16[768,128]{1,0:T(8,128)(2,1)S(1)}, u32[]{:S(2)}, u32[]{:S(2)}) collective-permute-start(bf16[768,128]{1,0:T(8,128)(2,1)S(1)} %get-tuple-element.55), channel_id=1, source_target_pairs={{0,16},{16,0},{4,20},{20,4},{8,24},{24,8},{12,28},{28,12},{1,17},{... | collective-permute-start | bytes 589832 | tf_op jit(solution)/shard_map/ppermute | solution.py:284
  23.2 19.3 %collective-permute-start.13 = (bf16[256,1280]{1,0:T(8,128)(2,1)S(1)}, bf16[256,1280]{1,0:T(8,128)(2,1)S(1)}, u32[]{:S(2)}, u32[]{:S(2)}) collective-permute-start(bf16[256,1280]{1,0:T(8,128)(2,1)S(1)} %collective-permute-done.4.refs_0_), channel_id=1, source_target_pairs={{0,4},{4,0},{8,12},{12,8},{16,20},{20,16},{24,28},{28,24},{1,5},{5... | collective-permute-start | bytes 1966088 | tf_op jit(solution)/shard_map/ppermute | solution.py:288
  23.7 17.3 %collective-permute-start.11 = (bf16[256,1280]{1,0:T(8,128)(2,1)S(1)}, bf16[256,1280]{1,0:T(8,128)(2,1)S(1)}, u32[]{:S(2)}, u32[]{:S(2)}) collective-permute-start(bf16[256,1280]{1,0:T(8,128)(2,1)S(1)} %shard_map.66), channel_id=1, source_target_pairs={{2,0},{3,1},{0,2},{1,3},{6,4},{7,5},{4,6},{5,7},{10,8},{11,9},{8,1... | collective-permute-start | bytes 1966088 | tf_op jit(solution)/shard_map/ppermute | solution.py:304
  36.3 3.6 %collective-permute-start.8 = (bf16[2,96,128]{2,1,0:T(8,128)(2,1)S(1)}, bf16[2,96,128]{2,1,0:T(8,128)(2,1)S(1)}, u32[]{:S(2)}, u32[]{:S(2)}) collective-permute-start(bf16[2,96,128]{2,1,0:T(8,128)(2,1)S(1)} %get-tuple-element.57), channel_id=1, source_target_pairs={{0,5},{1,4},{2,7},{3,6},{4,1},{5,0},{6,3},{7,2},{8,13},{9,12},{10,... | collective-permute-start | bytes 147464 | tf_op jit(solution)/shard_map/ppermute | solution.py:299
  36.4 4.6 %collective-permute-start.9 = (bf16[2,96,128]{2,1,0:T(8,128)(2,1)S(1)}, bf16[2,96,128]{2,1,0:T(8,128)(2,1)S(1)}, u32[]{:S(2)}, u32[]{:S(2)}) collective-permute-start(bf16[2,96,128]{2,1,0:T(8,128)(2,1)S(1)} %get-tuple-element.58), channel_id=1, source_target_pairs={{0,4},{4,0},{8,12},{12,8},{16,20},{20,16},{24,28},{28,24},{1,5},{5... | collective-permute-start | bytes 147464 | tf_op jit(solution)/shard_map/ppermute | solution.py:288
  37.0 4.0 %collective-permute-start.10 = (bf16[2,96,128]{2,1,0:T(8,128)(2,1)S(1)}, bf16[2,96,128]{2,1,0:T(8,128)(2,1)S(1)}, u32[]{:S(2)}, u32[]{:S(2)}) collective-permute-start(bf16[2,96,128]{2,1,0:T(8,128)(2,1)S(1)} %get-tuple-element.59), channel_id=1, source_target_pairs={{0,1},{1,0},{2,3},{3,2},{4,5},{5,4},{6,7},{7,6},{8,9},{9,8},{10,11... | collective-permute-start | bytes 147464 | tf_op jit(solution)/shard_map/ppermute | solution.py:292
  41.4 10.1 %collective-permute-start.12 = (bf16[96,1792]{1,0:T(8,128)(2,1)S(1)}, bf16[96,1792]{1,0:T(8,128)(2,1)S(1)}, u32[]{:S(2)}, u32[]{:S(2)}) collective-permute-start(bf16[96,1792]{1,0:T(8,128)(2,1)S(1)} %get-tuple-element.68), channel_id=1, source_target_pairs={{2,0},{3,1},{0,2},{1,3},{6,4},{7,5},{4,6},{5,7},{10,8},{11,9},{8,1... | collective-permute-start | bytes 1032200 | tf_op jit(solution)/shard_map/ppermute | solution.py:304
  42.5 8.9 %collective-permute-start.14 = (bf16[256,1280]{1,0:T(8,128)(2,1)S(1)}, bf16[256,1280]{1,0:T(8,128)(2,1)S(1)}, u32[]{:S(2)}, u32[]{:S(2)}) collective-permute-start(bf16[256,1280]{1,0:T(8,128)(2,1)S(1)} %collective-permute-done.4.refs_0_), channel_id=1, source_target_pairs={{0,1},{1,0},{2,3},{3,2},{4,5},{5,4},{6,7},{7,6},{8,9},{9,8},{10,11... | collective-permute-start | bytes 1966088 | tf_op jit(solution)/shard_map/ppermute | solution.py:292
  42.5 8.9 %collective-permute-start.15 = (bf16[256,1280]{1,0:T(8,128)(2,1)S(1)}, bf16[256,1280]{1,0:T(8,128)(2,1)S(1)}, u32[]{:S(2)}, u32[]{:S(2)}) collective-permute-start(bf16[256,1280]{1,0:T(8,128)(2,1)S(1)} %collective-permute-done.13.refs_2_), channel_id=1, source_target_pairs={{0,1},{1,0},{2,3},{3,2},{4,5},{5,4},{6,7},{7,6},{8,9},{9,8},{10,11... | collective-permute-start | bytes 1966088 | tf_op jit(solution)/shard_map/ppermute | solution.py:292
  43.1 8.4 %collective-permute-start.16 = (bf16[256,1280]{1,0:T(8,128)(2,1)S(1)}, bf16[256,1280]{1,0:T(8,128)(2,1)S(1)}, u32[]{:S(2)}, u32[]{:S(2)}) collective-permute-start(bf16[256,1280]{1,0:T(8,128)(2,1)S(1)} %collective-permute-done.11.refs_4_), channel_id=1, source_target_pairs={{0,1},{1,0},{2,3},{3,2},{4,5},{5,4},{6,7},{7,6},{8,9},{9,8},{10,11... | collective-permute-start | bytes 1966088 | tf_op jit(solution)/shard_map/ppermute | solution.py:292

commit v12 on v11

--- a/solution.py
+++ b/solution.py
@@ -69,12 +69,9 @@
             read(ref.at[:, columns], out.at[pl.ds(at, rows)])
     lane = lax.broadcasted_iota(jnp.int32, (FLAGS, HD), 1)
     flags = jnp.zeros((FLAGS, HD), F32)
-    for offset in range(-REACH, REACH + 1):
-        listed = jnp.int32(0)
-        for slot in range(list_ref.shape[1]):
-            found = (list_ref[0, slot] == tile_ref[0] + offset) & (slot < count_ref[0, 0])
-            listed = jnp.where(found, 1, listed)
-        flags = jnp.where(lane == offset + REACH, listed.astype(F32), flags)
+    for slot in range(list_ref.shape[1]):
+        place = jnp.where(slot < count_ref[0, 0], list_ref[0, slot] - tile_ref[0] + REACH, -1)
+        flags = jnp.where(lane == place, 1.0, flags)
     keep_q[rows:, :] = flags.astype(BF16)
     send[3 * rows :, :] = flags.astype(BF16)
     left = [len(reads)]

time: 53.2 us -> 53.2 us (level)
  waiting for transfers between devices: 20.3 us -> 18.5 us
  Pallas kernels: 11.2 us -> 12.9 us
    ppermute x5, waiting for transfers between devices: 10.2 us -> 8.5 us  [swap_pairs(): return lax.ppermute(value, 'ctx', pairs)]
    pallas_call x11, Pallas kernels: 11.2 us -> 12.9 us  [call(): pl.pallas_call(kernel, out_shape=outs, in_specs=[SMEM if s else HBM if i...]
  transfers between devices with their start and end apart: 17 -> 17, of which waited for: 5 -> 5; matrix products, arithmetic and copies ran while one was open for 0% -> 0% of each run, Pallas kernels for 13% -> 17%
where the time goes in v12:
time: 53.2 us; the launch traced here: 53 us
  starting transfers between devices  20.6 us (39%)
  waiting for transfers between devices  18.5 us (35%)
  Pallas kernels  12.9 us (24%)
  between operations  0.95 us (2%)
    pallas_call x11, Pallas kernels, call(): pl.pallas_call(kernel, out_shape=outs, in_specs=[SMEM if s else HBM if i...  12.9 us
    ppermute x5, starting transfers between devices, swap_pairs(): return lax.ppermute(value, 'ctx', pairs)  10.4 us
    ppermute x5, waiting for transfers between devices, swap_pairs(): return lax.ppermute(value, 'ctx', pairs)  8.5 us
    ppermute x3, waiting for transfers between devices, from_chip(): lax.ppermute(value, 'head', [((i + 2 * steps) % count, i) for i in range(...  7.32 us
    ppermute x3, starting transfers between devices, from_chip(): lax.ppermute(value, 'head', [((i + 2 * steps) % count, i) for i in range(...  5.21 us
    ppermute x3, starting transfers between devices, swap_tiles(): lax.ppermute(value, 'ctx', [(i, i ^ 1) for i in range(lax.axis_size('ctx'...  2.59 us
    ppermute x5, starting transfers between devices, swap_cores(): lax.ppermute(value, 'head', [(i, i ^ 1) for i in range(lax.axis_size('hea...  2.31 us
    ppermute x1, waiting for transfers between devices, swap_both(): return lax.ppermute(value, ('ctx', 'head'), pairs)  1.65 us
  transfers between devices with their start and end apart: 17, of which 5 were waited for; matrix products, arithmetic and copies ran while one was open for 0% of the time, Pallas kernels for 17%

profile of v12, /device:TPU:0, one launch (start us, length us, event | category | flops | bytes accessed | tf_op | source)
XLA Modules:
  0.0 53.0 jit_solution(14534108678304656520)
XLA Ops:
  0.0 0.0 copy-start
  0.8 2.5 %shard_map.64 = (bf16[400,128]{1,0:T(8,128)(2,1)}, bf16[768,128]{1,0:T(8,128)(2,1)}, bf16[1168,128]{1,0:T(8,128)(2,1)}) custom-call(s32[1]{0:T(128)} %bitcast.tile_ref, s32[1]{0:T(128)} %bitcast.1._.head_ref, s32[1,7]{1,0:T(1,128)} %list_ref.1, s32[1,1]{1,0:T(1,128)} %bitcast.3.count_ref, bf16[384,256]{1,0:T(8,128)(2,1)} %q_ref.1, bf16[384,256]{1,0:T(8,128)(2,1)} %k_ref.1, ...), custom_call_target="tpu_custom_call" | custom-call | bytes 1048576 | tf_op jit(solution)/shard_map/pallas_call | solution.py:30
  3.3 0.0 copy-start.3
  3.3 0.0 copy-start.1
  3.4 0.0 copy-start.2
  3.4 0.0 copy-done
  3.4 0.5 collective-permute-start.1
  3.9 2.6 %collective-permute-start.4 = (bf16[256,1280]{1,0:T(8,128)(2,1)S(1)}, bf16[256,1280]{1,0:T(8,128)(2,1)S(1)}, u32[]{:S(2)}, u32[]{:S(2)}) collective-permute-start(bf16[256,1280]{1,0:T(8,128)(2,1)S(1)} %shard_map.68), channel_id=1, source_target_pairs={{2,0},{3,1},{0,2},{1,3},{6,4},{7,5},{4,6},{5,7},{10,8},{11,9},{8,1... | collective-permute-start | bytes 1966088 | tf_op jit(solution)/shard_map/ppermute | solution.py:301
  6.5 0.0 copy-done.3
  6.5 1.5 %collective-permute-start = (bf16[1168,128]{1,0:T(8,128)(2,1)S(1)}, bf16[1168,128]{1,0:T(8,128)(2,1)S(1)}, u32[]{:S(2)}, u32[]{:S(2)}) collective-permute-start(bf16[1168,128]{1,0:T(8,128)(2,1)S(1)} %copy-done.3), channel_id=1, source_target_pairs={{0,4},{4,0},{8,12},{12,8},{16,20},{20,16},{24,28},{28,24},{1,5},{5... | collective-permute-start | bytes 897032 | tf_op jit(solution)/shard_map/ppermute | solution.py:285
  8.0 0.0 copy-done.1
  8.0 0.7 %collective-permute-start.3 = (bf16[768,128]{1,0:T(8,128)(2,1)S(1)}, bf16[768,128]{1,0:T(8,128)(2,1)S(1)}, u32[]{:S(2)}, u32[]{:S(2)}) collective-permute-start(bf16[768,128]{1,0:T(8,128)(2,1)S(1)} %copy-done.1), channel_id=1, source_target_pairs={{8,16},{16,8},{12,20},{20,12},{9,17},{17,9},{13,21},{21,13},{10,18... | collective-permute-start | bytes 589832 | tf_op jit(solution)/shard_map/ppermute | solution.py:281
  8.7 4.5 %collective-permute-start.2 = (bf16[768,128]{1,0:T(8,128)(2,1)S(1)}, bf16[768,128]{1,0:T(8,128)(2,1)S(1)}, u32[]{:S(2)}, u32[]{:S(2)}) collective-permute-start(bf16[768,128]{1,0:T(8,128)(2,1)S(1)} %copy-done.1), channel_id=1, source_target_pairs={{0,8},{8,0},{4,12},{12,4},{16,24},{24,16},{20,28},{28,20},{1,9},{9... | collective-permute-start | bytes 589832 | tf_op jit(solution)/shard_map/ppermute | solution.py:281
  13.2 0.0 copy-done.2
  13.2 0.0 collective-permute-done.3.kept_second_ref
  13.3 4.6 %collective-permute-done.2.kept_first_ref = bf16[768,128]{1,0:T(8,128)(2,1)S(1)} collective-permute-done((bf16[768,128]{1,0:T(8,128)(2,1)S(1)}, bf16[768,128]{1,0:T(8,128)(2,1)S(1)}, u32[]{:S(2)}, u32[]{:S(2)}) %collective-permute-start.2) | collective-permute-done | bytes 196640 | tf_op jit(solution)/shard_map/ppermute | solution.py:281
  17.9 0.0 collective-permute-done.came_ref
  17.9 0.0 collective-permute-done.1.wp_ref
  17.9 0.7 %collective-permute-start.6 = (bf16[768,128]{1,0:T(8,128)(2,1)S(1)}, bf16[768,128]{1,0:T(8,128)(2,1)S(1)}, u32[]{:S(2)}, u32[]{:S(2)}) collective-permute-start(bf16[768,128]{1,0:T(8,128)(2,1)S(1)} %get-tuple-element.52.came_ref), channel_id=1, source_target_pairs={{8,16},{16,8},{12,20},{20,12},{9,17},{17,9},{13,21},{21,13},{10,18... | collective-permute-start | bytes 589832 | tf_op jit(solution)/shard_map/ppermute | solution.py:281
  18.6 3.5 %collective-permute-start.5 = (bf16[768,128]{1,0:T(8,128)(2,1)S(1)}, bf16[768,128]{1,0:T(8,128)(2,1)S(1)}, u32[]{:S(2)}, u32[]{:S(2)}) collective-permute-start(bf16[768,128]{1,0:T(8,128)(2,1)S(1)} %get-tuple-element.52.came_ref), channel_id=1, source_target_pairs={{0,8},{8,0},{4,12},{12,4},{16,24},{24,16},{20,28},{28,20},{1,9},{9... | collective-permute-start | bytes 589832 | tf_op jit(solution)/shard_map/ppermute | solution.py:281
  22.1 1.1 %collective-permute-start.7 = (bf16[768,128]{1,0:T(8,128)(2,1)S(1)}, bf16[768,128]{1,0:T(8,128)(2,1)S(1)}, u32[]{:S(2)}, u32[]{:S(2)}) collective-permute-start(bf16[768,128]{1,0:T(8,128)(2,1)S(1)} %get-tuple-element.55), channel_id=1, source_target_pairs={{0,16},{16,0},{4,20},{20,4},{8,24},{24,8},{12,28},{28,12},{1,17},{... | collective-permute-start | bytes 589832 | tf_op jit(solution)/shard_map/ppermute | solution.py:281
  23.2 0.0 collective-permute-done.4.refs_0_
  23.2 0.5 collective-permute-start.13
  23.7 1.5 %collective-permute-start.11 = (bf16[256,1280]{1,0:T(8,128)(2,1)S(1)}, bf16[256,1280]{1,0:T(8,128)(2,1)S(1)}, u32[]{:S(2)}, u32[]{:S(2)}) collective-permute-start(bf16[256,1280]{1,0:T(8,128)(2,1)S(1)} %shard_map.66), channel_id=1, source_target_pairs={{2,0},{3,1},{0,2},{1,3},{6,4},{7,5},{4,6},{5,7},{10,8},{11,9},{8,1... | collective-permute-start | bytes 1966088 | tf_op jit(solution)/shard_map/ppermute | solution.py:301
  25.2 4.1 %shard_map.69._ = f32[2,136,384]{2,1,0:T(8,128)S(1)} custom-call(s32[8,128]{1,0:T(8,128)S(1)} %get-tuple-element.49.flag_ref, s32[1]{0:T(128)} %bitcast.tile_ref, bf16[2,384,128]{2,1,0:T(8,128)(2,1)S(1)} %get-tuple-element.51.q_ref, bf16[768,128]{1,0:T(8,128)(2,1)S(1)} %get-tuple-element.47.keep_kv_ref.own_ref, ...), custom_call_target="tpu_custom_call" | custom-call | flops 603979776 | bytes 1048576 | tf_op jit(solution)/shard_map/pallas_call | solution.py:30
  29.3 0.0 collective-permute-done.6.second_ref
  29.3 0.0 collective-permute-done.5.first_ref
  29.3 1.8 %shard_map.70.state_ref = f32[2,136,384]{2,1,0:T(8,128)S(1)} custom-call(s32[8,128]{1,0:T(8,128)S(1)} %get-tuple-element.49.flag_ref, s32[1]{0:T(128)} %bitcast.tile_ref, bf16[2,384,128]{2,1,0:T(8,128)(2,1)S(1)} %get-tuple-element.51.q_ref, bf16[768,128]{1,0:T(8,128)(2,1)S(1)} %collective-permute-done.5.first_ref, ...), custom_call_target="tpu_custom_call", output_to_operand_aliasing={{}: (5, {})} | custom-call | flops 301989888 | bytes 1048576 | tf_op jit(solution)/shard_map/pallas_call | solution.py:30
  31.1 3.9 %collective-permute-done.7.refs_0_ = bf16[768,128]{1,0:T(8,128)(2,1)S(1)} collective-permute-done((bf16[768,128]{1,0:T(8,128)(2,1)S(1)}, bf16[768,128]{1,0:T(8,128)(2,1)S(1)}, u32[]{:S(2)}, u32[]{:S(2)}) %collective-permute-start.7) | collective-permute-done | bytes 196640 | tf_op jit(solution)/shard_map/ppermute | solution.py:281
  35.0 1.3 %shard_map.71 = (bf16[2,96,128]{2,1,0:T(8,128)(2,1)S(1)}, bf16[2,96,128]{2,1,0:T(8,128)(2,1)S(1)}, bf16[2,96,128]{2,1,0:T(8,128)(2,1)S(1)}, bf16[2,96,128]{2,1,0:T(8,128)(2,1)S(1)}, f32[2,136,384]{2,1,0:T(8,128)S(1)}) custom-call(s32[8,128]{1,0:T(8,128)S(1)} %get-tuple-element.49.flag_ref, s32[1]{0:T(128)} %bitcast.tile_ref, ...), custom_call_target="tpu_custom_call", output_to_operand_aliasing={{4}: (4, {})} | custom-call | flops 5662310400 | bytes 1048576 | tf_op jit(solution)/shard_map/pallas_call | solution.py:30
  36.3 0.1 collective-permute-start.8
  36.4 0.6 %collective-permute-start.9 = (bf16[2,96,128]{2,1,0:T(8,128)(2,1)S(1)}, bf16[2,96,128]{2,1,0:T(8,128)(2,1)S(1)}, u32[]{:S(2)}, u32[]{:S(2)}) collective-permute-start(bf16[2,96,128]{2,1,0:T(8,128)(2,1)S(1)} %get-tuple-element.58), channel_id=1, source_target_pairs={{0,4},{4,0},{8,12},{12,8},{16,20},{20,16},{24,28},{28,24},{1,5},{5... | collective-permute-start | bytes 147464 | tf_op jit(solution)/shard_map/ppermute | solution.py:285
  37.0 1.3 %collective-permute-start.10 = (bf16[2,96,128]{2,1,0:T(8,128)(2,1)S(1)}, bf16[2,96,128]{2,1,0:T(8,128)(2,1)S(1)}, u32[]{:S(2)}, u32[]{:S(2)}) collective-permute-start(bf16[2,96,128]{2,1,0:T(8,128)(2,1)S(1)} %get-tuple-element.59), channel_id=1, source_target_pairs={{0,1},{1,0},{2,3},{3,2},{4,5},{5,4},{6,7},{7,6},{8,9},{9,8},{10,11... | collective-permute-start | bytes 147464 | tf_op jit(solution)/shard_map/ppermute | solution.py:289
  38.3 1.7 %collective-permute-done.8.cross_ref = bf16[2,96,128]{2,1,0:T(8,128)(2,1)S(1)} collective-permute-done((bf16[2,96,128]{2,1,0:T(8,128)(2,1)S(1)}, bf16[2,96,128]{2,1,0:T(8,128)(2,1)S(1)}, u32[]{:S(2)}, u32[]{:S(2)}) %collective-permute-start.8) | collective-permute-done | bytes 49184 | tf_op jit(solution)/shard_map/ppermute | solution.py:296
  39.9 1.1 %collective-permute-done.9.y_ref = bf16[2,96,128]{2,1,0:T(8,128)(2,1)S(1)} collective-permute-done((bf16[2,96,128]{2,1,0:T(8,128)(2,1)S(1)}, bf16[2,96,128]{2,1,0:T(8,128)(2,1)S(1)}, u32[]{:S(2)}, u32[]{:S(2)}) %collective-permute-start.9) | collective-permute-done | bytes 49184 | tf_op jit(solution)/shard_map/ppermute | solution.py:285
  41.0 0.0 collective-permute-done.10.core_ref
  41.0 0.0 collective-permute-done.11.refs_4_
  41.0 0.4 shard_map.72
  41.4 1.2 %collective-permute-start.12 = (bf16[96,1792]{1,0:T(8,128)(2,1)S(1)}, bf16[96,1792]{1,0:T(8,128)(2,1)S(1)}, u32[]{:S(2)}, u32[]{:S(2)}) collective-permute-start(bf16[96,1792]{1,0:T(8,128)(2,1)S(1)} %get-tuple-element.68), channel_id=1, source_target_pairs={{2,0},{3,1},{0,2},{1,3},{6,4},{7,5},{4,6},{5,7},{10,8},{11,9},{8,1... | collective-permute-start | bytes 1032200 | tf_op jit(solution)/shard_map/ppermute | solution.py:301
  42.5 0.0 collective-permute-done.13.refs_2_
  42.5 0.0 collective-permute-start.14
  42.5 0.5 collective-permute-start.15
  43.1 0.0 collective-permute-start.16
  43.1 1.0 %shard_map.73.near_ref = f32[96,5120]{1,0:T(8,128)S(1)} custom-call(bf16[96,512]{1,0:T(8,128)(2,1)S(1)} %get-tuple-element.67.a_ref, bf16[256,5120]{1,0:T(8,128)(2,1)S(1)} %copy-done, bf16[256,5120]{1,0:T(8,128)(2,1)S(1)} %collective-permute-done.1.wp_ref), custom_call_target="tpu_custom_call" | custom-call | flops 15099494400 | bytes 1048576 | tf_op jit(solution)/shard_map/pallas_call | solution.py:30
  44.1 7.3 %collective-permute-done.12.far_ref = bf16[96,1792]{1,0:T(8,128)(2,1)S(1)} collective-permute-done((bf16[96,1792]{1,0:T(8,128)(2,1)S(1)}, bf16[96,1792]{1,0:T(8,128)(2,1)S(1)}, u32[]{:S(2)}, u32[]{:S(2)}) %collective-permute-start.12) | collective-permute-done | bytes 344096 | tf_op jit(solution)/shard_map/ppermute | solution.py:301
  51.4 0.0 collective-permute-done.14.refs_1_
  51.4 0.0 collective-permute-done.15.refs_3_
  51.4 0.0 collective-permute-done.16.refs_5_
  51.4 1.6 %shard_map.74 = bf16[96,5120]{1,0:T(8,128)(2,1)} custom-call(s32[1]{0:T(128)} %bitcast.tile_ref, f32[96,5120]{1,0:T(8,128)S(1)} %shard_map.73.near_ref, bf16[96,1792]{1,0:T(8,128)(2,1)S(1)} %collective-permute-done.12.far_ref, bf16[256,1280]{1,0:T(8,128)(2,1)S(1)} %collective-permute-done.4.refs_0_, bf16[256,1280]{1,0:T(8,128)(2,1)S(1)} %collective-permute-done.14.refs_1_, ...), custom_call_target="tpu_custom_call" | custom-call | flops 503316480 | bytes 1048576 | tf_op jit(solution)/shard_map/pallas_call | solution.py:30
  (4 shorter events, 0.2 us)
Async XLA Ops:
  0.0 3.4 %copy-start = (bf16[256,5120]{1,0:T(8,128)(2,1)S(1)}, bf16[256,5120]{1,0:T(8,128)(2,1)}, u32[]{:S(2)}) copy-start(bf16[256,5120]{1,0:T(8,128)(2,1)} %w_ref.5) | copy-start | bytes 7864324
  3.3 3.2 %copy-start.3 = (bf16[1168,128]{1,0:T(8,128)(2,1)S(1)}, bf16[1168,128]{1,0:T(8,128)(2,1)}, u32[]{:S(2)}) copy-start(bf16[1168,128]{1,0:T(8,128)(2,1)} %get-tuple-element.39) | copy-start | bytes 897028
  3.3 4.7 %copy-start.1 = (bf16[768,128]{1,0:T(8,128)(2,1)S(1)}, bf16[768,128]{1,0:T(8,128)(2,1)}, u32[]{:S(2)}) copy-start(bf16[768,128]{1,0:T(8,128)(2,1)} %get-tuple-element.40.keep_kv_ref) | copy-start | bytes 589828
  3.4 9.8 %copy-start.2 = (bf16[400,128]{1,0:T(8,128)(2,1)S(1)}, bf16[400,128]{1,0:T(8,128)(2,1)}, u32[]{:S(2)}) copy-start(bf16[400,128]{1,0:T(8,128)(2,1)} %get-tuple-element.42.keep_q_ref) | copy-start | bytes 307204
  3.4 14.5 %collective-permute-start.1 = (bf16[256,5120]{1,0:T(8,128)(2,1)S(1)}, bf16[256,5120]{1,0:T(8,128)(2,1)S(1)}, u32[]{:S(2)}, u32[]{:S(2)}) collective-permute-start(bf16[256,5120]{1,0:T(8,128)(2,1)S(1)} %copy-done), channel_id=1, source_target_pairs={{0,1},{1,0},{2,3},{3,2},{4,5},{5,4},{6,7},{7,6},{8,9},{9,8},{10,11... | collective-permute-start | bytes 7864328 | tf_op jit(solution)/shard_map/ppermute | solution.py:289
  3.9 19.3 %collective-permute-start.4 = (bf16[256,1280]{1,0:T(8,128)(2,1)S(1)}, bf16[256,1280]{1,0:T(8,128)(2,1)S(1)}, u32[]{:S(2)}, u32[]{:S(2)}) collective-permute-start(bf16[256,1280]{1,0:T(8,128)(2,1)S(1)} %shard_map.68), channel_id=1, source_target_pairs={{2,0},{3,1},{0,2},{1,3},{6,4},{7,5},{4,6},{5,7},{10,8},{11,9},{8,1... | collective-permute-start | bytes 1966088 | tf_op jit(solution)/shard_map/ppermute | solution.py:301
  6.5 11.4 %collective-permute-start = (bf16[1168,128]{1,0:T(8,128)(2,1)S(1)}, bf16[1168,128]{1,0:T(8,128)(2,1)S(1)}, u32[]{:S(2)}, u32[]{:S(2)}) collective-permute-start(bf16[1168,128]{1,0:T(8,128)(2,1)S(1)} %copy-done.3), channel_id=1, source_target_pairs={{0,4},{4,0},{8,12},{12,8},{16,20},{20,16},{24,28},{28,24},{1,5},{5... | collective-permute-start | bytes 897032 | tf_op jit(solution)/shard_map/ppermute | solution.py:285
  8.0 5.2 %collective-permute-start.3 = (bf16[768,128]{1,0:T(8,128)(2,1)S(1)}, bf16[768,128]{1,0:T(8,128)(2,1)S(1)}, u32[]{:S(2)}, u32[]{:S(2)}) collective-permute-start(bf16[768,128]{1,0:T(8,128)(2,1)S(1)} %copy-done.1), channel_id=1, source_target_pairs={{8,16},{16,8},{12,20},{20,12},{9,17},{17,9},{13,21},{21,13},{10,18... | collective-permute-start | bytes 589832 | tf_op jit(solution)/shard_map/ppermute | solution.py:281
  8.7 9.2 %collective-permute-start.2 = (bf16[768,128]{1,0:T(8,128)(2,1)S(1)}, bf16[768,128]{1,0:T(8,128)(2,1)S(1)}, u32[]{:S(2)}, u32[]{:S(2)}) collective-permute-start(bf16[768,128]{1,0:T(8,128)(2,1)S(1)} %copy-done.1), channel_id=1, source_target_pairs={{0,8},{8,0},{4,12},{12,4},{16,24},{24,16},{20,28},{28,20},{1,9},{9... | collective-permute-start | bytes 589832 | tf_op jit(solution)/shard_map/ppermute | solution.py:281
  17.9 11.4 %collective-permute-start.6 = (bf16[768,128]{1,0:T(8,128)(2,1)S(1)}, bf16[768,128]{1,0:T(8,128)(2,1)S(1)}, u32[]{:S(2)}, u32[]{:S(2)}) collective-permute-start(bf16[768,128]{1,0:T(8,128)(2,1)S(1)} %get-tuple-element.52.came_ref), channel_id=1, source_target_pairs={{8,16},{16,8},{12,20},{20,12},{9,17},{17,9},{13,21},{21,13},{10,18... | collective-permute-start | bytes 589832 | tf_op jit(solution)/shard_map/ppermute | solution.py:281
  18.6 10.7 %collective-permute-start.5 = (bf16[768,128]{1,0:T(8,128)(2,1)S(1)}, bf16[768,128]{1,0:T(8,128)(2,1)S(1)}, u32[]{:S(2)}, u32[]{:S(2)}) collective-permute-start(bf16[768,128]{1,0:T(8,128)(2,1)S(1)} %get-tuple-element.52.came_ref), channel_id=1, source_target_pairs={{0,8},{8,0},{4,12},{12,4},{16,24},{24,16},{20,28},{28,20},{1,9},{9... | collective-permute-start | bytes 589832 | tf_op jit(solution)/shard_map/ppermute | solution.py:281
  22.1 12.9 %collective-permute-start.7 = (bf16[768,128]{1,0:T(8,128)(2,1)S(1)}, bf16[768,128]{1,0:T(8,128)(2,1)S(1)}, u32[]{:S(2)}, u32[]{:S(2)}) collective-permute-start(bf16[768,128]{1,0:T(8,128)(2,1)S(1)} %get-tuple-element.55), channel_id=1, source_target_pairs={{0,16},{16,0},{4,20},{20,4},{8,24},{24,8},{12,28},{28,12},{1,17},{... | collective-permute-start | bytes 589832 | tf_op jit(solution)/shard_map/ppermute | solution.py:281
  23.2 19.3 %collective-permute-start.13 = (bf16[256,1280]{1,0:T(8,128)(2,1)S(1)}, bf16[256,1280]{1,0:T(8,128)(2,1)S(1)}, u32[]{:S(2)}, u32[]{:S(2)}) collective-permute-start(bf16[256,1280]{1,0:T(8,128)(2,1)S(1)} %collective-permute-done.4.refs_0_), channel_id=1, source_target_pairs={{0,4},{4,0},{8,12},{12,8},{16,20},{20,16},{24,28},{28,24},{1,5},{5... | collective-permute-start | bytes 1966088 | tf_op jit(solution)/shard_map/ppermute | solution.py:285
  23.7 17.3 %collective-permute-start.11 = (bf16[256,1280]{1,0:T(8,128)(2,1)S(1)}, bf16[256,1280]{1,0:T(8,128)(2,1)S(1)}, u32[]{:S(2)}, u32[]{:S(2)}) collective-permute-start(bf16[256,1280]{1,0:T(8,128)(2,1)S(1)} %shard_map.66), channel_id=1, source_target_pairs={{2,0},{3,1},{0,2},{1,3},{6,4},{7,5},{4,6},{5,7},{10,8},{11,9},{8,1... | collective-permute-start | bytes 1966088 | tf_op jit(solution)/shard_map/ppermute | solution.py:301
  36.3 3.6 %collective-permute-start.8 = (bf16[2,96,128]{2,1,0:T(8,128)(2,1)S(1)}, bf16[2,96,128]{2,1,0:T(8,128)(2,1)S(1)}, u32[]{:S(2)}, u32[]{:S(2)}) collective-permute-start(bf16[2,96,128]{2,1,0:T(8,128)(2,1)S(1)} %get-tuple-element.57), channel_id=1, source_target_pairs={{0,5},{1,4},{2,7},{3,6},{4,1},{5,0},{6,3},{7,2},{8,13},{9,12},{10,... | collective-permute-start | bytes 147464 | tf_op jit(solution)/shard_map/ppermute | solution.py:296
  36.4 4.6 %collective-permute-start.9 = (bf16[2,96,128]{2,1,0:T(8,128)(2,1)S(1)}, bf16[2,96,128]{2,1,0:T(8,128)(2,1)S(1)}, u32[]{:S(2)}, u32[]{:S(2)}) collective-permute-start(bf16[2,96,128]{2,1,0:T(8,128)(2,1)S(1)} %get-tuple-element.58), channel_id=1, source_target_pairs={{0,4},{4,0},{8,12},{12,8},{16,20},{20,16},{24,28},{28,24},{1,5},{5... | collective-permute-start | bytes 147464 | tf_op jit(solution)/shard_map/ppermute | solution.py:285
  37.0 4.0 %collective-permute-start.10 = (bf16[2,96,128]{2,1,0:T(8,128)(2,1)S(1)}, bf16[2,96,128]{2,1,0:T(8,128)(2,1)S(1)}, u32[]{:S(2)}, u32[]{:S(2)}) collective-permute-start(bf16[2,96,128]{2,1,0:T(8,128)(2,1)S(1)} %get-tuple-element.59), channel_id=1, source_target_pairs={{0,1},{1,0},{2,3},{3,2},{4,5},{5,4},{6,7},{7,6},{8,9},{9,8},{10,11... | collective-permute-start | bytes 147464 | tf_op jit(solution)/shard_map/ppermute | solution.py:289
  41.4 10.1 %collective-permute-start.12 = (bf16[96,1792]{1,0:T(8,128)(2,1)S(1)}, bf16[96,1792]{1,0:T(8,128)(2,1)S(1)}, u32[]{:S(2)}, u32[]{:S(2)}) collective-permute-start(bf16[96,1792]{1,0:T(8,128)(2,1)S(1)} %get-tuple-element.68), channel_id=1, source_target_pairs={{2,0},{3,1},{0,2},{1,3},{6,4},{7,5},{4,6},{5,7},{10,8},{11,9},{8,1... | collective-permute-start | bytes 1032200 | tf_op jit(solution)/shard_map/ppermute | solution.py:301
  42.5 8.9 %collective-permute-start.14 = (bf16[256,1280]{1,0:T(8,128)(2,1)S(1)}, bf16[256,1280]{1,0:T(8,128)(2,1)S(1)}, u32[]{:S(2)}, u32[]{:S(2)}) collective-permute-start(bf16[256,1280]{1,0:T(8,128)(2,1)S(1)} %collective-permute-done.4.refs_0_), channel_id=1, source_target_pairs={{0,1},{1,0},{2,3},{3,2},{4,5},{5,4},{6,7},{7,6},{8,9},{9,8},{10,11... | collective-permute-start | bytes 1966088 | tf_op jit(solution)/shard_map/ppermute | solution.py:289
  42.5 8.9 %collective-permute-start.15 = (bf16[256,1280]{1,0:T(8,128)(2,1)S(1)}, bf16[256,1280]{1,0:T(8,128)(2,1)S(1)}, u32[]{:S(2)}, u32[]{:S(2)}) collective-permute-start(bf16[256,1280]{1,0:T(8,128)(2,1)S(1)} %collective-permute-done.13.refs_2_), channel_id=1, source_target_pairs={{0,1},{1,0},{2,3},{3,2},{4,5},{5,4},{6,7},{7,6},{8,9},{9,8},{10,11... | collective-permute-start | bytes 1966088 | tf_op jit(solution)/shard_map/ppermute | solution.py:289
  43.1 8.4 %collective-permute-start.16 = (bf16[256,1280]{1,0:T(8,128)(2,1)S(1)}, bf16[256,1280]{1,0:T(8,128)(2,1)S(1)}, u32[]{:S(2)}, u32[]{:S(2)}) collective-permute-start(bf16[256,1280]{1,0:T(8,128)(2,1)S(1)} %collective-permute-done.11.refs_4_), channel_id=1, source_target_pairs={{0,1},{1,0},{2,3},{3,2},{4,5},{5,4},{6,7},{7,6},{8,9},{9,8},{10,11... | collective-permute-start | bytes 1966088 | tf_op jit(solution)/shard_map/ppermute | solution.py:289
